TPU v7x, 32 devices: a whole 2x2x4 slice. The times are simulated.
32 devices in a mesh: tm: 8 (over z, x), space: 4 (over y, core).
Axes of the slice: x: 2, y: 2, z: 4, core: 2. Of those that a mesh axis runs over, the one named last changes fastest.
Arguments:
- layer_input: bfloat16 [8, 512, 2048], P('tm', 'space'), may hold values from -6 to 6
- frame_real: int32 [8], replicated, may hold values from 0 to 1, as said below
- gain_attn: bfloat16 [2048], P(('tm', 'space')), may hold values from 0.5 to 1.5
- w_qkv: bfloat16 [2048, 6144], P(('tm', 'space')), may hold values from -0.125 to 0.125
- w_out: bfloat16 [2048, 2048], P(('tm', 'space')), may hold values from -1.5 to 1.5
- gain_mlp: bfloat16 [2048], P(('tm', 'space')), may hold values from 0.5 to 1.5
- w_up: bfloat16 [2048, 8192], P(('tm', 'space')), may hold values from -0.125 to 0.125
- w_down: bfloat16 [2048, 8192], P(('tm', 'space')), may hold values from -0.0625 to 0.0625
- cotangent: bfloat16 [8, 512, 2048], P('tm', 'space'), may hold values from -6 to 6
Outputs:
- out: bfloat16 [8, 512, 2048], P('tm', 'space')
- grad_input: float32 [8, 512, 2048], P('tm', 'space')
- grad_gain_attn: float32 [2048], P(('tm', 'space'))
- grad_w_qkv: float32 [2048, 6144], P(('tm', 'space'))
- grad_w_out: float32 [2048, 2048], P(('tm', 'space'))
- grad_gain_mlp: float32 [2048], P(('tm', 'space'))
- grad_w_up: float32 [2048, 8192], P(('tm', 'space'))
- grad_w_down: float32 [2048, 8192], P(('tm', 'space'))
Inputs may be any that keep to these rules, and one draw needn't show every extreme that they name: `frame_real`: in every clip of 8 slots the first two frames and the last frame are real.
All inputs are finite; a program needn't handle non-finite values.
Results may differ from a plain program's by a relative error of at most 0.015.
Values may be sent and summed in bfloat16 or wider, within the bound.
No kernel may reach another device: no remote copies, remote signals or barrier semaphores. Data moves between devices by JAX's collectives and lax.ppermute only.
A program may use at most 512 MiB of HBM per device.

v0:
```python
import jax
import jax.numpy as jnp
from jax import lax
from jax.sharding import PartitionSpec as P

HEADS = 16
HEAD = 128


epsilon = 1e-05
masked_value = -1e30


def passed_along(value, axis, steps):
    count = lax.axis_size(axis)
    initial, last = (max(0, -steps), min(count, count - steps))
    return lax.ppermute(value, axis, [(source, source + steps) for source in range(initial, last)])


def from_behind(block, axis, distance):
    devices = range(lax.axis_size(axis))
    route = [((i - distance) % len(devices), i) for i in devices]
    return lax.ppermute(block, axis, route)


def layer_norm(values):
    center = jnp.mean(values, axis=-1, keepdims=True)
    shifted = values - center
    spread = jnp.mean(shifted * shifted, axis=-1, keepdims=True)
    return shifted * lax.rsqrt(spread + epsilon)


def rope_tables(positions):
    half_dim = HEAD // 2
    inverse_freq = jnp.exp(-jnp.log(10000.0) * jnp.arange(half_dim, dtype=jnp.float32) * 2.0 / HEAD)
    angles = positions.astype(jnp.float32)[:, None] * inverse_freq[None, :]
    angles = jnp.concatenate([angles, angles], axis=-1)
    return (jnp.cos(angles), jnp.sin(angles))


def rotate(tensor, cosine_table, sine_table):
    half_dim = HEAD // 2
    turned = jnp.concatenate([-tensor[..., half_dim:], tensor[..., :half_dim]], axis=-1)
    return tensor * cosine_table[:, None, :] + turned * sine_table[:, None, :]


def rotate_back(grads, cosine_table, sine_table):
    half_dim = HEAD // 2
    scaled = grads * sine_table[:, None, :]
    turned = jnp.concatenate([scaled[..., half_dim:], -scaled[..., :half_dim]], axis=-1)
    return grads * cosine_table[:, None, :] + turned


def on_device(layer_input, frame_real, gain_attn, w_qkv, w_out, gain_mlp, w_up, w_down, cotangent):
    n_rows = layer_input.shape[1]
    model_width = layer_input.shape[2]
    time_count = lax.axis_size("tm")
    space_count = lax.axis_size("space")
    clip_len = min(16, time_count)
    frame_len = n_rows * space_count
    time_index = lax.axis_index("tm")
    space_index = lax.axis_index("space")
    inv_root = HEAD ** (-0.5)
    inputs = layer_input[0].astype(jnp.float32)
    grad_out = cotangent[0]
    grad_float = grad_out.astype(jnp.float32)
    local_slot = time_index % clip_len
    places = space_index * n_rows + jnp.arange(n_rows, dtype=jnp.int32)
    cosine_table, sine_table = rope_tables(local_slot * frame_len + places)
    own_real = frame_real[time_index] > 0
    causal = jnp.arange(frame_len, dtype=jnp.int32)[None, :] <= places[:, None]

    def block_mask(turn_index):
        source = (time_index - turn_index) % time_count
        earlier = (local_slot >= turn_index) & own_real & (frame_real[source] > 0)
        return jnp.where(turn_index == 0, causal, earlier)

    def block_scores(queries, key_block, turn_index):
        scores = (
            jnp.einsum("rhe,khe->hrk", queries, key_block, preferred_element_type=jnp.float32)
            * inv_root
        )
        return (scores, block_mask(turn_index)[None, :, :])

    def pass_keys(key_block, value_block):
        return passed_along((key_block, value_block), "tm", 1)

    def whole_frame(key_rows, value_rows):
        return (
            lax.all_gather(key_rows, "space", axis=0, tiled=True),
            lax.all_gather(value_rows, "space", axis=0, tiled=True),
        )

    normed_one = layer_norm(inputs)

    def attention_weights():
        gain_piece = lax.all_gather(gain_attn, ("tm", "space"), axis=0, tiled=True)
        qkv_piece = lax.all_gather(w_qkv, ("tm", "space"), axis=0, tiled=True)
        out_piece = lax.all_gather(w_out, ("tm", "space"), axis=0, tiled=True)
        scaled = (normed_one * gain_piece.astype(jnp.float32)).astype(jnp.bfloat16)
        mixed_rows = jnp.dot(scaled, qkv_piece, preferred_element_type=jnp.float32)
        gain_full = gain_piece.astype(jnp.float32)
        return (mixed_rows, gain_full, out_piece)

    def split_heads(mixed_rows):
        query_heads = rotate(
            mixed_rows[:, :model_width].reshape(n_rows, HEADS, HEAD), cosine_table, sine_table
        )
        key_heads = rotate(
            mixed_rows[:, model_width : 2 * model_width].reshape(n_rows, HEADS, HEAD),
            cosine_table,
            sine_table,
        )
        value_heads = mixed_rows[:, 2 * model_width :].reshape(n_rows, HEADS, HEAD)
        return (
            query_heads.astype(jnp.bfloat16),
            key_heads.astype(jnp.bfloat16),
            value_heads.astype(jnp.bfloat16),
        )

    mixed_rows, gain_one, out_matrix = attention_weights()
    query_heads, key_heads, value_heads = split_heads(mixed_rows)
    frame_keys, frame_values = whole_frame(key_heads, value_heads)

    def chain_sweep(key_block, value_block, update, carry_state):
        carry_state = update(carry_state, key_block, value_block, 0)

        def one_turn(turn_index, carried):
            moved_keys, moved_values = pass_keys(carried[0], carried[1])
            return (
                moved_keys,
                moved_values,
                update(carried[2], moved_keys, moved_values, turn_index),
            )

        return lax.fori_loop(1, clip_len, one_turn, (key_block, value_block, carry_state))[2]

    def next_blocks(key_block, value_block):
        return pass_keys(key_block, value_block)

    def stats_update(carry_state, key_block, value_block, turn_index):
        row_max, row_total = carry_state
        scores, allowed = block_scores(query_heads, key_block, turn_index)
        scores = jnp.where(allowed, scores, masked_value)
        new_max = jnp.maximum(row_max, jnp.max(scores, axis=-1))
        row_total = row_total * jnp.exp(row_max - new_max) + jnp.sum(
            jnp.exp(scores - new_max[:, :, None]), axis=-1
        )
        return (new_max, row_total)

    stats_start = (
        jnp.full((HEADS, n_rows), masked_value, jnp.float32),
        jnp.zeros((HEADS, n_rows), jnp.float32),
    )
    row_max, row_total = chain_sweep(frame_keys, frame_values, stats_update, stats_start)
    log_total = row_max + jnp.log(row_total)

    def output_update(carry_state, key_block, value_block, turn_index):
        scores, allowed = block_scores(query_heads, key_block, turn_index)
        probs = jnp.where(allowed, jnp.exp(scores - log_total[:, :, None]), 0.0)
        return carry_state + jnp.einsum(
            "hrk,khe->rhe",
            probs.astype(jnp.bfloat16),
            value_block,
            preferred_element_type=jnp.float32,
        )

    attended = chain_sweep(
        frame_keys, frame_values, output_update, jnp.zeros((n_rows, HEADS, HEAD), jnp.float32)
    )
    attended_low = attended.reshape(n_rows, model_width).astype(jnp.bfloat16)
    middle = inputs + jnp.dot(attended_low, out_matrix, preferred_element_type=jnp.float32)
    normed_two = layer_norm(middle)
    gain_full = jnp.zeros((model_width,), jnp.float32)
    gain_piece = lax.all_gather(gain_mlp, ("tm", "space"), axis=0, tiled=True)
    up_rows = lax.all_gather(w_up, ("tm", "space"), axis=0, tiled=True)
    scaled = (normed_two * gain_piece.astype(jnp.float32)).astype(jnp.bfloat16)
    hidden_sum = jnp.dot(scaled, up_rows, preferred_element_type=jnp.float32)
    gain_full = gain_piece.astype(jnp.float32)
    gain_two = gain_full
    activated = jax.nn.gelu(hidden_sum).astype(jnp.bfloat16)
    shard_rows = lax.all_gather(w_down, ("tm", "space"), axis=0, tiled=True)
    out_part = jnp.dot(activated, shard_rows.T, preferred_element_type=jnp.float32)
    grad_part = jnp.dot(grad_out, shard_rows, preferred_element_type=jnp.float32)
    output = (middle + out_part).astype(jnp.bfloat16)
    gelu_value, gelu_back = jax.vjp(jax.nn.gelu, hidden_sum)
    grad_hidden = gelu_back(grad_part)[0].astype(jnp.bfloat16)
    grad_second = jnp.dot(
        grad_hidden,
        lax.all_gather(w_up, ("tm", "space"), axis=0, tiled=True).T,
        preferred_element_type=jnp.float32,
    )
    norm_value, norm_two_back = jax.vjp(lambda values: layer_norm(values) * gain_two, middle)
    grad_middle = grad_float + norm_two_back(grad_second)[0]
    grad_gain_two = jnp.sum(grad_second * normed_two, axis=0)
    grad_middle_low = grad_middle.astype(jnp.bfloat16)
    mixed_again, gain_again, out_again = attention_weights()
    grad_attended = jnp.dot(
        grad_middle_low, out_again.T, preferred_element_type=jnp.float32
    ).astype(jnp.bfloat16)
    query_again, key_again, value_again = split_heads(mixed_again)
    keys_again, values_again = whole_frame(key_again, value_again)
    grad_heads = grad_attended.reshape(n_rows, HEADS, HEAD)
    row_delta = jnp.einsum("rhe,rhe->hr", grad_heads.astype(jnp.float32), attended)

    def grad_block(key_block, value_block, turn_index):
        scores, allowed = block_scores(query_again, key_block, turn_index)
        probs = jnp.where(allowed, jnp.exp(scores - log_total[:, :, None]), 0.0)
        grad_probs = jnp.einsum(
            "rhe,khe->hrk", grad_heads, value_block, preferred_element_type=jnp.float32
        )
        grad_scores = (probs * (grad_probs - row_delta[:, :, None])).astype(jnp.bfloat16)
        grad_query = (
            jnp.einsum("hrk,khe->rhe", grad_scores, key_block, preferred_element_type=jnp.float32)
            * inv_root
        )
        grad_key = (
            jnp.einsum("hrk,rhe->khe", grad_scores, query_again, preferred_element_type=jnp.float32)
            * inv_root
        )
        grad_value = jnp.einsum(
            "hrk,rhe->khe",
            probs.astype(jnp.bfloat16),
            grad_heads,
            preferred_element_type=jnp.float32,
        )
        return (grad_query, grad_key, grad_value)

    first_query, first_key, first_value = grad_block(keys_again, values_again, 0)

    def back_turn(turn_index, carried):
        key_block, value_block, key_sum, value_sum, query_sum = carried
        key_block, value_block = next_blocks(key_block, value_block)
        key_sum, value_sum = (
            from_behind(key_sum.astype(jnp.bfloat16), "tm", 1).astype(key_sum.dtype),
            from_behind(value_sum.astype(jnp.bfloat16), "tm", 1).astype(value_sum.dtype),
        )
        part_query, part_key, part_value = grad_block(key_block, value_block, turn_index)
        return (
            key_block,
            value_block,
            key_sum + part_key,
            value_sum + part_value,
            query_sum + part_query,
        )

    finished = lax.fori_loop(
        1, clip_len, back_turn, (keys_again, values_again, first_key, first_value, first_query)
    )
    key_sum, value_sum, query_sum = (finished[2], finished[3], finished[4])
    key_home = from_behind(key_sum.astype(jnp.bfloat16), "tm", 1 - clip_len).astype(key_sum.dtype)
    value_home = from_behind(value_sum.astype(jnp.bfloat16), "tm", 1 - clip_len).astype(
        value_sum.dtype
    )
    key_total = lax.psum_scatter(
        key_home.astype(jnp.bfloat16), "space", scatter_dimension=0, tiled=True
    ).astype(jnp.float32)
    value_total = lax.psum_scatter(
        value_home.astype(jnp.bfloat16), "space", scatter_dimension=0, tiled=True
    ).astype(jnp.float32)
    grad_query_rows = rotate_back(query_sum, cosine_table, sine_table).reshape(n_rows, model_width)
    grad_key_rows = rotate_back(key_total, cosine_table, sine_table).reshape(n_rows, model_width)
    grad_value_rows = value_total.reshape(n_rows, model_width)
    grad_mixed = jnp.concatenate([grad_query_rows, grad_key_rows, grad_value_rows], axis=1).astype(
        jnp.bfloat16
    )
    grad_first = jnp.dot(
        grad_mixed,
        lax.all_gather(w_qkv, ("tm", "space"), axis=0, tiled=True).T,
        preferred_element_type=jnp.float32,
    )
    first_value_out, norm_one_back = jax.vjp(lambda values: layer_norm(values) * gain_one, inputs)
    grad_inputs = grad_middle + norm_one_back(grad_first)[0]
    grad_gain_one = jnp.sum(grad_first * normed_one, axis=0)
    first_low = (normed_one * gain_one).astype(jnp.bfloat16)
    second_low = (normed_two * gain_two).astype(jnp.bfloat16)
    results = (
        lax.psum_scatter(grad_gain_one, ("tm", "space"), scatter_dimension=0, tiled=True),
        lax.psum_scatter(
            jnp.dot(first_low.T, grad_mixed, preferred_element_type=jnp.float32),
            ("tm", "space"),
            scatter_dimension=0,
            tiled=True,
        ),
        lax.psum_scatter(
            jnp.dot(attended_low.T, grad_middle_low, preferred_element_type=jnp.float32),
            ("tm", "space"),
            scatter_dimension=0,
            tiled=True,
        ),
        lax.psum_scatter(grad_gain_two, ("tm", "space"), scatter_dimension=0, tiled=True),
        lax.psum_scatter(
            jnp.dot(second_low.T, grad_hidden, preferred_element_type=jnp.float32),
            ("tm", "space"),
            scatter_dimension=0,
            tiled=True,
        ),
        lax.psum_scatter(
            jnp.dot(grad_out.T, activated, preferred_element_type=jnp.float32),
            ("tm", "space"),
            scatter_dimension=0,
            tiled=True,
        ),
    )
    return (
        output[None],
        grad_inputs[None],
        results[0],
        results[1],
        results[2],
        results[3],
        results[4],
        results[5],
    )


def solution(mesh):
    placed = (
        P("tm", "space", None),
        P(),
        P(("tm", "space")),
        P(("tm", "space"), None),
        P(("tm", "space"), None),
        P(("tm", "space")),
        P(("tm", "space"), None),
        P(("tm", "space"), None),
        P("tm", "space", None),
    )
    return jax.shard_map(
        on_device,
        mesh=mesh,
        in_specs=placed,
        out_specs=(
            P("tm", "space", None),
            P("tm", "space", None),
            P(("tm", "space")),
            P(("tm", "space"), None),
            P(("tm", "space"), None),
            P(("tm", "space")),
            P(("tm", "space"), None),
            P(("tm", "space"), None),
        ),
        check_vma=False,
    )
```

profile of v0, /device:TPU:0, one launch (start us, length us, event | category | flops | bytes accessed | tf_op | source)
XLA Modules:
  0.0 5132.4 jit_solution(12868934773100808273)
XLA Ops:
  9.7 43.3 all-reduce.5
  55.5 114.0 %all-gather.7.cloned.1.call-done = bf16[2048,6144]{1,0:T(8,128)(2,1)} async-done(((bf16[64,6144]{1,0:T(8,128)(2,1)}), bf16[2048,6144]{1,0:T(8,128)(2,1)}) %all-gather.7.cloned.1.call-update) | async-done | bytes 25165840 | tf_op jit(solution)/shard_map/all_gather | solution.py:98
  237.4 591.5 %while.64 = (s32[]{:T(128)}, bf16[512,16,128]{2,0,1:T(8,128)(2,1)}, f32[16,128]{1,0:T(8,128)S(1)}, f32[16,128]{1,0:T(8,128)S(1)}, s32[]{:T(128)}, /*index=5*/pre...) while((s32[]{:T(128)}, bf16[512,16,128]{2,0,1:T(8,128)(2,1)}, ...), condition=%wide.region_7.8_spmd.clone, body=%wide.region_4.7_spmd.clone.sunk | while | flops 275910688 | bytes 23896960 | solution.py:136
  242.3 56.9 %collective-permute-done = bf16[512,16,128]{2,0,1:T(8,128)(2,1)S(1)} collective-permute-done((bf16[512,16,128]{2,0,1:T(8,128)(2,1)}, bf16[512,16,128]{2,0,1:T(8,128)(2,1)S(1)}, u32[]{:S(2)}, u32[]{:S(2)}) %collective-permute-start) | collective-permute-done | bytes 2097184 | tf_op jit(solution)/shard_map/while/body/eval_jaxpr/ppermute | solution.py:17
  323.1 50.7 collective-permute-done
  401.0 66.7 %collective-permute-done = bf16[512,16,128]{2,0,1:T(8,128)(2,1)S(1)} collective-permute-done((bf16[512,16,128]{2,0,1:T(8,128)(2,1)}, bf16[512,16,128]{2,0,1:T(8,128)(2,1)S(1)}, u32[]{:S(2)}, u32[]{:S(2)}) %collective-permute-start) | collective-permute-done | bytes 2097184 | tf_op jit(solution)/shard_map/while/body/eval_jaxpr/ppermute | solution.py:17
  491.6 89.2 %collective-permute-done = bf16[512,16,128]{2,0,1:T(8,128)(2,1)S(1)} collective-permute-done((bf16[512,16,128]{2,0,1:T(8,128)(2,1)}, bf16[512,16,128]{2,0,1:T(8,128)(2,1)S(1)}, u32[]{:S(2)}, u32[]{:S(2)}) %collective-permute-start) | collective-permute-done | bytes 2097184 | tf_op jit(solution)/shard_map/while/body/eval_jaxpr/ppermute | solution.py:17
  591.1 43.3 collective-permute-done
  637.9 35.8 collective-permute-start
  675.1 53.9 %collective-permute-done = bf16[512,16,128]{2,0,1:T(8,128)(2,1)S(1)} collective-permute-done((bf16[512,16,128]{2,0,1:T(8,128)(2,1)}, bf16[512,16,128]{2,0,1:T(8,128)(2,1)S(1)}, u32[]{:S(2)}, u32[]{:S(2)}) %collective-permute-start) | collective-permute-done | bytes 2097184 | tf_op jit(solution)/shard_map/while/body/eval_jaxpr/ppermute | solution.py:17
  732.5 33.9 collective-permute-start
  767.8 57.5 %collective-permute-done = bf16[512,16,128]{2,0,1:T(8,128)(2,1)S(1)} collective-permute-done((bf16[512,16,128]{2,0,1:T(8,128)(2,1)}, bf16[512,16,128]{2,0,1:T(8,128)(2,1)S(1)}, u32[]{:S(2)}, u32[]{:S(2)}) %collective-permute-start) | collective-permute-done | bytes 2097184 | tf_op jit(solution)/shard_map/while/body/eval_jaxpr/ppermute | solution.py:17
  837.4 758.4 %while.65 = (s32[]{:T(128)}, bf16[512,16,128]{2,0,1:T(8,128)(2,1)}, bf16[512,16,128]{2,0,1:T(8,128)(2,1)}, f32[128,16,128]{2,0,1:T(8,128)}, s32[]{:T(128)}, /*in...) while((s32[]{:T(128)}, bf16[512,16,128]{2,0,1:T(8,128)(2,1)}, ...), condition=%wide.region_9.10_spmd.clone, body=%wide.region_8.9_spmd.clone.sunk | while | flops 541458432 | bytes 32121768 | solution.py:136
  837.4 30.3 collective-permute-start.1
  884.8 30.9 collective-permute-done.1
  917.0 42.3 collective-permute-done.2
  966.7 48.3 collective-permute-start.1
  1022.8 38.4 collective-permute-done.1
  1062.5 38.2 collective-permute-done.2
  1124.8 35.0 collective-permute-done.1
  1161.0 37.3 collective-permute-done.2
  1223.4 38.3 collective-permute-done.1
  1263.1 37.4 collective-permute-done.2
  1321.2 38.4 collective-permute-done.1
  1360.8 36.5 collective-permute-done.2
  1418.0 38.4 collective-permute-done.1
  1457.7 35.6 collective-permute-done.2
  1513.9 38.4 collective-permute-done.1
  1553.6 34.6 collective-permute-done.2
  1684.5 1269.0 %while.66 = (s32[]{:T(128)}, bf16[512,16,128]{2,0,1:T(8,128)(2,1)}, bf16[512,16,128]{2,0,1:T(8,128)(2,1)}, bf16[512,16,128]{2,0,1:T(8,128)(2,1)}, bf16[512,16,12...) while((s32[]{:T(128)}, bf16[512,16,128]{2,0,1:T(8,128)(2,1)}, ...), condition=%wide.region_15.16_spmd.clone, body=%wide.region_14.15_spmd.clone.sunk | while | flops 1360658432 | bytes 90399856 | solution.py:247
  1703.3 33.0 collective-permute-done.3
  1737.7 43.6 collective-permute-done.4
  1785.1 41.1 collective-permute-done.6
  1833.8 27.5 collective-permute-done.5
  1885.7 33.0 collective-permute-done.3
  1920.1 43.6 collective-permute-done.4
  1967.5 41.1 collective-permute-done.6
  2016.1 26.6 collective-permute-done.5
  2067.1 33.0 collective-permute-done.3
  2101.5 43.6 collective-permute-done.4
  2149.0 41.1 collective-permute-done.6
  2247.8 33.0 collective-permute-done.3
  2282.2 43.6 collective-permute-done.4
  2329.6 41.1 collective-permute-done.6
  2428.4 33.0 collective-permute-done.3
  2462.8 43.6 collective-permute-done.4
  2510.2 41.1 collective-permute-done.6
  2558.8 25.8 collective-permute-done.5
  2609.0 33.0 collective-permute-done.3
  2643.4 43.6 collective-permute-done.4
  2690.8 41.1 collective-permute-done.6
  2789.6 33.0 collective-permute-done.3
  2824.0 43.6 collective-permute-done.4
  2871.4 41.1 collective-permute-done.6
  2920.1 27.6 collective-permute-done.5
  2956.9 37.1 collective-permute-done.7
  3002.8 32.7 collective-permute-done.8
  3052.3 33.5 reduce-scatter.19.cloned.1.call-done
  3136.8 26.4 convolution_bitcast_fusion
  3163.2 61.6 %copy.109 = f32[2048,8192]{1,0:T(8,128)} copy(f32[2048,8192]{0,1:T(8,128)} %convolution_bitcast_fusion) | data formatting | bytes 134217728
  3257.2 41.7 all-reduce.4
  3301.6 410.7 %reduce-scatter.13.cloned.1.call-done = f32[64,6144]{1,0:T(8,128)} async-done(((f32[2048,6144]{1,0:T(8,128)}), f32[64,6144]{1,0:T(8,128)}) %reduce-scatter.13.cloned.1.call-update) | async-done | bytes 1572880 | tf_op jit(solution)/shard_map/reduce_scatter | solution.py:279
  3712.3 704.3 %reduce-scatter.17.cloned.1.call-done = f32[64,8192]{1,0:T(8,128)} async-done(((f32[2048,8192]{1,0:T(8,128)}), f32[64,8192]{1,0:T(8,128)}) %reduce-scatter.17.cloned.1.call-update) | async-done | bytes 2097168 | tf_op jit(solution)/shard_map/reduce_scatter | solution.py:292
  4416.6 708.7 %reduce-scatter.21.cloned.1.call-done = f32[64,8192]{1,0:T(8,128)} async-done(((f32[2048,8192]{1,0:T(8,128)}), f32[64,8192]{1,0:T(8,128)}) %reduce-scatter.21.cloned.1.call-update) | async-done | bytes 2097168
  (441 shorter events, 870.0 us)
Async XLA Ops:
  7.2 162.3 %all-gather.7.cloned.1.call-start = ((), (), s32[]{:S(2)}) async-start(), calls=%async_computation.6 | async-start | bytes 25952256 | tf_op jit(solution)/shard_map/all_gather | solution.py:98
  7.9 195.8 %all-gather.11.cloned.1.call-start = ((), (), s32[]{:S(2)}) async-start(), calls=%async_computation.8 | async-start | bytes 2621440 | tf_op jit(solution)/shard_map/all_gather | solution.py:91
  182.5 45.9 all-gather.9.cloned.1.call-start
  187.2 1410.0 %all-gather.13.cloned.1.call-start = ((), (), s32[]{:S(2)}) async-start(), calls=%async_computation.9 | async-start | bytes 8650752 | tf_op jit(solution)/shard_map/all_gather | solution.py:99
  187.8 1414.7 %all-gather.15.cloned.1.call-start = ((), (), s32[]{:S(2)}) async-start(), calls=%async_computation.10 | async-start | bytes 34603008 | tf_op jit(solution)/shard_map/all_gather | solution.py:176
  188.4 1431.4 %all-gather.17.cloned.1.call-start = ((), (), s32[]{:S(2)}) async-start(), calls=%async_computation.11 | async-start | bytes 34603008 | tf_op jit(solution)/shard_map/all_gather | solution.py:182
  189.0 2858.7 %reduce-scatter.11.cloned.1.call-start = ((), (), s32[]{:S(2)}) async-start(), calls=%async_computation.12 | async-start | bytes 2621440 | tf_op jit(solution)/shard_map/reduce_scatter | solution.py:255
  237.4 61.8 %collective-permute-start = (bf16[512,16,128]{2,0,1:T(8,128)(2,1)}, bf16[512,16,128]{2,0,1:T(8,128)(2,1)S(1)}, u32[]{:S(2)}, u32[]{:S(2)}) collective-permute-start(bf16[512,16,128]{2,0,1:T(8,128)(2,1)} %get-tuple-element.1411), channel_id=1, source_target_pairs={{0,4},{4,8},{8,12},{12,16},{16,20},{20,24},{24,28},{1,5},{5,9},{9,... | collective-permute-start | bytes 6291464 | tf_op jit(solution)/shard_map/while/body/eval_jaxpr/ppermute | solution.py:17
  302.8 71.0 %collective-permute-start = (bf16[512,16,128]{2,0,1:T(8,128)(2,1)}, bf16[512,16,128]{2,0,1:T(8,128)(2,1)S(1)}, u32[]{:S(2)}, u32[]{:S(2)}) collective-permute-start(bf16[512,16,128]{2,0,1:T(8,128)(2,1)} %get-tuple-element.1411), channel_id=1, source_target_pairs={{0,4},{4,8},{8,12},{12,16},{16,20},{20,24},{24,28},{1,5},{5,9},{9,... | collective-permute-start | bytes 6291464 | tf_op jit(solution)/shard_map/while/body/eval_jaxpr/ppermute | solution.py:17
  377.3 90.4 %collective-permute-start = (bf16[512,16,128]{2,0,1:T(8,128)(2,1)}, bf16[512,16,128]{2,0,1:T(8,128)(2,1)S(1)}, u32[]{:S(2)}, u32[]{:S(2)}) collective-permute-start(bf16[512,16,128]{2,0,1:T(8,128)(2,1)} %get-tuple-element.1411), channel_id=1, source_target_pairs={{0,4},{4,8},{8,12},{12,16},{16,20},{20,24},{24,28},{1,5},{5,9},{9,... | collective-permute-start | bytes 6291464 | tf_op jit(solution)/shard_map/while/body/eval_jaxpr/ppermute | solution.py:17
  471.3 109.5 %collective-permute-start = (bf16[512,16,128]{2,0,1:T(8,128)(2,1)}, bf16[512,16,128]{2,0,1:T(8,128)(2,1)S(1)}, u32[]{:S(2)}, u32[]{:S(2)}) collective-permute-start(bf16[512,16,128]{2,0,1:T(8,128)(2,1)} %get-tuple-element.1411), channel_id=1, source_target_pairs={{0,4},{4,8},{8,12},{12,16},{16,20},{20,24},{24,28},{1,5},{5,9},{9,... | collective-permute-start | bytes 6291464 | tf_op jit(solution)/shard_map/while/body/eval_jaxpr/ppermute | solution.py:17
  584.4 50.0 collective-permute-start
  637.9 91.1 %collective-permute-start = (bf16[512,16,128]{2,0,1:T(8,128)(2,1)}, bf16[512,16,128]{2,0,1:T(8,128)(2,1)S(1)}, u32[]{:S(2)}, u32[]{:S(2)}) collective-permute-start(bf16[512,16,128]{2,0,1:T(8,128)(2,1)} %get-tuple-element.1411), channel_id=1, source_target_pairs={{0,4},{4,8},{8,12},{12,16},{16,20},{20,24},{24,28},{1,5},{5,9},{9,... | collective-permute-start | bytes 6291464 | tf_op jit(solution)/shard_map/while/body/eval_jaxpr/ppermute | solution.py:17
  732.5 92.8 %collective-permute-start = (bf16[512,16,128]{2,0,1:T(8,128)(2,1)}, bf16[512,16,128]{2,0,1:T(8,128)(2,1)S(1)}, u32[]{:S(2)}, u32[]{:S(2)}) collective-permute-start(bf16[512,16,128]{2,0,1:T(8,128)(2,1)} %get-tuple-element.1411), channel_id=1, source_target_pairs={{0,4},{4,8},{8,12},{12,16},{16,20},{20,24},{24,28},{1,5},{5,9},{9,... | collective-permute-start | bytes 6291464 | tf_op jit(solution)/shard_map/while/body/eval_jaxpr/ppermute | solution.py:17
  837.4 759.9 %copy-start.7 = (bf16[1,128,2048]{2,1,0:T(8,128)(2,1)S(1)}, bf16[1,128,2048]{2,1,0:T(8,128)(2,1)}, u32[]{:S(2)}) copy-start(bf16[1,128,2048]{2,1,0:T(8,128)(2,1)} %param.15) | copy-start | bytes 1572868
  837.4 78.4 %collective-permute-start.1 = (bf16[512,16,128]{2,0,1:T(8,128)(2,1)}, bf16[512,16,128]{2,0,1:T(8,128)(2,1)S(1)}, u32[]{:S(2)}, u32[]{:S(2)}) collective-permute-start(bf16[512,16,128]{2,0,1:T(8,128)(2,1)} %get-tuple-element.1457), channel_id=1, source_target_pairs={{0,4},{4,8},{8,12},{12,16},{16,20},{20,24},{24,28},{1,5},{5,9},{9,... | collective-permute-start | bytes 6291464 | tf_op jit(solution)/shard_map/while/body/eval_jaxpr/ppermute | solution.py:17
  867.7 91.6 %collective-permute-start.2 = (bf16[512,16,128]{2,0,1:T(8,128)(2,1)}, bf16[512,16,128]{2,0,1:T(8,128)(2,1)}, u32[]{:S(2)}, u32[]{:S(2)}) collective-permute-start(bf16[512,16,128]{2,0,1:T(8,128)(2,1)} %get-tuple-element.1458), channel_id=1, source_target_pairs={{0,4},{4,8},{8,12},{12,16},{16,20},{20,24},{24,28},{1,5},{5,9},{9,... | collective-permute-start | bytes 6291464 | tf_op jit(solution)/shard_map/while/body/eval_jaxpr/ppermute | solution.py:17
  966.7 94.5 %collective-permute-start.1 = (bf16[512,16,128]{2,0,1:T(8,128)(2,1)}, bf16[512,16,128]{2,0,1:T(8,128)(2,1)S(1)}, u32[]{:S(2)}, u32[]{:S(2)}) collective-permute-start(bf16[512,16,128]{2,0,1:T(8,128)(2,1)} %get-tuple-element.1457), channel_id=1, source_target_pairs={{0,4},{4,8},{8,12},{12,16},{16,20},{20,24},{24,28},{1,5},{5,9},{9,... | collective-permute-start | bytes 6291464 | tf_op jit(solution)/shard_map/while/body/eval_jaxpr/ppermute | solution.py:17
  1014.9 85.8 %collective-permute-start.2 = (bf16[512,16,128]{2,0,1:T(8,128)(2,1)}, bf16[512,16,128]{2,0,1:T(8,128)(2,1)}, u32[]{:S(2)}, u32[]{:S(2)}) collective-permute-start(bf16[512,16,128]{2,0,1:T(8,128)(2,1)} %get-tuple-element.1458), channel_id=1, source_target_pairs={{0,4},{4,8},{8,12},{12,16},{16,20},{20,24},{24,28},{1,5},{5,9},{9,... | collective-permute-start | bytes 6291464 | tf_op jit(solution)/shard_map/while/body/eval_jaxpr/ppermute | solution.py:17
  1108.1 51.7 %collective-permute-start.1 = (bf16[512,16,128]{2,0,1:T(8,128)(2,1)}, bf16[512,16,128]{2,0,1:T(8,128)(2,1)S(1)}, u32[]{:S(2)}, u32[]{:S(2)}) collective-permute-start(bf16[512,16,128]{2,0,1:T(8,128)(2,1)} %get-tuple-element.1457), channel_id=1, source_target_pairs={{0,4},{4,8},{8,12},{12,16},{16,20},{20,24},{24,28},{1,5},{5,9},{9,... | collective-permute-start | bytes 6291464 | tf_op jit(solution)/shard_map/while/body/eval_jaxpr/ppermute | solution.py:17
  1113.5 84.9 %collective-permute-start.2 = (bf16[512,16,128]{2,0,1:T(8,128)(2,1)}, bf16[512,16,128]{2,0,1:T(8,128)(2,1)}, u32[]{:S(2)}, u32[]{:S(2)}) collective-permute-start(bf16[512,16,128]{2,0,1:T(8,128)(2,1)} %get-tuple-element.1458), channel_id=1, source_target_pairs={{0,4},{4,8},{8,12},{12,16},{16,20},{20,24},{24,28},{1,5},{5,9},{9,... | collective-permute-start | bytes 6291464 | tf_op jit(solution)/shard_map/while/body/eval_jaxpr/ppermute | solution.py:17
  1205.7 56.1 %collective-permute-start.1 = (bf16[512,16,128]{2,0,1:T(8,128)(2,1)}, bf16[512,16,128]{2,0,1:T(8,128)(2,1)S(1)}, u32[]{:S(2)}, u32[]{:S(2)}) collective-permute-start(bf16[512,16,128]{2,0,1:T(8,128)(2,1)} %get-tuple-element.1457), channel_id=1, source_target_pairs={{0,4},{4,8},{8,12},{12,16},{16,20},{20,24},{24,28},{1,5},{5,9},{9,... | collective-permute-start | bytes 6291464 | tf_op jit(solution)/shard_map/while/body/eval_jaxpr/ppermute | solution.py:17
  1215.5 85.0 %collective-permute-start.2 = (bf16[512,16,128]{2,0,1:T(8,128)(2,1)}, bf16[512,16,128]{2,0,1:T(8,128)(2,1)}, u32[]{:S(2)}, u32[]{:S(2)}) collective-permute-start(bf16[512,16,128]{2,0,1:T(8,128)(2,1)} %get-tuple-element.1458), channel_id=1, source_target_pairs={{0,4},{4,8},{8,12},{12,16},{16,20},{20,24},{24,28},{1,5},{5,9},{9,... | collective-permute-start | bytes 6291464 | tf_op jit(solution)/shard_map/while/body/eval_jaxpr/ppermute | solution.py:17
  1307.8 51.7 %collective-permute-start.1 = (bf16[512,16,128]{2,0,1:T(8,128)(2,1)}, bf16[512,16,128]{2,0,1:T(8,128)(2,1)S(1)}, u32[]{:S(2)}, u32[]{:S(2)}) collective-permute-start(bf16[512,16,128]{2,0,1:T(8,128)(2,1)} %get-tuple-element.1457), channel_id=1, source_target_pairs={{0,4},{4,8},{8,12},{12,16},{16,20},{20,24},{24,28},{1,5},{5,9},{9,... | collective-permute-start | bytes 6291464 | tf_op jit(solution)/shard_map/while/body/eval_jaxpr/ppermute | solution.py:17
  1313.3 84.1 %collective-permute-start.2 = (bf16[512,16,128]{2,0,1:T(8,128)(2,1)}, bf16[512,16,128]{2,0,1:T(8,128)(2,1)}, u32[]{:S(2)}, u32[]{:S(2)}) collective-permute-start(bf16[512,16,128]{2,0,1:T(8,128)(2,1)} %get-tuple-element.1458), channel_id=1, source_target_pairs={{0,4},{4,8},{8,12},{12,16},{16,20},{20,24},{24,28},{1,5},{5,9},{9,... | collective-permute-start | bytes 6291464 | tf_op jit(solution)/shard_map/while/body/eval_jaxpr/ppermute | solution.py:17
  1404.7 51.7 %collective-permute-start.1 = (bf16[512,16,128]{2,0,1:T(8,128)(2,1)}, bf16[512,16,128]{2,0,1:T(8,128)(2,1)S(1)}, u32[]{:S(2)}, u32[]{:S(2)}) collective-permute-start(bf16[512,16,128]{2,0,1:T(8,128)(2,1)} %get-tuple-element.1457), channel_id=1, source_target_pairs={{0,4},{4,8},{8,12},{12,16},{16,20},{20,24},{24,28},{1,5},{5,9},{9,... | collective-permute-start | bytes 6291464 | tf_op jit(solution)/shard_map/while/body/eval_jaxpr/ppermute | solution.py:17
  1410.1 83.1 %collective-permute-start.2 = (bf16[512,16,128]{2,0,1:T(8,128)(2,1)}, bf16[512,16,128]{2,0,1:T(8,128)(2,1)}, u32[]{:S(2)}, u32[]{:S(2)}) collective-permute-start(bf16[512,16,128]{2,0,1:T(8,128)(2,1)} %get-tuple-element.1458), channel_id=1, source_target_pairs={{0,4},{4,8},{8,12},{12,16},{16,20},{20,24},{24,28},{1,5},{5,9},{9,... | collective-permute-start | bytes 6291464 | tf_op jit(solution)/shard_map/while/body/eval_jaxpr/ppermute | solution.py:17
  1500.6 51.7 %collective-permute-start.1 = (bf16[512,16,128]{2,0,1:T(8,128)(2,1)}, bf16[512,16,128]{2,0,1:T(8,128)(2,1)S(1)}, u32[]{:S(2)}, u32[]{:S(2)}) collective-permute-start(bf16[512,16,128]{2,0,1:T(8,128)(2,1)} %get-tuple-element.1457), channel_id=1, source_target_pairs={{0,4},{4,8},{8,12},{12,16},{16,20},{20,24},{24,28},{1,5},{5,9},{9,... | collective-permute-start | bytes 6291464 | tf_op jit(solution)/shard_map/while/body/eval_jaxpr/ppermute | solution.py:17
  1506.0 82.2 %collective-permute-start.2 = (bf16[512,16,128]{2,0,1:T(8,128)(2,1)}, bf16[512,16,128]{2,0,1:T(8,128)(2,1)}, u32[]{:S(2)}, u32[]{:S(2)}) collective-permute-start(bf16[512,16,128]{2,0,1:T(8,128)(2,1)} %get-tuple-element.1458), channel_id=1, source_target_pairs={{0,4},{4,8},{8,12},{12,16},{16,20},{20,24},{24,28},{1,5},{5,9},{9,... | collective-permute-start | bytes 6291464 | tf_op jit(solution)/shard_map/while/body/eval_jaxpr/ppermute | solution.py:17
  1684.7 51.7 %collective-permute-start.3 = (bf16[512,16,128]{2,0,1:T(8,128)(2,1)}, bf16[512,16,128]{2,0,1:T(8,128)(2,1)S(1)}, u32[]{:S(2)}, u32[]{:S(2)}) collective-permute-start(bf16[512,16,128]{2,0,1:T(8,128)(2,1)} %get-tuple-element.1509), channel_id=1, source_target_pairs={{0,4},{4,8},{8,12},{12,16},{16,20},{20,24},{24,28},{1,5},{5,9},{9,... | collective-permute-start | bytes 6291464 | tf_op jit(solution)/shard_map/while/body/eval_jaxpr/ppermute | solution.py:17
  1690.1 91.2 %collective-permute-start.4 = (bf16[512,16,128]{2,0,1:T(8,128)(2,1)}, bf16[512,16,128]{2,0,1:T(8,128)(2,1)}, u32[]{:S(2)}, u32[]{:S(2)}) collective-permute-start(bf16[512,16,128]{2,0,1:T(8,128)(2,1)} %get-tuple-element.1510), channel_id=1, source_target_pairs={{0,4},{4,8},{8,12},{12,16},{16,20},{20,24},{24,28},{1,5},{5,9},{9,... | collective-permute-start | bytes 6291464 | tf_op jit(solution)/shard_map/while/body/eval_jaxpr/ppermute | solution.py:17
  1696.6 129.6 %collective-permute-start.6 = (bf16[512,16,128]{2,0,1:T(8,128)(2,1)}, bf16[512,16,128]{2,0,1:T(8,128)(2,1)}, u32[]{:S(2)}, u32[]{:S(2)}) collective-permute-start(bf16[512,16,128]{2,0,1:T(8,128)(2,1)} %get-tuple-element.1512), channel_id=1, source_target_pairs={{28,0},{0,4},{4,8},{8,12},{12,16},{16,20},{20,24},{24,28},{29,1},{... | collective-permute-start | bytes 6291464 | tf_op jit(solution)/shard_map/while/body/eval_jaxpr/ppermute | solution.py:23
  1698.6 162.7 %collective-permute-start.5 = (bf16[512,16,128]{2,0,1:T(8,128)(2,1)}, bf16[512,16,128]{2,0,1:T(8,128)(2,1)}, u32[]{:S(2)}, u32[]{:S(2)}) collective-permute-start(bf16[512,16,128]{2,0,1:T(8,128)(2,1)} %get-tuple-element.1511), channel_id=1, source_target_pairs={{28,0},{0,4},{4,8},{8,12},{12,16},{16,20},{20,24},{24,28},{29,1},{... | collective-permute-start | bytes 6291464 | tf_op jit(solution)/shard_map/while/body/eval_jaxpr/ppermute | solution.py:23
  1867.1 51.7 %collective-permute-start.3 = (bf16[512,16,128]{2,0,1:T(8,128)(2,1)}, bf16[512,16,128]{2,0,1:T(8,128)(2,1)S(1)}, u32[]{:S(2)}, u32[]{:S(2)}) collective-permute-start(bf16[512,16,128]{2,0,1:T(8,128)(2,1)} %get-tuple-element.1509), channel_id=1, source_target_pairs={{0,4},{4,8},{8,12},{12,16},{16,20},{20,24},{24,28},{1,5},{5,9},{9,... | collective-permute-start | bytes 6291464 | tf_op jit(solution)/shard_map/while/body/eval_jaxpr/ppermute | solution.py:17
  1872.5 91.2 %collective-permute-start.4 = (bf16[512,16,128]{2,0,1:T(8,128)(2,1)}, bf16[512,16,128]{2,0,1:T(8,128)(2,1)}, u32[]{:S(2)}, u32[]{:S(2)}) collective-permute-start(bf16[512,16,128]{2,0,1:T(8,128)(2,1)} %get-tuple-element.1510), channel_id=1, source_target_pairs={{0,4},{4,8},{8,12},{12,16},{16,20},{20,24},{24,28},{1,5},{5,9},{9,... | collective-permute-start | bytes 6291464 | tf_op jit(solution)/shard_map/while/body/eval_jaxpr/ppermute | solution.py:17
  1879.0 129.6 %collective-permute-start.6 = (bf16[512,16,128]{2,0,1:T(8,128)(2,1)}, bf16[512,16,128]{2,0,1:T(8,128)(2,1)}, u32[]{:S(2)}, u32[]{:S(2)}) collective-permute-start(bf16[512,16,128]{2,0,1:T(8,128)(2,1)} %get-tuple-element.1512), channel_id=1, source_target_pairs={{28,0},{0,4},{4,8},{8,12},{12,16},{16,20},{20,24},{24,28},{29,1},{... | collective-permute-start | bytes 6291464 | tf_op jit(solution)/shard_map/while/body/eval_jaxpr/ppermute | solution.py:23
  1881.0 161.8 %collective-permute-start.5 = (bf16[512,16,128]{2,0,1:T(8,128)(2,1)}, bf16[512,16,128]{2,0,1:T(8,128)(2,1)}, u32[]{:S(2)}, u32[]{:S(2)}) collective-permute-start(bf16[512,16,128]{2,0,1:T(8,128)(2,1)} %get-tuple-element.1511), channel_id=1, source_target_pairs={{28,0},{0,4},{4,8},{8,12},{12,16},{16,20},{20,24},{24,28},{29,1},{... | collective-permute-start | bytes 6291464 | tf_op jit(solution)/shard_map/while/body/eval_jaxpr/ppermute | solution.py:23
  2048.5 51.7 %collective-permute-start.3 = (bf16[512,16,128]{2,0,1:T(8,128)(2,1)}, bf16[512,16,128]{2,0,1:T(8,128)(2,1)S(1)}, u32[]{:S(2)}, u32[]{:S(2)}) collective-permute-start(bf16[512,16,128]{2,0,1:T(8,128)(2,1)} %get-tuple-element.1509), channel_id=1, source_target_pairs={{0,4},{4,8},{8,12},{12,16},{16,20},{20,24},{24,28},{1,5},{5,9},{9,... | collective-permute-start | bytes 6291464 | tf_op jit(solution)/shard_map/while/body/eval_jaxpr/ppermute | solution.py:17
  2053.9 91.2 %collective-permute-start.4 = (bf16[512,16,128]{2,0,1:T(8,128)(2,1)}, bf16[512,16,128]{2,0,1:T(8,128)(2,1)}, u32[]{:S(2)}, u32[]{:S(2)}) collective-permute-start(bf16[512,16,128]{2,0,1:T(8,128)(2,1)} %get-tuple-element.1510), channel_id=1, source_target_pairs={{0,4},{4,8},{8,12},{12,16},{16,20},{20,24},{24,28},{1,5},{5,9},{9,... | collective-permute-start | bytes 6291464 | tf_op jit(solution)/shard_map/while/body/eval_jaxpr/ppermute | solution.py:17
  2060.5 129.6 %collective-permute-start.6 = (bf16[512,16,128]{2,0,1:T(8,128)(2,1)}, bf16[512,16,128]{2,0,1:T(8,128)(2,1)}, u32[]{:S(2)}, u32[]{:S(2)}) collective-permute-start(bf16[512,16,128]{2,0,1:T(8,128)(2,1)} %get-tuple-element.1512), channel_id=1, source_target_pairs={{28,0},{0,4},{4,8},{8,12},{12,16},{16,20},{20,24},{24,28},{29,1},{... | collective-permute-start | bytes 6291464 | tf_op jit(solution)/shard_map/while/body/eval_jaxpr/ppermute | solution.py:23
  2062.4 160.9 %collective-permute-start.5 = (bf16[512,16,128]{2,0,1:T(8,128)(2,1)}, bf16[512,16,128]{2,0,1:T(8,128)(2,1)}, u32[]{:S(2)}, u32[]{:S(2)}) collective-permute-start(bf16[512,16,128]{2,0,1:T(8,128)(2,1)} %get-tuple-element.1511), channel_id=1, source_target_pairs={{28,0},{0,4},{4,8},{8,12},{12,16},{16,20},{20,24},{24,28},{29,1},{... | collective-permute-start | bytes 6291464 | tf_op jit(solution)/shard_map/while/body/eval_jaxpr/ppermute | solution.py:23
  2229.1 51.7 %collective-permute-start.3 = (bf16[512,16,128]{2,0,1:T(8,128)(2,1)}, bf16[512,16,128]{2,0,1:T(8,128)(2,1)S(1)}, u32[]{:S(2)}, u32[]{:S(2)}) collective-permute-start(bf16[512,16,128]{2,0,1:T(8,128)(2,1)} %get-tuple-element.1509), channel_id=1, source_target_pairs={{0,4},{4,8},{8,12},{12,16},{16,20},{20,24},{24,28},{1,5},{5,9},{9,... | collective-permute-start | bytes 6291464 | tf_op jit(solution)/shard_map/while/body/eval_jaxpr/ppermute | solution.py:17
  2234.5 91.2 %collective-permute-start.4 = (bf16[512,16,128]{2,0,1:T(8,128)(2,1)}, bf16[512,16,128]{2,0,1:T(8,128)(2,1)}, u32[]{:S(2)}, u32[]{:S(2)}) collective-permute-start(bf16[512,16,128]{2,0,1:T(8,128)(2,1)} %get-tuple-element.1510), channel_id=1, source_target_pairs={{0,4},{4,8},{8,12},{12,16},{16,20},{20,24},{24,28},{1,5},{5,9},{9,... | collective-permute-start | bytes 6291464 | tf_op jit(solution)/shard_map/while/body/eval_jaxpr/ppermute | solution.py:17
  2241.1 129.6 %collective-permute-start.6 = (bf16[512,16,128]{2,0,1:T(8,128)(2,1)}, bf16[512,16,128]{2,0,1:T(8,128)(2,1)}, u32[]{:S(2)}, u32[]{:S(2)}) collective-permute-start(bf16[512,16,128]{2,0,1:T(8,128)(2,1)} %get-tuple-element.1512), channel_id=1, source_target_pairs={{28,0},{0,4},{4,8},{8,12},{12,16},{16,20},{20,24},{24,28},{29,1},{... | collective-permute-start | bytes 6291464 | tf_op jit(solution)/shard_map/while/body/eval_jaxpr/ppermute | solution.py:23
  2243.0 160.9 %collective-permute-start.5 = (bf16[512,16,128]{2,0,1:T(8,128)(2,1)}, bf16[512,16,128]{2,0,1:T(8,128)(2,1)}, u32[]{:S(2)}, u32[]{:S(2)}) collective-permute-start(bf16[512,16,128]{2,0,1:T(8,128)(2,1)} %get-tuple-element.1511), channel_id=1, source_target_pairs={{28,0},{0,4},{4,8},{8,12},{12,16},{16,20},{20,24},{24,28},{29,1},{... | collective-permute-start | bytes 6291464 | tf_op jit(solution)/shard_map/while/body/eval_jaxpr/ppermute | solution.py:23
  2409.8 51.7 %collective-permute-start.3 = (bf16[512,16,128]{2,0,1:T(8,128)(2,1)}, bf16[512,16,128]{2,0,1:T(8,128)(2,1)S(1)}, u32[]{:S(2)}, u32[]{:S(2)}) collective-permute-start(bf16[512,16,128]{2,0,1:T(8,128)(2,1)} %get-tuple-element.1509), channel_id=1, source_target_pairs={{0,4},{4,8},{8,12},{12,16},{16,20},{20,24},{24,28},{1,5},{5,9},{9,... | collective-permute-start | bytes 6291464 | tf_op jit(solution)/shard_map/while/body/eval_jaxpr/ppermute | solution.py:17
  2415.2 91.2 %collective-permute-start.4 = (bf16[512,16,128]{2,0,1:T(8,128)(2,1)}, bf16[512,16,128]{2,0,1:T(8,128)(2,1)}, u32[]{:S(2)}, u32[]{:S(2)}) collective-permute-start(bf16[512,16,128]{2,0,1:T(8,128)(2,1)} %get-tuple-element.1510), channel_id=1, source_target_pairs={{0,4},{4,8},{8,12},{12,16},{16,20},{20,24},{24,28},{1,5},{5,9},{9,... | collective-permute-start | bytes 6291464 | tf_op jit(solution)/shard_map/while/body/eval_jaxpr/ppermute | solution.py:17
  2421.7 129.6 %collective-permute-start.6 = (bf16[512,16,128]{2,0,1:T(8,128)(2,1)}, bf16[512,16,128]{2,0,1:T(8,128)(2,1)}, u32[]{:S(2)}, u32[]{:S(2)}) collective-permute-start(bf16[512,16,128]{2,0,1:T(8,128)(2,1)} %get-tuple-element.1512), channel_id=1, source_target_pairs={{28,0},{0,4},{4,8},{8,12},{12,16},{16,20},{20,24},{24,28},{29,1},{... | collective-permute-start | bytes 6291464 | tf_op jit(solution)/shard_map/while/body/eval_jaxpr/ppermute | solution.py:23
  2423.6 160.9 %collective-permute-start.5 = (bf16[512,16,128]{2,0,1:T(8,128)(2,1)}, bf16[512,16,128]{2,0,1:T(8,128)(2,1)}, u32[]{:S(2)}, u32[]{:S(2)}) collective-permute-start(bf16[512,16,128]{2,0,1:T(8,128)(2,1)} %get-tuple-element.1511), channel_id=1, source_target_pairs={{28,0},{0,4},{4,8},{8,12},{12,16},{16,20},{20,24},{24,28},{29,1},{... | collective-permute-start | bytes 6291464 | tf_op jit(solution)/shard_map/while/body/eval_jaxpr/ppermute | solution.py:23
  2590.4 51.7 %collective-permute-start.3 = (bf16[512,16,128]{2,0,1:T(8,128)(2,1)}, bf16[512,16,128]{2,0,1:T(8,128)(2,1)S(1)}, u32[]{:S(2)}, u32[]{:S(2)}) collective-permute-start(bf16[512,16,128]{2,0,1:T(8,128)(2,1)} %get-tuple-element.1509), channel_id=1, source_target_pairs={{0,4},{4,8},{8,12},{12,16},{16,20},{20,24},{24,28},{1,5},{5,9},{9,... | collective-permute-start | bytes 6291464 | tf_op jit(solution)/shard_map/while/body/eval_jaxpr/ppermute | solution.py:17
  2595.8 91.2 %collective-permute-start.4 = (bf16[512,16,128]{2,0,1:T(8,128)(2,1)}, bf16[512,16,128]{2,0,1:T(8,128)(2,1)}, u32[]{:S(2)}, u32[]{:S(2)}) collective-permute-start(bf16[512,16,128]{2,0,1:T(8,128)(2,1)} %get-tuple-element.1510), channel_id=1, source_target_pairs={{0,4},{4,8},{8,12},{12,16},{16,20},{20,24},{24,28},{1,5},{5,9},{9,... | collective-permute-start | bytes 6291464 | tf_op jit(solution)/shard_map/while/body/eval_jaxpr/ppermute | solution.py:17
  2602.3 129.6 %collective-permute-start.6 = (bf16[512,16,128]{2,0,1:T(8,128)(2,1)}, bf16[512,16,128]{2,0,1:T(8,128)(2,1)}, u32[]{:S(2)}, u32[]{:S(2)}) collective-permute-start(bf16[512,16,128]{2,0,1:T(8,128)(2,1)} %get-tuple-element.1512), channel_id=1, source_target_pairs={{28,0},{0,4},{4,8},{8,12},{12,16},{16,20},{20,24},{24,28},{29,1},{... | collective-permute-start | bytes 6291464 | tf_op jit(solution)/shard_map/while/body/eval_jaxpr/ppermute | solution.py:23
  2604.3 160.9 %collective-permute-start.5 = (bf16[512,16,128]{2,0,1:T(8,128)(2,1)}, bf16[512,16,128]{2,0,1:T(8,128)(2,1)}, u32[]{:S(2)}, u32[]{:S(2)}) collective-permute-start(bf16[512,16,128]{2,0,1:T(8,128)(2,1)} %get-tuple-element.1511), channel_id=1, source_target_pairs={{28,0},{0,4},{4,8},{8,12},{12,16},{16,20},{20,24},{24,28},{29,1},{... | collective-permute-start | bytes 6291464 | tf_op jit(solution)/shard_map/while/body/eval_jaxpr/ppermute | solution.py:23
  2771.0 51.7 %collective-permute-start.3 = (bf16[512,16,128]{2,0,1:T(8,128)(2,1)}, bf16[512,16,128]{2,0,1:T(8,128)(2,1)S(1)}, u32[]{:S(2)}, u32[]{:S(2)}) collective-permute-start(bf16[512,16,128]{2,0,1:T(8,128)(2,1)} %get-tuple-element.1509), channel_id=1, source_target_pairs={{0,4},{4,8},{8,12},{12,16},{16,20},{20,24},{24,28},{1,5},{5,9},{9,... | collective-permute-start | bytes 6291464 | tf_op jit(solution)/shard_map/while/body/eval_jaxpr/ppermute | solution.py:17
  2776.4 91.2 %collective-permute-start.4 = (bf16[512,16,128]{2,0,1:T(8,128)(2,1)}, bf16[512,16,128]{2,0,1:T(8,128)(2,1)}, u32[]{:S(2)}, u32[]{:S(2)}) collective-permute-start(bf16[512,16,128]{2,0,1:T(8,128)(2,1)} %get-tuple-element.1510), channel_id=1, source_target_pairs={{0,4},{4,8},{8,12},{12,16},{16,20},{20,24},{24,28},{1,5},{5,9},{9,... | collective-permute-start | bytes 6291464 | tf_op jit(solution)/shard_map/while/body/eval_jaxpr/ppermute | solution.py:17
  2782.9 129.6 %collective-permute-start.6 = (bf16[512,16,128]{2,0,1:T(8,128)(2,1)}, bf16[512,16,128]{2,0,1:T(8,128)(2,1)}, u32[]{:S(2)}, u32[]{:S(2)}) collective-permute-start(bf16[512,16,128]{2,0,1:T(8,128)(2,1)} %get-tuple-element.1512), channel_id=1, source_target_pairs={{28,0},{0,4},{4,8},{8,12},{12,16},{16,20},{20,24},{24,28},{29,1},{... | collective-permute-start | bytes 6291464 | tf_op jit(solution)/shard_map/while/body/eval_jaxpr/ppermute | solution.py:23
  2784.9 162.8 %collective-permute-start.5 = (bf16[512,16,128]{2,0,1:T(8,128)(2,1)}, bf16[512,16,128]{2,0,1:T(8,128)(2,1)}, u32[]{:S(2)}, u32[]{:S(2)}) collective-permute-start(bf16[512,16,128]{2,0,1:T(8,128)(2,1)} %get-tuple-element.1511), channel_id=1, source_target_pairs={{28,0},{0,4},{4,8},{8,12},{12,16},{16,20},{20,24},{24,28},{29,1},{... | collective-permute-start | bytes 6291464 | tf_op jit(solution)/shard_map/while/body/eval_jaxpr/ppermute | solution.py:23
  2953.5 40.4 collective-permute-start.7
  2995.3 90.5 %reduce-scatter.19.cloned.1.call-start = ((), (), s32[]{:S(2)}) async-start(), calls=%async_computation.16 | async-start | bytes 2621440
  2999.3 36.1 collective-permute-start.8
  3039.4 262.3 %reduce-scatter.15.cloned.1.call-start = ((), (), s32[]{:S(2)}) async-start(), calls=%async_computation.14 | async-start | bytes 17301504 | tf_op jit(solution)/shard_map/reduce_scatter | solution.py:285
  3047.6 664.7 %reduce-scatter.13.cloned.1.call-start = ((), (), s32[]{:S(2)}) async-start(), calls=%async_computation.13 | async-start | bytes 51904512 | tf_op jit(solution)/shard_map/reduce_scatter | solution.py:279
  3109.0 1307.6 %reduce-scatter.17.cloned.1.call-start = ((), (), s32[]{:S(2)}) async-start(), calls=%async_computation.15 | async-start | bytes 69206016 | tf_op jit(solution)/shard_map/reduce_scatter | solution.py:292
  3135.7 1989.5 %reduce-scatter.21.cloned.1.call-start = ((), (), s32[]{:S(2)}) async-start(), calls=%async_computation.17 | async-start | bytes 69206016
  (62 other events, 1644.2 us)
Sparse Core Ops, SparseCore 0:
  10.9 158.5 all-gather.6
  182.7 21.0 all-gather.10
  205.9 22.5 all-gather.8
  231.2 99.7 all-gather.12
  333.7 292.9 all-gather.14
  629.4 303.3 all-gather.16
  2995.5 48.1 reduce-scatter.10
  3046.9 38.8 reduce-scatter.18
  3088.7 183.1 reduce-scatter.14
  3278.8 433.4 reduce-scatter.12
  3715.2 701.3 reduce-scatter.16
  4419.4 705.8 reduce-scatter.20
where the time goes:
time: 5140 us; the launch traced here: 5130 us
  waiting for transfers between devices  4020 us (78%)
  starting transfers between devices  435 us (8%)
  matrix products  330 us (6%)
  local copies, waits for them, and re-layouts  202 us (4%)
  blocking collectives  85 us (2%)
    ppermute x35, waiting for transfers between devices, passed_along(): lax.ppermute(value, axis, [(source, source + steps) for source in range(i...  1470 us
    unnamed x14, waiting for transfers between devices  745 us
    reduce_scatter x1, waiting for transfers between devices, on_device(): lax.psum_scatter(jnp.dot(second_low.T, grad_hidden, preferred_element_typ...  704 us
    ppermute x16, waiting for transfers between devices, from_behind(): return lax.ppermute(block, axis, route)  542 us
    reduce_scatter x1, waiting for transfers between devices, on_device(): lax.psum_scatter(jnp.dot(first_low.T, grad_mixed, preferred_element_type=...  411 us
    ppermute x35, starting transfers between devices, passed_along(): lax.ppermute(value, axis, [(source, source + steps) for source in range(i...  391 us
    all_gather x1, waiting for transfers between devices, attention_weights(): qkv_piece = lax.all_gather(w_qkv, ('tm', 'space'), axis=0, tiled=True)  114 us
  transfers between devices with their start and end apart: 63, of which 58 were waited for; matrix products, arithmetic and copies ran while one was open for 8% of the time, Pallas kernels for 0%

commit v1 on v0

v1 whole, which is shorter than its diff:
```python
import functools

import jax
import jax.numpy as jnp
import numpy as np
from jax import lax
from jax.experimental import pallas as pl
from jax.experimental.pallas import tpu as pltpu
from jax.sharding import PartitionSpec as P

HEADS = 16
HEAD = 128
AXES = ("tm", "space")
BLOCK = 128

epsilon = 1e-05
masked_value = -1e30
inv_root = HEAD ** (-0.5)
to_log2 = inv_root * 1.4426950408889634

bf16 = jnp.bfloat16
f32 = jnp.float32


def matmul(left, right, dims=((1,), (0,))):
    return lax.dot_general(left, right, (dims, ((), ())), preferred_element_type=f32)


def tied(*values):
    return lax.optimization_barrier(values)


class Plan:
    def __init__(self, tm, space, frame_rows):
        self.count = tm * space
        self.space = space
        self.slots = tm
        self.clip = min(16, tm)
        count = self.count
        self.team = (count // 4, space // 2)
        self.heads = (count // 2, count // 8)
        bits = [1 << i for i in range(count.bit_length() - 1)]
        taken = set(self.team + self.heads)
        self.parts = [b for b in reversed(bits) if b not in taken]
        self.gather = [self.heads[0], self.heads[1]] + [b for b in self.parts if b != 1]
        self.team_rel = [0, self.team[1], self.team[0], self.team[0] | self.team[1]]
        self.head_rel = [0, self.heads[1], self.heads[0], self.heads[0] | self.heads[1]]
        self.block_rel = [h | t for h in self.head_rel for t in self.team_rel]
        self.part_rel = [
            sum(b for j, b in enumerate(self.parts) if (i >> j) & 1)
            for i in range(1 << len(self.parts))
        ]
        devices = range(count)
        octet = self.team[0] | self.team[1] | 1
        self.octets = self.groups(octet)
        self.square = sum(self.team) + sum(self.heads)
        self.squares = self.groups(self.square)
        self.square_bits = [b for b in reversed(bits) if b & self.square]
        self.devices = devices

    def groups(self, mask):
        held = {}
        for d in range(self.count):
            held.setdefault(d & ~mask, []).append(d)
        return list(held.values())

    def swap(self, value, mask):
        return lax.ppermute(value, AXES, [(d, d ^ mask) for d in self.devices])


def layer_norm(values):
    center = jnp.mean(values, axis=-1, keepdims=True)
    shifted = values - center
    spread = jnp.mean(shifted * shifted, axis=-1, keepdims=True)
    scale = lax.rsqrt(spread + epsilon)
    return shifted * scale, scale


def layer_norm_back(grads, normed, scale):
    inner = jnp.mean(grads * normed, axis=-1, keepdims=True)
    return (grads - jnp.mean(grads, axis=-1, keepdims=True) - normed * inner) * scale


def transposed(tile):
    return tile.astype(f32).T.astype(tile.dtype)


def attend_kernel(plan, info, real, own, other, out, out_t, lse, keys, values, values_t):
    me = info[0]
    n_blocks = len(plan.block_rel)
    for part, part_rel in enumerate(plan.part_rel):

        def place(b, _, part=part, part_rel=part_rel):
            home = me ^ part_rel ^ info[24 + b]
            if part == 0:
                key, value = own[b, :, HEAD : 2 * HEAD], own[b, :, 2 * HEAD :]
            else:
                key, value = other[part - 1, b, :, :HEAD], other[part - 1, b, :, HEAD:]
            rows = pl.ds(pl.multiple_of(home * BLOCK, BLOCK), BLOCK)
            keys[rows, :] = key
            values[rows, :] = value
            values_t[home] = transposed(value)
            return 0

        lax.fori_loop(0, n_blocks, place, 0)

    frame = plan.space * BLOCK
    two = 2 * BLOCK
    lane = lax.broadcasted_iota(jnp.int32, (1, two), 1)
    q_place = jnp.where(lane < BLOCK, info[1] + lane, info[2] + lane - BLOCK)

    def tile(i, _):
        slot, first = info[8 + i], info[16 + i]
        q = jnp.concatenate([own[2 * i, :, :HEAD], own[2 * i + 1, :, :HEAD]], axis=0)

        def scores(g):
            key = keys[pl.ds(pl.multiple_of(g * frame, frame), frame), :]
            return matmul(key, q, ((1,), (1,)))

        def value_t(g):
            return jnp.concatenate(
                [values_t[g * plan.space + s] for s in range(plan.space)], axis=1
            )

        s = scores(slot)
        k_place = lax.broadcasted_iota(jnp.int32, (frame, two), 0)
        s = jnp.where(k_place <= q_place, s, masked_value)
        top = jnp.max(s, axis=0, keepdims=True)
        p = jnp.exp2((s - top) * to_log2)
        total = jnp.sum(p, axis=0, keepdims=True)
        acc = matmul(value_t(slot), p.astype(bf16))

        def step(g, carry):
            def use(carry):
                top, total, acc = carry
                s = scores(g)
                new = jnp.maximum(top, jnp.max(s, axis=0, keepdims=True))
                fade = jnp.exp2((top - new) * to_log2)
                p = jnp.exp2((s - new) * to_log2)
                total = total * fade + jnp.sum(p, axis=0, keepdims=True)
                acc = acc * fade + matmul(value_t(g), p.astype(bf16))
                return new, total, acc

            return lax.cond(real[g] > 0, use, lambda c: c, carry)

        first = jnp.where(real[slot] > 0, first, slot)
        top, total, acc = lax.fori_loop(first, slot, step, (top, total, acc))
        lse[i] = top * to_log2 + jnp.log2(total)
        acc = acc / total
        out_t[i] = acc
        back = acc.T.astype(bf16)
        out[info[40 + 2 * i]] = back[:BLOCK]
        out[info[40 + 2 * i + 1]] = back[BLOCK:]
        return 0

    lax.fori_loop(0, n_blocks // 2, tile, 0)


def attend_back_kernel(
    plan, info, real, own, keys, values, grads, out_t, lse, dq, dkv_own, dkv_other, dk, dv, keys_t
):
    me = info[0]
    n_blocks = len(plan.block_rel)

    def clear(b, _):
        rows = pl.ds(pl.multiple_of(b * BLOCK, BLOCK), BLOCK)
        dk[rows, :] = jnp.zeros((BLOCK, HEAD), f32)
        dv[rows, :] = jnp.zeros((BLOCK, HEAD), f32)
        keys_t[b] = transposed(keys[rows, :])
        return 0

    lax.fori_loop(0, plan.count, clear, 0)

    frame = plan.space * BLOCK
    two = 2 * BLOCK
    lane = lax.broadcasted_iota(jnp.int32, (1, two), 1)
    q_place = jnp.where(lane < BLOCK, info[1] + lane, info[2] + lane - BLOCK)

    def tile(i, _):
        slot, first = info[8 + i], info[16 + i]
        q = jnp.concatenate([own[2 * i, :, :HEAD], own[2 * i + 1, :, :HEAD]], axis=0)
        do = jnp.concatenate([grads[info[40 + 2 * i]], grads[info[40 + 2 * i + 1]]], axis=0)
        delta = jnp.sum(do.astype(f32).T * out_t[i], axis=0, keepdims=True)
        log_total = lse[i]

        def turn(g, mask):
            rows = pl.ds(pl.multiple_of(g * frame, frame), frame)
            key, value = keys[rows, :], values[rows, :]
            s = matmul(key, q, ((1,), (1,)))
            dp = matmul(value, do, ((1,), (1,)))
            p = jnp.exp2(s * to_log2 - log_total)
            if mask:
                k_place = lax.broadcasted_iota(jnp.int32, (frame, two), 0)
                p = jnp.where(k_place <= q_place, p, 0.0)
            ds = (p * (dp - delta)).astype(bf16)
            dv[rows, :] += matmul(p.astype(bf16), do)
            dk[rows, :] += matmul(ds, q)
            key_t = jnp.concatenate(
                [keys_t[g * plan.space + s] for s in range(plan.space)], axis=1
            )
            return matmul(key_t, ds)

        dq_t = turn(slot, True)

        def step(g, dq_t):
            return lax.cond(real[g] > 0, lambda c: c + turn(g, False), lambda c: c, dq_t)

        first = jnp.where(real[slot] > 0, first, slot)
        dq_t = lax.fori_loop(first, slot, step, dq_t)
        back = (dq_t * inv_root).T.astype(bf16)
        dq[2 * i] = back[:BLOCK]
        dq[2 * i + 1] = back[BLOCK:]
        return 0

    lax.fori_loop(0, n_blocks // 2, tile, 0)

    for part, part_rel in enumerate(plan.part_rel):

        def hand_out(b, _, part=part, part_rel=part_rel):
            home = me ^ part_rel ^ info[24 + b]
            rows = pl.ds(pl.multiple_of(home * BLOCK, BLOCK), BLOCK)
            pair = jnp.concatenate([dk[rows, :] * inv_root, dv[rows, :]], axis=1).astype(bf16)
            if part == 0:
                dkv_own[b] = pair
            else:
                dkv_other[part - 1, b] = pair
            return 0

        lax.fori_loop(0, n_blocks, hand_out, 0)


def call(kernel, n_scalar, n_in, outs, scratch, cost):
    return pl.pallas_call(
        kernel,
        out_shape=outs,
        in_specs=[pl.BlockSpec(memory_space=pltpu.SMEM)] * n_scalar
        + [pl.BlockSpec(memory_space=pltpu.VMEM)] * n_in,
        out_specs=tuple(pl.BlockSpec(memory_space=pltpu.VMEM) for _ in outs),
        scratch_shapes=scratch,
        cost_estimate=cost,
        compiler_params=pltpu.CompilerParams(vmem_limit_bytes=58 << 20),
    )


def attend(plan, info, real, own, other):
    blocks = len(plan.block_rel)
    tokens = plan.count * BLOCK
    work = blocks * BLOCK * min(plan.clip * plan.space * BLOCK, tokens) // 2
    shape = jax.ShapeDtypeStruct
    return call(
        functools.partial(attend_kernel, plan),
        2,
        2,
        (
            shape((blocks, BLOCK, HEAD), bf16),
            shape((blocks // 2, HEAD, 2 * BLOCK), f32),
            shape((blocks // 2, 1, 2 * BLOCK), f32),
            shape((tokens, HEAD), bf16),
            shape((tokens, HEAD), bf16),
        ),
        [pltpu.VMEM((plan.count, HEAD, BLOCK), bf16)],
        pl.CostEstimate(flops=8 * work * HEAD, bytes_accessed=8 << 20, transcendentals=work),
    )(info, real, own, other)


def attend_back(plan, info, real, own, keys, values, grads, out_t, lse):
    blocks = len(plan.block_rel)
    tokens = plan.count * BLOCK
    work = blocks * BLOCK * min(plan.clip * plan.space * BLOCK, tokens) // 2
    shape = jax.ShapeDtypeStruct
    return call(
        functools.partial(attend_back_kernel, plan),
        2,
        6,
        (
            shape((blocks, BLOCK, HEAD), bf16),
            shape((blocks, BLOCK, 2 * HEAD), bf16),
            shape((len(plan.part_rel) - 1, blocks, BLOCK, 2 * HEAD), bf16),
        ),
        [
            pltpu.VMEM((tokens, HEAD), f32),
            pltpu.VMEM((tokens, HEAD), f32),
            pltpu.VMEM((plan.count, HEAD, BLOCK), bf16),
        ],
        pl.CostEstimate(flops=20 * work * HEAD, bytes_accessed=8 << 20, transcendentals=work),
    )(info, real, own, keys, values, grads, out_t, lse)


def on_device(
    plan, layer_input, frame_real, gain_attn, w_qkv, w_out, gain_mlp, w_up, w_down, cotangent
):
    rows = layer_input.shape[1]
    width = layer_input.shape[2]
    shard = w_up.shape[0]
    count, space = plan.count, plan.space
    me = lax.axis_index("tm") * space + lax.axis_index("space")
    inputs = layer_input[0].astype(f32)
    grad_out = cotangent[0].astype(f32)
    swap = plan.swap
    team_hi, team_lo = plan.team
    n_gather = len(plan.gather)
    k_count = 1 << n_gather
    low_gather = min(plan.gather)
    chunk = low_gather * shard
    n_chunks = width // chunk

    def has(bit):
        return (me & bit) != 0

    order = [
        (
            sum(b for j, b in enumerate(plan.gather) if (i >> j) & 1) + (team_hi if t else 0)
        )
        // low_gather
        for i in range(k_count)
        for t in range(2)
    ]
    inverse = [order.index(m) for m in range(n_chunks)]

    def flipped(pieces):
        for bit in plan.gather:
            step = bit // low_gather
            pieces = [
                jnp.where(has(bit), pieces[m ^ step], pieces[m]) for m in range(n_chunks)
            ]
        return pieces

    def to_rel(value):
        pieces = flipped([value[:, m * chunk : (m + 1) * chunk] for m in range(n_chunks)])
        return jnp.concatenate([pieces[m] for m in order], axis=1)

    def from_rel(value):
        pieces = [value[:, m * chunk : (m + 1) * chunk] for m in range(n_chunks)]
        return jnp.concatenate(flipped([pieces[m] for m in inverse]), axis=1)

    half = rows // 2

    def team_gather(value):
        a, b = value[:half], value[half:]
        a_lo = swap(a, team_lo)
        b_hi = swap(b, team_hi)
        a_hi, a_both = jnp.split(swap(jnp.concatenate([a, a_lo]), team_hi), 2)
        b_lo, b_both = jnp.split(swap(jnp.concatenate([b, b_hi]), team_lo), 2)
        return jnp.concatenate([a, b, a_lo, b_lo, a_hi, b_hi, a_both, b_both])

    def team_scatter(parts):
        parts = parts.reshape(4, 2, half, width)
        a, b = parts[:, 0], parts[:, 1]
        a_got = swap(a[2:], team_hi)
        b_got = swap(jnp.stack([b[1], b[3]]), team_lo)
        a_lo = a[1].astype(f32) + a_got[1].astype(f32)
        b_hi = b[2].astype(f32) + b_got[1].astype(f32)
        a_last = swap(a_lo.astype(bf16), team_lo)
        b_last = swap(b_hi.astype(bf16), team_hi)
        a_sum = a[0].astype(f32) + a_got[0].astype(f32) + a_last.astype(f32)
        b_sum = b[0].astype(f32) + b_got[0].astype(f32) + b_last.astype(f32)
        return jnp.concatenate([a_sum, b_sum])

    def octet(value):
        return lax.all_to_all(value, AXES, 0, 0, axis_index_groups=plan.octets)

    def square(value):
        return lax.all_to_all(value, AXES, 0, 0, axis_index_groups=plan.squares)

    def spread(weight):
        block = octet(weight).reshape(8 * shard, -1)
        for bit in plan.gather:
            block = jnp.concatenate([block, swap(block, bit)])
        return block, swap(block, 1)

    def collected(mine, others):
        block = mine.astype(f32) + swap(others, 1).astype(f32)
        for bit in reversed(plan.gather):
            block = block.reshape(2, block.shape[0] // 2, -1)
            block = block[0] + swap(block[1].astype(bf16), bit).astype(f32)
        block = octet(block.astype(bf16).reshape(8, shard, -1))
        return block.astype(f32)

    gain_one = gain_attn.astype(f32)[:, None]
    gain_two = gain_mlp.astype(f32)[:, None]
    qkv_scaled = (w_qkv.astype(f32) * gain_one).astype(bf16)
    up_scaled = (w_up.astype(f32) * gain_two).astype(bf16)
    n_ff = w_up.shape[1] // 8
    qkv_sent = (
        qkv_scaled.reshape(shard, 3, 8, 2 * HEAD).transpose(2, 0, 1, 3).reshape(8, shard, 6 * HEAD)
    )
    up_sent = up_scaled.reshape(shard, 8, n_ff).transpose(1, 0, 2)
    down_sent = w_down.reshape(shard, 8, n_ff).transpose(1, 0, 2)

    normed_one, scale_one = layer_norm(inputs)
    first_all = team_gather(to_rel(normed_one.astype(bf16)))
    qkv_mine, qkv_other = spread(qkv_sent)
    out_matrix = lax.all_gather(w_out, AXES, axis=0, tiled=True)
    up_mine, up_other = spread(up_sent)
    down_mine, down_other = spread(down_sent)
    grad_all = team_gather(to_rel(cotangent[0]))

    team_device = me ^ jnp.array(plan.team_rel, jnp.int32)
    row_index = jnp.arange(rows, dtype=jnp.int32)
    positions = (
        ((team_device // space) % plan.clip * (space * rows) + (team_device % space) * rows)[:, None]
        + row_index[None, :]
    ).reshape(4 * rows)
    half_dim = HEAD // 2
    inverse_freq = jnp.exp(-jnp.log(10000.0) * jnp.arange(half_dim, dtype=f32) * 2.0 / HEAD)
    angles = positions.astype(f32)[:, None] * inverse_freq[None, :]
    angles = jnp.concatenate([angles, angles], axis=-1)
    cosine, sine = jnp.cos(angles), jnp.sin(angles)

    def rotate(value):
        turned = jnp.concatenate([-value[:, half_dim:], value[:, :half_dim]], axis=-1)
        return value * cosine + turned * sine

    def rotate_back(value):
        scaled = value * sine
        turned = jnp.concatenate([scaled[:, half_dim:], -scaled[:, :half_dim]], axis=-1)
        return value * cosine + turned

    def head_triples(mixed):
        found = []
        for j in range(2):
            q, k, v = (
                mixed[:, (2 * i + j) * HEAD : (2 * i + j + 1) * HEAD] for i in range(3)
            )
            found.append(jnp.concatenate([rotate(q), rotate(k), v], axis=1).astype(bf16))
        return found

    mixed_mine = matmul(first_all, qkv_mine)
    mixed_other = matmul(first_all, qkv_other)
    stack = jnp.stack(head_triples(mixed_mine) + head_triples(mixed_other))
    my_head = jnp.where(has(plan.heads[0]), 2, 0) + jnp.where(has(plan.heads[1]), 1, 0)
    core_flip = jnp.where(has(1), 2, 0)
    pick = [(my_head ^ r) ^ core_flip for r in range(4)]
    sent = [lax.dynamic_index_in_dim(stack, pick[r], 0, keepdims=False) for r in range(4)]
    own = jnp.stack([sent[0]] + [swap(sent[r], plan.head_rel[r]) for r in range(1, 4)])
    own = own.reshape(16, rows, 3 * HEAD)
    shared = own[:, :, HEAD:]
    other = jnp.stack([swap(shared, rel) for rel in plan.part_rel[1:]])

    block_rel = jnp.array(plan.block_rel, jnp.int32)
    tile_rel = jnp.array(plan.block_rel[::2], jnp.int32)
    tile_slot = (me ^ tile_rel) // space
    homes = me ^ block_rel
    place_in_square = jnp.zeros_like(homes)
    for i, bit in enumerate(reversed(plan.square_bits)):
        place_in_square = place_in_square + jnp.where((homes & bit) != 0, 1 << i, 0)
    info = jnp.concatenate(
        [
            jnp.stack([me, (me % space) * rows, ((me ^ team_lo) % space) * rows]),
            jnp.zeros((5,), jnp.int32),
            tile_slot,
            tile_slot // plan.clip * plan.clip,
            block_rel,
            place_in_square,
        ]
    ).astype(jnp.int32)

    attended, attended_t, log_total, keys, values = attend(plan, info, frame_real, own, other)
    square_bits = plan.square_bits
    by_head = [square_bits.index(b) for b in plan.team + plan.heads]
    heads_here = square(attended).reshape(2, 2, 2, 2, rows, HEAD)
    attended_low = heads_here.transpose(4, *by_head, 5).reshape(rows, width)
    middle = inputs + matmul(attended_low, out_matrix)
    normed_two, scale_two = layer_norm(middle)
    second_all = team_gather(to_rel(normed_two.astype(bf16)))

    def feed(up, down):
        hidden = matmul(second_all, up)
        grad_act = matmul(grad_all, down)
        activated, back = jax.vjp(functools.partial(jax.nn.gelu, approximate=True), hidden)
        return activated.astype(bf16), back(grad_act)[0].astype(bf16)

    act_mine, hid_mine = feed(up_mine, down_mine)
    act_other, hid_other = feed(up_other, down_other)
    second_parts = matmul(hid_mine, up_mine, ((1,), (1,))) + matmul(hid_other, up_other, ((1,), (1,)))
    grad_second = from_rel(team_scatter(second_parts.astype(bf16)))
    out_parts = matmul(act_mine, down_mine, ((1,), (1,))) + matmul(act_other, down_other, ((1,), (1,)))
    output = (middle + from_rel(team_scatter(out_parts.astype(bf16)))).astype(bf16)
    down_mine_grad = matmul(grad_all, act_mine, ((0,), (0,))).astype(bf16)
    down_other_grad = matmul(grad_all, act_other, ((0,), (0,))).astype(bf16)
    up_mine_grad = matmul(second_all, hid_mine, ((0,), (0,))).astype(bf16)
    up_other_grad = matmul(second_all, hid_other, ((0,), (0,))).astype(bf16)

    grad_middle = grad_out + layer_norm_back(grad_second, normed_two, scale_two)
    grad_middle_low = grad_middle.astype(bf16)
    grad_attended = matmul(grad_middle_low, out_matrix, ((1,), (1,))).astype(bf16)
    to_square = [0] * 4
    for i, axis in enumerate(by_head):
        to_square[axis] = i
    grad_sent = grad_attended.reshape(rows, 2, 2, 2, 2, HEAD).transpose(
        *[1 + i for i in to_square], 0, 5
    )
    grad_heads = square(grad_sent.reshape(16, rows, HEAD))
    dq, dkv_own, dkv_other = attend_back(
        plan, info, frame_real, own, keys, values, grad_heads, attended_t, log_total
    )
    dkv = dkv_own.astype(f32)
    for i, rel in enumerate(plan.part_rel[1:]):
        dkv = dkv + swap(dkv_other[i], rel).astype(f32)
    triple = jnp.concatenate([dq, dkv.astype(bf16)], axis=2).reshape(4, 4 * rows, 3 * HEAD)
    got = jnp.stack([triple[0]] + [swap(triple[r], plan.head_rel[r]) for r in range(1, 4)])

    def rejoin(first):
        pieces = [[], [], []]
        for j in range(2):
            place = ((first + j) ^ core_flip) ^ my_head
            t = lax.dynamic_index_in_dim(got, place, 0, keepdims=False).astype(f32)
            pieces[0].append(rotate_back(t[:, :HEAD]))
            pieces[1].append(rotate_back(t[:, HEAD : 2 * HEAD]))
            pieces[2].append(t[:, 2 * HEAD :])
        return jnp.concatenate(pieces[0] + pieces[1] + pieces[2], axis=1).astype(bf16)

    mixed_grad_mine, mixed_grad_other = rejoin(0), rejoin(2)
    first_parts = matmul(mixed_grad_mine, qkv_mine, ((1,), (1,))) + matmul(
        mixed_grad_other, qkv_other, ((1,), (1,))
    )
    grad_first = from_rel(team_scatter(first_parts.astype(bf16)))
    grad_inputs = grad_middle + layer_norm_back(grad_first, normed_one, scale_one)
    qkv_mine_grad = matmul(first_all, mixed_grad_mine, ((0,), (0,))).astype(bf16)
    qkv_other_grad = matmul(first_all, mixed_grad_other, ((0,), (0,))).astype(bf16)

    grad_down = collected(down_mine_grad, down_other_grad).transpose(1, 0, 2).reshape(shard, 8 * n_ff)
    raw_up = collected(up_mine_grad, up_other_grad).transpose(1, 0, 2).reshape(shard, 8 * n_ff)
    grad_w_out = lax.psum_scatter(
        matmul(attended_low, grad_middle_low, ((0,), (0,))).astype(bf16),
        AXES,
        scatter_dimension=0,
        tiled=True,
    ).astype(f32)
    raw_qkv = (
        collected(qkv_mine_grad, qkv_other_grad)
        .reshape(8, shard, 3, 2 * HEAD)
        .transpose(1, 2, 0, 3)
        .reshape(shard, 3 * width)
    )
    grad_gain_two = jnp.sum(raw_up * w_up.astype(f32), axis=1)
    grad_gain_one = jnp.sum(raw_qkv * w_qkv.astype(f32), axis=1)
    return (
        output[None],
        grad_inputs[None],
        grad_gain_one,
        raw_qkv * gain_one,
        grad_w_out,
        grad_gain_two,
        raw_up * gain_two,
        grad_down,
    )


def solution(mesh):
    plan = Plan(mesh.shape["tm"], mesh.shape["space"], BLOCK)
    tokens = P("tm", "space", None)
    line = P(("tm", "space"))
    table = P(("tm", "space"), None)
    return jax.shard_map(
        functools.partial(on_device, plan),
        mesh=mesh,
        in_specs=(tokens, P(), line, table, table, line, table, table, tokens),
        out_specs=(tokens, tokens, line, table, table, line, table, table),
        check_vma=False,
    )
```

time: 5140 us -> 916 us (0.18)
  waiting for transfers between devices: 4020 us -> 475 us
  starting transfers between devices: 435 us -> 118 us
  matrix products: 330 us -> 107 us
  local copies, waits for them, and re-layouts: 202 us -> 53.3 us
  blocking collectives: 85 us -> 0 us
  other arithmetic: 25.3 us -> 99.7 us
    ppermute x51 -> x50, waiting for transfers between devices: 2020 us -> 455 us  [swap(): return lax.ppermute(value, AXES, [(d, d ^ mask) for d in self.devices])]
    reduce_scatter x4 -> x1, waiting for transfers between devices: 1110 us -> 0.01 us  [on_device(): lax.psum_scatter(matmul(attended_low, grad_middle_low, ((0,), (0,))).asty...]
    unnamed x14 -> x2, waiting for transfers between devices: 745 us -> 0.7 us
    ppermute x51 -> x50, starting transfers between devices: 435 us -> 61.2 us  [swap(): return lax.ppermute(value, AXES, [(d, d ^ mask) for d in self.devices])]
    dot_general x67 -> x21, matrix products: 330 us -> 107 us  [matmul(): lax.dot_general(left, right, (dims, ((), ())), preferred_element_type=f32)]
    all_gather x6 -> x1, waiting for transfers between devices: 147 us -> 0.02 us  [on_device(): out_matrix = lax.all_gather(w_out, AXES, axis=0, tiled=True)]
    unnamed x2 -> x0, blocking collectives: 85 us -> none
    while x86 -> x0, local copies, waits for them, and re-layouts: 84 us -> none
  transfers between devices with their start and end apart: 63 -> 60, of which waited for: 58 -> 31; matrix products, arithmetic and copies ran while one was open for 8% -> 24% of each run, Pallas kernels for 0% -> 4%
where the time goes in v1:
time: 916 us; the launch traced here: 906 us
  waiting for transfers between devices  475 us (52%)
  starting transfers between devices  118 us (13%)
  matrix products  107 us (12%)
  other arithmetic  99.7 us (11%)
  local copies, waits for them, and re-layouts  53.3 us (6%)
  Pallas kernels  36.6 us (4%)
  between operations  16.4 us (2%)
    ppermute x50, waiting for transfers between devices, swap(): return lax.ppermute(value, AXES, [(d, d ^ mask) for d in self.devices])  455 us
    dot_general x21, matrix products, matmul(): lax.dot_general(left, right, (dims, ((), ())), preferred_element_type=f32)  107 us
    ppermute x50, starting transfers between devices, swap(): return lax.ppermute(value, AXES, [(d, d ^ mask) for d in self.devices])  61.2 us
    all_to_all x6, starting transfers between devices, octet(): return lax.all_to_all(value, AXES, 0, 0, axis_index_groups=plan.octets)  44.2 us
    unnamed x157, local copies, waits for them, and re-layouts  27.5 us
    unnamed x64, other arithmetic  21 us
    all_to_all x6, waiting for transfers between devices, octet(): return lax.all_to_all(value, AXES, 0, 0, axis_index_groups=plan.octets)  19.1 us
    pallas_call x1, Pallas kernels, attend_back(): call(functools.partial(attend_back_kernel, plan), 2, 6, (shape((blocks, B...  18.7 us
  transfers between devices with their start and end apart: 60, of which 31 were waited for; matrix products, arithmetic and copies ran while one was open for 24% of the time, Pallas kernels for 4%

profile of v1, /device:TPU:0, one launch (start us, length us, event | category | flops | bytes accessed | tf_op | source)
XLA Modules:
  0.0 905.8 jit_solution(2081251007087797800)
XLA Ops:
  24.8 3.5 all-to-all-start
  40.4 3.6 all-to-all-start.2
  48.1 48.4 %collective-permute-done.4 = bf16[512,768]{1,0:T(8,128)(2,1)S(1)} collective-permute-done((bf16[512,768]{1,0:T(8,128)(2,1)S(1)}, bf16[512,768]{1,0:T(8,128)(2,1)S(1)}, u32[]{:S(2)}, u32[]{:S(2)}) %collective-permute-start.4) | collective-permute-done | bytes 786464 | tf_op jit(solution)/shard_map/ppermute | solution.py:68
  118.3 30.1 %collective-permute-done.5 = bf16[1024,768]{1,0:T(8,128)(2,1)} collective-permute-done((bf16[1024,768]{1,0:T(8,128)(2,1)}, bf16[1024,768]{1,0:T(8,128)(2,1)}, u32[]{:S(2)}, u32[]{:S(2)}) %collective-permute-start.5) | collective-permute-done | bytes 1572896 | tf_op jit(solution)/shard_map/ppermute | solution.py:68
  148.4 3.4 pad_maximum_fusion.2
  151.8 3.8 all-to-all-start.3
  163.9 3.3 collective-permute-start.15
  167.2 6.9 all-to-all-done.3
  174.1 4.0 fusion.157
  179.9 4.3 fusion.156
  187.6 3.9 collective-permute-start.9
  191.5 61.7 %collective-permute-done.15 = bf16[512,1024]{1,0:T(8,128)(2,1)} collective-permute-done((bf16[512,1024]{1,0:T(8,128)(2,1)S(1)}, bf16[512,1024]{1,0:T(8,128)(2,1)}, u32[]{:S(2)}, u32[]{:S(2)}) %collective-permute-start.15) | collective-permute-done | bytes 1048608 | tf_op jit(solution)/shard_map/ppermute | solution.py:68
  259.3 16.2 %collective-permute-done.17 = bf16[512,1024]{1,0:T(8,128)(2,1)S(1)} collective-permute-done((bf16[512,1024]{1,0:T(8,128)(2,1)S(1)}, bf16[512,1024]{1,0:T(8,128)(2,1)S(1)}, u32[]{:S(2)}, u32[]{:S(2)}) %collective-permute-start.17) | collective-permute-done | bytes 1048608 | tf_op jit(solution)/shard_map/ppermute | solution.py:68
  278.9 6.3 collective-permute-done.9
  285.5 6.8 collective-permute-done.8
  297.9 17.9 %shard_map.179 = (bf16[16,128,128]{2,1,0:T(8,128)(2,1)}, f32[8,128,256]{2,1,0:T(8,128)}, f32[8,1,256]{2,1,0:T(1,128)}, bf16[4096,128]{1,0:T(8,128)(2,1)}, bf16[4096,128]{1,0:T(8,128)(2,1)}) custom-call(s32[56]{0:T(128)} %concatenate.211.info, s32[8]{0:T(128)} %real.3, bf16[16,128,384]{2,1,0:T(8,128)(2,1)} %bitcast.338, bf16[1,16,128,256]{3,2,1,0:T(8,128)(2,1)} %bitcast.368), custom_call_target="tpu_custom_call" | custom-call | flops 4294967296 | bytes 8388608 | tf_op jit(solution)/shard_map/pallas_call | solution.py:250
  315.9 7.2 all-to-all-start.1
  324.8 8.0 collective-permute-done.16
  332.7 3.6 pad_maximum_fusion
  336.3 43.0 %collective-permute-done.18 = bf16[1024,1024]{1,0:T(8,128)(2,1)} collective-permute-done((bf16[1024,1024]{1,0:T(8,128)(2,1)}, bf16[1024,1024]{1,0:T(8,128)(2,1)}, u32[]{:S(2)}, u32[]{:S(2)}) %collective-permute-start.18) | collective-permute-done | bytes 2097184 | tf_op jit(solution)/shard_map/ppermute | solution.py:68
  379.3 3.9 pad_maximum_fusion.1
  384.6 4.7 fusion.158
  392.1 6.9 collective-permute-done.12
  401.2 11.4 %collective-permute-done.13 = bf16[128,2048]{1,0:T(8,128)(2,1)S(1)} collective-permute-done((bf16[128,2048]{1,0:T(8,128)(2,1)S(1)}, bf16[128,2048]{1,0:T(8,128)(2,1)S(1)}, u32[]{:S(2)}, u32[]{:S(2)}) %collective-permute-start.13) | collective-permute-done | bytes 524320 | tf_op jit(solution)/shard_map/ppermute | solution.py:68
  414.3 5.3 fusion.159
  419.7 5.3 fusion.160
  425.0 7.0 fusion.8
  432.0 6.8 fusion.15
  439.7 4.6 fusion.161
  444.3 4.6 add_convert_fusion.1
  450.8 4.7 fusion.132
  455.6 4.8 add_convert_fusion.2
  463.5 9.1 %collective-permute-done.21 = bf16[2,64,2048]{2,1,0:T(8,128)(2,1)S(1)} collective-permute-done((bf16[2,64,2048]{2,1,0:T(8,128)(2,1)S(1)}, bf16[2,64,2048]{2,1,0:T(8,128)(2,1)S(1)}, u32[]{:S(2)}, u32[]{:S(2)}) %collective-permute-start.21) | collective-permute-done | bytes 524320 | tf_op jit(solution)/shard_map/ppermute | solution.py:68
  473.5 8.1 collective-permute-done.30
  486.0 4.0 collective-permute-done.32
  501.7 5.4 all-to-all-start.4
  507.1 6.4 convolution_convert_fusion.2
  513.5 6.2 convolution_convert_fusion.1
  521.0 18.7 %shard_map.180 = (bf16[16,128,128]{2,1,0:T(8,128)(2,1)}, bf16[16,128,256]{2,1,0:T(8,128)(2,1)}, bf16[1,16,128,256]{3,2,1,0:T(8,128)(2,1)}) custom-call(s32[56]{0:T(128)} %concatenate.211.info, s32[8]{0:T(128)} %real.3, bf16[16,128,384]{2,1,0:T(8,128)(2,1)} %bitcast.339, bf16[4096,128]{1,0:T(8,128)(2,1)} %get-tuple-element.17.keys, ...), custom_call_target="tpu_custom_call" | custom-call | flops 10737418240 | bytes 8388608 | tf_op jit(solution)/shard_map/pallas_call | solution.py:271
  539.7 5.7 fusion.163
  545.4 6.3 fusion.131
  553.8 3.7 collective-permute-start.36
  558.2 5.7 convolution_convert_fusion
  563.9 20.9 %collective-permute-done.36 = bf16[512,384]{1,0:T(8,128)(2,1)} collective-permute-done((bf16[512,384]{1,0:T(8,128)(2,1)}, bf16[512,384]{1,0:T(8,128)(2,1)}, u32[]{:S(2)}, u32[]{:S(2)}) %collective-permute-start.36) | collective-permute-done | bytes 393248 | tf_op jit(solution)/shard_map/ppermute | solution.py:68
  584.8 15.7 %collective-permute-done.35 = bf16[512,384]{1,0:T(8,128)(2,1)} collective-permute-done((bf16[512,384]{1,0:T(8,128)(2,1)}, bf16[512,384]{1,0:T(8,128)(2,1)}, u32[]{:S(2)}, u32[]{:S(2)}) %collective-permute-start.35) | collective-permute-done | bytes 393248 | tf_op jit(solution)/shard_map/ppermute | solution.py:68
  613.4 4.0 fusion.162
  617.5 3.2 add_convert_fusion
  623.0 5.3 convolution_convert_fusion.3
  628.3 11.4 %collective-permute-done.37 = bf16[2,64,2048]{2,1,0:T(8,128)(2,1)S(1)} collective-permute-done((bf16[2,64,2048]{2,1,0:T(8,128)(2,1)S(1)}, bf16[2,64,2048]{2,1,0:T(8,128)(2,1)S(1)}, u32[]{:S(2)}, u32[]{:S(2)}) %collective-permute-start.37) | collective-permute-done | bytes 524320 | tf_op jit(solution)/shard_map/ppermute | solution.py:68
  639.9 4.4 convert_add_fusion.1
  646.7 5.5 convert_add_fusion
  653.9 3.6 collective-permute-done.38
  658.6 4.8 collective-permute-start.40
  663.5 5.2 convolution_convert_fusion.4
  672.7 40.8 %collective-permute-done.45 = bf16[1024,1024]{1,0:T(8,128)(2,1)} collective-permute-done((bf16[1024,1024]{1,0:T(8,128)(2,1)}, bf16[1024,1024]{1,0:T(8,128)(2,1)}, u32[]{:S(2)}, u32[]{:S(2)}) %collective-permute-start.45) | collective-permute-done | bytes 2097184 | tf_op jit(solution)/shard_map/ppermute | solution.py:68
  718.3 38.4 %collective-permute-done.48 = bf16[1024,1024]{1,0:T(8,128)(2,1)S(1)} collective-permute-done((bf16[1024,1024]{1,0:T(8,128)(2,1)S(1)}, bf16[1024,1024]{1,0:T(8,128)(2,1)S(1)}, u32[]{:S(2)}, u32[]{:S(2)}) %collective-permute-start.48) | collective-permute-done | bytes 2097184 | tf_op jit(solution)/shard_map/ppermute | solution.py:68
  763.4 24.6 %all-to-all-start.6 = ((bf16[8,64,1024]{2,1,0:T(8,128)(2,1)}), bf16[8,64,1024]{2,1,0:T(8,128)(2,1)}, u32[]{:S(2)}, u32[]{:S(2)}) async-start(bf16[8,64,1024]{2,1,0:T(8,128)(2,1)} %bitcast.90), calls=%async_computation.7 | async-start | bytes 2097152 | tf_op jit(solution)/shard_map/all_to_all | solution.py:360
  788.0 3.5 convert_add_fusion.2
  797.7 9.0 collective-permute-done.49
  809.3 8.5 all-to-all-done.6
  817.8 4.3 all-to-all-start.7
  822.2 10.8 %collective-permute-done.42 = bf16[1024,768]{1,0:T(8,128)(2,1)} collective-permute-done((bf16[1024,768]{1,0:T(8,128)(2,1)}, bf16[1024,768]{1,0:T(8,128)(2,1)}, u32[]{:S(2)}, u32[]{:S(2)}) %collective-permute-start.42) | collective-permute-done | bytes 1572896 | tf_op jit(solution)/shard_map/ppermute | solution.py:68
  838.0 34.9 %collective-permute-done.43 = bf16[512,768]{1,0:T(8,128)(2,1)S(1)} collective-permute-done((bf16[512,768]{1,0:T(8,128)(2,1)S(1)}, bf16[512,768]{1,0:T(8,128)(2,1)S(1)}, u32[]{:S(2)}, u32[]{:S(2)}) %collective-permute-start.43) | collective-permute-done | bytes 786464 | tf_op jit(solution)/shard_map/ppermute | solution.py:68
  874.0 4.5 all-to-all-start.5
  (432 shorter events, 191.0 us)
Async XLA Ops:
  17.7 89.3 %collective-permute-start = (bf16[64,2048]{1,0:T(8,128)(2,1)}, bf16[64,2048]{1,0:T(8,128)(2,1)}, u32[]{:S(2)}, u32[]{:S(2)}) collective-permute-start(bf16[64,2048]{1,0:T(8,128)(2,1)} %get-tuple-element.201), channel_id=1, source_target_pairs={{0,2},{1,3},{2,0},{3,1},{4,6},{5,7},{6,4},{7,5},{8,10},{9,11},{10,... | collective-permute-start | bytes 786440 | tf_op jit(solution)/shard_map/ppermute | solution.py:68
  20.7 82.8 %collective-permute-start.1 = (bf16[64,2048]{1,0:T(8,128)(2,1)}, bf16[64,2048]{1,0:T(8,128)(2,1)S(1)}, u32[]{:S(2)}, u32[]{:S(2)}) collective-permute-start(bf16[64,2048]{1,0:T(8,128)(2,1)} %get-tuple-element.200), channel_id=1, source_target_pairs={{0,8},{1,9},{2,10},{3,11},{4,12},{5,13},{6,14},{7,15},{8,0},{9,1},... | collective-permute-start | bytes 786440 | tf_op jit(solution)/shard_map/ppermute | solution.py:68
  24.8 15.6 %all-to-all-start = ((bf16[8,64,768]{2,1,0:T(8,128)(2,1)}), bf16[8,64,768]{2,1,0:T(8,128)(2,1)S(1)}, u32[]{:S(2)}, u32[]{:S(2)}) async-start(bf16[8,64,768]{2,1,0:T(8,128)(2,1)} %reshape.506), calls=%async_computation | async-start | bytes 1572864 | tf_op jit(solution)/shard_map/all_to_all | solution.py:360
  28.4 356.2 %all-gather.2.cloned.1.call-start = ((), (), s32[]{:S(2)}) async-start(), calls=%async_computation.9 | async-start | bytes 8650752 | tf_op jit(solution)/shard_map/all_gather | solution.py:393
  30.0 81.5 %collective-permute-start.25 = (bf16[64,2048]{1,0:T(8,128)(2,1)}, bf16[64,2048]{1,0:T(8,128)(2,1)}, u32[]{:S(2)}, u32[]{:S(2)}) collective-permute-start(bf16[64,2048]{1,0:T(8,128)(2,1)} %get-tuple-element.197), channel_id=1, source_target_pairs={{0,2},{1,3},{2,0},{3,1},{4,6},{5,7},{6,4},{7,5},{8,10},{9,11},{10,... | collective-permute-start | bytes 786440 | tf_op jit(solution)/shard_map/ppermute | solution.py:68
  31.9 77.5 %collective-permute-start.26 = (bf16[64,2048]{1,0:T(8,128)(2,1)}, bf16[64,2048]{1,0:T(8,128)(2,1)S(1)}, u32[]{:S(2)}, u32[]{:S(2)}) collective-permute-start(bf16[64,2048]{1,0:T(8,128)(2,1)} %get-tuple-element.196), channel_id=1, source_target_pairs={{0,8},{1,9},{2,10},{3,11},{4,12},{5,13},{6,14},{7,15},{8,0},{9,1},... | collective-permute-start | bytes 786440 | tf_op jit(solution)/shard_map/ppermute | solution.py:68
  40.4 111.3 %all-to-all-start.2 = ((bf16[8,64,1024]{2,1,0:T(8,128)(2,1)}), bf16[8,64,1024]{2,1,0:T(8,128)(2,1)S(1)}, u32[]{:S(2)}, u32[]{:S(2)}) async-start(bf16[8,64,1024]{2,1,0:T(8,128)(2,1)} %copy.48), calls=%async_computation.2 | async-start | bytes 2097152 | tf_op jit(solution)/shard_map/all_to_all | solution.py:360
  44.0 55.3 %copy-start.54 = (s32[16]{0:T(128)S(1)}, s32[16]{0:T(128)}, u32[]{:S(2)}) copy-start(s32[16]{0:T(128)} %constant.152.clone) | copy-start | bytes 196
  44.0 52.5 %collective-permute-start.4 = (bf16[512,768]{1,0:T(8,128)(2,1)S(1)}, bf16[512,768]{1,0:T(8,128)(2,1)S(1)}, u32[]{:S(2)}, u32[]{:S(2)}) collective-permute-start(bf16[512,768]{1,0:T(8,128)(2,1)S(1)} %bitcast.326), channel_id=1, source_target_pairs={{0,16},{1,17},{2,18},{3,19},{4,20},{5,21},{6,22},{7,23},{8,24},{9,... | collective-permute-start | bytes 2359304 | tf_op jit(solution)/shard_map/ppermute | solution.py:68
  96.5 51.9 %copy-start.13 = (bf16[512,768]{1,0:T(8,128)(2,1)}, bf16[512,768]{1,0:T(8,128)(2,1)S(1)}, u32[]{:S(2)}) copy-start(bf16[512,768]{1,0:T(8,128)(2,1)S(1)} %collective-permute-done.4) | copy-start | bytes 2359300
  97.9 50.5 %collective-permute-start.5 = (bf16[1024,768]{1,0:T(8,128)(2,1)}, bf16[1024,768]{1,0:T(8,128)(2,1)}, u32[]{:S(2)}, u32[]{:S(2)}) collective-permute-start(bf16[1024,768]{1,0:T(8,128)(2,1)} %pad_maximum_fusion.5), channel_id=1, source_target_pairs={{0,4},{1,5},{2,6},{3,7},{4,0},{5,1},{6,2},{7,3},{8,12},{9,13},{10,... | collective-permute-start | bytes 4718600 | tf_op jit(solution)/shard_map/ppermute | solution.py:68
  105.3 50.2 %collective-permute-start.2 = (bf16[128,2048]{1,0:T(8,128)(2,1)}, bf16[128,2048]{1,0:T(8,128)(2,1)}, u32[]{:S(2)}, u32[]{:S(2)}) collective-permute-start(bf16[128,2048]{1,0:T(8,128)(2,1)} %pad_maximum_fusion.8), channel_id=1, source_target_pairs={{0,2},{1,3},{2,0},{3,1},{4,6},{5,7},{6,4},{7,5},{8,10},{9,11},{10,... | collective-permute-start | bytes 1572872 | tf_op jit(solution)/shard_map/ppermute | solution.py:68
  108.9 48.3 %collective-permute-start.3 = (bf16[128,2048]{1,0:T(8,128)(2,1)}, bf16[128,2048]{1,0:T(8,128)(2,1)}, u32[]{:S(2)}, u32[]{:S(2)}) collective-permute-start(bf16[128,2048]{1,0:T(8,128)(2,1)} %pad_maximum_fusion.9), channel_id=1, source_target_pairs={{0,8},{1,9},{2,10},{3,11},{4,12},{5,13},{6,14},{7,15},{8,0},{9,1},... | collective-permute-start | bytes 1572872 | tf_op jit(solution)/shard_map/ppermute | solution.py:68
  111.2 80.3 %collective-permute-start.27 = (bf16[128,2048]{1,0:T(8,128)(2,1)}, bf16[128,2048]{1,0:T(8,128)(2,1)}, u32[]{:S(2)}, u32[]{:S(2)}) collective-permute-start(bf16[128,2048]{1,0:T(8,128)(2,1)} %pad_maximum_fusion.13), channel_id=1, source_target_pairs={{0,2},{1,3},{2,0},{3,1},{4,6},{5,7},{6,4},{7,5},{8,10},{9,11},{10,... | collective-permute-start | bytes 1572872 | tf_op jit(solution)/shard_map/ppermute | solution.py:68
  113.4 179.3 %collective-permute-start.28 = (bf16[128,2048]{1,0:T(8,128)(2,1)}, bf16[128,2048]{1,0:T(8,128)(2,1)}, u32[]{:S(2)}, u32[]{:S(2)}) collective-permute-start(bf16[128,2048]{1,0:T(8,128)(2,1)} %pad_maximum_fusion.14), channel_id=1, source_target_pairs={{0,8},{1,9},{2,10},{3,11},{4,12},{5,13},{6,14},{7,15},{8,0},{9,1},... | collective-permute-start | bytes 1572872 | tf_op jit(solution)/shard_map/ppermute | solution.py:68
  151.8 28.1 %collective-permute-start.6 = (bf16[2048,768]{1,0:T(8,128)(2,1)}, bf16[2048,768]{1,0:T(8,128)(2,1)}, u32[]{:S(2)}, u32[]{:S(2)}) collective-permute-start(bf16[2048,768]{1,0:T(8,128)(2,1)} %pad_maximum_fusion.2), channel_id=1, source_target_pairs={{0,1},{1,0},{2,3},{3,2},{4,5},{5,4},{6,7},{7,6},{8,9},{9,8},{10,11... | collective-permute-start | bytes 9437192 | tf_op jit(solution)/shard_map/ppermute | solution.py:68
  151.8 22.3 %all-to-all-start.3 = ((bf16[8,64,1024]{2,1,0:T(8,128)(2,1)}), bf16[8,64,1024]{2,1,0:T(8,128)(2,1)S(1)}, u32[]{:S(2)}, u32[]{:S(2)}) async-start(bf16[8,64,1024]{2,1,0:T(8,128)(2,1)} %copy.49), calls=%async_computation.3 | async-start | bytes 2097152 | tf_op jit(solution)/shard_map/all_to_all | solution.py:360
  163.9 89.3 %collective-permute-start.15 = (bf16[512,1024]{1,0:T(8,128)(2,1)S(1)}, bf16[512,1024]{1,0:T(8,128)(2,1)}, u32[]{:S(2)}, u32[]{:S(2)}) collective-permute-start(bf16[512,1024]{1,0:T(8,128)(2,1)S(1)} %bitcast.318), channel_id=1, source_target_pairs={{0,16},{1,17},{2,18},{3,19},{4,20},{5,21},{6,22},{7,23},{8,24},{9,... | collective-permute-start | bytes 3145736 | tf_op jit(solution)/shard_map/ppermute | solution.py:68
  174.1 101.5 %collective-permute-start.17 = (bf16[512,1024]{1,0:T(8,128)(2,1)S(1)}, bf16[512,1024]{1,0:T(8,128)(2,1)S(1)}, u32[]{:S(2)}, u32[]{:S(2)}) collective-permute-start(bf16[512,1024]{1,0:T(8,128)(2,1)S(1)} %bitcast.321), channel_id=1, source_target_pairs={{0,16},{1,17},{2,18},{3,19},{4,20},{5,21},{6,22},{7,23},{8,24},{9,... | collective-permute-start | bytes 3145736 | tf_op jit(solution)/shard_map/ppermute | solution.py:68
  187.6 97.6 %collective-permute-start.9 = (bf16[512,384]{1,0:T(8,128)(2,1)S(1)}, bf16[512,384]{1,0:T(8,128)(2,1)S(1)}, u32[]{:S(2)}, u32[]{:S(2)}) collective-permute-start(bf16[512,384]{1,0:T(8,128)(2,1)S(1)} %get-tuple-element.147), channel_id=1, source_target_pairs={{0,20},{1,21},{2,22},{3,23},{4,16},{5,17},{6,18},{7,19},{8,28},{9,... | collective-permute-start | bytes 1179656 | tf_op jit(solution)/shard_map/ppermute | solution.py:68
  191.5 100.8 %collective-permute-start.8 = (bf16[512,384]{1,0:T(8,128)(2,1)S(1)}, bf16[512,384]{1,0:T(8,128)(2,1)S(1)}, u32[]{:S(2)}, u32[]{:S(2)}) collective-permute-start(bf16[512,384]{1,0:T(8,128)(2,1)S(1)} %get-tuple-element.148), channel_id=1, source_target_pairs={{0,16},{1,17},{2,18},{3,19},{4,20},{5,21},{6,22},{7,23},{8,24},{9,... | collective-permute-start | bytes 1179656 | tf_op jit(solution)/shard_map/ppermute | solution.py:68
  253.2 39.1 %collective-permute-start.7 = (bf16[512,384]{1,0:T(8,128)(2,1)S(1)}, bf16[512,384]{1,0:T(8,128)(2,1)S(1)}, u32[]{:S(2)}, u32[]{:S(2)}) collective-permute-start(bf16[512,384]{1,0:T(8,128)(2,1)S(1)} %get-tuple-element.149), channel_id=1, source_target_pairs={{0,4},{1,5},{2,6},{3,7},{4,0},{5,1},{6,2},{7,3},{8,12},{9,13},{10,... | collective-permute-start | bytes 1179656 | tf_op jit(solution)/shard_map/ppermute | solution.py:68
  275.6 57.2 %collective-permute-start.16 = (bf16[1024,1024]{1,0:T(8,128)(2,1)}, bf16[1024,1024]{1,0:T(8,128)(2,1)}, u32[]{:S(2)}, u32[]{:S(2)}) collective-permute-start(bf16[1024,1024]{1,0:T(8,128)(2,1)} %pad_maximum_fusion.3), channel_id=1, source_target_pairs={{0,4},{1,5},{2,6},{3,7},{4,0},{5,1},{6,2},{7,3},{8,12},{9,13},{10,... | collective-permute-start | bytes 6291464 | tf_op jit(solution)/shard_map/ppermute | solution.py:68
  285.2 94.1 %collective-permute-start.18 = (bf16[1024,1024]{1,0:T(8,128)(2,1)}, bf16[1024,1024]{1,0:T(8,128)(2,1)}, u32[]{:S(2)}, u32[]{:S(2)}) collective-permute-start(bf16[1024,1024]{1,0:T(8,128)(2,1)} %pad_maximum_fusion.4), channel_id=1, source_target_pairs={{0,4},{1,5},{2,6},{3,7},{4,0},{5,1},{6,2},{7,3},{8,12},{9,13},{10,... | collective-permute-start | bytes 6291464 | tf_op jit(solution)/shard_map/ppermute | solution.py:68
  292.6 4.4 collective-permute-start.10
  315.9 67.4 %all-to-all-start.1 = ((bf16[16,128,128]{2,1,0:T(8,128)(2,1)}), bf16[16,128,128]{2,1,0:T(8,128)(2,1)}, u32[]{:S(2)}, u32[]{:S(2)}) async-start(bf16[16,128,128]{2,1,0:T(8,128)(2,1)} %get-tuple-element.16), calls=%async_computation.1 | async-start | bytes 1048576 | tf_op jit(solution)/shard_map/all_to_all | solution.py:363
  324.8 54.5 %copy-start.12 = (bf16[512,1024]{1,0:T(8,128)(2,1)S(1)}, bf16[512,1024]{1,0:T(8,128)(2,1)}, u32[]{:S(2)}) copy-start(bf16[512,1024]{1,0:T(8,128)(2,1)} %copy-done.11) | copy-start | bytes 3145732
  336.3 48.3 %copy-start.1 = (bf16[1,128,2048]{2,1,0:T(8,128)(2,1)S(1)}, bf16[1,128,2048]{2,1,0:T(8,128)(2,1)}, u32[]{:S(2)}) copy-start(bf16[1,128,2048]{2,1,0:T(8,128)(2,1)} %param.12) | copy-start | bytes 1572868
  336.3 83.3 %collective-permute-start.19 = (bf16[2048,1024]{1,0:T(8,128)(2,1)}, bf16[2048,1024]{1,0:T(8,128)(2,1)}, u32[]{:S(2)}, u32[]{:S(2)}) collective-permute-start(bf16[2048,1024]{1,0:T(8,128)(2,1)} %pad_maximum_fusion), channel_id=1, source_target_pairs={{0,1},{1,0},{2,3},{3,2},{4,5},{5,4},{6,7},{7,6},{8,9},{9,8},{10,11... | collective-permute-start | bytes 12582920 | tf_op jit(solution)/shard_map/ppermute | solution.py:68
  383.2 48.8 %collective-permute-start.20 = (bf16[2048,1024]{1,0:T(8,128)(2,1)}, bf16[2048,1024]{1,0:T(8,128)(2,1)}, u32[]{:S(2)}, u32[]{:S(2)}) collective-permute-start(bf16[2048,1024]{1,0:T(8,128)(2,1)} %pad_maximum_fusion.1), channel_id=1, source_target_pairs={{0,1},{1,0},{2,3},{3,2},{4,5},{5,4},{6,7},{7,6},{8,9},{9,8},{10,11... | collective-permute-start | bytes 12582920 | tf_op jit(solution)/shard_map/ppermute | solution.py:68
  390.2 8.8 collective-permute-start.12
  390.4 10.5 %collective-permute-start.11 = (bf16[64,2048]{1,0:T(8,128)(2,1)S(1)}, bf16[64,2048]{1,0:T(8,128)(2,1)S(1)}, u32[]{:S(2)}, u32[]{:S(2)}) collective-permute-start(bf16[64,2048]{1,0:T(8,128)(2,1)S(1)} %get-tuple-element.199), channel_id=1, source_target_pairs={{0,2},{1,3},{2,0},{3,1},{4,6},{5,7},{6,4},{7,5},{8,10},{9,11},{10,... | collective-permute-start | bytes 786440 | tf_op jit(solution)/shard_map/ppermute | solution.py:68
  399.1 13.6 %collective-permute-start.13 = (bf16[128,2048]{1,0:T(8,128)(2,1)S(1)}, bf16[128,2048]{1,0:T(8,128)(2,1)S(1)}, u32[]{:S(2)}, u32[]{:S(2)}) collective-permute-start(bf16[128,2048]{1,0:T(8,128)(2,1)S(1)} %pad_maximum_fusion.10), channel_id=1, source_target_pairs={{0,2},{1,3},{2,0},{3,1},{4,6},{5,7},{6,4},{7,5},{8,10},{9,11},{10,... | collective-permute-start | bytes 1572872 | tf_op jit(solution)/shard_map/ppermute | solution.py:68
  400.9 13.3 %collective-permute-start.14 = (bf16[128,2048]{1,0:T(8,128)(2,1)S(1)}, bf16[128,2048]{1,0:T(8,128)(2,1)S(1)}, u32[]{:S(2)}, u32[]{:S(2)}) collective-permute-start(bf16[128,2048]{1,0:T(8,128)(2,1)S(1)} %pad_maximum_fusion.11), channel_id=1, source_target_pairs={{0,8},{1,9},{2,10},{3,11},{4,12},{5,13},{6,14},{7,15},{8,0},{9,1},... | collective-permute-start | bytes 1572872 | tf_op jit(solution)/shard_map/ppermute | solution.py:68
  449.0 14.0 %collective-permute-start.29 = (bf16[2,64,2048]{2,1,0:T(8,128)(2,1)S(1)}, bf16[2,64,2048]{2,1,0:T(8,128)(2,1)S(1)}, u32[]{:S(2)}, u32[]{:S(2)}) collective-permute-start(bf16[2,64,2048]{2,1,0:T(8,128)(2,1)S(1)} %slice_bitcast_fusion.1), channel_id=1, source_target_pairs={{0,8},{1,9},{2,10},{3,11},{4,12},{5,13},{6,14},{7,15},{8,0},{9,1},... | collective-permute-start | bytes 1572872 | tf_op jit(solution)/shard_map/ppermute | solution.py:68
  449.6 23.9 %collective-permute-start.31 = (bf16[2,64,2048]{2,1,0:T(8,128)(2,1)S(1)}, bf16[2,64,2048]{2,1,0:T(8,128)(2,1)S(1)}, u32[]{:S(2)}, u32[]{:S(2)}) collective-permute-start(bf16[2,64,2048]{2,1,0:T(8,128)(2,1)S(1)} %pad_maximum_fusion.15), channel_id=1, source_target_pairs={{0,2},{1,3},{2,0},{3,1},{4,6},{5,7},{6,4},{7,5},{8,10},{9,11},{10,... | collective-permute-start | bytes 1572872 | tf_op jit(solution)/shard_map/ppermute | solution.py:68
  460.4 12.2 %collective-permute-start.21 = (bf16[2,64,2048]{2,1,0:T(8,128)(2,1)S(1)}, bf16[2,64,2048]{2,1,0:T(8,128)(2,1)S(1)}, u32[]{:S(2)}, u32[]{:S(2)}) collective-permute-start(bf16[2,64,2048]{2,1,0:T(8,128)(2,1)S(1)} %slice_bitcast_fusion.2), channel_id=1, source_target_pairs={{0,8},{1,9},{2,10},{3,11},{4,12},{5,13},{6,14},{7,15},{8,0},{9,1},... | collective-permute-start | bytes 1572872 | tf_op jit(solution)/shard_map/ppermute | solution.py:68
  461.3 21.8 %collective-permute-start.23 = (bf16[2,64,2048]{2,1,0:T(8,128)(2,1)S(1)}, bf16[2,64,2048]{2,1,0:T(8,128)(2,1)S(1)}, u32[]{:S(2)}, u32[]{:S(2)}) collective-permute-start(bf16[2,64,2048]{2,1,0:T(8,128)(2,1)S(1)} %pad_maximum_fusion.12), channel_id=1, source_target_pairs={{0,2},{1,3},{2,0},{3,1},{4,6},{5,7},{6,4},{7,5},{8,10},{9,11},{10,... | collective-permute-start | bytes 1572872 | tf_op jit(solution)/shard_map/ppermute | solution.py:68
  463.1 18.5 %collective-permute-start.30 = (bf16[64,2048]{1,0:T(8,128)(2,1)S(1)}, bf16[64,2048]{1,0:T(8,128)(2,1)S(1)}, u32[]{:S(2)}, u32[]{:S(2)}) collective-permute-start(bf16[64,2048]{1,0:T(8,128)(2,1)S(1)} %fusion.41), channel_id=1, source_target_pairs={{0,2},{1,3},{2,0},{3,1},{4,6},{5,7},{6,4},{7,5},{8,10},{9,11},{10,... | collective-permute-start | bytes 786440 | tf_op jit(solution)/shard_map/ppermute | solution.py:68
  472.7 11.7 %collective-permute-start.22 = (bf16[64,2048]{1,0:T(8,128)(2,1)S(1)}, bf16[64,2048]{1,0:T(8,128)(2,1)S(1)}, u32[]{:S(2)}, u32[]{:S(2)}) collective-permute-start(bf16[64,2048]{1,0:T(8,128)(2,1)S(1)} %fusion.45), channel_id=1, source_target_pairs={{0,2},{1,3},{2,0},{3,1},{4,6},{5,7},{6,4},{7,5},{8,10},{9,11},{10,... | collective-permute-start | bytes 786440 | tf_op jit(solution)/shard_map/ppermute | solution.py:68
  481.8 8.1 collective-permute-start.32
  484.6 8.1 collective-permute-start.24
  501.7 18.5 %all-to-all-start.4 = ((bf16[16,128,128]{2,1,0:T(8,128)(2,1)}), bf16[16,128,128]{2,1,0:T(8,128)(2,1)S(1)}, u32[]{:S(2)}, u32[]{:S(2)}) async-start(bf16[16,128,128]{2,1,0:T(8,128)(2,1)} %bitcast.61), calls=%async_computation.4 | async-start | bytes 1048576 | tf_op jit(solution)/shard_map/all_to_all | solution.py:363
  507.0 389.7 %reduce-scatter.2.cloned.1.call-start = ((), (), s32[]{:S(2)}) async-start(), calls=%async_computation.10 | async-start | bytes 8650752 | tf_op jit(solution)/shard_map/reduce_scatter | solution.py:524
  513.5 126.4 %collective-permute-start.44 = (bf16[2048,1024]{1,0:T(8,128)(2,1)}, bf16[2048,1024]{1,0:T(8,128)(2,1)}, u32[]{:S(2)}, u32[]{:S(2)}) collective-permute-start(bf16[2048,1024]{1,0:T(8,128)(2,1)} %convolution_convert_fusion.2), channel_id=1, source_target_pairs={{0,1},{1,0},{2,3},{3,2},{4,5},{5,4},{6,7},{7,6},{8,9},{9,8},{10,11... | collective-permute-start | bytes 12582920 | tf_op jit(solution)/shard_map/ppermute | solution.py:68
  519.7 127.0 %collective-permute-start.47 = (bf16[2048,1024]{1,0:T(8,128)(2,1)}, bf16[2048,1024]{1,0:T(8,128)(2,1)}, u32[]{:S(2)}, u32[]{:S(2)}) collective-permute-start(bf16[2048,1024]{1,0:T(8,128)(2,1)} %convolution_convert_fusion.1), channel_id=1, source_target_pairs={{0,1},{1,0},{2,3},{3,2},{4,5},{5,4},{6,7},{7,6},{8,9},{9,8},{10,11... | collective-permute-start | bytes 12582920 | tf_op jit(solution)/shard_map/ppermute | solution.py:68
  539.7 12.0 %collective-permute-start.33 = (bf16[16,128,256]{2,1,0:T(8,128)(2,1)}, bf16[16,128,256]{2,1,0:T(8,128)(2,1)S(1)}, u32[]{:S(2)}, u32[]{:S(2)}) collective-permute-start(bf16[16,128,256]{2,1,0:T(8,128)(2,1)} %bitcast.369), channel_id=1, source_target_pairs={{0,1},{1,0},{2,3},{3,2},{4,5},{5,4},{6,7},{7,6},{8,9},{9,8},{10,11... | collective-permute-start | bytes 3145736 | tf_op jit(solution)/shard_map/ppermute | solution.py:68
  553.8 31.0 %collective-permute-start.36 = (bf16[512,384]{1,0:T(8,128)(2,1)}, bf16[512,384]{1,0:T(8,128)(2,1)}, u32[]{:S(2)}, u32[]{:S(2)}) collective-permute-start(bf16[512,384]{1,0:T(8,128)(2,1)} %bitcast.68), channel_id=1, source_target_pairs={{0,20},{1,21},{2,22},{3,23},{4,16},{5,17},{6,18},{7,19},{8,28},{9,... | collective-permute-start | bytes 1179656 | tf_op jit(solution)/shard_map/ppermute | solution.py:68
  557.6 43.0 %collective-permute-start.35 = (bf16[512,384]{1,0:T(8,128)(2,1)}, bf16[512,384]{1,0:T(8,128)(2,1)}, u32[]{:S(2)}, u32[]{:S(2)}) collective-permute-start(bf16[512,384]{1,0:T(8,128)(2,1)} %bitcast.66), channel_id=1, source_target_pairs={{0,16},{1,17},{2,18},{3,19},{4,20},{5,21},{6,22},{7,23},{8,24},{9,... | collective-permute-start | bytes 1179656 | tf_op jit(solution)/shard_map/ppermute | solution.py:68
  558.1 42.4 %collective-permute-start.34 = (bf16[512,384]{1,0:T(8,128)(2,1)S(1)}, bf16[512,384]{1,0:T(8,128)(2,1)}, u32[]{:S(2)}, u32[]{:S(2)}) collective-permute-start(bf16[512,384]{1,0:T(8,128)(2,1)S(1)} %bitcast.366), channel_id=1, source_target_pairs={{0,4},{1,5},{2,6},{3,7},{4,0},{5,1},{6,2},{7,3},{8,12},{9,13},{10,... | collective-permute-start | bytes 1179656 | tf_op jit(solution)/shard_map/ppermute | solution.py:68
  620.8 19.0 %collective-permute-start.37 = (bf16[2,64,2048]{2,1,0:T(8,128)(2,1)S(1)}, bf16[2,64,2048]{2,1,0:T(8,128)(2,1)S(1)}, u32[]{:S(2)}, u32[]{:S(2)}) collective-permute-start(bf16[2,64,2048]{2,1,0:T(8,128)(2,1)S(1)} %slice_bitcast_fusion), channel_id=1, source_target_pairs={{0,8},{1,9},{2,10},{3,11},{4,12},{5,13},{6,14},{7,15},{8,0},{9,1},... | collective-permute-start | bytes 1572872 | tf_op jit(solution)/shard_map/ppermute | solution.py:68
  622.9 30.9 %collective-permute-start.39 = (bf16[2,64,2048]{2,1,0:T(8,128)(2,1)S(1)}, bf16[2,64,2048]{2,1,0:T(8,128)(2,1)S(1)}, u32[]{:S(2)}, u32[]{:S(2)}) collective-permute-start(bf16[2,64,2048]{2,1,0:T(8,128)(2,1)S(1)} %pad_maximum_fusion.16), channel_id=1, source_target_pairs={{0,2},{1,3},{2,0},{3,1},{4,6},{5,7},{6,4},{7,5},{8,10},{9,11},{10,... | collective-permute-start | bytes 1572872 | tf_op jit(solution)/shard_map/ppermute | solution.py:68
  628.3 159.7 %collective-permute-start.41 = (bf16[2048,768]{1,0:T(8,128)(2,1)}, bf16[2048,768]{1,0:T(8,128)(2,1)}, u32[]{:S(2)}, u32[]{:S(2)}) collective-permute-start(bf16[2048,768]{1,0:T(8,128)(2,1)} %convolution_convert_fusion.3), channel_id=1, source_target_pairs={{0,1},{1,0},{2,3},{3,2},{4,5},{5,4},{6,7},{7,6},{8,9},{9,8},{10,11... | collective-permute-start | bytes 9437192 | tf_op jit(solution)/shard_map/ppermute | solution.py:68
  639.8 17.6 %collective-permute-start.38 = (bf16[64,2048]{1,0:T(8,128)(2,1)S(1)}, bf16[64,2048]{1,0:T(8,128)(2,1)S(1)}, u32[]{:S(2)}, u32[]{:S(2)}) collective-permute-start(bf16[64,2048]{1,0:T(8,128)(2,1)S(1)} %fusion.37), channel_id=1, source_target_pairs={{0,2},{1,3},{2,0},{3,1},{4,6},{5,7},{6,4},{7,5},{8,10},{9,11},{10,... | collective-permute-start | bytes 786440 | tf_op jit(solution)/shard_map/ppermute | solution.py:68
  645.9 67.5 %collective-permute-start.45 = (bf16[1024,1024]{1,0:T(8,128)(2,1)}, bf16[1024,1024]{1,0:T(8,128)(2,1)}, u32[]{:S(2)}, u32[]{:S(2)}) collective-permute-start(bf16[1024,1024]{1,0:T(8,128)(2,1)} %slice.1463), channel_id=1, source_target_pairs={{0,4},{1,5},{2,6},{3,7},{4,0},{5,1},{6,2},{7,3},{8,12},{9,13},{10,... | collective-permute-start | bytes 6291464 | tf_op jit(solution)/shard_map/ppermute | solution.py:68
  652.6 104.2 %collective-permute-start.48 = (bf16[1024,1024]{1,0:T(8,128)(2,1)S(1)}, bf16[1024,1024]{1,0:T(8,128)(2,1)S(1)}, u32[]{:S(2)}, u32[]{:S(2)}) collective-permute-start(bf16[1024,1024]{1,0:T(8,128)(2,1)S(1)} %slice.1462), channel_id=1, source_target_pairs={{0,4},{1,5},{2,6},{3,7},{4,0},{5,1},{6,2},{7,3},{8,12},{9,13},{10,... | collective-permute-start | bytes 6291464 | tf_op jit(solution)/shard_map/ppermute | solution.py:68
  658.6 13.0 %collective-permute-start.40 = (bf16[64,2048]{1,0:T(8,128)(2,1)S(1)}, bf16[64,2048]{1,0:T(8,128)(2,1)S(1)}, u32[]{:S(2)}, u32[]{:S(2)}) collective-permute-start(bf16[64,2048]{1,0:T(8,128)(2,1)S(1)} %get-tuple-element.117), channel_id=1, source_target_pairs={{0,8},{1,9},{2,10},{3,11},{4,12},{5,13},{6,14},{7,15},{8,0},{9,1},... | collective-permute-start | bytes 786440 | tf_op jit(solution)/shard_map/ppermute | solution.py:68
  715.9 46.1 %collective-permute-start.46 = (bf16[512,1024]{1,0:T(8,128)(2,1)S(1)}, bf16[512,1024]{1,0:T(8,128)(2,1)S(1)}, u32[]{:S(2)}, u32[]{:S(2)}) collective-permute-start(bf16[512,1024]{1,0:T(8,128)(2,1)S(1)} %slice.1466), channel_id=1, source_target_pairs={{0,16},{1,17},{2,18},{3,19},{4,20},{5,21},{6,22},{7,23},{8,24},{9,... | collective-permute-start | bytes 3145736 | tf_op jit(solution)/shard_map/ppermute | solution.py:68
  758.7 48.0 %collective-permute-start.49 = (bf16[512,1024]{1,0:T(8,128)(2,1)}, bf16[512,1024]{1,0:T(8,128)(2,1)}, u32[]{:S(2)}, u32[]{:S(2)}) collective-permute-start(bf16[512,1024]{1,0:T(8,128)(2,1)} %slice.1465), channel_id=1, source_target_pairs={{0,16},{1,17},{2,18},{3,19},{4,20},{5,21},{6,22},{7,23},{8,24},{9,... | collective-permute-start | bytes 3145736 | tf_op jit(solution)/shard_map/ppermute | solution.py:68
  763.4 54.5 %all-to-all-start.6 = ((bf16[8,64,1024]{2,1,0:T(8,128)(2,1)}), bf16[8,64,1024]{2,1,0:T(8,128)(2,1)}, u32[]{:S(2)}, u32[]{:S(2)}) async-start(bf16[8,64,1024]{2,1,0:T(8,128)(2,1)} %bitcast.90), calls=%async_computation.7 | async-start | bytes 2097152 | tf_op jit(solution)/shard_map/all_to_all | solution.py:360
  795.4 37.5 %collective-permute-start.42 = (bf16[1024,768]{1,0:T(8,128)(2,1)}, bf16[1024,768]{1,0:T(8,128)(2,1)}, u32[]{:S(2)}, u32[]{:S(2)}) collective-permute-start(bf16[1024,768]{1,0:T(8,128)(2,1)} %slice.1464), channel_id=1, source_target_pairs={{0,4},{1,5},{2,6},{3,7},{4,0},{5,1},{6,2},{7,3},{8,12},{9,13},{10,... | collective-permute-start | bytes 4718600 | tf_op jit(solution)/shard_map/ppermute | solution.py:68
  817.8 56.2 %all-to-all-start.7 = ((bf16[8,64,1024]{2,1,0:T(8,128)(2,1)}), bf16[8,64,1024]{2,1,0:T(8,128)(2,1)}, u32[]{:S(2)}, u32[]{:S(2)}) async-start(bf16[8,64,1024]{2,1,0:T(8,128)(2,1)} %bitcast.92), calls=%async_computation.8 | async-start | bytes 2097152 | tf_op jit(solution)/shard_map/all_to_all | solution.py:360
  835.7 37.2 %collective-permute-start.43 = (bf16[512,768]{1,0:T(8,128)(2,1)S(1)}, bf16[512,768]{1,0:T(8,128)(2,1)S(1)}, u32[]{:S(2)}, u32[]{:S(2)}) collective-permute-start(bf16[512,768]{1,0:T(8,128)(2,1)S(1)} %slice.1467), channel_id=1, source_target_pairs={{0,16},{1,17},{2,18},{3,19},{4,20},{5,21},{6,22},{7,23},{8,24},{9,... | collective-permute-start | bytes 2359304 | tf_op jit(solution)/shard_map/ppermute | solution.py:68
  874.0 16.1 %all-to-all-start.5 = ((bf16[8,64,768]{2,1,0:T(8,128)(2,1)}), bf16[8,64,768]{2,1,0:T(8,128)(2,1)}, u32[]{:S(2)}, u32[]{:S(2)}) async-start(bf16[8,64,768]{2,1,0:T(8,128)(2,1)} %bitcast.87), calls=%async_computation.5 | async-start | bytes 1572864 | tf_op jit(solution)/shard_map/all_to_all | solution.py:360
  (64 other events, 453.1 us)
Sparse Core Ops, SparseCore 0:
  32.1 118.6 all-gather.1
  564.0 157.0 reduce-scatter.1

commit v2 on v1

v2 whole, which is shorter than its diff:
```python
import functools

import jax
import jax.numpy as jnp
import numpy as np
from jax import lax
from jax.experimental import pallas as pl
from jax.experimental.pallas import tpu as pltpu
from jax.sharding import PartitionSpec as P

HEADS = 16
HEAD = 128
AXES = ("tm", "space")
BLOCK = 128

epsilon = 1e-05
masked_value = -1e30
inv_root = HEAD ** (-0.5)
to_log2 = inv_root * 1.4426950408889634

bf16 = jnp.bfloat16
f32 = jnp.float32


def matmul(left, right, dims=((1,), (0,))):
    return lax.dot_general(left, right, (dims, ((), ())), preferred_element_type=f32)


def tied(*values):
    return lax.optimization_barrier(values)


class Plan:
    def __init__(self, tm, space, frame_rows):
        self.count = tm * space
        self.space = space
        self.slots = tm
        self.clip = min(16, tm)
        count = self.count
        self.team = (count // 2, count // 16)
        self.heads = (count // 4, count // 8)
        self.feed_team = (count // 4, count // 16)
        bits = [1 << i for i in range(count.bit_length() - 1)]
        taken = set(self.team + self.heads)
        self.parts = [b for b in reversed(bits) if b not in taken]
        rest = [b for b in self.parts if b != 1]
        self.gather = [*self.heads, *rest]
        self.feed_gather = [count // 2, count // 8, *rest]
        self.team_rel = [0, self.team[1], self.team[0], self.team[0] | self.team[1]]
        self.head_rel = [0, self.heads[1], self.heads[0], self.heads[0] | self.heads[1]]
        self.block_rel = [h | t for h in self.head_rel for t in self.team_rel]
        self.part_rel = [
            sum(b for j, b in enumerate(self.parts) if (i >> j) & 1)
            for i in range(1 << len(self.parts))
        ]
        devices = range(count)
        self.octets = self.groups(sum(self.team) | 1)
        self.feed_octets = self.groups(sum(self.feed_team) | 1)
        self.tile_blocks = 2 if self.team[1] < space else 1
        self.devices = devices

    def groups(self, mask):
        held = {}
        for d in range(self.count):
            held.setdefault(d & ~mask, []).append(d)
        return list(held.values())

    def swap(self, value, mask):
        return lax.ppermute(value, AXES, [(d, d ^ mask) for d in self.devices])


def layer_norm(values):
    center = jnp.mean(values, axis=-1, keepdims=True)
    shifted = values - center
    spread = jnp.mean(shifted * shifted, axis=-1, keepdims=True)
    scale = lax.rsqrt(spread + epsilon)
    return shifted * scale, scale


def layer_norm_back(grads, normed, scale):
    inner = jnp.mean(grads * normed, axis=-1, keepdims=True)
    return (grads - jnp.mean(grads, axis=-1, keepdims=True) - normed * inner) * scale


def transposed(tile):
    return tile.astype(f32).T.astype(tile.dtype)


def attend_kernel(plan, info, real, own, other, out, out_t, lse, keys, values, values_t):
    me = info[0]
    n_blocks = len(plan.block_rel)
    for part, part_rel in enumerate(plan.part_rel):

        def place(b, _, part=part, part_rel=part_rel):
            home = me ^ part_rel ^ info[8 + b]
            if part == 0:
                key, value = own[b, :, HEAD : 2 * HEAD], own[b, :, 2 * HEAD :]
            else:
                key, value = other[part - 1, b, :, :HEAD], other[part - 1, b, :, HEAD:]
            rows = pl.ds(pl.multiple_of(home * BLOCK, BLOCK), BLOCK)
            keys[rows, :] = key
            values[rows, :] = value
            values_t[home] = transposed(value)
            return 0

        lax.fori_loop(0, n_blocks, place, 0)

    frame = plan.space * BLOCK
    per_tile = plan.tile_blocks
    two = per_tile * BLOCK
    lane = lax.broadcasted_iota(jnp.int32, (1, two), 1)
    q_place = jnp.where(lane < BLOCK, info[1] + lane, info[2] + lane - BLOCK)

    def tile(i, _):
        slot, first = info[24 + i], info[40 + i]
        q = jnp.concatenate([own[per_tile * i + j, :, :HEAD] for j in range(per_tile)], axis=0)

        def scores(g):
            key = keys[pl.ds(pl.multiple_of(g * frame, frame), frame), :]
            return matmul(key, q, ((1,), (1,)))

        def value_t(g):
            return jnp.concatenate(
                [values_t[g * plan.space + s] for s in range(plan.space)], axis=1
            )

        s = scores(slot)
        k_place = lax.broadcasted_iota(jnp.int32, (frame, two), 0)
        s = jnp.where(k_place <= q_place, s, masked_value)
        top = jnp.max(s, axis=0, keepdims=True)
        p = jnp.exp2((s - top) * to_log2)
        total = jnp.sum(p, axis=0, keepdims=True)
        acc = matmul(value_t(slot), p.astype(bf16))

        def step(g, carry):
            def use(carry):
                top, total, acc = carry
                s = scores(g)
                new = jnp.maximum(top, jnp.max(s, axis=0, keepdims=True))
                fade = jnp.exp2((top - new) * to_log2)
                p = jnp.exp2((s - new) * to_log2)
                total = total * fade + jnp.sum(p, axis=0, keepdims=True)
                acc = acc * fade + matmul(value_t(g), p.astype(bf16))
                return new, total, acc

            return lax.cond(real[g] > 0, use, lambda c: c, carry)

        first = jnp.where(real[slot] > 0, first, slot)
        top, total, acc = lax.fori_loop(first, slot, step, (top, total, acc))
        lse[i] = top * to_log2 + jnp.log2(total)
        acc = acc / total
        out_t[i] = acc
        back = acc.T.astype(bf16)
        for j in range(per_tile):
            out[per_tile * i + j] = back[j * BLOCK : (j + 1) * BLOCK]
        return 0

    lax.fori_loop(0, n_blocks // per_tile, tile, 0)


def attend_back_kernel(
    plan, info, real, own, keys, values, grads, out_t, lse, dq, dkv_own, dkv_other, dk, dv, keys_t
):
    me = info[0]
    n_blocks = len(plan.block_rel)

    def clear(b, _):
        rows = pl.ds(pl.multiple_of(b * BLOCK, BLOCK), BLOCK)
        dk[rows, :] = jnp.zeros((BLOCK, HEAD), f32)
        dv[rows, :] = jnp.zeros((BLOCK, HEAD), f32)
        keys_t[b] = transposed(keys[rows, :])
        return 0

    lax.fori_loop(0, plan.count, clear, 0)

    frame = plan.space * BLOCK
    per_tile = plan.tile_blocks
    two = per_tile * BLOCK
    lane = lax.broadcasted_iota(jnp.int32, (1, two), 1)
    q_place = jnp.where(lane < BLOCK, info[1] + lane, info[2] + lane - BLOCK)

    def tile(i, _):
        slot, first = info[24 + i], info[40 + i]
        q = jnp.concatenate([own[per_tile * i + j, :, :HEAD] for j in range(per_tile)], axis=0)
        do = jnp.concatenate([grads[per_tile * i + j] for j in range(per_tile)], axis=0)
        delta = jnp.sum(do.astype(f32).T * out_t[i], axis=0, keepdims=True)
        log_total = lse[i]

        def turn(g, mask):
            rows = pl.ds(pl.multiple_of(g * frame, frame), frame)
            key, value = keys[rows, :], values[rows, :]
            s = matmul(key, q, ((1,), (1,)))
            dp = matmul(value, do, ((1,), (1,)))
            p = jnp.exp2(s * to_log2 - log_total)
            if mask:
                k_place = lax.broadcasted_iota(jnp.int32, (frame, two), 0)
                p = jnp.where(k_place <= q_place, p, 0.0)
            ds = (p * (dp - delta)).astype(bf16)
            dv[rows, :] += matmul(p.astype(bf16), do)
            dk[rows, :] += matmul(ds, q)
            key_t = jnp.concatenate(
                [keys_t[g * plan.space + s] for s in range(plan.space)], axis=1
            )
            return matmul(key_t, ds)

        dq_t = turn(slot, True)

        def step(g, dq_t):
            return lax.cond(real[g] > 0, lambda c: c + turn(g, False), lambda c: c, dq_t)

        first = jnp.where(real[slot] > 0, first, slot)
        dq_t = lax.fori_loop(first, slot, step, dq_t)
        back = (dq_t * inv_root).T.astype(bf16)
        for j in range(per_tile):
            dq[per_tile * i + j] = back[j * BLOCK : (j + 1) * BLOCK]
        return 0

    lax.fori_loop(0, n_blocks // per_tile, tile, 0)

    for part, part_rel in enumerate(plan.part_rel):

        def hand_out(b, _, part=part, part_rel=part_rel):
            home = me ^ part_rel ^ info[8 + b]
            rows = pl.ds(pl.multiple_of(home * BLOCK, BLOCK), BLOCK)
            pair = jnp.concatenate([dk[rows, :] * inv_root, dv[rows, :]], axis=1).astype(bf16)
            if part == 0:
                dkv_own[b] = pair
            else:
                dkv_other[part - 1, b] = pair
            return 0

        lax.fori_loop(0, n_blocks, hand_out, 0)


def call(kernel, n_scalar, n_in, outs, scratch, cost):
    return pl.pallas_call(
        kernel,
        out_shape=outs,
        in_specs=[pl.BlockSpec(memory_space=pltpu.SMEM)] * n_scalar
        + [pl.BlockSpec(memory_space=pltpu.VMEM)] * n_in,
        out_specs=tuple(pl.BlockSpec(memory_space=pltpu.VMEM) for _ in outs),
        scratch_shapes=scratch,
        cost_estimate=cost,
        compiler_params=pltpu.CompilerParams(vmem_limit_bytes=50 << 20),
    )


def moving(n_bytes):
    return pl.CostEstimate(flops=n_bytes, bytes_accessed=n_bytes, transcendentals=0)


def arrange_kernel(normed, chunk, lanes, value, out, held):
    x = value[...].astype(f32)
    if normed:
        x = layer_norm(x)[0]
    held[...] = x.astype(bf16)
    for j in range(x.shape[1] // chunk):
        at = pl.multiple_of(lanes[j], chunk)
        out[:, j * chunk : (j + 1) * chunk] = held[:, pl.ds(at, chunk)]


def arrange(normed, chunk, lanes, value):
    shape = value.shape
    return call(
        functools.partial(arrange_kernel, normed, chunk),
        1,
        1,
        (jax.ShapeDtypeStruct(shape, bf16),),
        [pltpu.VMEM(shape, bf16)],
        moving(4 * value.size),
    )(lanes, value)[0]


def team_rows_kernel(a, b, a_lo, b_hi, a_far, b_far, out):
    one, two = a.shape[0], b.shape[0]
    pieces = (a[...], b[...], a_lo[...], b_far[:two], a_far[:one], b_hi[...], a_far[one:], b_far[two:])
    start = 0
    for piece in pieces:
        out[start : start + piece.shape[0]] = piece
        start += piece.shape[0]


def team_rows(*pieces):
    rows, width = pieces[0].shape[0] + pieces[1].shape[0], pieces[0].shape[1]
    return call(
        team_rows_kernel,
        0,
        6,
        (jax.ShapeDtypeStruct((4 * rows, width), bf16),),
        [],
        moving(16 * rows * width),
    )(*pieces)[0]


def turn_back_kernel(places, cosine, sine, *refs):
    heads, out = refs[:4], refs[4]
    half_dim = HEAD // 2
    cos, sin = cosine[...], sine[...]
    for r in range(4):
        found = []
        for i in range(2):
            t = heads[r][:, i * HEAD : (i + 1) * HEAD].astype(f32)
            scaled = t * sin
            turned = jnp.concatenate([scaled[:, half_dim:], -scaled[:, :half_dim]], axis=-1)
            found.append((t * cos + turned).astype(bf16))
        found.append(heads[r][:, 2 * HEAD :])
        whole = jnp.concatenate(found, axis=1)
        place = places[r]

        @pl.when(place % 2 == 0)
        def _():
            out[place // 2, :, : 3 * HEAD] = whole

        @pl.when(place % 2 == 1)
        def _():
            out[place // 2, :, 3 * HEAD :] = whole


def turn_back(places, cosine, sine, heads):
    rows = cosine.shape[0]
    return call(
        turn_back_kernel,
        1,
        6,
        (jax.ShapeDtypeStruct((2, rows, 6 * HEAD), bf16),),
        [],
        moving(8 * rows * 3 * HEAD * 2),
    )(places, cosine, sine, *heads)[0]


def deliver_kernel(columns, got, weight, gain, out, gain_grad):
    total = None
    for block, start, end, target in columns:
        value = got[block, :, start:end].astype(f32)
        span = slice(target, target + end - start)
        part = jnp.sum(value * weight[:, span].astype(f32), axis=1, keepdims=True)
        total = part if total is None else total + part
        out[:, span] = value * gain[...]
    gain_grad[...] = jnp.broadcast_to(total, gain_grad.shape)


def deliver(columns, got, weight, gain):
    rows, width = weight.shape
    return call(
        functools.partial(deliver_kernel, columns),
        0,
        3,
        (jax.ShapeDtypeStruct((rows, width), f32), jax.ShapeDtypeStruct((rows, 128), f32)),
        [],
        moving(8 * rows * width),
    )(got, weight, gain)


def attend(plan, info, real, own, other):
    blocks = len(plan.block_rel)
    tokens = plan.count * BLOCK
    work = blocks * BLOCK * min(plan.clip * plan.space * BLOCK, tokens) // 2
    shape = jax.ShapeDtypeStruct
    return call(
        functools.partial(attend_kernel, plan),
        2,
        2,
        (
            shape((blocks, BLOCK, HEAD), bf16),
            shape((blocks // plan.tile_blocks, HEAD, plan.tile_blocks * BLOCK), f32),
            shape((blocks // plan.tile_blocks, 1, plan.tile_blocks * BLOCK), f32),
            shape((tokens, HEAD), bf16),
            shape((tokens, HEAD), bf16),
        ),
        [pltpu.VMEM((plan.count, HEAD, BLOCK), bf16)],
        pl.CostEstimate(flops=8 * work * HEAD, bytes_accessed=8 << 20, transcendentals=work),
    )(info, real, own, other)


def attend_back(plan, info, real, own, keys, values, grads, out_t, lse):
    blocks = len(plan.block_rel)
    tokens = plan.count * BLOCK
    work = blocks * BLOCK * min(plan.clip * plan.space * BLOCK, tokens) // 2
    shape = jax.ShapeDtypeStruct
    return call(
        functools.partial(attend_back_kernel, plan),
        2,
        6,
        (
            shape((blocks, BLOCK, HEAD), bf16),
            shape((blocks, BLOCK, 2 * HEAD), bf16),
            shape((len(plan.part_rel) - 1, blocks, BLOCK, 2 * HEAD), bf16),
        ),
        [
            pltpu.VMEM((tokens, HEAD), f32),
            pltpu.VMEM((tokens, HEAD), f32),
            pltpu.VMEM((plan.count, HEAD, BLOCK), bf16),
        ],
        pl.CostEstimate(flops=20 * work * HEAD, bytes_accessed=8 << 20, transcendentals=work),
    )(info, real, own, keys, values, grads, out_t, lse)


def added(*values):
    return sum(v.astype(f32) for v in values).astype(bf16)


def quarters(value):
    return jnp.split(value, 4)


class Side:
    def __init__(self, plan, me, team, gather, groups, shard, width, rows, cut):
        self.plan, self.me, self.groups = plan, me, groups
        self.team_hi, self.team_lo = team
        self.gather, self.shard, self.cut = gather, shard, cut
        self.first, self.second = gather[:2]
        low = self.low = min(gather)
        self.chunk = low * shard
        self.n_chunks = width // self.chunk
        self.order = [
            (
                sum(b for j, b in enumerate(gather) if (i >> j) & 1)
                + (self.team_hi if hi else 0)
                + (self.team_lo if lo else 0)
            )
            // low
            for i in range(1 << len(gather))
            for hi in range(2)
            for lo in range(2 if self.team_lo > low else 1)
        ]
        self.inverse = [self.order.index(m) for m in range(self.n_chunks)]
        at = jnp.array(self.order, jnp.int32) ^ ((me & sum(gather)) // low)
        self.lanes = at * self.chunk

    def swap(self, value, bit):
        return self.plan.swap(value, bit)

    def flipped(self, pieces):
        for bit in self.gather:
            step = bit // self.low
            own = (self.me & bit) != 0
            pieces = [jnp.where(own, pieces[m ^ step], pieces[m]) for m in range(self.n_chunks)]
        return pieces

    def pieces(self, value):
        chunk = self.chunk
        return [value[:, m * chunk : (m + 1) * chunk] for m in range(self.n_chunks)]

    def to_rel(self, value, normed):
        if self.chunk % 128 == 0:
            return arrange(normed, self.chunk, self.lanes, value)
        value = layer_norm(value.astype(f32))[0] if normed else value
        pieces = self.flipped(self.pieces(value.astype(bf16)))
        return jnp.concatenate([pieces[m] for m in self.order], axis=1)

    def from_rel(self, value):
        pieces = self.pieces(value)
        return jnp.concatenate(self.flipped([pieces[m] for m in self.inverse]), axis=1)

    def gather_one(self, value):
        a, b = value[: self.cut], value[self.cut :]
        return a, b, self.swap(a, self.team_lo), self.swap(b, self.team_hi)

    def gather_two(self, a, b, a_lo, b_hi):
        return (
            self.swap(jnp.concatenate([a, a_lo]), self.team_hi),
            self.swap(jnp.concatenate([b, b_hi]), self.team_lo),
        )

    def scatter_one(self, parts):
        parts = parts.reshape(4, parts.shape[0] // 4, -1)
        a, b = parts[:, : self.cut], parts[:, self.cut :]
        a_got = self.swap(a[2:], self.team_hi)
        b_got = self.swap(jnp.stack([b[1], b[3]]), self.team_lo)
        return a[:2], jnp.stack([b[0], b[2]]), a_got, b_got

    def scatter_two(self, a, b, a_got, b_got):
        a_last = self.swap(added(a[1], a_got[1]), self.team_lo)
        b_last = self.swap(added(b[1], b_got[1]), self.team_hi)
        a_sum = a[0].astype(f32) + a_got[0].astype(f32) + a_last.astype(f32)
        b_sum = b[0].astype(f32) + b_got[0].astype(f32) + b_last.astype(f32)
        return jnp.concatenate([a_sum, b_sum])

    def octet(self, value):
        value = value.reshape(8, self.shard, -1)
        return lax.all_to_all(value, AXES, 0, 0, axis_index_groups=self.groups)

    def joined(self, *blocks):
        whole = jnp.concatenate(blocks)
        for bit in self.gather[2:]:
            whole = jnp.concatenate([whole, self.swap(whole, bit)])
        return whole

    def first_sum(self, mine, others_swapped):
        block = added(mine, others_swapped)
        for bit in reversed(self.gather[2:]):
            block = block.reshape(2, block.shape[0] // 2, -1)
            block = added(block[0], self.swap(block[1], bit))
        return block.reshape(4, 8 * self.shard, -1)


def on_device(
    plan, layer_input, frame_real, gain_attn, w_qkv, w_out, gain_mlp, w_up, w_down, cotangent
):
    rows = layer_input.shape[1]
    width = layer_input.shape[2]
    shard = w_up.shape[0]
    space = plan.space
    me = lax.axis_index("tm") * space + lax.axis_index("space")
    inputs = layer_input[0].astype(f32)
    grad_out = cotangent[0].astype(f32)
    swap = plan.swap
    attn = Side(plan, me, plan.team, plan.gather, plan.octets, shard, width, rows, rows * 3 // 8)
    feed = Side(
        plan, me, plan.feed_team, plan.feed_gather, plan.feed_octets, shard, width, rows, rows // 2
    )

    def has(bit):
        return (me & bit) != 0

    gain_one = gain_attn.astype(f32)[:, None]
    gain_two = gain_mlp.astype(f32)[:, None]
    qkv_scaled = (w_qkv.astype(f32) * gain_one).astype(bf16)
    up_scaled = (w_up.astype(f32) * gain_two).astype(bf16)
    n_ff = w_up.shape[1] // 8
    qkv_sent = (
        qkv_scaled.reshape(shard, 3, 2, 2, 2, 2, HEAD)
        .transpose(2, 5, 3, 0, 4, 1, 6)
        .reshape(8, shard, 6 * HEAD)
    )
    qkv_columns = [
        (
            4 * hi + 2 * lo + c,
            (3 * jj + i) * HEAD,
            (3 * jj + i + 1) * HEAD,
            (i * HEADS + 8 * hi + 4 * c + 2 * jj + lo) * HEAD,
        )
        for hi in range(2)
        for lo in range(2)
        for c in range(2)
        for jj in range(2)
        for i in range(3)
    ]
    ff_columns = [(b, 0, n_ff, b * n_ff) for b in range(8)]
    up_sent = up_scaled.reshape(shard, 8, n_ff).transpose(1, 0, 2)
    down_sent = w_down.reshape(shard, 8, n_ff).transpose(1, 0, 2)

    first_rel = attn.to_rel(layer_input[0], True)
    grad_rel = feed.to_rel(cotangent[0], False)
    qkv_block = attn.octet(qkv_sent).reshape(8 * shard, -1)
    qkv_block, first_rel, grad_rel, up_sent, down_sent = tied(
        qkv_block, first_rel, grad_rel, up_sent, down_sent
    )
    qkv_first = swap(qkv_block, attn.first)
    qkv_second = swap(qkv_block, attn.second)
    first_near = attn.gather_one(first_rel)
    qkv_first, qkv_second, first_near, up_sent = tied(qkv_first, qkv_second, first_near, up_sent)
    qkv_both = swap(qkv_first, attn.second)
    first_far = attn.gather_two(*first_near)
    up_block = feed.octet(up_sent).reshape(8 * shard, -1)
    qkv_both, first_far, up_block, down_sent, w_out = tied(
        qkv_both, first_far, up_block, down_sent, w_out
    )
    qkv_mine = attn.joined(qkv_block, qkv_first, qkv_second, qkv_both)
    qkv_other = swap(qkv_mine, 1)
    first_all = team_rows(*first_near, *first_far)
    up_rows = quarters(up_block)
    up_z = [swap(up_rows[i], feed.first) for i in (0, 1)]
    up_x = [swap(up_rows[i], feed.second) for i in (0, 1)]
    out_x = swap(w_out, attn.second)
    down_block = feed.octet(down_sent).reshape(8 * shard, -1)

    team_device = me ^ jnp.array(plan.team_rel, jnp.int32)
    row_index = jnp.arange(rows, dtype=jnp.int32)
    positions = (
        ((team_device // space) % plan.clip * (space * rows) + (team_device % space) * rows)[:, None]
        + row_index[None, :]
    ).reshape(4 * rows)
    half_dim = HEAD // 2
    inverse_freq = jnp.exp(-jnp.log(10000.0) * jnp.arange(half_dim, dtype=f32) * 2.0 / HEAD)
    angles = positions.astype(f32)[:, None] * inverse_freq[None, :]
    angles = jnp.concatenate([angles, angles], axis=-1)
    cosine, sine = jnp.cos(angles), jnp.sin(angles)

    def rotate(value):
        turned = jnp.concatenate([-value[:, half_dim:], value[:, :half_dim]], axis=-1)
        return value * cosine + turned * sine

    def rotate_back(value):
        scaled = value * sine
        turned = jnp.concatenate([scaled[:, half_dim:], -scaled[:, :half_dim]], axis=-1)
        return value * cosine + turned

    def head_triples(mixed):
        found = []
        for j in range(2):
            q, k, v = (
                mixed[:, (3 * j + i) * HEAD : (3 * j + i + 1) * HEAD] for i in range(3)
            )
            found.append(jnp.concatenate([rotate(q), rotate(k), v], axis=1).astype(bf16))
        return found

    mixed_mine = matmul(first_all, qkv_mine)
    mixed_other = matmul(first_all, qkv_other)
    stack = jnp.stack(head_triples(mixed_mine) + head_triples(mixed_other))
    my_head = jnp.where(has(plan.heads[0]), 2, 0) + jnp.where(has(plan.heads[1]), 1, 0)
    core_flip = jnp.where(has(1), 2, 0)
    pick = [(my_head ^ r) ^ core_flip for r in range(4)]
    sent = [lax.dynamic_index_in_dim(stack, pick[r], 0, keepdims=False) for r in range(4)]
    sent, up_z, up_x, out_x, down_block, up_rows = tied(
        sent, up_z, up_x, out_x, down_block, up_rows
    )
    got = [swap(sent[r], plan.head_rel[r]) for r in range(1, 4)]
    up_z += [swap(up_rows[i], feed.first) for i in (2, 3)]
    got, up_z, up_rows, down_block, grad_rel = tied(got, up_z, up_rows, down_block, grad_rel)
    down_rows = quarters(down_block)
    own = jnp.stack([sent[0]] + got).reshape(16, rows, 3 * HEAD)
    down_z = [swap(down_rows[i], feed.first) for i in (0, 1)]
    up_x += [swap(up_rows[i], feed.second) for i in (2, 3)]
    up_both = [swap(up_z[i], feed.second) for i in (0, 1)]
    grad_near = feed.gather_one(grad_rel)
    out_z = swap(jnp.stack([w_out, out_x]), attn.first)
    shared = own[:, :, HEAD:]
    other = jnp.stack([swap(shared, rel) for rel in plan.part_rel[1:]])

    block_rel = jnp.array(plan.block_rel, jnp.int32)
    tile_rel = jnp.array(plan.block_rel[:: plan.tile_blocks], jnp.int32)
    tile_slot = (me ^ tile_rel) // space
    no_more = jnp.zeros((16 - tile_slot.shape[0],), jnp.int32)
    info = jnp.concatenate(
        [
            jnp.stack([me, (me % space) * rows, ((me ^ plan.team[1]) % space) * rows]),
            jnp.zeros((5,), jnp.int32),
            block_rel,
            tile_slot,
            no_more,
            tile_slot // plan.clip * plan.clip,
            no_more,
        ]
    ).astype(jnp.int32)

    attended, attended_t, log_total, keys, values = attend(plan, info, frame_real, own, other)
    attended, down_z, up_x, up_both, grad_near, out_z, down_rows = tied(
        attended, down_z, up_x, up_both, grad_near, out_z, down_rows
    )
    attended = attended.reshape(4, 4 * rows, HEAD)
    heads_got = [swap(attended[r], plan.head_rel[r]) for r in range(1, 4)]
    down_z += [swap(down_rows[2], feed.first)]
    grad_far = feed.gather_two(*grad_near)
    w_team = jnp.stack([w_out, out_x, out_z[0], out_z[1]])
    for bit in reversed(plan.parts):
        w_got = swap(w_team, bit)
        w_team = jnp.where(
            has(bit),
            jnp.concatenate([w_got, w_team], axis=1),
            jnp.concatenate([w_team, w_got], axis=1),
        )
    w_team = w_team.reshape(4 * HEAD, width)
    heads_got, w_team, down_z, grad_far, up_z, down_rows = tied(
        heads_got, w_team, down_z, grad_far, up_z, down_rows
    )
    attended_team = jnp.concatenate([attended[0]] + heads_got, axis=1)
    branch = matmul(attended_team, w_team).astype(bf16)
    branch_near = attn.scatter_one(branch)
    up_both += [swap(up_z[i], feed.second) for i in (2, 3)]
    down_x = [swap(down_rows[i], feed.second) for i in (0, 1)]
    grad_all = team_rows(*grad_near, *grad_far)
    branch_near, up_both, down_x, grad_all, down_rows, down_z = tied(
        branch_near, up_both, down_x, grad_all, down_rows, down_z
    )
    middle = attn.scatter_two(*branch_near)
    down_x += [swap(down_rows[i], feed.second) for i in (2, 3)]
    up_mine = feed.joined(up_block, *up_z, *up_x, *up_both)
    middle, down_x, up_mine, down_rows, down_z = tied(middle, down_x, up_mine, down_rows, down_z)
    middle = inputs + middle
    second_near = feed.gather_one(feed.to_rel(middle, True))
    down_z += [swap(down_rows[3], feed.first)]
    down_both = [swap(down_z[0], feed.second)]
    up_other = swap(up_mine, 1)
    second_near, down_z, down_both, up_other = tied(second_near, down_z, down_both, up_other)
    second_far = feed.gather_two(*second_near)
    down_both += [swap(down_z[i], feed.second) for i in (1, 2, 3)]
    second_far, down_both = tied(second_far, down_both)
    second_all = team_rows(*second_near, *second_far)
    normed_two, scale_two = layer_norm(middle)
    down_mine = feed.joined(down_block, *down_z, *down_x, *down_both)
    down_other = swap(down_mine, 1)
    gelu = functools.partial(jax.nn.gelu, approximate=True)
    hidden_other = matmul(second_all, up_other)
    hidden_mine = matmul(second_all, up_mine)
    act_other = gelu(hidden_other).astype(bf16)
    act_mine = gelu(hidden_mine).astype(bf16)
    down_other_grad = matmul(grad_all, act_other, ((0,), (0,))).astype(bf16)
    down_other_grad, down_other, down_mine, act_mine, act_other = tied(
        down_other_grad, down_other, down_mine, act_mine, act_other
    )
    down_swapped = swap(down_other_grad, 1)
    down_mine_grad = matmul(grad_all, act_mine, ((0,), (0,))).astype(bf16)

    def back(hidden, down):
        return jax.vjp(gelu, hidden)[1](matmul(grad_all, down))[0].astype(bf16)

    hid_mine, hid_other = back(hidden_mine, down_mine), back(hidden_other, down_other)
    second_parts = matmul(hid_mine, up_mine, ((1,), (1,))) + matmul(hid_other, up_other, ((1,), (1,)))
    second_parts, hid_mine, hid_other, down_swapped, down_mine_grad = tied(
        second_parts.astype(bf16), hid_mine, hid_other, down_swapped, down_mine_grad
    )
    second_back = feed.scatter_one(second_parts)
    down_sum = feed.first_sum(down_mine_grad, down_swapped)
    down_sum = [quarters(part) for part in down_sum]
    down_x3 = [swap(down_sum[3][i], feed.second) for i in (0, 1)]
    second_back, down_x3, down_sum = tied(second_back, down_x3, down_sum)
    grad_second = feed.scatter_two(*second_back)
    down_x3 += [swap(down_sum[3][2], feed.second)]
    down_z1 = [swap(added(down_sum[1][0], down_x3[0]), feed.first)]
    grad_second, down_x3, down_z1, down_sum = tied(grad_second, down_x3, down_z1, down_sum)
    grad_second = feed.from_rel(grad_second)
    grad_middle = grad_out + layer_norm_back(grad_second, normed_two, scale_two)
    middle_near = attn.gather_one(grad_middle.astype(bf16))
    down_x3 += [swap(down_sum[3][3], feed.second)]
    down_x2 = [swap(down_sum[2][0], feed.second)]
    out_parts = (
        matmul(act_mine, down_mine, ((1,), (1,))) + matmul(act_other, down_other, ((1,), (1,)))
    ).astype(bf16)
    middle_near, down_x3, down_x2, down_sum, out_parts, hid_other, hid_mine = tied(
        middle_near, down_x3, down_x2, down_sum, out_parts, hid_other, hid_mine
    )
    middle_far = attn.gather_two(*middle_near)
    down_x2 += [swap(down_sum[2][i], feed.second) for i in (1, 2, 3)]
    up_other_grad = matmul(second_all, hid_other, ((0,), (0,))).astype(bf16)
    up_mine_grad = matmul(second_all, hid_mine, ((0,), (0,))).astype(bf16)
    middle_far, down_x2, up_other_grad, up_mine_grad, down_sum, down_x3 = tied(
        middle_far, down_x2, up_other_grad, up_mine_grad, down_sum, down_x3
    )
    middle_all = team_rows(*middle_near, *middle_far)
    grad_heads = matmul(middle_all, w_team, ((1,), (1,))).astype(bf16)
    grad_own = grad_heads[:, :HEAD]
    grad_got = [
        swap(grad_heads[:, r * HEAD : (r + 1) * HEAD], plan.head_rel[r]) for r in range(1, 4)
    ]
    up_swapped = swap(up_other_grad, 1)
    down_z1 += [swap(added(down_sum[1][1], down_x3[1]), feed.first)]
    out_grad = matmul(attended_team, middle_all, ((0,), (0,))).astype(bf16).reshape(4, HEAD, width)
    up_sum = feed.first_sum(up_mine_grad, up_swapped)
    up_sum = [quarters(part) for part in up_sum]
    grad_got, up_sum, down_z1, out_grad, down_sum, down_x3 = tied(
        grad_got, up_sum, down_z1, out_grad, down_sum, down_x3
    )
    up_x3 = [swap(up_sum[3][i], feed.second) for i in range(4)]
    down_z1 += [swap(added(down_sum[1][i], down_x3[i]), feed.first) for i in (2, 3)]
    out_near = feed.scatter_one(out_parts)
    for bit in plan.parts:
        lower, upper = jnp.split(out_grad, 2, axis=1)
        kept = jnp.where(has(bit), upper, lower)
        out_grad = added(kept, swap(jnp.where(has(bit), lower, upper), bit))
    dq, dkv_own, dkv_other = attend_back(
        plan,
        info,
        frame_real,
        own,
        keys,
        values,
        jnp.stack([grad_own] + grad_got).reshape(16, rows, HEAD),
        attended_t,
        log_total,
    )
    dq, dkv_own, dkv_other, up_x3, down_z1, out_near, out_grad = tied(
        dq, dkv_own, dkv_other, up_x3, down_z1, out_near, out_grad
    )
    dkv = dkv_own.astype(f32)
    for i, rel in enumerate(plan.part_rel[1:]):
        dkv = dkv + swap(dkv_other[i], rel).astype(f32)
    triple = jnp.concatenate([dq, dkv.astype(bf16)], axis=2).reshape(4, 4 * rows, 3 * HEAD)
    triple, up_sum, up_x3, down_z1 = tied(triple, up_sum, up_x3, down_z1)
    got = [swap(triple[r], plan.head_rel[r]) for r in range(1, 4)]
    up_z1 = [swap(added(up_sum[1][i], up_x3[i]), feed.first) for i in (0, 1)]
    down_done = jnp.concatenate(
        [added(down_sum[0][i], down_x2[i], down_z1[i]) for i in range(4)]
    )
    got, up_z1, down_done, up_sum, up_x3, out_near, out_grad = tied(
        got, up_z1, down_done, up_sum, up_x3, out_near, out_grad
    )
    places = (my_head ^ jnp.arange(4, dtype=jnp.int32)) ^ core_flip
    mixed_grad = turn_back(places, cosine, sine, [triple[0]] + got)
    mixed_grad_mine, mixed_grad_other = mixed_grad[0], mixed_grad[1]
    qkv_other_grad = matmul(first_all, mixed_grad_other, ((0,), (0,))).astype(bf16)
    up_x2 = [swap(up_sum[2][i], feed.second) for i in (0, 1)]
    up_z1 += [swap(added(up_sum[1][2], up_x3[2]), feed.first)]
    out_sum = feed.scatter_two(*out_near)
    out_grad = added(out_grad[:2], swap(out_grad[2:], attn.first))
    qkv_other_grad, mixed_grad_mine, up_x2, up_z1, out_sum, out_grad, up_sum, down_done = tied(
        qkv_other_grad, mixed_grad_mine, up_x2, up_z1, out_sum, out_grad, up_sum, down_done
    )
    qkv_swapped = swap(qkv_other_grad, 1)
    qkv_mine_grad = matmul(first_all, mixed_grad_mine, ((0,), (0,))).astype(bf16)
    first_parts = matmul(mixed_grad_mine, qkv_mine, ((1,), (1,))) + matmul(
        mixed_grad_other, qkv_other, ((1,), (1,))
    )
    up_x2 += [swap(up_sum[2][i], feed.second) for i in (2, 3)]
    up_z1 += [swap(added(up_sum[1][3], up_x3[3]), feed.first)]
    down_got = feed.octet(down_done)
    qkv_sum = attn.first_sum(qkv_mine_grad, qkv_swapped)
    qkv_sum, first_parts, up_x2, up_z1, down_got, up_sum = tied(
        qkv_sum, first_parts.astype(bf16), up_x2, up_z1, down_got, up_sum
    )
    qkv_x3 = swap(qkv_sum[3], attn.second)
    first_back = attn.scatter_one(first_parts)
    up_done = jnp.concatenate([added(up_sum[0][i], up_x2[i], up_z1[i]) for i in range(4)])
    up_got = feed.octet(up_done)
    output = (middle + feed.from_rel(out_sum)).astype(bf16)
    qkv_x3, first_back, up_got, qkv_sum, out_grad, output = tied(
        qkv_x3, first_back, up_got, qkv_sum, out_grad, output
    )
    qkv_z1 = swap(added(qkv_sum[1], qkv_x3), attn.first)
    qkv_x2 = swap(qkv_sum[2], attn.second)
    first_rows = attn.scatter_two(*first_back)
    grad_down = down_got.transpose(1, 0, 2).reshape(shard, 8 * n_ff).astype(f32)
    grad_up, grad_gain_two = deliver(ff_columns, up_got, w_up, gain_two)
    qkv_z1, qkv_x2, first_rows, grad_down, grad_up, out_grad = tied(
        qkv_z1, qkv_x2, first_rows, grad_down, grad_up, out_grad
    )
    qkv_got = attn.octet(added(qkv_sum[0], qkv_x2, qkv_z1))
    grad_first = attn.from_rel(first_rows)
    grad_inputs = grad_middle + layer_norm_back(grad_first, *layer_norm(inputs))
    out_grad = out_grad[0].astype(f32) + swap(out_grad[1], attn.second).astype(f32)
    grad_qkv, grad_gain_one = deliver(qkv_columns, qkv_got, w_qkv, gain_one)
    return (
        output[None],
        grad_inputs[None],
        grad_gain_one[:, 0],
        grad_qkv,
        out_grad,
        grad_gain_two[:, 0],
        grad_up,
        grad_down,
    )


def solution(mesh):
    plan = Plan(mesh.shape["tm"], mesh.shape["space"], BLOCK)
    tokens = P("tm", "space", None)
    line = P(("tm", "space"))
    table = P(("tm", "space"), None)
    return jax.shard_map(
        functools.partial(on_device, plan),
        mesh=mesh,
        in_specs=(tokens, P(), line, table, table, line, table, table, tokens),
        out_specs=(tokens, tokens, line, table, table, line, table, table),
        check_vma=False,
    )
```

time: 916 us -> 734 us (0.80)
  waiting for transfers between devices: 475 us -> 328 us
  other arithmetic: 99.7 us -> 49.1 us
  matrix products: 107 us -> 78.2 us
  Pallas kernels: 36.6 us -> 60.4 us
  starting transfers between devices: 118 us -> 140 us
  local copies, waits for them, and re-layouts: 53.3 us -> 67.2 us
  between operations: 16.4 us -> 3.71 us
    ppermute x50 -> x112, waiting for transfers between devices: 455 us -> 294 us  [swap(): return lax.ppermute(value, AXES, [(d, d ^ mask) for d in self.devices])]
    ppermute x50 -> x112, starting transfers between devices: 61.2 us -> 113 us  [swap(): return lax.ppermute(value, AXES, [(d, d ^ mask) for d in self.devices])]
    all_to_all x8 -> x6, starting transfers between devices: 56.7 us -> 27.2 us  [octet(): return lax.all_to_all(value, AXES, 0, 0, axis_index_groups=self.groups)]
    dot_general x21, matrix products: 107 us -> 78.2 us  [matmul(): lax.dot_general(left, right, (dims, ((), ())), preferred_element_type=f32)]
    concatenate x17, other arithmetic: 24.7 us -> 2.82 us  [the longest x1 1.04 us: on_device(): jnp.concatenate([added(down_sum[0][i], down_x2[i], down_z1[i]) for i in r...]
    add x14 -> x9, other arithmetic: 23.2 us -> 1.59 us  [the longest x1 0.85 us: on_device(): out_grad[0].astype(f32) + swap(out_grad[1], attn.second).astype(f32)]
    unnamed x64 -> x22, other arithmetic: 21 us -> 0.86 us
    convert_element_type x12 -> x33, other arithmetic: 8.96 us -> 26.2 us  [the longest x31 23.7 us: added(): return sum((v.astype(f32) for v in values)).astype(bf16)]
  transfers between devices with their start and end apart: 60 -> 118, of which waited for: 31 -> 53; matrix products, arithmetic and copies ran while one was open for 24% -> 21% of each run, Pallas kernels for 4% -> 8%
where the time goes in v2:
time: 734 us; the launch traced here: 727 us
  waiting for transfers between devices  328 us (45%)
  starting transfers between devices  140 us (19%)
  matrix products  78.2 us (11%)
  local copies, waits for them, and re-layouts  67.2 us (9%)
  Pallas kernels  60.4 us (8%)
  other arithmetic  49.1 us (7%)
    ppermute x112, waiting for transfers between devices, swap(): return lax.ppermute(value, AXES, [(d, d ^ mask) for d in self.devices])  294 us
    ppermute x112, starting transfers between devices, swap(): return lax.ppermute(value, AXES, [(d, d ^ mask) for d in self.devices])  113 us
    dot_general x21, matrix products, matmul(): lax.dot_general(left, right, (dims, ((), ())), preferred_element_type=f32)  78.2 us
    unnamed x297, local copies, waits for them, and re-layouts  40.6 us
    all_to_all x6, waiting for transfers between devices, octet(): return lax.all_to_all(value, AXES, 0, 0, axis_index_groups=self.groups)  34.4 us
    all_to_all x6, starting transfers between devices, octet(): return lax.all_to_all(value, AXES, 0, 0, axis_index_groups=self.groups)  27.2 us
    convert_element_type x31, other arithmetic, added(): return sum((v.astype(f32) for v in values)).astype(bf16)  23.7 us
    pallas_call x1, Pallas kernels, attend_back(): call(functools.partial(attend_back_kernel, plan), 2, 6, (shape((blocks, B...  23.6 us
  transfers between devices with their start and end apart: 118, of which 53 were waited for; matrix products, arithmetic and copies ran while one was open for 21% of the time, Pallas kernels for 8%

profile of v2, /device:TPU:0, one launch (start us, length us, event | category | flops | bytes accessed | tf_op | source)
XLA Modules:
  0.0 727.5 jit_solution(14658730233844396064)
XLA Ops:
  5.6 6.3 all-to-all-start
  17.5 15.5 %all-to-all-done = bf16[8,64,768]{2,1,0:T(8,128)(2,1)} async-done(((bf16[8,64,768]{2,1,0:T(8,128)(2,1)}), bf16[8,64,768]{2,1,0:T(8,128)(2,1)}, u32[]{:S(2)}, u32[]{:S(2)}) %all-to-all-start) | async-done | bytes 786464 | tf_op jit(solution)/shard_map/all_to_all | solution.py:481
  38.1 4.4 collective-permute-done.2.a_lo
  42.5 15.8 %collective-permute-done.3.b_hi = bf16[80,2048]{1,0:T(8,128)(2,1)S(1)} collective-permute-done((bf16[80,2048]{1,0:T(8,128)(2,1)S(1)}, bf16[80,2048]{1,0:T(8,128)(2,1)S(1)}, u32[]{:S(2)}, u32[]{:S(2)}) %collective-permute-start.3) | collective-permute-done | bytes 327712 | tf_op jit(solution)/shard_map/ppermute | solution.py:69
  63.4 4.2 all-to-all-start.1
  75.0 13.3 %collective-permute-done.5.a_far = bf16[96,2048]{1,0:T(8,128)(2,1)S(1)} collective-permute-done((bf16[96,2048]{1,0:T(8,128)(2,1)S(1)}, bf16[96,2048]{1,0:T(8,128)(2,1)S(1)}, u32[]{:S(2)}, u32[]{:S(2)}) %collective-permute-start.5) | collective-permute-done | bytes 393248 | tf_op jit(solution)/shard_map/ppermute | solution.py:69
  88.3 7.7 %collective-permute-done.6.b_far = bf16[160,2048]{1,0:T(8,128)(2,1)S(1)} collective-permute-done((bf16[160,2048]{1,0:T(8,128)(2,1)S(1)}, bf16[160,2048]{1,0:T(8,128)(2,1)S(1)}, u32[]{:S(2)}, u32[]{:S(2)}) %collective-permute-start.6) | collective-permute-done | bytes 655392 | tf_op jit(solution)/shard_map/ppermute | solution.py:69
  107.8 4.7 all-to-all-start.2
  116.3 3.4 fusion.103
  122.1 3.7 fusion.102
  130.3 6.9 all-to-all-done.2
  143.6 18.0 %collective-permute-done.16 = bf16[128,1024]{1,0:T(8,128)(2,1)S(1)} collective-permute-done((bf16[128,1024]{1,0:T(8,128)(2,1)}, bf16[128,1024]{1,0:T(8,128)(2,1)S(1)}, u32[]{:S(2)}, u32[]{:S(2)}) %collective-permute-start.16) | collective-permute-done | bytes 262176 | tf_op jit(solution)/shard_map/ppermute | solution.py:69
  161.7 4.3 collective-permute-done.17
  177.6 9.4 %collective-permute-done.27 = bf16[2,64,2048]{2,1,0:T(8,128)(2,1)S(1)} collective-permute-done((bf16[2,64,2048]{2,1,0:T(8,128)(2,1)S(1)}, bf16[2,64,2048]{2,1,0:T(8,128)(2,1)S(1)}, u32[]{:S(2)}, u32[]{:S(2)}) %collective-permute-start.27) | collective-permute-done | bytes 524320 | tf_op jit(solution)/shard_map/ppermute | solution.py:69
  190.1 3.3 collective-permute-done.23
  196.3 22.3 %shard_map.200 = (bf16[16,128,128]{2,1,0:T(8,128)(2,1)S(1)}, f32[8,128,256]{2,1,0:T(8,128)S(1)}, f32[8,1,256]{2,1,0:T(1,128)S(1)}, bf16[4096,128]{1,0:T(8,128)(2,1)S(1)}, bf16[4096,128]{1,0:T(8,128)(2,1)S(1)}) custom-call(s32[56]{0:T(128)S(1)} %concatenate.173.info, s32[8]{0:T(128)S(1)} %copy-done.8, bf16[16,128,384]{2,1,0:T(8,128)(2,1)} %bitcast.212, ...), custom_call_target="tpu_custom_call" | custom-call | flops 4294967296 | bytes 8388608 | tf_op jit(solution)/shard_map/pallas_call | solution.py:359
  230.6 14.9 %collective-permute-done.29 = bf16[512,128]{1,0:T(8,128)(2,1)S(1)} collective-permute-done((bf16[512,128]{1,0:T(8,128)(2,1)S(1)}, bf16[512,128]{1,0:T(8,128)(2,1)S(1)}, u32[]{:S(2)}, u32[]{:S(2)}) %collective-permute-start.29) | collective-permute-done | bytes 131104 | tf_op jit(solution)/shard_map/ppermute | solution.py:69
  268.3 4.3 collective-permute-done.40
  281.2 11.9 %collective-permute-done.42 = bf16[80,2048]{1,0:T(8,128)(2,1)S(1)} collective-permute-done((bf16[80,2048]{1,0:T(8,128)(2,1)S(1)}, bf16[80,2048]{1,0:T(8,128)(2,1)S(1)}, u32[]{:S(2)}, u32[]{:S(2)}) %collective-permute-start.42) | collective-permute-done | bytes 327712 | tf_op jit(solution)/shard_map/ppermute | solution.py:69
  301.0 7.0 collective-permute-done.47
  314.5 5.6 collective-permute-done.52
  320.1 5.6 collective-permute-done.53
  325.7 4.0 collective-permute-done.54
  332.5 6.9 multiply_convert_fusion.1
  339.4 4.4 convolution_convert_fusion.3
  343.8 6.5 multiply_convert_fusion
  352.9 4.4 convolution_convert_fusion.2
  357.3 3.4 fusion.6
  360.8 5.0 fusion.104
  365.8 3.4 fusion.13
  369.2 5.4 add_convert_fusion.5
  375.7 4.3 add_convert_fusion.1
  386.0 4.7 collective-permute-done.60
  390.6 4.9 collective-permute-done.59
  400.3 7.7 %collective-permute-done.62 = bf16[64,2048]{1,0:T(8,128)(2,1)S(1)} collective-permute-done((bf16[64,2048]{1,0:T(8,128)(2,1)S(1)}, bf16[64,2048]{1,0:T(8,128)(2,1)S(1)}, u32[]{:S(2)}, u32[]{:S(2)}) %collective-permute-start.62) | collective-permute-done | bytes 262176 | tf_op jit(solution)/shard_map/ppermute | solution.py:69
  421.9 3.7 collective-permute-done.68
  425.5 6.0 collective-permute-done.66.b_hi
  434.9 4.6 convolution_convert_fusion.1
  441.9 4.4 collective-permute-done.72
  446.3 4.7 collective-permute-done.73
  466.7 4.3 add_convert_fusion
  474.6 5.8 collective-permute-done.78
  484.0 23.6 %shard_map.205 = (bf16[16,128,128]{2,1,0:T(8,128)(2,1)S(1)}, bf16[16,128,256]{2,1,0:T(8,128)(2,1)S(1)}, bf16[1,16,128,256]{3,2,1,0:T(8,128)(2,1)}) custom-call(s32[56]{0:T(128)S(1)} %concatenate.173.info, s32[8]{0:T(128)S(1)} %copy-done.8, bf16[16,128,384]{2,1,0:T(8,128)(2,1)} %bitcast.213, bf16[4096,128]{1,0:T(8,128)(2,1)} %copy-done.10, ...), custom_call_target="tpu_custom_call" | custom-call | flops 10737418240 | bytes 8388608 | tf_op jit(solution)/shard_map/pallas_call | solution.py:380
  513.2 3.5 collective-permute-done.79
  516.7 5.6 collective-permute-done.80
  522.3 5.6 collective-permute-done.81
  527.9 5.2 collective-permute-done.82
  547.5 11.6 %collective-permute-done.93 = bf16[128,1024]{1,0:T(8,128)(2,1)S(1)} collective-permute-done((bf16[128,1024]{1,0:T(8,128)(2,1)S(1)}, bf16[128,1024]{1,0:T(8,128)(2,1)S(1)}, u32[]{:S(2)}, u32[]{:S(2)}) %collective-permute-start.93) | collective-permute-done | bytes 262176 | tf_op jit(solution)/shard_map/ppermute | solution.py:69
  559.0 5.5 collective-permute-done.92
  566.4 6.9 collective-permute-done.90.refs_2_
  582.0 3.6 convolution_convert_fusion.5
  585.6 5.7 fusion.27
  592.5 10.8 %collective-permute-done.99 = bf16[2,64,2048]{2,1,0:T(8,128)(2,1)S(1)} collective-permute-done((bf16[2,64,2048]{2,1,0:T(8,128)(2,1)S(1)}, bf16[2,64,2048]{2,1,0:T(8,128)(2,1)S(1)}, u32[]{:S(2)}, u32[]{:S(2)}) %collective-permute-start.99) | collective-permute-done | bytes 524320 | tf_op jit(solution)/shard_map/ppermute | solution.py:69
  605.7 3.8 all-to-all-start.3
  619.4 3.2 add_convert_fusion.3
  633.4 4.6 all-to-all-start.4
  646.4 16.4 %collective-permute-done.105 = bf16[2,48,2048]{2,1,0:T(8,128)(2,1)S(1)} collective-permute-done((bf16[2,48,2048]{2,1,0:T(8,128)(2,1)S(1)}, bf16[2,48,2048]{2,1,0:T(8,128)(2,1)S(1)}, u32[]{:S(2)}, u32[]{:S(2)}) %collective-permute-start.105) | collective-permute-done | bytes 393248 | tf_op jit(solution)/shard_map/ppermute | solution.py:69
  662.8 3.7 collective-permute-done.106
  678.3 9.1 %collective-permute-done.110 = bf16[80,2048]{1,0:T(8,128)(2,1)S(1)} collective-permute-done((bf16[80,2048]{1,0:T(8,128)(2,1)S(1)}, bf16[80,2048]{1,0:T(8,128)(2,1)S(1)}, u32[]{:S(2)}, u32[]{:S(2)}) %collective-permute-start.110) | collective-permute-done | bytes 327712 | tf_op jit(solution)/shard_map/ppermute | solution.py:69
  687.6 4.7 collective-permute-done.108
  692.3 6.1 collective-permute-done.107
  699.9 3.5 all-to-all-start.5
  707.8 4.3 collective-permute-done.111
  713.0 11.3 %all-to-all-done.5.got = bf16[8,64,768]{2,1,0:T(8,128)(2,1)S(1)} async-done(((bf16[8,64,768]{2,1,0:T(8,128)(2,1)}), bf16[8,64,768]{2,1,0:T(8,128)(2,1)S(1)}, u32[]{:S(2)}, u32[]{:S(2)}) %all-to-all-start.5) | async-done | bytes 786464 | tf_op jit(solution)/shard_map/all_to_all | solution.py:481
  (677 shorter events, 274.3 us)
Async XLA Ops:
  5.6 27.4 %all-to-all-start = ((bf16[8,64,768]{2,1,0:T(8,128)(2,1)}), bf16[8,64,768]{2,1,0:T(8,128)(2,1)}, u32[]{:S(2)}, u32[]{:S(2)}) async-start(bf16[8,64,768]{2,1,0:T(8,128)(2,1)} %reshape.464), calls=%async_computation | async-start | bytes 1572864 | tf_op jit(solution)/shard_map/all_to_all | solution.py:481
  33.0 25.4 %collective-permute-start.1 = (bf16[512,768]{1,0:T(8,128)(2,1)}, bf16[512,768]{1,0:T(8,128)(2,1)}, u32[]{:S(2)}, u32[]{:S(2)}) collective-permute-start(bf16[512,768]{1,0:T(8,128)(2,1)} %bitcast.1), channel_id=1, source_target_pairs={{0,4},{1,5},{2,6},{3,7},{4,0},{5,1},{6,2},{7,3},{8,12},{9,13},{10,... | collective-permute-start | bytes 2359304 | tf_op jit(solution)/shard_map/ppermute | solution.py:69
  34.5 26.1 %collective-permute-start = (bf16[512,768]{1,0:T(8,128)(2,1)}, bf16[512,768]{1,0:T(8,128)(2,1)}, u32[]{:S(2)}, u32[]{:S(2)}) collective-permute-start(bf16[512,768]{1,0:T(8,128)(2,1)} %bitcast.1), channel_id=1, source_target_pairs={{0,8},{1,9},{2,10},{3,11},{4,12},{5,13},{6,14},{7,15},{8,0},{9,1},... | collective-permute-start | bytes 2359304 | tf_op jit(solution)/shard_map/ppermute | solution.py:69
  34.5 23.8 %collective-permute-start.3 = (bf16[80,2048]{1,0:T(8,128)(2,1)S(1)}, bf16[80,2048]{1,0:T(8,128)(2,1)S(1)}, u32[]{:S(2)}, u32[]{:S(2)}) collective-permute-start(bf16[80,2048]{1,0:T(8,128)(2,1)S(1)} %slice.531.b), channel_id=1, source_target_pairs={{0,16},{1,17},{2,18},{3,19},{4,20},{5,21},{6,22},{7,23},{8,24},{9,... | collective-permute-start | bytes 983048 | tf_op jit(solution)/shard_map/ppermute | solution.py:69
  63.4 33.5 %all-to-all-start.1 = ((bf16[8,64,1024]{2,1,0:T(8,128)(2,1)}), bf16[8,64,1024]{2,1,0:T(8,128)(2,1)}, u32[]{:S(2)}, u32[]{:S(2)}) async-start(bf16[8,64,1024]{2,1,0:T(8,128)(2,1)} %copy.36), calls=%async_computation.1 | async-start | bytes 2097152 | tf_op jit(solution)/shard_map/all_to_all | solution.py:481
  67.7 29.2 %collective-permute-start.4 = (bf16[512,768]{1,0:T(8,128)(2,1)}, bf16[512,768]{1,0:T(8,128)(2,1)}, u32[]{:S(2)}, u32[]{:S(2)}) collective-permute-start(bf16[512,768]{1,0:T(8,128)(2,1)} %collective-permute-done), channel_id=1, source_target_pairs={{0,4},{1,5},{2,6},{3,7},{4,0},{5,1},{6,2},{7,3},{8,12},{9,13},{10,... | collective-permute-start | bytes 2359304 | tf_op jit(solution)/shard_map/ppermute | solution.py:69
  68.3 27.7 %collective-permute-start.6 = (bf16[160,2048]{1,0:T(8,128)(2,1)S(1)}, bf16[160,2048]{1,0:T(8,128)(2,1)S(1)}, u32[]{:S(2)}, u32[]{:S(2)}) collective-permute-start(bf16[160,2048]{1,0:T(8,128)(2,1)S(1)} %pad_maximum_fusion.9), channel_id=1, source_target_pairs={{0,2},{1,3},{2,0},{3,1},{4,6},{5,7},{6,4},{7,5},{8,10},{9,11},{10,... | collective-permute-start | bytes 1966088 | tf_op jit(solution)/shard_map/ppermute | solution.py:69
  70.2 18.1 %collective-permute-start.5 = (bf16[96,2048]{1,0:T(8,128)(2,1)S(1)}, bf16[96,2048]{1,0:T(8,128)(2,1)S(1)}, u32[]{:S(2)}, u32[]{:S(2)}) collective-permute-start(bf16[96,2048]{1,0:T(8,128)(2,1)S(1)} %pad_maximum_fusion.26), channel_id=1, source_target_pairs={{0,16},{1,17},{2,18},{3,19},{4,20},{5,21},{6,22},{7,23},{8,24},{9,... | collective-permute-start | bytes 1179656 | tf_op jit(solution)/shard_map/ppermute | solution.py:69
  99.0 22.5 %collective-permute-start.7 = (bf16[2048,768]{1,0:T(8,128)(2,1)}, bf16[2048,768]{1,0:T(8,128)(2,1)}, u32[]{:S(2)}, u32[]{:S(2)}) collective-permute-start(bf16[2048,768]{1,0:T(8,128)(2,1)} %constant_dynamic-update-slice_fusion), channel_id=1, source_target_pairs={{0,1},{1,0},{2,3},{3,2},{4,5},{5,4},{6,7},{7,6},{8,9},{9,8},{10,11... | collective-permute-start | bytes 9437192 | tf_op jit(solution)/shard_map/ppermute | solution.py:69
  101.3 28.9 %collective-permute-start.11 = (bf16[128,1024]{1,0:T(8,128)(2,1)}, bf16[128,1024]{1,0:T(8,128)(2,1)}, u32[]{:S(2)}, u32[]{:S(2)}) collective-permute-start(bf16[128,1024]{1,0:T(8,128)(2,1)} %get-tuple-element.866), channel_id=1, source_target_pairs={{0,4},{1,5},{2,6},{3,7},{4,0},{5,1},{6,2},{7,3},{8,12},{9,13},{10,... | collective-permute-start | bytes 786440 | tf_op jit(solution)/shard_map/ppermute | solution.py:69
  101.9 28.4 %collective-permute-start.9 = (bf16[128,1024]{1,0:T(8,128)(2,1)}, bf16[128,1024]{1,0:T(8,128)(2,1)}, u32[]{:S(2)}, u32[]{:S(2)}) collective-permute-start(bf16[128,1024]{1,0:T(8,128)(2,1)} %get-tuple-element.866), channel_id=1, source_target_pairs={{0,16},{1,17},{2,18},{3,19},{4,20},{5,21},{6,22},{7,23},{8,24},{9,... | collective-permute-start | bytes 786440 | tf_op jit(solution)/shard_map/ppermute | solution.py:69
  103.0 27.3 %collective-permute-start.10 = (bf16[128,1024]{1,0:T(8,128)(2,1)}, bf16[128,1024]{1,0:T(8,128)(2,1)}, u32[]{:S(2)}, u32[]{:S(2)}) collective-permute-start(bf16[128,1024]{1,0:T(8,128)(2,1)} %get-tuple-element.867), channel_id=1, source_target_pairs={{0,4},{1,5},{2,6},{3,7},{4,0},{5,1},{6,2},{7,3},{8,12},{9,13},{10,... | collective-permute-start | bytes 786440 | tf_op jit(solution)/shard_map/ppermute | solution.py:69
  104.5 25.8 %collective-permute-start.8 = (bf16[128,1024]{1,0:T(8,128)(2,1)}, bf16[128,1024]{1,0:T(8,128)(2,1)}, u32[]{:S(2)}, u32[]{:S(2)}) collective-permute-start(bf16[128,1024]{1,0:T(8,128)(2,1)} %get-tuple-element.867), channel_id=1, source_target_pairs={{0,16},{1,17},{2,18},{3,19},{4,20},{5,21},{6,22},{7,23},{8,24},{9,... | collective-permute-start | bytes 786440 | tf_op jit(solution)/shard_map/ppermute | solution.py:69
  107.8 29.4 %all-to-all-start.2 = ((bf16[8,64,1024]{2,1,0:T(8,128)(2,1)}), bf16[8,64,1024]{2,1,0:T(8,128)(2,1)}, u32[]{:S(2)}, u32[]{:S(2)}) async-start(bf16[8,64,1024]{2,1,0:T(8,128)(2,1)} %copy.37), calls=%async_computation.2 | async-start | bytes 2097152 | tf_op jit(solution)/shard_map/all_to_all | solution.py:481
  137.2 28.7 %collective-permute-start.13 = (bf16[512,384]{1,0:T(8,128)(2,1)}, bf16[512,384]{1,0:T(8,128)(2,1)S(1)}, u32[]{:S(2)}, u32[]{:S(2)}) collective-permute-start(bf16[512,384]{1,0:T(8,128)(2,1)} %get-tuple-element.378), channel_id=1, source_target_pairs={{0,4},{1,5},{2,6},{3,7},{4,0},{5,1},{6,2},{7,3},{8,12},{9,13},{10,... | collective-permute-start | bytes 1179656 | tf_op jit(solution)/shard_map/ppermute | solution.py:69
  137.8 28.2 %collective-permute-start.14 = (bf16[512,384]{1,0:T(8,128)(2,1)}, bf16[512,384]{1,0:T(8,128)(2,1)S(1)}, u32[]{:S(2)}, u32[]{:S(2)}) collective-permute-start(bf16[512,384]{1,0:T(8,128)(2,1)} %get-tuple-element.379), channel_id=1, source_target_pairs={{0,8},{1,9},{2,10},{3,11},{4,12},{5,13},{6,14},{7,15},{8,0},{9,1},... | collective-permute-start | bytes 1179656 | tf_op jit(solution)/shard_map/ppermute | solution.py:69
  137.8 31.2 %collective-permute-start.15 = (bf16[512,384]{1,0:T(8,128)(2,1)}, bf16[512,384]{1,0:T(8,128)(2,1)S(1)}, u32[]{:S(2)}, u32[]{:S(2)}) collective-permute-start(bf16[512,384]{1,0:T(8,128)(2,1)} %get-tuple-element.380), channel_id=1, source_target_pairs={{0,12},{1,13},{2,14},{3,15},{4,8},{5,9},{6,10},{7,11},{8,4},{9,5},... | collective-permute-start | bytes 1179656 | tf_op jit(solution)/shard_map/ppermute | solution.py:69
  140.7 21.0 %collective-permute-start.16 = (bf16[128,1024]{1,0:T(8,128)(2,1)}, bf16[128,1024]{1,0:T(8,128)(2,1)S(1)}, u32[]{:S(2)}, u32[]{:S(2)}) collective-permute-start(bf16[128,1024]{1,0:T(8,128)(2,1)} %get-tuple-element.396), channel_id=1, source_target_pairs={{0,16},{1,17},{2,18},{3,19},{4,20},{5,21},{6,22},{7,23},{8,24},{9,... | collective-permute-start | bytes 786440 | tf_op jit(solution)/shard_map/ppermute | solution.py:69
  141.1 24.9 %collective-permute-start.17 = (bf16[128,1024]{1,0:T(8,128)(2,1)}, bf16[128,1024]{1,0:T(8,128)(2,1)S(1)}, u32[]{:S(2)}, u32[]{:S(2)}) collective-permute-start(bf16[128,1024]{1,0:T(8,128)(2,1)} %get-tuple-element.397), channel_id=1, source_target_pairs={{0,16},{1,17},{2,18},{3,19},{4,20},{5,21},{6,22},{7,23},{8,24},{9,... | collective-permute-start | bytes 786440 | tf_op jit(solution)/shard_map/ppermute | solution.py:69
  172.4 23.5 %collective-permute-start.18 = (bf16[16,128,256]{2,1,0:T(8,128)(2,1)}, bf16[16,128,256]{2,1,0:T(8,128)(2,1)}, u32[]{:S(2)}, u32[]{:S(2)}) collective-permute-start(bf16[16,128,256]{2,1,0:T(8,128)(2,1)} %slice.699), channel_id=1, source_target_pairs={{0,1},{1,0},{2,3},{3,2},{4,5},{5,4},{6,7},{7,6},{8,9},{9,8},{10,11... | collective-permute-start | bytes 3145736 | tf_op jit(solution)/shard_map/ppermute | solution.py:69
  174.9 18.5 %collective-permute-start.23 = (bf16[128,1024]{1,0:T(8,128)(2,1)}, bf16[128,1024]{1,0:T(8,128)(2,1)S(1)}, u32[]{:S(2)}, u32[]{:S(2)}) collective-permute-start(bf16[128,1024]{1,0:T(8,128)(2,1)} %collective-permute-done.8), channel_id=1, source_target_pairs={{0,4},{1,5},{2,6},{3,7},{4,0},{5,1},{6,2},{7,3},{8,12},{9,13},{10,... | collective-permute-start | bytes 786440 | tf_op jit(solution)/shard_map/ppermute | solution.py:69
  187.1 31.6 %collective-permute-start.24 = (bf16[128,1024]{1,0:T(8,128)(2,1)}, bf16[128,1024]{1,0:T(8,128)(2,1)S(1)}, u32[]{:S(2)}, u32[]{:S(2)}) collective-permute-start(bf16[128,1024]{1,0:T(8,128)(2,1)} %collective-permute-done.9), channel_id=1, source_target_pairs={{0,4},{1,5},{2,6},{3,7},{4,0},{5,1},{6,2},{7,3},{8,12},{9,13},{10,... | collective-permute-start | bytes 786440 | tf_op jit(solution)/shard_map/ppermute | solution.py:69
  187.6 31.1 %collective-permute-start.26 = (bf16[64,2048]{1,0:T(8,128)(2,1)S(1)}, bf16[64,2048]{1,0:T(8,128)(2,1)S(1)}, u32[]{:S(2)}, u32[]{:S(2)}) collective-permute-start(bf16[64,2048]{1,0:T(8,128)(2,1)S(1)} %get-tuple-element.409.b), channel_id=1, source_target_pairs={{0,8},{1,9},{2,10},{3,11},{4,12},{5,13},{6,14},{7,15},{8,0},{9,1},... | collective-permute-start | bytes 786440 | tf_op jit(solution)/shard_map/ppermute | solution.py:69
  188.6 30.1 %collective-permute-start.25 = (bf16[64,2048]{1,0:T(8,128)(2,1)S(1)}, bf16[64,2048]{1,0:T(8,128)(2,1)S(1)}, u32[]{:S(2)}, u32[]{:S(2)}) collective-permute-start(bf16[64,2048]{1,0:T(8,128)(2,1)S(1)} %get-tuple-element.407.a), channel_id=1, source_target_pairs={{0,2},{1,3},{2,0},{3,1},{4,6},{5,7},{6,4},{7,5},{8,10},{9,11},{10,... | collective-permute-start | bytes 786440 | tf_op jit(solution)/shard_map/ppermute | solution.py:69
  193.4 25.3 %collective-permute-start.20 = (bf16[128,1024]{1,0:T(8,128)(2,1)S(1)}, bf16[128,1024]{1,0:T(8,128)(2,1)S(1)}, u32[]{:S(2)}, u32[]{:S(2)}) collective-permute-start(bf16[128,1024]{1,0:T(8,128)(2,1)S(1)} %get-tuple-element.425), channel_id=1, source_target_pairs={{0,16},{1,17},{2,18},{3,19},{4,20},{5,21},{6,22},{7,23},{8,24},{9,... | collective-permute-start | bytes 786440 | tf_op jit(solution)/shard_map/ppermute | solution.py:69
  195.9 22.8 %collective-permute-start.19 = (bf16[128,1024]{1,0:T(8,128)(2,1)S(1)}, bf16[128,1024]{1,0:T(8,128)(2,1)S(1)}, u32[]{:S(2)}, u32[]{:S(2)}) collective-permute-start(bf16[128,1024]{1,0:T(8,128)(2,1)S(1)} %get-tuple-element.424), channel_id=1, source_target_pairs={{0,16},{1,17},{2,18},{3,19},{4,20},{5,21},{6,22},{7,23},{8,24},{9,... | collective-permute-start | bytes 786440 | tf_op jit(solution)/shard_map/ppermute | solution.py:69
  221.1 24.5 %collective-permute-start.34 = (bf16[128,2048]{1,0:T(8,128)(2,1)S(1)}, bf16[128,2048]{1,0:T(8,128)(2,1)S(1)}, u32[]{:S(2)}, u32[]{:S(2)}) collective-permute-start(bf16[128,2048]{1,0:T(8,128)(2,1)S(1)} %pad_maximum_fusion.17), channel_id=1, source_target_pairs={{0,2},{1,3},{2,0},{3,1},{4,6},{5,7},{6,4},{7,5},{8,10},{9,11},{10,... | collective-permute-start | bytes 1572872 | tf_op jit(solution)/shard_map/ppermute | solution.py:69
  222.4 23.1 %collective-permute-start.33 = (bf16[128,2048]{1,0:T(8,128)(2,1)S(1)}, bf16[128,2048]{1,0:T(8,128)(2,1)S(1)}, u32[]{:S(2)}, u32[]{:S(2)}) collective-permute-start(bf16[128,2048]{1,0:T(8,128)(2,1)S(1)} %pad_maximum_fusion.16), channel_id=1, source_target_pairs={{0,8},{1,9},{2,10},{3,11},{4,12},{5,13},{6,14},{7,15},{8,0},{9,1},... | collective-permute-start | bytes 1572872 | tf_op jit(solution)/shard_map/ppermute | solution.py:69
  226.1 19.5 %collective-permute-start.29 = (bf16[512,128]{1,0:T(8,128)(2,1)S(1)}, bf16[512,128]{1,0:T(8,128)(2,1)S(1)}, u32[]{:S(2)}, u32[]{:S(2)}) collective-permute-start(bf16[512,128]{1,0:T(8,128)(2,1)S(1)} %bitcast.248), channel_id=1, source_target_pairs={{0,8},{1,9},{2,10},{3,11},{4,12},{5,13},{6,14},{7,15},{8,0},{9,1},... | collective-permute-start | bytes 393224 | tf_op jit(solution)/shard_map/ppermute | solution.py:69
  226.9 18.6 %collective-permute-start.28 = (bf16[512,128]{1,0:T(8,128)(2,1)S(1)}, bf16[512,128]{1,0:T(8,128)(2,1)S(1)}, u32[]{:S(2)}, u32[]{:S(2)}) collective-permute-start(bf16[512,128]{1,0:T(8,128)(2,1)S(1)} %bitcast.247), channel_id=1, source_target_pairs={{0,4},{1,5},{2,6},{3,7},{4,0},{5,1},{6,2},{7,3},{8,12},{9,13},{10,... | collective-permute-start | bytes 393224 | tf_op jit(solution)/shard_map/ppermute | solution.py:69
  255.3 19.3 %collective-permute-start.35 = (bf16[2,48,2048]{2,1,0:T(8,128)(2,1)S(1)}, bf16[2,48,2048]{2,1,0:T(8,128)(2,1)S(1)}, u32[]{:S(2)}, u32[]{:S(2)}) collective-permute-start(bf16[2,48,2048]{2,1,0:T(8,128)(2,1)S(1)} %get-tuple-element.804), channel_id=1, source_target_pairs={{0,16},{1,17},{2,18},{3,19},{4,20},{5,21},{6,22},{7,23},{8,24},{9,... | collective-permute-start | bytes 1179656 | tf_op jit(solution)/shard_map/ppermute | solution.py:69
  293.3 17.6 %collective-permute-start.49 = (bf16[2048,1024]{1,0:T(8,128)(2,1)}, bf16[2048,1024]{1,0:T(8,128)(2,1)}, u32[]{:S(2)}, u32[]{:S(2)}) collective-permute-start(bf16[2048,1024]{1,0:T(8,128)(2,1)} %constant_dynamic-update-slice_fusion.4), channel_id=1, source_target_pairs={{0,1},{1,0},{2,3},{3,2},{4,5},{5,4},{6,7},{7,6},{8,9},{9,8},{10,11... | collective-permute-start | bytes 12582920 | tf_op jit(solution)/shard_map/ppermute | solution.py:69
  329.8 20.5 %collective-permute-start.55 = (bf16[2048,1024]{1,0:T(8,128)(2,1)S(1)}, bf16[2048,1024]{1,0:T(8,128)(2,1)S(1)}, u32[]{:S(2)}, u32[]{:S(2)}) collective-permute-start(bf16[2048,1024]{1,0:T(8,128)(2,1)S(1)} %constant_dynamic-update-slice_fusion.17), channel_id=1, source_target_pairs={{0,1},{1,0},{2,3},{3,2},{4,5},{5,4},{6,7},{7,6},{8,9},{9,8},{10,11... | collective-permute-start | bytes 12582920 | tf_op jit(solution)/shard_map/ppermute | solution.py:69
  352.5 22.1 %collective-permute-start.56 = (bf16[2048,1024]{1,0:T(8,128)(2,1)}, bf16[2048,1024]{1,0:T(8,128)(2,1)}, u32[]{:S(2)}, u32[]{:S(2)}) collective-permute-start(bf16[2048,1024]{1,0:T(8,128)(2,1)} %convolution_convert_fusion.3), channel_id=1, source_target_pairs={{0,1},{1,0},{2,3},{3,2},{4,5},{5,4},{6,7},{7,6},{8,9},{9,8},{10,11... | collective-permute-start | bytes 12582920 | tf_op jit(solution)/shard_map/ppermute | solution.py:69
  374.9 20.6 %collective-permute-start.58 = (bf16[2,64,2048]{2,1,0:T(8,128)(2,1)S(1)}, bf16[2,64,2048]{2,1,0:T(8,128)(2,1)S(1)}, u32[]{:S(2)}, u32[]{:S(2)}) collective-permute-start(bf16[2,64,2048]{2,1,0:T(8,128)(2,1)S(1)} %pad_maximum_fusion.22), channel_id=1, source_target_pairs={{0,2},{1,3},{2,0},{3,1},{4,6},{5,7},{6,4},{7,5},{8,10},{9,11},{10,... | collective-permute-start | bytes 1572872 | tf_op jit(solution)/shard_map/ppermute | solution.py:69
  375.7 19.8 %collective-permute-start.57 = (bf16[2,64,2048]{2,1,0:T(8,128)(2,1)S(1)}, bf16[2,64,2048]{2,1,0:T(8,128)(2,1)S(1)}, u32[]{:S(2)}, u32[]{:S(2)}) collective-permute-start(bf16[2,64,2048]{2,1,0:T(8,128)(2,1)S(1)} %get-tuple-element.798), channel_id=1, source_target_pairs={{0,8},{1,9},{2,10},{3,11},{4,12},{5,13},{6,14},{7,15},{8,0},{9,1},... | collective-permute-start | bytes 1572872 | tf_op jit(solution)/shard_map/ppermute | solution.py:69
  433.5 17.4 %collective-permute-start.73 = (bf16[128,1024]{1,0:T(8,128)(2,1)S(1)}, bf16[128,1024]{1,0:T(8,128)(2,1)S(1)}, u32[]{:S(2)}, u32[]{:S(2)}) collective-permute-start(bf16[128,1024]{1,0:T(8,128)(2,1)S(1)} %get-tuple-element.533), channel_id=1, source_target_pairs={{0,4},{1,5},{2,6},{3,7},{4,0},{5,1},{6,2},{7,3},{8,12},{9,13},{10,... | collective-permute-start | bytes 786440 | tf_op jit(solution)/shard_map/ppermute | solution.py:69
  434.1 18.7 %collective-permute-start.69 = (bf16[96,2048]{1,0:T(8,128)(2,1)S(1)}, bf16[96,2048]{1,0:T(8,128)(2,1)S(1)}, u32[]{:S(2)}, u32[]{:S(2)}) collective-permute-start(bf16[96,2048]{1,0:T(8,128)(2,1)S(1)} %pad_maximum_fusion.27), channel_id=1, source_target_pairs={{0,16},{1,17},{2,18},{3,19},{4,20},{5,21},{6,22},{7,23},{8,24},{9,... | collective-permute-start | bytes 1179656 | tf_op jit(solution)/shard_map/ppermute | solution.py:69
  434.3 18.6 %collective-permute-start.70 = (bf16[160,2048]{1,0:T(8,128)(2,1)S(1)}, bf16[160,2048]{1,0:T(8,128)(2,1)S(1)}, u32[]{:S(2)}, u32[]{:S(2)}) collective-permute-start(bf16[160,2048]{1,0:T(8,128)(2,1)S(1)} %pad_maximum_fusion.12), channel_id=1, source_target_pairs={{0,2},{1,3},{2,0},{3,1},{4,6},{5,7},{6,4},{7,5},{8,10},{9,11},{10,... | collective-permute-start | bytes 1966088 | tf_op jit(solution)/shard_map/ppermute | solution.py:69
  453.0 54.5 %collective-permute-start.86 = (bf16[2,64,2048]{2,1,0:T(8,128)(2,1)S(1)}, bf16[2,64,2048]{2,1,0:T(8,128)(2,1)S(1)}, u32[]{:S(2)}, u32[]{:S(2)}) collective-permute-start(bf16[2,64,2048]{2,1,0:T(8,128)(2,1)S(1)} %pad_maximum_fusion.25), channel_id=1, source_target_pairs={{0,2},{1,3},{2,0},{3,1},{4,6},{5,7},{6,4},{7,5},{8,10},{9,11},{10,... | collective-permute-start | bytes 1572872 | tf_op jit(solution)/shard_map/ppermute | solution.py:69
  472.6 36.4 %collective-permute-start.85 = (bf16[2,64,2048]{2,1,0:T(8,128)(2,1)}, bf16[2,64,2048]{2,1,0:T(8,128)(2,1)S(1)}, u32[]{:S(2)}, u32[]{:S(2)}) collective-permute-start(bf16[2,64,2048]{2,1,0:T(8,128)(2,1)} %get-tuple-element.792), channel_id=1, source_target_pairs={{0,8},{1,9},{2,10},{3,11},{4,12},{5,13},{6,14},{7,15},{8,0},{9,1},... | collective-permute-start | bytes 1572872 | tf_op jit(solution)/shard_map/ppermute | solution.py:69
  480.5 29.1 %collective-permute-start.84 = (bf16[128,1024]{1,0:T(8,128)(2,1)S(1)}, bf16[128,1024]{1,0:T(8,128)(2,1)S(1)}, u32[]{:S(2)}, u32[]{:S(2)}) collective-permute-start(bf16[128,1024]{1,0:T(8,128)(2,1)S(1)} %add_convert_fusion.26), channel_id=1, source_target_pairs={{0,16},{1,17},{2,18},{3,19},{4,20},{5,21},{6,22},{7,23},{8,24},{9,... | collective-permute-start | bytes 786440 | tf_op jit(solution)/shard_map/ppermute | solution.py:69
  480.7 32.5 %collective-permute-start.83 = (bf16[128,1024]{1,0:T(8,128)(2,1)S(1)}, bf16[128,1024]{1,0:T(8,128)(2,1)S(1)}, u32[]{:S(2)}, u32[]{:S(2)}) collective-permute-start(bf16[128,1024]{1,0:T(8,128)(2,1)S(1)} %add_convert_fusion.27), channel_id=1, source_target_pairs={{0,16},{1,17},{2,18},{3,19},{4,20},{5,21},{6,22},{7,23},{8,24},{9,... | collective-permute-start | bytes 786440 | tf_op jit(solution)/shard_map/ppermute | solution.py:69
  483.8 27.3 %collective-permute-start.87 = (bf16[4,64,2048]{2,1,0:T(8,128)(2,1)S(1)}, bf16[4,64,2048]{2,1,0:T(8,128)(2,1)S(1)}, u32[]{:S(2)}, u32[]{:S(2)}) collective-permute-start(bf16[4,64,2048]{2,1,0:T(8,128)(2,1)S(1)} %broadcast_select_fusion), channel_id=1, source_target_pairs={{0,1},{1,0},{2,3},{3,2},{4,5},{5,4},{6,7},{7,6},{8,9},{9,8},{10,11... | collective-permute-start | bytes 3145736 | tf_op jit(solution)/shard_map/ppermute | solution.py:69
  509.6 18.3 %collective-permute-start.81 = (bf16[128,1024]{1,0:T(8,128)(2,1)S(1)}, bf16[128,1024]{1,0:T(8,128)(2,1)S(1)}, u32[]{:S(2)}, u32[]{:S(2)}) collective-permute-start(bf16[128,1024]{1,0:T(8,128)(2,1)S(1)} %get-tuple-element.571), channel_id=1, source_target_pairs={{0,4},{1,5},{2,6},{3,7},{4,0},{5,1},{6,2},{7,3},{8,12},{9,13},{10,... | collective-permute-start | bytes 786440 | tf_op jit(solution)/shard_map/ppermute | solution.py:69
  511.1 22.1 %collective-permute-start.82 = (bf16[128,1024]{1,0:T(8,128)(2,1)S(1)}, bf16[128,1024]{1,0:T(8,128)(2,1)S(1)}, u32[]{:S(2)}, u32[]{:S(2)}) collective-permute-start(bf16[128,1024]{1,0:T(8,128)(2,1)S(1)} %get-tuple-element.572), channel_id=1, source_target_pairs={{0,4},{1,5},{2,6},{3,7},{4,0},{5,1},{6,2},{7,3},{8,12},{9,13},{10,... | collective-permute-start | bytes 786440 | tf_op jit(solution)/shard_map/ppermute | solution.py:69
  539.1 20.0 %collective-permute-start.93 = (bf16[128,1024]{1,0:T(8,128)(2,1)S(1)}, bf16[128,1024]{1,0:T(8,128)(2,1)S(1)}, u32[]{:S(2)}, u32[]{:S(2)}) collective-permute-start(bf16[128,1024]{1,0:T(8,128)(2,1)S(1)} %add_convert_fusion.24), channel_id=1, source_target_pairs={{0,16},{1,17},{2,18},{3,19},{4,20},{5,21},{6,22},{7,23},{8,24},{9,... | collective-permute-start | bytes 786440 | tf_op jit(solution)/shard_map/ppermute | solution.py:69
  539.3 25.3 %collective-permute-start.92 = (bf16[128,1024]{1,0:T(8,128)(2,1)S(1)}, bf16[128,1024]{1,0:T(8,128)(2,1)S(1)}, u32[]{:S(2)}, u32[]{:S(2)}) collective-permute-start(bf16[128,1024]{1,0:T(8,128)(2,1)S(1)} %add_convert_fusion.25), channel_id=1, source_target_pairs={{0,16},{1,17},{2,18},{3,19},{4,20},{5,21},{6,22},{7,23},{8,24},{9,... | collective-permute-start | bytes 786440 | tf_op jit(solution)/shard_map/ppermute | solution.py:69
  542.2 24.1 %collective-permute-start.91 = (bf16[512,384]{1,0:T(8,128)(2,1)S(1)}, bf16[512,384]{1,0:T(8,128)(2,1)S(1)}, u32[]{:S(2)}, u32[]{:S(2)}) collective-permute-start(bf16[512,384]{1,0:T(8,128)(2,1)S(1)} %get-tuple-element.812), channel_id=1, source_target_pairs={{0,12},{1,13},{2,14},{3,15},{4,8},{5,9},{6,10},{7,11},{8,4},{9,5},... | collective-permute-start | bytes 1179656 | tf_op jit(solution)/shard_map/ppermute | solution.py:69
  542.7 30.6 %collective-permute-start.90 = (bf16[512,384]{1,0:T(8,128)(2,1)S(1)}, bf16[512,384]{1,0:T(8,128)(2,1)S(1)}, u32[]{:S(2)}, u32[]{:S(2)}) collective-permute-start(bf16[512,384]{1,0:T(8,128)(2,1)S(1)} %get-tuple-element.813), channel_id=1, source_target_pairs={{0,8},{1,9},{2,10},{3,11},{4,12},{5,13},{6,14},{7,15},{8,0},{9,1},... | collective-permute-start | bytes 1179656 | tf_op jit(solution)/shard_map/ppermute | solution.py:69
  545.1 28.2 %collective-permute-start.89 = (bf16[512,384]{1,0:T(8,128)(2,1)S(1)}, bf16[512,384]{1,0:T(8,128)(2,1)S(1)}, u32[]{:S(2)}, u32[]{:S(2)}) collective-permute-start(bf16[512,384]{1,0:T(8,128)(2,1)S(1)} %get-tuple-element.814), channel_id=1, source_target_pairs={{0,4},{1,5},{2,6},{3,7},{4,0},{5,1},{6,2},{7,3},{8,12},{9,13},{10,... | collective-permute-start | bytes 1179656 | tf_op jit(solution)/shard_map/ppermute | solution.py:69
  573.4 18.8 %collective-permute-start.98 = (bf16[64,2048]{1,0:T(8,128)(2,1)S(1)}, bf16[64,2048]{1,0:T(8,128)(2,1)S(1)}, u32[]{:S(2)}, u32[]{:S(2)}) collective-permute-start(bf16[64,2048]{1,0:T(8,128)(2,1)S(1)} %fusion.33), channel_id=1, source_target_pairs={{0,8},{1,9},{2,10},{3,11},{4,12},{5,13},{6,14},{7,15},{8,0},{9,1},... | collective-permute-start | bytes 786440 | tf_op jit(solution)/shard_map/ppermute | solution.py:69
  573.6 18.8 %collective-permute-start.97 = (bf16[64,2048]{1,0:T(8,128)(2,1)S(1)}, bf16[64,2048]{1,0:T(8,128)(2,1)S(1)}, u32[]{:S(2)}, u32[]{:S(2)}) collective-permute-start(bf16[64,2048]{1,0:T(8,128)(2,1)S(1)} %fusion.32), channel_id=1, source_target_pairs={{0,2},{1,3},{2,0},{3,1},{4,6},{5,7},{6,4},{7,5},{8,10},{9,11},{10,... | collective-permute-start | bytes 786440 | tf_op jit(solution)/shard_map/ppermute | solution.py:69
  575.2 29.0 %collective-permute-start.96 = (bf16[128,1024]{1,0:T(8,128)(2,1)S(1)}, bf16[128,1024]{1,0:T(8,128)(2,1)S(1)}, u32[]{:S(2)}, u32[]{:S(2)}) collective-permute-start(bf16[128,1024]{1,0:T(8,128)(2,1)S(1)} %add_convert_fusion.19), channel_id=1, source_target_pairs={{0,16},{1,17},{2,18},{3,19},{4,20},{5,21},{6,22},{7,23},{8,24},{9,... | collective-permute-start | bytes 786440 | tf_op jit(solution)/shard_map/ppermute | solution.py:69
  577.7 26.5 %collective-permute-start.94 = (bf16[128,1024]{1,0:T(8,128)(2,1)S(1)}, bf16[128,1024]{1,0:T(8,128)(2,1)S(1)}, u32[]{:S(2)}, u32[]{:S(2)}) collective-permute-start(bf16[128,1024]{1,0:T(8,128)(2,1)S(1)} %copy-done.59), channel_id=1, source_target_pairs={{0,4},{1,5},{2,6},{3,7},{4,0},{5,1},{6,2},{7,3},{8,12},{9,13},{10,... | collective-permute-start | bytes 786440 | tf_op jit(solution)/shard_map/ppermute | solution.py:69
  578.1 26.1 %collective-permute-start.95 = (bf16[128,1024]{1,0:T(8,128)(2,1)S(1)}, bf16[128,1024]{1,0:T(8,128)(2,1)S(1)}, u32[]{:S(2)}, u32[]{:S(2)}) collective-permute-start(bf16[128,1024]{1,0:T(8,128)(2,1)S(1)} %copy-done.58), channel_id=1, source_target_pairs={{0,4},{1,5},{2,6},{3,7},{4,0},{5,1},{6,2},{7,3},{8,12},{9,13},{10,... | collective-permute-start | bytes 786440 | tf_op jit(solution)/shard_map/ppermute | solution.py:69
  605.7 23.8 %all-to-all-start.3 = ((bf16[8,64,1024]{2,1,0:T(8,128)(2,1)}), bf16[8,64,1024]{2,1,0:T(8,128)(2,1)S(1)}, u32[]{:S(2)}, u32[]{:S(2)}) async-start(bf16[8,64,1024]{2,1,0:T(8,128)(2,1)} %bitcast.217), calls=%async_computation.3 | async-start | bytes 2097152 | tf_op jit(solution)/shard_map/all_to_all | solution.py:481
  633.4 34.0 %all-to-all-start.4 = ((bf16[8,64,1024]{2,1,0:T(8,128)(2,1)}), bf16[8,64,1024]{2,1,0:T(8,128)(2,1)S(1)}, u32[]{:S(2)}, u32[]{:S(2)}) async-start(bf16[8,64,1024]{2,1,0:T(8,128)(2,1)} %bitcast.74), calls=%async_computation.4 | async-start | bytes 2097152 | tf_op jit(solution)/shard_map/all_to_all | solution.py:481
  638.2 28.3 %collective-permute-start.106 = (bf16[2,80,2048]{2,1,0:T(8,128)(2,1)S(1)}, bf16[2,80,2048]{2,1,0:T(8,128)(2,1)S(1)}, u32[]{:S(2)}, u32[]{:S(2)}) collective-permute-start(bf16[2,80,2048]{2,1,0:T(8,128)(2,1)S(1)} %pad_maximum_fusion.14), channel_id=1, source_target_pairs={{0,2},{1,3},{2,0},{3,1},{4,6},{5,7},{6,4},{7,5},{8,10},{9,11},{10,... | collective-permute-start | bytes 1966088 | tf_op jit(solution)/shard_map/ppermute | solution.py:69
  641.5 25.8 %collective-permute-start.104 = (bf16[512,768]{1,0:T(8,128)(2,1)S(1)}, bf16[512,768]{1,0:T(8,128)(2,1)}, u32[]{:S(2)}, u32[]{:S(2)}) collective-permute-start(bf16[512,768]{1,0:T(8,128)(2,1)S(1)} %slice_bitcast_fusion.3), channel_id=1, source_target_pairs={{0,4},{1,5},{2,6},{3,7},{4,0},{5,1},{6,2},{7,3},{8,12},{9,13},{10,... | collective-permute-start | bytes 2359304 | tf_op jit(solution)/shard_map/ppermute | solution.py:69
  642.8 20.0 %collective-permute-start.105 = (bf16[2,48,2048]{2,1,0:T(8,128)(2,1)S(1)}, bf16[2,48,2048]{2,1,0:T(8,128)(2,1)S(1)}, u32[]{:S(2)}, u32[]{:S(2)}) collective-permute-start(bf16[2,48,2048]{2,1,0:T(8,128)(2,1)S(1)} %get-tuple-element.786), channel_id=1, source_target_pairs={{0,16},{1,17},{2,18},{3,19},{4,20},{5,21},{6,22},{7,23},{8,24},{9,... | collective-permute-start | bytes 1179656 | tf_op jit(solution)/shard_map/ppermute | solution.py:69
  673.5 18.8 %collective-permute-start.108 = (bf16[512,768]{1,0:T(8,128)(2,1)S(1)}, bf16[512,768]{1,0:T(8,128)(2,1)S(1)}, u32[]{:S(2)}, u32[]{:S(2)}) collective-permute-start(bf16[512,768]{1,0:T(8,128)(2,1)S(1)} %slice_bitcast_fusion.2), channel_id=1, source_target_pairs={{0,4},{1,5},{2,6},{3,7},{4,0},{5,1},{6,2},{7,3},{8,12},{9,13},{10,... | collective-permute-start | bytes 2359304 | tf_op jit(solution)/shard_map/ppermute | solution.py:69
  674.0 24.4 %collective-permute-start.107 = (bf16[512,768]{1,0:T(8,128)(2,1)S(1)}, bf16[512,768]{1,0:T(8,128)(2,1)S(1)}, u32[]{:S(2)}, u32[]{:S(2)}) collective-permute-start(bf16[512,768]{1,0:T(8,128)(2,1)S(1)} %fusion.16), channel_id=1, source_target_pairs={{0,8},{1,9},{2,10},{3,11},{4,12},{5,13},{6,14},{7,15},{8,0},{9,1},... | collective-permute-start | bytes 2359304 | tf_op jit(solution)/shard_map/ppermute | solution.py:69
  699.9 24.5 %all-to-all-start.5 = ((bf16[8,64,768]{2,1,0:T(8,128)(2,1)}), bf16[8,64,768]{2,1,0:T(8,128)(2,1)S(1)}, u32[]{:S(2)}, u32[]{:S(2)}) async-start(bf16[8,64,768]{2,1,0:T(8,128)(2,1)} %bitcast.86), calls=%async_computation.5 | async-start | bytes 1572864 | tf_op jit(solution)/shard_map/all_to_all | solution.py:481
  (188 other events, 1756.1 us)

commit v3 on v2

--- a/solution.py
+++ b/solution.py
@@ -17,6 +17,7 @@
 masked_value = -1e30
 inv_root = HEAD ** (-0.5)
 to_log2 = inv_root * 1.4426950408889634
+q_unscale = inv_root / to_log2
 
 bf16 = jnp.bfloat16
 f32 = jnp.float32
@@ -103,7 +104,7 @@
             values_t[home] = transposed(value)
             return 0
 
-        lax.fori_loop(0, n_blocks, place, 0)
+        lax.fori_loop(0, n_blocks, place, 0, unroll=4)
 
     frame = plan.space * BLOCK
     per_tile = plan.tile_blocks
@@ -124,30 +125,31 @@
                 [values_t[g * plan.space + s] for s in range(plan.space)], axis=1
             )
 
-        s = scores(slot)
+        def fold(carry, s, g):
+            top, total, acc = carry
+            new = jnp.maximum(top, jnp.max(s, axis=0, keepdims=True))
+            fade = jnp.exp2(top - new)
+            p = jnp.exp2(s - new)
+            total = total * fade + jnp.sum(p, axis=0, keepdims=True)
+            acc = acc * fade + matmul(value_t(g), p.astype(bf16))
+            return new, total, acc
+
+        def step(g, carry):
+            ahead = scores(g + 1)
+            s = carry[3] + jnp.where(real[g] > 0, 0.0, masked_value)
+            return (*fold(carry[:3], s, g), ahead)
+
+        first = jnp.where(real[slot] > 0, first, slot)
+        start = (
+            jnp.full((1, two), masked_value, f32),
+            jnp.zeros((1, two), f32),
+            jnp.zeros((HEAD, two), f32),
+            scores(first),
+        )
+        *carry, s = lax.fori_loop(first, slot, step, start)
         k_place = lax.broadcasted_iota(jnp.int32, (frame, two), 0)
-        s = jnp.where(k_place <= q_place, s, masked_value)
-        top = jnp.max(s, axis=0, keepdims=True)
-        p = jnp.exp2((s - top) * to_log2)
-        total = jnp.sum(p, axis=0, keepdims=True)
-        acc = matmul(value_t(slot), p.astype(bf16))
-
-        def step(g, carry):
-            def use(carry):
-                top, total, acc = carry
-                s = scores(g)
-                new = jnp.maximum(top, jnp.max(s, axis=0, keepdims=True))
-                fade = jnp.exp2((top - new) * to_log2)
-                p = jnp.exp2((s - new) * to_log2)
-                total = total * fade + jnp.sum(p, axis=0, keepdims=True)
-                acc = acc * fade + matmul(value_t(g), p.astype(bf16))
-                return new, total, acc
-
-            return lax.cond(real[g] > 0, use, lambda c: c, carry)
-
-        first = jnp.where(real[slot] > 0, first, slot)
-        top, total, acc = lax.fori_loop(first, slot, step, (top, total, acc))
-        lse[i] = top * to_log2 + jnp.log2(total)
+        top, total, acc = fold(carry, jnp.where(k_place <= q_place, s, masked_value), slot)
+        lse[i] = top + jnp.log2(total)
         acc = acc / total
         out_t[i] = acc
         back = acc.T.astype(bf16)
@@ -171,7 +173,7 @@
         keys_t[b] = transposed(keys[rows, :])
         return 0
 
-    lax.fori_loop(0, plan.count, clear, 0)
+    lax.fori_loop(0, plan.count, clear, 0, unroll=4)
 
     frame = plan.space * BLOCK
     per_tile = plan.tile_blocks
@@ -191,7 +193,10 @@
             key, value = keys[rows, :], values[rows, :]
             s = matmul(key, q, ((1,), (1,)))
             dp = matmul(value, do, ((1,), (1,)))
-            p = jnp.exp2(s * to_log2 - log_total)
+            if mask:
+                p = jnp.exp2(s - log_total)
+            else:
+                p = jnp.exp2(s - jnp.where(real[g] > 0, log_total, -masked_value))
             if mask:
                 k_place = lax.broadcasted_iota(jnp.int32, (frame, two), 0)
                 p = jnp.where(k_place <= q_place, p, 0.0)
@@ -203,13 +208,11 @@
             )
             return matmul(key_t, ds)
 
-        dq_t = turn(slot, True)
-
         def step(g, dq_t):
-            return lax.cond(real[g] > 0, lambda c: c + turn(g, False), lambda c: c, dq_t)
+            return dq_t + turn(g, False)
 
         first = jnp.where(real[slot] > 0, first, slot)
-        dq_t = lax.fori_loop(first, slot, step, dq_t)
+        dq_t = lax.fori_loop(first, slot, step, turn(slot, True))
         back = (dq_t * inv_root).T.astype(bf16)
         for j in range(per_tile):
             dq[per_tile * i + j] = back[j * BLOCK : (j + 1) * BLOCK]
@@ -222,17 +225,17 @@
         def hand_out(b, _, part=part, part_rel=part_rel):
             home = me ^ part_rel ^ info[8 + b]
             rows = pl.ds(pl.multiple_of(home * BLOCK, BLOCK), BLOCK)
-            pair = jnp.concatenate([dk[rows, :] * inv_root, dv[rows, :]], axis=1).astype(bf16)
+            pair = jnp.concatenate([dk[rows, :] * q_unscale, dv[rows, :]], axis=1).astype(bf16)
             if part == 0:
                 dkv_own[b] = pair
             else:
                 dkv_other[part - 1, b] = pair
             return 0
 
-        lax.fori_loop(0, n_blocks, hand_out, 0)
-
-
-def call(kernel, n_scalar, n_in, outs, scratch, cost):
+        lax.fori_loop(0, n_blocks, hand_out, 0, unroll=4)
+
+
+def call(kernel, n_scalar, n_in, outs, scratch, cost, room=16):
     return pl.pallas_call(
         kernel,
         out_shape=outs,
@@ -241,7 +244,7 @@
         out_specs=tuple(pl.BlockSpec(memory_space=pltpu.VMEM) for _ in outs),
         scratch_shapes=scratch,
         cost_estimate=cost,
-        compiler_params=pltpu.CompilerParams(vmem_limit_bytes=50 << 20),
+        compiler_params=pltpu.CompilerParams(vmem_limit_bytes=room << 20),
     )
 
 
@@ -369,6 +372,7 @@
         ),
         [pltpu.VMEM((plan.count, HEAD, BLOCK), bf16)],
         pl.CostEstimate(flops=8 * work * HEAD, bytes_accessed=8 << 20, transcendentals=work),
+        min(56, 8 + plan.count * 3 // 4),
     )(info, real, own, other)
 
 
@@ -392,15 +396,12 @@
             pltpu.VMEM((plan.count, HEAD, BLOCK), bf16),
         ],
         pl.CostEstimate(flops=20 * work * HEAD, bytes_accessed=8 << 20, transcendentals=work),
+        min(56, 8 + plan.count * 3 // 4),
     )(info, real, own, keys, values, grads, out_t, lse)
 
 
 def added(*values):
     return sum(v.astype(f32) for v in values).astype(bf16)
-
-
-def quarters(value):
-    return jnp.split(value, 4)
 
 
 class Side:
@@ -540,29 +541,34 @@
     up_sent = up_scaled.reshape(shard, 8, n_ff).transpose(1, 0, 2)
     down_sent = w_down.reshape(shard, 8, n_ff).transpose(1, 0, 2)
 
-    first_rel = attn.to_rel(layer_input[0], True)
+    qkv_sent, tokens = tied(qkv_sent, layer_input[0])
+    first_rel = attn.to_rel(tokens, True)
     grad_rel = feed.to_rel(cotangent[0], False)
     qkv_block = attn.octet(qkv_sent).reshape(8 * shard, -1)
-    qkv_block, first_rel, grad_rel, up_sent, down_sent = tied(
-        qkv_block, first_rel, grad_rel, up_sent, down_sent
-    )
+    qkv_block, first_rel, grad_rel, up_sent, down_sent, w_out = tied(
+        qkv_block, first_rel, grad_rel, up_sent, down_sent, w_out
+    )
+    first_near = attn.gather_one(first_rel)
     qkv_first = swap(qkv_block, attn.first)
     qkv_second = swap(qkv_block, attn.second)
-    first_near = attn.gather_one(first_rel)
-    qkv_first, qkv_second, first_near, up_sent = tied(qkv_first, qkv_second, first_near, up_sent)
+    qkv_first, qkv_second, up_sent, first_near, w_out = tied(
+        qkv_first, qkv_second, up_sent, first_near, w_out
+    )
     qkv_both = swap(qkv_first, attn.second)
     first_far = attn.gather_two(*first_near)
+    out_z = swap(w_out, attn.first)
     up_block = feed.octet(up_sent).reshape(8 * shard, -1)
-    qkv_both, first_far, up_block, down_sent, w_out = tied(
-        qkv_both, first_far, up_block, down_sent, w_out
+    qkv_both, first_far, up_block, down_sent, out_z, w_out, grad_rel = tied(
+        qkv_both, first_far, up_block, down_sent, out_z, w_out, grad_rel
     )
     qkv_mine = attn.joined(qkv_block, qkv_first, qkv_second, qkv_both)
     qkv_other = swap(qkv_mine, 1)
     first_all = team_rows(*first_near, *first_far)
-    up_rows = quarters(up_block)
-    up_z = [swap(up_rows[i], feed.first) for i in (0, 1)]
-    up_x = [swap(up_rows[i], feed.second) for i in (0, 1)]
-    out_x = swap(w_out, attn.second)
+    n_block = up_block.shape[0]
+    half = n_block // 2
+    up_za = swap(up_block[:half], feed.first)
+    up_x = swap(up_block, feed.second)
+    grad_near = feed.gather_one(grad_rel)
     down_block = feed.octet(down_sent).reshape(8 * shard, -1)
 
     team_device = me ^ jnp.array(plan.team_rel, jnp.int32)
@@ -592,7 +598,9 @@
             q, k, v = (
                 mixed[:, (3 * j + i) * HEAD : (3 * j + i + 1) * HEAD] for i in range(3)
             )
-            found.append(jnp.concatenate([rotate(q), rotate(k), v], axis=1).astype(bf16))
+            found.append(
+                jnp.concatenate([rotate(q) * to_log2, rotate(k), v], axis=1).astype(bf16)
+            )
         return found
 
     mixed_mine = matmul(first_all, qkv_mine)
@@ -602,19 +610,21 @@
     core_flip = jnp.where(has(1), 2, 0)
     pick = [(my_head ^ r) ^ core_flip for r in range(4)]
     sent = [lax.dynamic_index_in_dim(stack, pick[r], 0, keepdims=False) for r in range(4)]
-    sent, up_z, up_x, out_x, down_block, up_rows = tied(
-        sent, up_z, up_x, out_x, down_block, up_rows
+    out_pair = jnp.stack([w_out, out_z])
+    sent, up_za, up_x, grad_near, up_block, up_half, down_block, out_z, w_out, out_pair = tied(
+        sent, up_za, up_x, grad_near, up_block, up_block[half:], down_block, out_z, w_out, out_pair
     )
     got = [swap(sent[r], plan.head_rel[r]) for r in range(1, 4)]
-    up_z += [swap(up_rows[i], feed.first) for i in (2, 3)]
-    got, up_z, up_rows, down_block, grad_rel = tied(got, up_z, up_rows, down_block, grad_rel)
-    down_rows = quarters(down_block)
+    up_zb = swap(up_half, feed.first)
+    out_x = swap(out_pair, attn.second)
+    cut_z = [0, n_block // 2, n_block * 3 // 4, n_block]
+    got, up_za, up_zb, down_block, grad_near, out_x, down_first = tied(
+        got, up_za, up_zb, down_block, grad_near, out_x, down_block[: cut_z[1]]
+    )
     own = jnp.stack([sent[0]] + got).reshape(16, rows, 3 * HEAD)
-    down_z = [swap(down_rows[i], feed.first) for i in (0, 1)]
-    up_x += [swap(up_rows[i], feed.second) for i in (2, 3)]
-    up_both = [swap(up_z[i], feed.second) for i in (0, 1)]
-    grad_near = feed.gather_one(grad_rel)
-    out_z = swap(jnp.stack([w_out, out_x]), attn.first)
+    down_z = [swap(down_first, feed.first)]
+    up_both = [swap(up_za, feed.second), swap(up_zb, feed.second)]
+    grad_far = feed.gather_two(*grad_near)
     shared = own[:, :, HEAD:]
     other = jnp.stack([swap(shared, rel) for rel in plan.part_rel[1:]])
 
@@ -635,51 +645,53 @@
     ).astype(jnp.int32)
 
     attended, attended_t, log_total, keys, values = attend(plan, info, frame_real, own, other)
-    attended, down_z, up_x, up_both, grad_near, out_z, down_rows = tied(
-        attended, down_z, up_x, up_both, grad_near, out_z, down_rows
-    )
+    w_team = jnp.stack([w_out, out_x[0], out_z, out_x[1]])
+    attended, down_z, up_both, grad_far, w_team, down_block, up_x, up_za, up_zb, up_block = tied(
+        attended, down_z, up_both, grad_far, w_team, down_block, up_x, up_za, up_zb, up_block
+    )
+    w_got = swap(w_team, plan.parts[-1])
     attended = attended.reshape(4, 4 * rows, HEAD)
     heads_got = [swap(attended[r], plan.head_rel[r]) for r in range(1, 4)]
-    down_z += [swap(down_rows[2], feed.first)]
-    grad_far = feed.gather_two(*grad_near)
-    w_team = jnp.stack([w_out, out_x, out_z[0], out_z[1]])
+    down_z += [swap(down_block[cut_z[1] : cut_z[2]], feed.first)]
+    up_mine = feed.joined(up_block, up_za, up_zb, up_x, *up_both)
     for bit in reversed(plan.parts):
-        w_got = swap(w_team, bit)
+        w_got = w_got if bit == plan.parts[-1] else swap(w_team, bit)
         w_team = jnp.where(
             has(bit),
             jnp.concatenate([w_got, w_team], axis=1),
             jnp.concatenate([w_team, w_got], axis=1),
         )
     w_team = w_team.reshape(4 * HEAD, width)
-    heads_got, w_team, down_z, grad_far, up_z, down_rows = tied(
-        heads_got, w_team, down_z, grad_far, up_z, down_rows
+    heads_got, w_team, down_z, grad_far, down_block, up_mine = tied(
+        heads_got, w_team, down_z, grad_far, down_block, up_mine
     )
     attended_team = jnp.concatenate([attended[0]] + heads_got, axis=1)
     branch = matmul(attended_team, w_team).astype(bf16)
     branch_near = attn.scatter_one(branch)
-    up_both += [swap(up_z[i], feed.second) for i in (2, 3)]
-    down_x = [swap(down_rows[i], feed.second) for i in (0, 1)]
+    cut_x = n_block * 5 // 8
+    down_x = [swap(down_block[:cut_x], feed.second)]
+    up_other = swap(up_mine, 1)
     grad_all = team_rows(*grad_near, *grad_far)
-    branch_near, up_both, down_x, grad_all, down_rows, down_z = tied(
-        branch_near, up_both, down_x, grad_all, down_rows, down_z
+    branch_near, down_x, up_other, down_z, grad_all, down_block = tied(
+        branch_near, down_x, up_other, down_z, grad_all, down_block
     )
     middle = attn.scatter_two(*branch_near)
-    down_x += [swap(down_rows[i], feed.second) for i in (2, 3)]
-    up_mine = feed.joined(up_block, *up_z, *up_x, *up_both)
-    middle, down_x, up_mine, down_rows, down_z = tied(middle, down_x, up_mine, down_rows, down_z)
+    down_x += [swap(down_block[cut_x:], feed.second)]
+    middle, down_x, down_z, down_block = tied(middle, down_x, down_z, down_block)
     middle = inputs + middle
     second_near = feed.gather_one(feed.to_rel(middle, True))
-    down_z += [swap(down_rows[3], feed.first)]
-    down_both = [swap(down_z[0], feed.second)]
-    up_other = swap(up_mine, 1)
-    second_near, down_z, down_both, up_other = tied(second_near, down_z, down_both, up_other)
+    down_z += [swap(down_block[cut_z[2] :], feed.first)]
+    cut_both = n_block * 5 // 16
+    down_both = [swap(down_z[0][:cut_both], feed.second)]
+    second_near, down_both, down_z = tied(second_near, down_both, down_z)
     second_far = feed.gather_two(*second_near)
-    down_both += [swap(down_z[i], feed.second) for i in (1, 2, 3)]
-    second_far, down_both = tied(second_far, down_both)
+    down_z = jnp.concatenate(down_z)
+    down_both += [swap(down_z[cut_both:], feed.second)]
+    second_far, down_both, down_z = tied(second_far, down_both, down_z)
+    down_mine = feed.joined(down_block, down_z, *down_x, *down_both)
+    down_other = swap(down_mine, 1)
     second_all = team_rows(*second_near, *second_far)
     normed_two, scale_two = layer_norm(middle)
-    down_mine = feed.joined(down_block, *down_z, *down_x, *down_both)
-    down_other = swap(down_mine, 1)
     gelu = functools.partial(jax.nn.gelu, approximate=True)
     hidden_other = matmul(second_all, up_other)
     hidden_mine = matmul(second_all, up_mine)
@@ -702,30 +714,35 @@
     )
     second_back = feed.scatter_one(second_parts)
     down_sum = feed.first_sum(down_mine_grad, down_swapped)
-    down_sum = [quarters(part) for part in down_sum]
-    down_x3 = [swap(down_sum[3][i], feed.second) for i in (0, 1)]
+    c1, c2, c3 = n_block * 3 // 8, n_block * 3 // 4, n_block * 3 // 8
+    down_x3 = [swap(down_sum[3][:c1], feed.second)]
     second_back, down_x3, down_sum = tied(second_back, down_x3, down_sum)
     grad_second = feed.scatter_two(*second_back)
-    down_x3 += [swap(down_sum[3][2], feed.second)]
-    down_z1 = [swap(added(down_sum[1][0], down_x3[0]), feed.first)]
-    grad_second, down_x3, down_z1, down_sum = tied(grad_second, down_x3, down_z1, down_sum)
+    z1, z2 = n_block * 3 // 16, n_block * 3 // 8
+    down_z1 = [swap(added(down_sum[1][:z1], down_x3[0][:z1]), feed.first)]
+    down_x3 += [swap(down_sum[3][c1:c2], feed.second)]
+    grad_second, down_z1, down_x3, down_sum, act_mine, act_other = tied(
+        grad_second, down_z1, down_x3, down_sum, act_mine, act_other
+    )
     grad_second = feed.from_rel(grad_second)
     grad_middle = grad_out + layer_norm_back(grad_second, normed_two, scale_two)
     middle_near = attn.gather_one(grad_middle.astype(bf16))
-    down_x3 += [swap(down_sum[3][3], feed.second)]
-    down_x2 = [swap(down_sum[2][0], feed.second)]
+    down_x32 = swap(jnp.concatenate([down_sum[3][c2:], down_sum[2][:c3]]), feed.second)
     out_parts = (
         matmul(act_mine, down_mine, ((1,), (1,))) + matmul(act_other, down_other, ((1,), (1,)))
     ).astype(bf16)
-    middle_near, down_x3, down_x2, down_sum, out_parts, hid_other, hid_mine = tied(
-        middle_near, down_x3, down_x2, down_sum, out_parts, hid_other, hid_mine
+    middle_near, out_parts, hid_other, hid_mine, down_x32, down_sum, down_x3 = tied(
+        middle_near, out_parts, hid_other, hid_mine, down_x32, down_sum, down_x3
     )
     middle_far = attn.gather_two(*middle_near)
-    down_x2 += [swap(down_sum[2][i], feed.second) for i in (1, 2, 3)]
+    down_x3 = jnp.concatenate([*down_x3, down_x32[: n_block - c2]])
+    down_x2 = [down_x32[n_block - c2 :], swap(down_sum[2][c3:], feed.second)]
     up_other_grad = matmul(second_all, hid_other, ((0,), (0,))).astype(bf16)
+    up_swapped = swap(up_other_grad, 1)
     up_mine_grad = matmul(second_all, hid_mine, ((0,), (0,))).astype(bf16)
-    middle_far, down_x2, up_other_grad, up_mine_grad, down_sum, down_x3 = tied(
-        middle_far, down_x2, up_other_grad, up_mine_grad, down_sum, down_x3
+    down_z1b = added(down_sum[1][z1:z2], down_x3[z1:z2])
+    middle_far, up_swapped, up_mine_grad, down_x2, down_x3, down_sum, down_z1b = tied(
+        middle_far, up_swapped, up_mine_grad, down_x2, down_x3, down_sum, down_z1b
     )
     middle_all = team_rows(*middle_near, *middle_far)
     grad_heads = matmul(middle_all, w_team, ((1,), (1,))).astype(bf16)
@@ -733,16 +750,15 @@
     grad_got = [
         swap(grad_heads[:, r * HEAD : (r + 1) * HEAD], plan.head_rel[r]) for r in range(1, 4)
     ]
-    up_swapped = swap(up_other_grad, 1)
-    down_z1 += [swap(added(down_sum[1][1], down_x3[1]), feed.first)]
+    down_z1 += [swap(down_z1b, feed.first)]
     out_grad = matmul(attended_team, middle_all, ((0,), (0,))).astype(bf16).reshape(4, HEAD, width)
     up_sum = feed.first_sum(up_mine_grad, up_swapped)
-    up_sum = [quarters(part) for part in up_sum]
-    grad_got, up_sum, down_z1, out_grad, down_sum, down_x3 = tied(
-        grad_got, up_sum, down_z1, out_grad, down_sum, down_x3
-    )
-    up_x3 = [swap(up_sum[3][i], feed.second) for i in range(4)]
-    down_z1 += [swap(added(down_sum[1][i], down_x3[i]), feed.first) for i in (2, 3)]
+    down_z1c = added(down_sum[1][z2:], down_x3[z2:])
+    grad_got, up_sum, out_grad, down_z1, down_z1c, out_parts = tied(
+        grad_got, up_sum, out_grad, down_z1, down_z1c, out_parts
+    )
+    up_x3 = swap(up_sum[3], feed.second)
+    down_z1 += [swap(down_z1c, feed.first)]
     out_near = feed.scatter_one(out_parts)
     for bit in plan.parts:
         lower, upper = jnp.split(out_grad, 2, axis=1)
@@ -766,58 +782,56 @@
     for i, rel in enumerate(plan.part_rel[1:]):
         dkv = dkv + swap(dkv_other[i], rel).astype(f32)
     triple = jnp.concatenate([dq, dkv.astype(bf16)], axis=2).reshape(4, 4 * rows, 3 * HEAD)
-    triple, up_sum, up_x3, down_z1 = tied(triple, up_sum, up_x3, down_z1)
+    up_z1 = added(up_sum[1], up_x3)
+    triple, up_sum, up_z1, up_z1a, down_z1 = tied(triple, up_sum, up_z1, up_z1[:half], down_z1)
     got = [swap(triple[r], plan.head_rel[r]) for r in range(1, 4)]
-    up_z1 = [swap(added(up_sum[1][i], up_x3[i]), feed.first) for i in (0, 1)]
-    down_done = jnp.concatenate(
-        [added(down_sum[0][i], down_x2[i], down_z1[i]) for i in range(4)]
-    )
-    got, up_z1, down_done, up_sum, up_x3, out_near, out_grad = tied(
-        got, up_z1, down_done, up_sum, up_x3, out_near, out_grad
+    up_z1a = swap(up_z1a, feed.first)
+    down_done = added(down_sum[0], jnp.concatenate(down_x2), jnp.concatenate(down_z1))
+    got, up_z1a, up_z1, down_done, up_sum, out_grad, out_near = tied(
+        got, up_z1a, up_z1, down_done, up_sum, out_grad, out_near
     )
     places = (my_head ^ jnp.arange(4, dtype=jnp.int32)) ^ core_flip
     mixed_grad = turn_back(places, cosine, sine, [triple[0]] + got)
     mixed_grad_mine, mixed_grad_other = mixed_grad[0], mixed_grad[1]
     qkv_other_grad = matmul(first_all, mixed_grad_other, ((0,), (0,))).astype(bf16)
-    up_x2 = [swap(up_sum[2][i], feed.second) for i in (0, 1)]
-    up_z1 += [swap(added(up_sum[1][2], up_x3[2]), feed.first)]
     out_sum = feed.scatter_two(*out_near)
-    out_grad = added(out_grad[:2], swap(out_grad[2:], attn.first))
-    qkv_other_grad, mixed_grad_mine, up_x2, up_z1, out_sum, out_grad, up_sum, down_done = tied(
-        qkv_other_grad, mixed_grad_mine, up_x2, up_z1, out_sum, out_grad, up_sum, down_done
+    kept, sent = out_grad.reshape(2, 2, -1, width)[:, 0], out_grad.reshape(2, 2, -1, width)[:, 1]
+    out_grad = added(kept, swap(sent, attn.second))
+    qkv_other_grad, mixed_grad_mine, up_sum, up_z1, down_done, out_sum, out_grad, up_z1b = tied(
+        qkv_other_grad, mixed_grad_mine, up_sum, up_z1, down_done, out_sum, out_grad, up_z1[half:]
     )
     qkv_swapped = swap(qkv_other_grad, 1)
+    up_x2 = swap(up_sum[2], feed.second)
+    up_z1b = swap(up_z1b, feed.first)
+    down_got = feed.octet(down_done)
     qkv_mine_grad = matmul(first_all, mixed_grad_mine, ((0,), (0,))).astype(bf16)
     first_parts = matmul(mixed_grad_mine, qkv_mine, ((1,), (1,))) + matmul(
         mixed_grad_other, qkv_other, ((1,), (1,))
     )
-    up_x2 += [swap(up_sum[2][i], feed.second) for i in (2, 3)]
-    up_z1 += [swap(added(up_sum[1][3], up_x3[3]), feed.first)]
-    down_got = feed.octet(down_done)
     qkv_sum = attn.first_sum(qkv_mine_grad, qkv_swapped)
-    qkv_sum, first_parts, up_x2, up_z1, down_got, up_sum = tied(
-        qkv_sum, first_parts.astype(bf16), up_x2, up_z1, down_got, up_sum
+    qkv_sum, first_parts, up_x2, up_sum, up_z1b, down_got, out_grad = tied(
+        qkv_sum, first_parts.astype(bf16), up_x2, up_sum, up_z1b, down_got, out_grad
     )
     qkv_x3 = swap(qkv_sum[3], attn.second)
     first_back = attn.scatter_one(first_parts)
-    up_done = jnp.concatenate([added(up_sum[0][i], up_x2[i], up_z1[i]) for i in range(4)])
+    up_done = added(up_sum[0], up_x2, jnp.concatenate([up_z1a, up_z1b]))
+    grad_down = down_got.transpose(1, 0, 2).reshape(shard, 8 * n_ff).astype(f32)
     up_got = feed.octet(up_done)
-    output = (middle + feed.from_rel(out_sum)).astype(bf16)
-    qkv_x3, first_back, up_got, qkv_sum, out_grad, output = tied(
-        qkv_x3, first_back, up_got, qkv_sum, out_grad, output
+    qkv_x3, first_back, up_got, qkv_sum, grad_down = tied(
+        qkv_x3, first_back, up_got, qkv_sum, grad_down
     )
     qkv_z1 = swap(added(qkv_sum[1], qkv_x3), attn.first)
     qkv_x2 = swap(qkv_sum[2], attn.second)
     first_rows = attn.scatter_two(*first_back)
-    grad_down = down_got.transpose(1, 0, 2).reshape(shard, 8 * n_ff).astype(f32)
+    output = (middle + feed.from_rel(out_sum)).astype(bf16)
     grad_up, grad_gain_two = deliver(ff_columns, up_got, w_up, gain_two)
-    qkv_z1, qkv_x2, first_rows, grad_down, grad_up, out_grad = tied(
-        qkv_z1, qkv_x2, first_rows, grad_down, grad_up, out_grad
+    qkv_z1, qkv_x2, first_rows, out_grad, output, grad_up = tied(
+        qkv_z1, qkv_x2, first_rows, out_grad, output, grad_up
     )
     qkv_got = attn.octet(added(qkv_sum[0], qkv_x2, qkv_z1))
     grad_first = attn.from_rel(first_rows)
     grad_inputs = grad_middle + layer_norm_back(grad_first, *layer_norm(inputs))
-    out_grad = out_grad[0].astype(f32) + swap(out_grad[1], attn.second).astype(f32)
+    out_grad = out_grad[0].astype(f32) + swap(out_grad[1], attn.first).astype(f32)
     grad_qkv, grad_gain_one = deliver(qkv_columns, qkv_got, w_qkv, gain_one)
     return (
         output[None],

time: 734 us -> 658 us (0.90)
  starting transfers between devices: 140 us -> 109 us
  waiting for transfers between devices: 328 us -> 311 us
  Pallas kernels: 60.4 us -> 46 us
  matrix products: 78.2 us -> 68.3 us
    ppermute x112 -> x87, starting transfers between devices: 113 us -> 81.7 us  [swap(): return lax.ppermute(value, AXES, [(d, d ^ mask) for d in self.devices])]
    all_to_all x6, waiting for transfers between devices: 34.4 us -> 20.4 us  [octet(): return lax.all_to_all(value, AXES, 0, 0, axis_index_groups=self.groups)]
    unnamed x297 -> x257, local copies, waits for them, and re-layouts: 40.6 us -> 28 us
    slice x1 -> x19, local copies, waits for them, and re-layouts: 0.04 us -> 10.2 us  [the longest x1 2.06 us: on_device(): up_block[half:]]
    dot_general x21, matrix products: 78.2 us -> 68.3 us  [matmul(): lax.dot_general(left, right, (dims, ((), ())), preferred_element_type=f32)]
    ppermute x112 -> x87, waiting for transfers between devices: 294 us -> 291 us  [swap(): return lax.ppermute(value, AXES, [(d, d ^ mask) for d in self.devices])]
    convert_element_type x31 -> x20, other arithmetic: 23.7 us -> 23.6 us  [added(): return sum((v.astype(f32) for v in values)).astype(bf16)]
  transfers between devices with their start and end apart: 118 -> 93, of which waited for: 53 -> 40; matrix products, arithmetic and copies ran while one was open for 21% -> 20% of each run, Pallas kernels for 8% -> 7%
where the time goes in v3:
time: 658 us; the launch traced here: 651 us
  waiting for transfers between devices  311 us (47%)
  starting transfers between devices  109 us (17%)
  matrix products  68.3 us (10%)
  local copies, waits for them, and re-layouts  61.7 us (9%)
  other arithmetic  51.7 us (8%)
  Pallas kernels  46 us (7%)
    ppermute x87, waiting for transfers between devices, swap(): return lax.ppermute(value, AXES, [(d, d ^ mask) for d in self.devices])  291 us
    ppermute x87, starting transfers between devices, swap(): return lax.ppermute(value, AXES, [(d, d ^ mask) for d in self.devices])  81.7 us
    dot_general x21, matrix products, matmul(): lax.dot_general(left, right, (dims, ((), ())), preferred_element_type=f32)  68.3 us
    unnamed x257, local copies, waits for them, and re-layouts  28 us
    all_to_all x6, starting transfers between devices, octet(): return lax.all_to_all(value, AXES, 0, 0, axis_index_groups=self.groups)  27.4 us
    convert_element_type x20, other arithmetic, added(): return sum((v.astype(f32) for v in values)).astype(bf16)  23.6 us
    all_to_all x6, waiting for transfers between devices, octet(): return lax.all_to_all(value, AXES, 0, 0, axis_index_groups=self.groups)  20.4 us
    pallas_call x1, Pallas kernels, attend_back(): call(functools.partial(attend_back_kernel, plan), 2, 6, (shape((blocks, B...  18.9 us
  transfers between devices with their start and end apart: 93, of which 40 were waited for; matrix products, arithmetic and copies ran while one was open for 20% of the time, Pallas kernels for 7%

profile of v3, /device:TPU:0, one launch (start us, length us, event | category | flops | bytes accessed | tf_op | source)
XLA Modules:
  0.0 651.5 jit_solution(12914126996461817594)
XLA Ops:
  5.6 6.3 all-to-all-start
  17.5 15.5 %all-to-all-done = bf16[8,64,768]{2,1,0:T(8,128)(2,1)} async-done(((bf16[8,64,768]{2,1,0:T(8,128)(2,1)}), bf16[8,64,768]{2,1,0:T(8,128)(2,1)}, u32[]{:S(2)}, u32[]{:S(2)}) %all-to-all-start) | async-done | bytes 786464 | tf_op jit(solution)/shard_map/all_to_all | solution.py:482
  38.1 4.4 collective-permute-done.2.a_lo
  42.5 15.8 %collective-permute-done.3.b_hi = bf16[80,2048]{1,0:T(8,128)(2,1)S(1)} collective-permute-done((bf16[80,2048]{1,0:T(8,128)(2,1)S(1)}, bf16[80,2048]{1,0:T(8,128)(2,1)S(1)}, u32[]{:S(2)}, u32[]{:S(2)}) %collective-permute-start.3) | collective-permute-done | bytes 327712 | tf_op jit(solution)/shard_map/ppermute | solution.py:70
  60.6 2.8 copy.38
  63.4 4.2 all-to-all-start.1
  76.6 19.5 %collective-permute-done.7 = bf16[64,2048]{1,0:T(8,128)(2,1)S(1)} collective-permute-done((bf16[64,2048]{1,0:T(8,128)(2,1)S(1)}, bf16[64,2048]{1,0:T(8,128)(2,1)S(1)}, u32[]{:S(2)}, u32[]{:S(2)}) %collective-permute-start.7) | collective-permute-done | bytes 262176 | tf_op jit(solution)/shard_map/ppermute | solution.py:70
  102.0 2.8 copy.39
  104.8 4.6 all-to-all-start.2
  118.4 3.7 fusion.113
  126.5 11.8 %collective-permute-done.9 = bf16[256,1024]{1,0:T(8,128)(2,1)} collective-permute-done((bf16[256,1024]{1,0:T(8,128)(2,1)S(1)}, bf16[256,1024]{1,0:T(8,128)(2,1)}, u32[]{:S(2)}, u32[]{:S(2)}) %collective-permute-start.9) | collective-permute-done | bytes 524320 | tf_op jit(solution)/shard_map/ppermute | solution.py:70
  140.5 2.8 collective-permute-start.14
  146.1 15.8 %collective-permute-done.13 = bf16[512,384]{1,0:T(8,128)(2,1)S(1)} collective-permute-done((bf16[512,384]{1,0:T(8,128)(2,1)}, bf16[512,384]{1,0:T(8,128)(2,1)S(1)}, u32[]{:S(2)}, u32[]{:S(2)}) %collective-permute-start.13) | collective-permute-done | bytes 393248 | tf_op jit(solution)/shard_map/ppermute | solution.py:70
  161.9 2.8 collective-permute-done.14
  164.6 6.8 %collective-permute-done.15 = bf16[512,384]{1,0:T(8,128)(2,1)S(1)} collective-permute-done((bf16[512,384]{1,0:T(8,128)(2,1)}, bf16[512,384]{1,0:T(8,128)(2,1)S(1)}, u32[]{:S(2)}, u32[]{:S(2)}) %collective-permute-start.15) | collective-permute-done | bytes 393248 | tf_op jit(solution)/shard_map/ppermute | solution.py:70
  183.2 17.0 %shard_map.200 = (bf16[16,128,128]{2,1,0:T(8,128)(2,1)S(1)}, f32[8,128,256]{2,1,0:T(8,128)S(1)}, f32[8,1,256]{2,1,0:T(1,128)S(1)}, bf16[4096,128]{1,0:T(8,128)(2,1)S(1)}, bf16[4096,128]{1,0:T(8,128)(2,1)S(1)}) custom-call(s32[56]{0:T(128)S(1)} %concatenate.185.info, s32[8]{0:T(128)S(1)} %copy-done.23, bf16[16,128,384]{2,1,0:T(8,128)(2,1)S(1)} %bitcast.247, ...), custom_call_target="tpu_custom_call" | custom-call | flops 4294967296 | bytes 8388608 | tf_op jit(solution)/shard_map/pallas_call | solution.py:362
  214.4 8.5 %collective-permute-done.28 = bf16[128,1024]{1,0:T(8,128)(2,1)S(1)} collective-permute-done((bf16[128,1024]{1,0:T(8,128)(2,1)S(1)}, bf16[128,1024]{1,0:T(8,128)(2,1)S(1)}, u32[]{:S(2)}, u32[]{:S(2)}) %collective-permute-start.28) | collective-permute-done | bytes 262176 | tf_op jit(solution)/shard_map/ppermute | solution.py:70
  228.3 18.4 %collective-permute-done.29 = bf16[2,48,2048]{2,1,0:T(8,128)(2,1)S(1)} collective-permute-done((bf16[2,48,2048]{2,1,0:T(8,128)(2,1)S(1)}, bf16[2,48,2048]{2,1,0:T(8,128)(2,1)S(1)}, u32[]{:S(2)}, u32[]{:S(2)}) %collective-permute-start.29) | collective-permute-done | bytes 393248 | tf_op jit(solution)/shard_map/ppermute | solution.py:70
  251.1 2.6 collective-permute-done.33
  253.8 11.1 %collective-permute-done.34 = bf16[80,2048]{1,0:T(8,128)(2,1)S(1)} collective-permute-done((bf16[80,2048]{1,0:T(8,128)(2,1)S(1)}, bf16[80,2048]{1,0:T(8,128)(2,1)S(1)}, u32[]{:S(2)}, u32[]{:S(2)}) %collective-permute-start.34) | collective-permute-done | bytes 327712 | tf_op jit(solution)/shard_map/ppermute | solution.py:70
  269.1 2.7 collective-permute-start.37
  272.3 8.2 %collective-permute-done.39 = bf16[128,1024]{1,0:T(8,128)(2,1)S(1)} collective-permute-done((bf16[128,1024]{1,0:T(8,128)(2,1)S(1)}, bf16[128,1024]{1,0:T(8,128)(2,1)S(1)}, u32[]{:S(2)}, u32[]{:S(2)}) %collective-permute-start.39) | collective-permute-done | bytes 262176 | tf_op jit(solution)/shard_map/ppermute | solution.py:70
  280.5 2.7 collective-permute-done.37.b_hi
  286.1 9.9 %collective-permute-done.41.b_far = bf16[128,2048]{1,0:T(8,128)(2,1)S(1)} collective-permute-done((bf16[128,2048]{1,0:T(8,128)(2,1)S(1)}, bf16[128,2048]{1,0:T(8,128)(2,1)S(1)}, u32[]{:S(2)}, u32[]{:S(2)}) %collective-permute-start.41) | collective-permute-done | bytes 524320 | tf_op jit(solution)/shard_map/ppermute | solution.py:70
  296.9 3.8 collective-permute-done.42
  303.0 4.0 multiply_convert_fusion.1
  307.0 4.4 convolution_convert_fusion.3
  311.4 4.5 multiply_convert_fusion
  318.2 4.4 convolution_convert_fusion.2
  322.6 3.4 fusion.6
  328.9 3.4 fusion.13
  332.3 2.7 add_convert_fusion.5
  336.9 4.3 add_convert_fusion.1
  341.9 10.6 %collective-permute-done.47 = bf16[192,1024]{1,0:T(8,128)(2,1)S(1)} collective-permute-done((bf16[192,1024]{1,0:T(8,128)(2,1)S(1)}, bf16[192,1024]{1,0:T(8,128)(2,1)S(1)}, u32[]{:S(2)}, u32[]{:S(2)}) %collective-permute-start.47) | collective-permute-done | bytes 393248 | tf_op jit(solution)/shard_map/ppermute | solution.py:70
  356.5 8.8 %collective-permute-done.49 = bf16[64,2048]{1,0:T(8,128)(2,1)S(1)} collective-permute-done((bf16[64,2048]{1,0:T(8,128)(2,1)S(1)}, bf16[64,2048]{1,0:T(8,128)(2,1)S(1)}, u32[]{:S(2)}, u32[]{:S(2)}) %collective-permute-start.49) | collective-permute-done | bytes 262176 | tf_op jit(solution)/shard_map/ppermute | solution.py:70
  376.3 3.8 add_convert_fusion.4
  380.1 8.9 %collective-permute-done.53.b_hi = bf16[80,2048]{1,0:T(8,128)(2,1)S(1)} collective-permute-done((bf16[80,2048]{1,0:T(8,128)(2,1)S(1)}, bf16[80,2048]{1,0:T(8,128)(2,1)S(1)}, u32[]{:S(2)}, u32[]{:S(2)}) %collective-permute-start.53) | collective-permute-done | bytes 327712 | tf_op jit(solution)/shard_map/ppermute | solution.py:70
  389.0 2.8 convolution_convert_fusion.1
  398.9 15.8 %collective-permute-done.55.a_far = bf16[96,2048]{1,0:T(8,128)(2,1)S(1)} collective-permute-done((bf16[96,2048]{1,0:T(8,128)(2,1)S(1)}, bf16[96,2048]{1,0:T(8,128)(2,1)S(1)}, u32[]{:S(2)}, u32[]{:S(2)}) %collective-permute-start.55) | collective-permute-done | bytes 393248 | tf_op jit(solution)/shard_map/ppermute | solution.py:70
  429.8 4.1 collective-permute-done.62
  438.5 2.4 collective-permute-start.65
  441.6 18.9 %shard_map.205 = (bf16[16,128,128]{2,1,0:T(8,128)(2,1)S(1)}, bf16[16,128,256]{2,1,0:T(8,128)(2,1)S(1)}, bf16[1,16,128,256]{3,2,1,0:T(8,128)(2,1)}) custom-call(s32[56]{0:T(128)S(1)} %concatenate.185.info, s32[8]{0:T(128)S(1)} %copy-done.23, bf16[16,128,384]{2,1,0:T(8,128)(2,1)S(1)} %bitcast.248, bf16[4096,128]{1,0:T(8,128)(2,1)S(1)} %copy-done.27, ...), custom_call_target="tpu_custom_call" | custom-call | flops 10737418240 | bytes 8388608 | tf_op jit(solution)/shard_map/pallas_call | solution.py:384
  462.1 3.9 collective-permute-done.64
  471.7 2.6 collective-permute-start.71
  475.7 3.1 fusion.17
  478.7 13.5 %collective-permute-done.71.refs_3_ = bf16[512,384]{1,0:T(8,128)(2,1)S(1)} collective-permute-done((bf16[512,384]{1,0:T(8,128)(2,1)S(1)}, bf16[512,384]{1,0:T(8,128)(2,1)S(1)}, u32[]{:S(2)}, u32[]{:S(2)}) %collective-permute-start.71) | collective-permute-done | bytes 393248 | tf_op jit(solution)/shard_map/ppermute | solution.py:70
  492.3 10.6 %collective-permute-done.70.refs_2_ = bf16[512,384]{1,0:T(8,128)(2,1)S(1)} collective-permute-done((bf16[512,384]{1,0:T(8,128)(2,1)S(1)}, bf16[512,384]{1,0:T(8,128)(2,1)S(1)}, u32[]{:S(2)}, u32[]{:S(2)}) %collective-permute-start.70) | collective-permute-done | bytes 393248 | tf_op jit(solution)/shard_map/ppermute | solution.py:70
  508.6 3.6 convolution_convert_fusion.5
  512.2 5.8 fusion.34
  521.1 4.5 all-to-all-start.3
  525.6 2.6 collective-permute-start.78
  532.9 5.4 add_convert_fusion.3
  539.2 3.7 add_convert_fusion.2
  542.9 6.3 collective-permute-done.78
  549.2 6.0 collective-permute-done.77
  555.3 3.3 fusion.15
  558.6 4.3 all-to-all-start.4
  571.7 16.4 %collective-permute-done.80 = bf16[2,48,2048]{2,1,0:T(8,128)(2,1)S(1)} collective-permute-done((bf16[2,48,2048]{2,1,0:T(8,128)(2,1)S(1)}, bf16[2,48,2048]{2,1,0:T(8,128)(2,1)S(1)}, u32[]{:S(2)}, u32[]{:S(2)}) %collective-permute-start.80) | collective-permute-done | bytes 393248 | tf_op jit(solution)/shard_map/ppermute | solution.py:70
  588.1 3.3 collective-permute-done.81
  601.4 11.6 %collective-permute-done.85 = bf16[80,2048]{1,0:T(8,128)(2,1)S(1)} collective-permute-done((bf16[80,2048]{1,0:T(8,128)(2,1)S(1)}, bf16[80,2048]{1,0:T(8,128)(2,1)S(1)}, u32[]{:S(2)}, u32[]{:S(2)}) %collective-permute-start.85) | collective-permute-done | bytes 327712 | tf_op jit(solution)/shard_map/ppermute | solution.py:70
  614.9 7.8 %collective-permute-done.82 = bf16[512,768]{1,0:T(8,128)(2,1)S(1)} collective-permute-done((bf16[512,768]{1,0:T(8,128)(2,1)S(1)}, bf16[512,768]{1,0:T(8,128)(2,1)S(1)}, u32[]{:S(2)}, u32[]{:S(2)}) %collective-permute-start.82) | collective-permute-done | bytes 786464 | tf_op jit(solution)/shard_map/ppermute | solution.py:70
  623.9 3.6 all-to-all-start.5
  633.0 9.8 %collective-permute-done.86 = bf16[64,2048]{1,0:T(8,128)(2,1)S(1)} collective-permute-done((bf16[64,2048]{1,0:T(8,128)(2,1)S(1)}, bf16[64,2048]{1,0:T(8,128)(2,1)S(1)}, u32[]{:S(2)}, u32[]{:S(2)}) %collective-permute-start.86) | collective-permute-done | bytes 262176 | tf_op jit(solution)/shard_map/ppermute | solution.py:70
  643.6 4.9 all-to-all-done.5.got
  (594 shorter events, 199.9 us)
Async XLA Ops:
  5.6 27.4 %all-to-all-start = ((bf16[8,64,768]{2,1,0:T(8,128)(2,1)}), bf16[8,64,768]{2,1,0:T(8,128)(2,1)}, u32[]{:S(2)}, u32[]{:S(2)}) async-start(bf16[8,64,768]{2,1,0:T(8,128)(2,1)} %reshape.472), calls=%async_computation | async-start | bytes 1572864 | tf_op jit(solution)/shard_map/all_to_all | solution.py:482
  33.0 25.4 %collective-permute-start.1 = (bf16[512,768]{1,0:T(8,128)(2,1)}, bf16[512,768]{1,0:T(8,128)(2,1)}, u32[]{:S(2)}, u32[]{:S(2)}) collective-permute-start(bf16[512,768]{1,0:T(8,128)(2,1)} %bitcast.2), channel_id=1, source_target_pairs={{0,4},{1,5},{2,6},{3,7},{4,0},{5,1},{6,2},{7,3},{8,12},{9,13},{10,... | collective-permute-start | bytes 2359304 | tf_op jit(solution)/shard_map/ppermute | solution.py:70
  34.5 26.1 %collective-permute-start = (bf16[512,768]{1,0:T(8,128)(2,1)}, bf16[512,768]{1,0:T(8,128)(2,1)}, u32[]{:S(2)}, u32[]{:S(2)}) collective-permute-start(bf16[512,768]{1,0:T(8,128)(2,1)} %bitcast.2), channel_id=1, source_target_pairs={{0,8},{1,9},{2,10},{3,11},{4,12},{5,13},{6,14},{7,15},{8,0},{9,1},... | collective-permute-start | bytes 2359304 | tf_op jit(solution)/shard_map/ppermute | solution.py:70
  34.5 23.8 %collective-permute-start.3 = (bf16[80,2048]{1,0:T(8,128)(2,1)S(1)}, bf16[80,2048]{1,0:T(8,128)(2,1)S(1)}, u32[]{:S(2)}, u32[]{:S(2)}) collective-permute-start(bf16[80,2048]{1,0:T(8,128)(2,1)S(1)} %slice.606.b), channel_id=1, source_target_pairs={{0,16},{1,17},{2,18},{3,19},{4,20},{5,21},{6,22},{7,23},{8,24},{9,... | collective-permute-start | bytes 983048 | tf_op jit(solution)/shard_map/ppermute | solution.py:70
  63.4 34.3 %all-to-all-start.1 = ((bf16[8,64,1024]{2,1,0:T(8,128)(2,1)}), bf16[8,64,1024]{2,1,0:T(8,128)(2,1)}, u32[]{:S(2)}, u32[]{:S(2)}) async-start(bf16[8,64,1024]{2,1,0:T(8,128)(2,1)} %copy.38), calls=%async_computation.1 | async-start | bytes 2097152 | tf_op jit(solution)/shard_map/all_to_all | solution.py:482
  67.7 30.1 %collective-permute-start.4 = (bf16[512,768]{1,0:T(8,128)(2,1)}, bf16[512,768]{1,0:T(8,128)(2,1)}, u32[]{:S(2)}, u32[]{:S(2)}) collective-permute-start(bf16[512,768]{1,0:T(8,128)(2,1)} %collective-permute-done), channel_id=1, source_target_pairs={{0,4},{1,5},{2,6},{3,7},{4,0},{5,1},{6,2},{7,3},{8,12},{9,13},{10,... | collective-permute-start | bytes 2359304 | tf_op jit(solution)/shard_map/ppermute | solution.py:70
  68.3 28.6 %collective-permute-start.6 = (bf16[160,2048]{1,0:T(8,128)(2,1)S(1)}, bf16[160,2048]{1,0:T(8,128)(2,1)S(1)}, u32[]{:S(2)}, u32[]{:S(2)}) collective-permute-start(bf16[160,2048]{1,0:T(8,128)(2,1)S(1)} %pad_maximum_fusion.8), channel_id=1, source_target_pairs={{0,2},{1,3},{2,0},{3,1},{4,6},{5,7},{6,4},{7,5},{8,10},{9,11},{10,... | collective-permute-start | bytes 1966088 | tf_op jit(solution)/shard_map/ppermute | solution.py:70
  70.2 25.9 %collective-permute-start.5 = (bf16[96,2048]{1,0:T(8,128)(2,1)S(1)}, bf16[96,2048]{1,0:T(8,128)(2,1)S(1)}, u32[]{:S(2)}, u32[]{:S(2)}) collective-permute-start(bf16[96,2048]{1,0:T(8,128)(2,1)S(1)} %pad_maximum_fusion.26), channel_id=1, source_target_pairs={{0,16},{1,17},{2,18},{3,19},{4,20},{5,21},{6,22},{7,23},{8,24},{9,... | collective-permute-start | bytes 1179656 | tf_op jit(solution)/shard_map/ppermute | solution.py:70
  72.6 23.5 %collective-permute-start.7 = (bf16[64,2048]{1,0:T(8,128)(2,1)S(1)}, bf16[64,2048]{1,0:T(8,128)(2,1)S(1)}, u32[]{:S(2)}, u32[]{:S(2)}) collective-permute-start(bf16[64,2048]{1,0:T(8,128)(2,1)S(1)} %copy-done.48), channel_id=1, source_target_pairs={{0,8},{1,9},{2,10},{3,11},{4,12},{5,13},{6,14},{7,15},{8,0},{9,1},... | collective-permute-start | bytes 786440 | tf_op jit(solution)/shard_map/ppermute | solution.py:70
  99.8 18.6 %collective-permute-start.8 = (bf16[2048,768]{1,0:T(8,128)(2,1)}, bf16[2048,768]{1,0:T(8,128)(2,1)}, u32[]{:S(2)}, u32[]{:S(2)}) collective-permute-start(bf16[2048,768]{1,0:T(8,128)(2,1)} %constant_dynamic-update-slice_fusion), channel_id=1, source_target_pairs={{0,1},{1,0},{2,3},{3,2},{4,5},{5,4},{6,7},{7,6},{8,9},{9,8},{10,11... | collective-permute-start | bytes 9437192 | tf_op jit(solution)/shard_map/ppermute | solution.py:70
  100.0 26.5 %collective-permute-start.12 = (bf16[64,2048]{1,0:T(8,128)(2,1)S(1)}, bf16[64,2048]{1,0:T(8,128)(2,1)S(1)}, u32[]{:S(2)}, u32[]{:S(2)}) collective-permute-start(bf16[64,2048]{1,0:T(8,128)(2,1)S(1)} %get-tuple-element.281.b), channel_id=1, source_target_pairs={{0,8},{1,9},{2,10},{3,11},{4,12},{5,13},{6,14},{7,15},{8,0},{9,1},... | collective-permute-start | bytes 786440 | tf_op jit(solution)/shard_map/ppermute | solution.py:70
  100.7 25.8 %collective-permute-start.11 = (bf16[64,2048]{1,0:T(8,128)(2,1)S(1)}, bf16[64,2048]{1,0:T(8,128)(2,1)}, u32[]{:S(2)}, u32[]{:S(2)}) collective-permute-start(bf16[64,2048]{1,0:T(8,128)(2,1)S(1)} %get-tuple-element.279.a), channel_id=1, source_target_pairs={{0,2},{1,3},{2,0},{3,1},{4,6},{5,7},{6,4},{7,5},{8,10},{9,11},{10,... | collective-permute-start | bytes 786440 | tf_op jit(solution)/shard_map/ppermute | solution.py:70
  104.8 33.5 %all-to-all-start.2 = ((bf16[8,64,1024]{2,1,0:T(8,128)(2,1)}), bf16[8,64,1024]{2,1,0:T(8,128)(2,1)}, u32[]{:S(2)}, u32[]{:S(2)}) async-start(bf16[8,64,1024]{2,1,0:T(8,128)(2,1)} %copy.39), calls=%async_computation.2 | async-start | bytes 2097152 | tf_op jit(solution)/shard_map/all_to_all | solution.py:482
  109.4 28.9 %collective-permute-start.10 = (bf16[512,1024]{1,0:T(8,128)(2,1)}, bf16[512,1024]{1,0:T(8,128)(2,1)}, u32[]{:S(2)}, u32[]{:S(2)}) collective-permute-start(bf16[512,1024]{1,0:T(8,128)(2,1)} %bitcast.6), channel_id=1, source_target_pairs={{0,4},{1,5},{2,6},{3,7},{4,0},{5,1},{6,2},{7,3},{8,12},{9,13},{10,... | collective-permute-start | bytes 3145736 | tf_op jit(solution)/shard_map/ppermute | solution.py:70
  112.0 26.3 %collective-permute-start.9 = (bf16[256,1024]{1,0:T(8,128)(2,1)S(1)}, bf16[256,1024]{1,0:T(8,128)(2,1)}, u32[]{:S(2)}, u32[]{:S(2)}) collective-permute-start(bf16[256,1024]{1,0:T(8,128)(2,1)S(1)} %get-tuple-element.577), channel_id=1, source_target_pairs={{0,16},{1,17},{2,18},{3,19},{4,20},{5,21},{6,22},{7,23},{8,24},{9,... | collective-permute-start | bytes 1572872 | tf_op jit(solution)/shard_map/ppermute | solution.py:70
  138.3 33.1 %collective-permute-start.16 = (bf16[256,1024]{1,0:T(8,128)(2,1)S(1)}, bf16[256,1024]{1,0:T(8,128)(2,1)S(1)}, u32[]{:S(2)}, u32[]{:S(2)}) collective-permute-start(bf16[256,1024]{1,0:T(8,128)(2,1)S(1)} %copy-done.67), channel_id=1, source_target_pairs={{0,16},{1,17},{2,18},{3,19},{4,20},{5,21},{6,22},{7,23},{8,24},{9,... | collective-permute-start | bytes 1572872 | tf_op jit(solution)/shard_map/ppermute | solution.py:70
  138.4 33.0 %collective-permute-start.17 = (bf16[2,64,2048]{2,1,0:T(8,128)(2,1)S(1)}, bf16[2,64,2048]{2,1,0:T(8,128)(2,1)S(1)}, u32[]{:S(2)}, u32[]{:S(2)}) collective-permute-start(bf16[2,64,2048]{2,1,0:T(8,128)(2,1)S(1)} %pad_maximum_fusion.15), channel_id=1, source_target_pairs={{0,4},{1,5},{2,6},{3,7},{4,0},{5,1},{6,2},{7,3},{8,12},{9,13},{10,... | collective-permute-start | bytes 1572872 | tf_op jit(solution)/shard_map/ppermute | solution.py:70
  140.0 21.9 %collective-permute-start.13 = (bf16[512,384]{1,0:T(8,128)(2,1)}, bf16[512,384]{1,0:T(8,128)(2,1)S(1)}, u32[]{:S(2)}, u32[]{:S(2)}) collective-permute-start(bf16[512,384]{1,0:T(8,128)(2,1)} %get-tuple-element.259), channel_id=1, source_target_pairs={{0,4},{1,5},{2,6},{3,7},{4,0},{5,1},{6,2},{7,3},{8,12},{9,13},{10,... | collective-permute-start | bytes 1179656 | tf_op jit(solution)/shard_map/ppermute | solution.py:70
  140.5 24.1 %collective-permute-start.14 = (bf16[512,384]{1,0:T(8,128)(2,1)}, bf16[512,384]{1,0:T(8,128)(2,1)S(1)}, u32[]{:S(2)}, u32[]{:S(2)}) collective-permute-start(bf16[512,384]{1,0:T(8,128)(2,1)} %get-tuple-element.260), channel_id=1, source_target_pairs={{0,8},{1,9},{2,10},{3,11},{4,12},{5,13},{6,14},{7,15},{8,0},{9,1},... | collective-permute-start | bytes 1179656 | tf_op jit(solution)/shard_map/ppermute | solution.py:70
  143.3 28.2 %collective-permute-start.15 = (bf16[512,384]{1,0:T(8,128)(2,1)}, bf16[512,384]{1,0:T(8,128)(2,1)S(1)}, u32[]{:S(2)}, u32[]{:S(2)}) collective-permute-start(bf16[512,384]{1,0:T(8,128)(2,1)} %get-tuple-element.261), channel_id=1, source_target_pairs={{0,12},{1,13},{2,14},{3,15},{4,8},{5,9},{6,10},{7,11},{8,4},{9,5},... | collective-permute-start | bytes 1179656 | tf_op jit(solution)/shard_map/ppermute | solution.py:70
  174.0 26.3 %collective-permute-start.23 = (bf16[128,2048]{1,0:T(8,128)(2,1)S(1)}, bf16[128,2048]{1,0:T(8,128)(2,1)S(1)}, u32[]{:S(2)}, u32[]{:S(2)}) collective-permute-start(bf16[128,2048]{1,0:T(8,128)(2,1)S(1)} %pad_maximum_fusion.17), channel_id=1, source_target_pairs={{0,2},{1,3},{2,0},{3,1},{4,6},{5,7},{6,4},{7,5},{8,10},{9,11},{10,... | collective-permute-start | bytes 1572872 | tf_op jit(solution)/shard_map/ppermute | solution.py:70
  176.5 24.2 %collective-permute-start.22 = (bf16[128,2048]{1,0:T(8,128)(2,1)S(1)}, bf16[128,2048]{1,0:T(8,128)(2,1)S(1)}, u32[]{:S(2)}, u32[]{:S(2)}) collective-permute-start(bf16[128,2048]{1,0:T(8,128)(2,1)S(1)} %pad_maximum_fusion.16), channel_id=1, source_target_pairs={{0,8},{1,9},{2,10},{3,11},{4,12},{5,13},{6,14},{7,15},{8,0},{9,1},... | collective-permute-start | bytes 1572872 | tf_op jit(solution)/shard_map/ppermute | solution.py:70
  176.6 26.5 %collective-permute-start.19 = (bf16[256,1024]{1,0:T(8,128)(2,1)}, bf16[256,1024]{1,0:T(8,128)(2,1)S(1)}, u32[]{:S(2)}, u32[]{:S(2)}) collective-permute-start(bf16[256,1024]{1,0:T(8,128)(2,1)} %slice.639), channel_id=1, source_target_pairs={{0,16},{1,17},{2,18},{3,19},{4,20},{5,21},{6,22},{7,23},{8,24},{9,... | collective-permute-start | bytes 1572872 | tf_op jit(solution)/shard_map/ppermute | solution.py:70
  178.9 24.2 %collective-permute-start.20 = (bf16[256,1024]{1,0:T(8,128)(2,1)}, bf16[256,1024]{1,0:T(8,128)(2,1)S(1)}, u32[]{:S(2)}, u32[]{:S(2)}) collective-permute-start(bf16[256,1024]{1,0:T(8,128)(2,1)} %collective-permute-done.9), channel_id=1, source_target_pairs={{0,4},{1,5},{2,6},{3,7},{4,0},{5,1},{6,2},{7,3},{8,12},{9,13},{10,... | collective-permute-start | bytes 1572872 | tf_op jit(solution)/shard_map/ppermute | solution.py:70
  180.5 23.3 %collective-permute-start.21 = (bf16[256,1024]{1,0:T(8,128)(2,1)}, bf16[256,1024]{1,0:T(8,128)(2,1)S(1)}, u32[]{:S(2)}, u32[]{:S(2)}) collective-permute-start(bf16[256,1024]{1,0:T(8,128)(2,1)} %copy-done.64), channel_id=1, source_target_pairs={{0,4},{1,5},{2,6},{3,7},{4,0},{5,1},{6,2},{7,3},{8,12},{9,13},{10,... | collective-permute-start | bytes 1572872 | tf_op jit(solution)/shard_map/ppermute | solution.py:70
  222.9 23.9 %collective-permute-start.32 = (bf16[2048,1024]{1,0:T(8,128)(2,1)S(1)}, bf16[2048,1024]{1,0:T(8,128)(2,1)S(1)}, u32[]{:S(2)}, u32[]{:S(2)}) collective-permute-start(bf16[2048,1024]{1,0:T(8,128)(2,1)S(1)} %constant_dynamic-update-slice_fusion.4), channel_id=1, source_target_pairs={{0,1},{1,0},{2,3},{3,2},{4,5},{5,4},{6,7},{7,6},{8,9},{9,8},{10,11... | collective-permute-start | bytes 12582920 | tf_op jit(solution)/shard_map/ppermute | solution.py:70
  224.2 22.6 %collective-permute-start.31 = (bf16[320,1024]{1,0:T(8,128)(2,1)S(1)}, bf16[320,1024]{1,0:T(8,128)(2,1)S(1)}, u32[]{:S(2)}, u32[]{:S(2)}) collective-permute-start(bf16[320,1024]{1,0:T(8,128)(2,1)S(1)} %slice.654), channel_id=1, source_target_pairs={{0,4},{1,5},{2,6},{3,7},{4,0},{5,1},{6,2},{7,3},{8,12},{9,13},{10,... | collective-permute-start | bytes 1966088 | tf_op jit(solution)/shard_map/ppermute | solution.py:70
  226.3 20.5 %collective-permute-start.30 = (bf16[2,80,2048]{2,1,0:T(8,128)(2,1)S(1)}, bf16[2,80,2048]{2,1,0:T(8,128)(2,1)S(1)}, u32[]{:S(2)}, u32[]{:S(2)}) collective-permute-start(bf16[2,80,2048]{2,1,0:T(8,128)(2,1)S(1)} %pad_maximum_fusion.10), channel_id=1, source_target_pairs={{0,2},{1,3},{2,0},{3,1},{4,6},{5,7},{6,4},{7,5},{8,10},{9,11},{10,... | collective-permute-start | bytes 1966088 | tf_op jit(solution)/shard_map/ppermute | solution.py:70
  227.0 19.7 %collective-permute-start.29 = (bf16[2,48,2048]{2,1,0:T(8,128)(2,1)S(1)}, bf16[2,48,2048]{2,1,0:T(8,128)(2,1)S(1)}, u32[]{:S(2)}, u32[]{:S(2)}) collective-permute-start(bf16[2,48,2048]{2,1,0:T(8,128)(2,1)S(1)} %get-tuple-element.520), channel_id=1, source_target_pairs={{0,16},{1,17},{2,18},{3,19},{4,20},{5,21},{6,22},{7,23},{8,24},{9,... | collective-permute-start | bytes 1179656 | tf_op jit(solution)/shard_map/ppermute | solution.py:70
  248.5 16.4 %collective-permute-start.34 = (bf16[80,2048]{1,0:T(8,128)(2,1)S(1)}, bf16[80,2048]{1,0:T(8,128)(2,1)S(1)}, u32[]{:S(2)}, u32[]{:S(2)}) collective-permute-start(bf16[80,2048]{1,0:T(8,128)(2,1)S(1)} %fusion.37), channel_id=1, source_target_pairs={{0,16},{1,17},{2,18},{3,19},{4,20},{5,21},{6,22},{7,23},{8,24},{9,... | collective-permute-start | bytes 983048 | tf_op jit(solution)/shard_map/ppermute | solution.py:70
  249.6 15.5 %collective-permute-start.35 = (bf16[192,1024]{1,0:T(8,128)(2,1)S(1)}, bf16[192,1024]{1,0:T(8,128)(2,1)S(1)}, u32[]{:S(2)}, u32[]{:S(2)}) collective-permute-start(bf16[192,1024]{1,0:T(8,128)(2,1)S(1)} %slice.663), channel_id=1, source_target_pairs={{0,4},{1,5},{2,6},{3,7},{4,0},{5,1},{6,2},{7,3},{8,12},{9,13},{10,... | collective-permute-start | bytes 1179656 | tf_op jit(solution)/shard_map/ppermute | solution.py:70
  266.2 17.0 %collective-permute-start.38 = (bf16[160,1024]{1,0:T(8,128)(2,1)S(1)}, bf16[160,1024]{1,0:T(8,128)(2,1)S(1)}, u32[]{:S(2)}, u32[]{:S(2)}) collective-permute-start(bf16[160,1024]{1,0:T(8,128)(2,1)S(1)} %slice.666), channel_id=1, source_target_pairs={{0,4},{1,5},{2,6},{3,7},{4,0},{5,1},{6,2},{7,3},{8,12},{9,13},{10,... | collective-permute-start | bytes 983048 | tf_op jit(solution)/shard_map/ppermute | solution.py:70
  284.0 16.7 %collective-permute-start.42 = (bf16[352,1024]{1,0:T(8,128)(2,1)S(1)}, bf16[352,1024]{1,0:T(8,128)(2,1)S(1)}, u32[]{:S(2)}, u32[]{:S(2)}) collective-permute-start(bf16[352,1024]{1,0:T(8,128)(2,1)S(1)} %slice.818), channel_id=1, source_target_pairs={{0,4},{1,5},{2,6},{3,7},{4,0},{5,1},{6,2},{7,3},{8,12},{9,13},{10,... | collective-permute-start | bytes 2162696 | tf_op jit(solution)/shard_map/ppermute | solution.py:70
  317.9 17.1 %collective-permute-start.44 = (bf16[2048,1024]{1,0:T(8,128)(2,1)}, bf16[2048,1024]{1,0:T(8,128)(2,1)}, u32[]{:S(2)}, u32[]{:S(2)}) collective-permute-start(bf16[2048,1024]{1,0:T(8,128)(2,1)} %convolution_convert_fusion.3), channel_id=1, source_target_pairs={{0,1},{1,0},{2,3},{3,2},{4,5},{5,4},{6,7},{7,6},{8,9},{9,8},{10,11... | collective-permute-start | bytes 12582920 | tf_op jit(solution)/shard_map/ppermute | solution.py:70
  335.3 17.2 %collective-permute-start.46 = (bf16[2,64,2048]{2,1,0:T(8,128)(2,1)S(1)}, bf16[2,64,2048]{2,1,0:T(8,128)(2,1)S(1)}, u32[]{:S(2)}, u32[]{:S(2)}) collective-permute-start(bf16[2,64,2048]{2,1,0:T(8,128)(2,1)S(1)} %pad_maximum_fusion.22), channel_id=1, source_target_pairs={{0,2},{1,3},{2,0},{3,1},{4,6},{5,7},{6,4},{7,5},{8,10},{9,11},{10,... | collective-permute-start | bytes 1572872 | tf_op jit(solution)/shard_map/ppermute | solution.py:70
  336.9 15.6 %collective-permute-start.45 = (bf16[2,64,2048]{2,1,0:T(8,128)(2,1)S(1)}, bf16[2,64,2048]{2,1,0:T(8,128)(2,1)S(1)}, u32[]{:S(2)}, u32[]{:S(2)}) collective-permute-start(bf16[2,64,2048]{2,1,0:T(8,128)(2,1)S(1)} %get-tuple-element.514), channel_id=1, source_target_pairs={{0,8},{1,9},{2,10},{3,11},{4,12},{5,13},{6,14},{7,15},{8,0},{9,1},... | collective-permute-start | bytes 1572872 | tf_op jit(solution)/shard_map/ppermute | solution.py:70
  372.7 16.3 %collective-permute-start.54 = (bf16[320,1024]{1,0:T(8,128)(2,1)S(1)}, bf16[320,1024]{1,0:T(8,128)(2,1)S(1)}, u32[]{:S(2)}, u32[]{:S(2)}) collective-permute-start(bf16[320,1024]{1,0:T(8,128)(2,1)S(1)} %pad_maximum_fusion.11), channel_id=1, source_target_pairs={{0,4},{1,5},{2,6},{3,7},{4,0},{5,1},{6,2},{7,3},{8,12},{9,13},{10,... | collective-permute-start | bytes 1966088 | tf_op jit(solution)/shard_map/ppermute | solution.py:70
  391.8 22.9 %collective-permute-start.57 = (bf16[2048,1024]{1,0:T(8,128)(2,1)S(1)}, bf16[2048,1024]{1,0:T(8,128)(2,1)S(1)}, u32[]{:S(2)}, u32[]{:S(2)}) collective-permute-start(bf16[2048,1024]{1,0:T(8,128)(2,1)S(1)} %convolution_convert_fusion.1), channel_id=1, source_target_pairs={{0,1},{1,0},{2,3},{3,2},{4,5},{5,4},{6,7},{7,6},{8,9},{9,8},{10,11... | collective-permute-start | bytes 12582920 | tf_op jit(solution)/shard_map/ppermute | solution.py:70
  392.0 22.8 %collective-permute-start.58 = (bf16[320,1024]{1,0:T(8,128)(2,1)S(1)}, bf16[320,1024]{1,0:T(8,128)(2,1)S(1)}, u32[]{:S(2)}, u32[]{:S(2)}) collective-permute-start(bf16[320,1024]{1,0:T(8,128)(2,1)S(1)} %slice_bitcast_fusion.8), channel_id=1, source_target_pairs={{0,4},{1,5},{2,6},{3,7},{4,0},{5,1},{6,2},{7,3},{8,12},{9,13},{10,... | collective-permute-start | bytes 1966088 | tf_op jit(solution)/shard_map/ppermute | solution.py:70
  393.6 21.2 %collective-permute-start.56 = (bf16[160,2048]{1,0:T(8,128)(2,1)S(1)}, bf16[160,2048]{1,0:T(8,128)(2,1)S(1)}, u32[]{:S(2)}, u32[]{:S(2)}) collective-permute-start(bf16[160,2048]{1,0:T(8,128)(2,1)S(1)} %pad_maximum_fusion.12), channel_id=1, source_target_pairs={{0,2},{1,3},{2,0},{3,1},{4,6},{5,7},{6,4},{7,5},{8,10},{9,11},{10,... | collective-permute-start | bytes 1966088 | tf_op jit(solution)/shard_map/ppermute | solution.py:70
  395.1 19.6 %collective-permute-start.55 = (bf16[96,2048]{1,0:T(8,128)(2,1)S(1)}, bf16[96,2048]{1,0:T(8,128)(2,1)S(1)}, u32[]{:S(2)}, u32[]{:S(2)}) collective-permute-start(bf16[96,2048]{1,0:T(8,128)(2,1)S(1)} %pad_maximum_fusion.27), channel_id=1, source_target_pairs={{0,16},{1,17},{2,18},{3,19},{4,20},{5,21},{6,22},{7,23},{8,24},{9,... | collective-permute-start | bytes 1179656 | tf_op jit(solution)/shard_map/ppermute | solution.py:70
  436.7 29.3 %collective-permute-start.64 = (bf16[320,1024]{1,0:T(8,128)(2,1)S(1)}, bf16[320,1024]{1,0:T(8,128)(2,1)S(1)}, u32[]{:S(2)}, u32[]{:S(2)}) collective-permute-start(bf16[320,1024]{1,0:T(8,128)(2,1)S(1)} %fusion.22), channel_id=1, source_target_pairs={{0,16},{1,17},{2,18},{3,19},{4,20},{5,21},{6,22},{7,23},{8,24},{9,... | collective-permute-start | bytes 1966088 | tf_op jit(solution)/shard_map/ppermute | solution.py:70
  437.0 25.1 %collective-permute-start.66 = (bf16[2,64,2048]{2,1,0:T(8,128)(2,1)S(1)}, bf16[2,64,2048]{2,1,0:T(8,128)(2,1)S(1)}, u32[]{:S(2)}, u32[]{:S(2)}) collective-permute-start(bf16[2,64,2048]{2,1,0:T(8,128)(2,1)S(1)} %pad_maximum_fusion.25), channel_id=1, source_target_pairs={{0,2},{1,3},{2,0},{3,1},{4,6},{5,7},{6,4},{7,5},{8,10},{9,11},{10,... | collective-permute-start | bytes 1572872 | tf_op jit(solution)/shard_map/ppermute | solution.py:70
  438.5 23.6 %collective-permute-start.65 = (bf16[2,64,2048]{2,1,0:T(8,128)(2,1)S(1)}, bf16[2,64,2048]{2,1,0:T(8,128)(2,1)S(1)}, u32[]{:S(2)}, u32[]{:S(2)}) collective-permute-start(bf16[2,64,2048]{2,1,0:T(8,128)(2,1)S(1)} %get-tuple-element.508), channel_id=1, source_target_pairs={{0,8},{1,9},{2,10},{3,11},{4,12},{5,13},{6,14},{7,15},{8,0},{9,1},... | collective-permute-start | bytes 1572872 | tf_op jit(solution)/shard_map/ppermute | solution.py:70
  440.9 25.1 %collective-permute-start.63 = (bf16[512,1024]{1,0:T(8,128)(2,1)S(1)}, bf16[512,1024]{1,0:T(8,128)(2,1)S(1)}, u32[]{:S(2)}, u32[]{:S(2)}) collective-permute-start(bf16[512,1024]{1,0:T(8,128)(2,1)S(1)} %slice_bitcast_fusion.1), channel_id=1, source_target_pairs={{0,4},{1,5},{2,6},{3,7},{4,0},{5,1},{6,2},{7,3},{8,12},{9,13},{10,... | collective-permute-start | bytes 3145736 | tf_op jit(solution)/shard_map/ppermute | solution.py:70
  441.4 20.0 %collective-permute-start.67 = (bf16[4,64,2048]{2,1,0:T(8,128)(2,1)S(1)}, bf16[4,64,2048]{2,1,0:T(8,128)(2,1)S(1)}, u32[]{:S(2)}, u32[]{:S(2)}) collective-permute-start(bf16[4,64,2048]{2,1,0:T(8,128)(2,1)S(1)} %broadcast_select_fusion), channel_id=1, source_target_pairs={{0,1},{1,0},{2,3},{3,2},{4,5},{5,4},{6,7},{7,6},{8,9},{9,8},{10,11... | collective-permute-start | bytes 3145736 | tf_op jit(solution)/shard_map/ppermute | solution.py:70
  471.4 31.4 %collective-permute-start.72 = (bf16[256,1024]{1,0:T(8,128)(2,1)S(1)}, bf16[256,1024]{1,0:T(8,128)(2,1)S(1)}, u32[]{:S(2)}, u32[]{:S(2)}) collective-permute-start(bf16[256,1024]{1,0:T(8,128)(2,1)S(1)} %slice.838), channel_id=1, source_target_pairs={{0,16},{1,17},{2,18},{3,19},{4,20},{5,21},{6,22},{7,23},{8,24},{9,... | collective-permute-start | bytes 1572872 | tf_op jit(solution)/shard_map/ppermute | solution.py:70
  471.7 20.6 %collective-permute-start.71 = (bf16[512,384]{1,0:T(8,128)(2,1)S(1)}, bf16[512,384]{1,0:T(8,128)(2,1)S(1)}, u32[]{:S(2)}, u32[]{:S(2)}) collective-permute-start(bf16[512,384]{1,0:T(8,128)(2,1)S(1)} %get-tuple-element.528), channel_id=1, source_target_pairs={{0,12},{1,13},{2,14},{3,15},{4,8},{5,9},{6,10},{7,11},{8,4},{9,5},... | collective-permute-start | bytes 1179656 | tf_op jit(solution)/shard_map/ppermute | solution.py:70
  474.2 28.6 %collective-permute-start.70 = (bf16[512,384]{1,0:T(8,128)(2,1)S(1)}, bf16[512,384]{1,0:T(8,128)(2,1)S(1)}, u32[]{:S(2)}, u32[]{:S(2)}) collective-permute-start(bf16[512,384]{1,0:T(8,128)(2,1)S(1)} %get-tuple-element.529), channel_id=1, source_target_pairs={{0,8},{1,9},{2,10},{3,11},{4,12},{5,13},{6,14},{7,15},{8,0},{9,1},... | collective-permute-start | bytes 1179656 | tf_op jit(solution)/shard_map/ppermute | solution.py:70
  474.2 28.6 %collective-permute-start.69 = (bf16[512,384]{1,0:T(8,128)(2,1)S(1)}, bf16[512,384]{1,0:T(8,128)(2,1)S(1)}, u32[]{:S(2)}, u32[]{:S(2)}) collective-permute-start(bf16[512,384]{1,0:T(8,128)(2,1)S(1)} %get-tuple-element.530), channel_id=1, source_target_pairs={{0,4},{1,5},{2,6},{3,7},{4,0},{5,1},{6,2},{7,3},{8,12},{9,13},{10,... | collective-permute-start | bytes 1179656 | tf_op jit(solution)/shard_map/ppermute | solution.py:70
  502.9 16.0 %collective-permute-start.74 = (bf16[64,2048]{1,0:T(8,128)(2,1)S(1)}, bf16[64,2048]{1,0:T(8,128)(2,1)S(1)}, u32[]{:S(2)}, u32[]{:S(2)}) collective-permute-start(bf16[64,2048]{1,0:T(8,128)(2,1)S(1)} %fusion.42), channel_id=1, source_target_pairs={{0,8},{1,9},{2,10},{3,11},{4,12},{5,13},{6,14},{7,15},{8,0},{9,1},... | collective-permute-start | bytes 786440 | tf_op jit(solution)/shard_map/ppermute | solution.py:70
  503.1 15.9 %collective-permute-start.73 = (bf16[64,2048]{1,0:T(8,128)(2,1)S(1)}, bf16[64,2048]{1,0:T(8,128)(2,1)S(1)}, u32[]{:S(2)}, u32[]{:S(2)}) collective-permute-start(bf16[64,2048]{1,0:T(8,128)(2,1)S(1)} %fusion.41), channel_id=1, source_target_pairs={{0,2},{1,3},{2,0},{3,1},{4,6},{5,7},{6,4},{7,5},{8,10},{9,11},{10,... | collective-permute-start | bytes 786440 | tf_op jit(solution)/shard_map/ppermute | solution.py:70
  521.1 34.1 %all-to-all-start.3 = ((bf16[8,64,1024]{2,1,0:T(8,128)(2,1)}), bf16[8,64,1024]{2,1,0:T(8,128)(2,1)}, u32[]{:S(2)}, u32[]{:S(2)}) async-start(bf16[8,64,1024]{2,1,0:T(8,128)(2,1)} %bitcast.272), calls=%async_computation.3 | async-start | bytes 2097152 | tf_op jit(solution)/shard_map/all_to_all | solution.py:482
  525.6 23.6 %collective-permute-start.78 = (bf16[256,1024]{1,0:T(8,128)(2,1)}, bf16[256,1024]{1,0:T(8,128)(2,1)}, u32[]{:S(2)}, u32[]{:S(2)}) collective-permute-start(bf16[256,1024]{1,0:T(8,128)(2,1)} %slice.740), channel_id=1, source_target_pairs={{0,16},{1,17},{2,18},{3,19},{4,20},{5,21},{6,22},{7,23},{8,24},{9,... | collective-permute-start | bytes 1572872 | tf_op jit(solution)/shard_map/ppermute | solution.py:70
  529.7 25.6 %collective-permute-start.77 = (bf16[512,1024]{1,0:T(8,128)(2,1)S(1)}, bf16[512,1024]{1,0:T(8,128)(2,1)}, u32[]{:S(2)}, u32[]{:S(2)}) collective-permute-start(bf16[512,1024]{1,0:T(8,128)(2,1)S(1)} %slice_bitcast_fusion), channel_id=1, source_target_pairs={{0,4},{1,5},{2,6},{3,7},{4,0},{5,1},{6,2},{7,3},{8,12},{9,13},{10,... | collective-permute-start | bytes 3145736 | tf_op jit(solution)/shard_map/ppermute | solution.py:70
  558.6 33.6 %all-to-all-start.4 = ((bf16[8,64,1024]{2,1,0:T(8,128)(2,1)}), bf16[8,64,1024]{2,1,0:T(8,128)(2,1)S(1)}, u32[]{:S(2)}, u32[]{:S(2)}) async-start(bf16[8,64,1024]{2,1,0:T(8,128)(2,1)} %bitcast.93), calls=%async_computation.4 | async-start | bytes 2097152 | tf_op jit(solution)/shard_map/all_to_all | solution.py:482
  563.1 28.3 %collective-permute-start.81 = (bf16[2,80,2048]{2,1,0:T(8,128)(2,1)S(1)}, bf16[2,80,2048]{2,1,0:T(8,128)(2,1)S(1)}, u32[]{:S(2)}, u32[]{:S(2)}) collective-permute-start(bf16[2,80,2048]{2,1,0:T(8,128)(2,1)S(1)} %pad_maximum_fusion.14), channel_id=1, source_target_pairs={{0,2},{1,3},{2,0},{3,1},{4,6},{5,7},{6,4},{7,5},{8,10},{9,11},{10,... | collective-permute-start | bytes 1966088 | tf_op jit(solution)/shard_map/ppermute | solution.py:70
  566.4 25.9 %collective-permute-start.79 = (bf16[512,768]{1,0:T(8,128)(2,1)S(1)}, bf16[512,768]{1,0:T(8,128)(2,1)}, u32[]{:S(2)}, u32[]{:S(2)}) collective-permute-start(bf16[512,768]{1,0:T(8,128)(2,1)S(1)} %slice_bitcast_fusion.5), channel_id=1, source_target_pairs={{0,4},{1,5},{2,6},{3,7},{4,0},{5,1},{6,2},{7,3},{8,12},{9,13},{10,... | collective-permute-start | bytes 2359304 | tf_op jit(solution)/shard_map/ppermute | solution.py:70
  568.2 20.0 %collective-permute-start.80 = (bf16[2,48,2048]{2,1,0:T(8,128)(2,1)S(1)}, bf16[2,48,2048]{2,1,0:T(8,128)(2,1)S(1)}, u32[]{:S(2)}, u32[]{:S(2)}) collective-permute-start(bf16[2,48,2048]{2,1,0:T(8,128)(2,1)S(1)} %get-tuple-element.502), channel_id=1, source_target_pairs={{0,16},{1,17},{2,18},{3,19},{4,20},{5,21},{6,22},{7,23},{8,24},{9,... | collective-permute-start | bytes 1179656 | tf_op jit(solution)/shard_map/ppermute | solution.py:70
  595.7 17.4 %collective-permute-start.85 = (bf16[80,2048]{1,0:T(8,128)(2,1)S(1)}, bf16[80,2048]{1,0:T(8,128)(2,1)S(1)}, u32[]{:S(2)}, u32[]{:S(2)}) collective-permute-start(bf16[80,2048]{1,0:T(8,128)(2,1)S(1)} %fusion.38), channel_id=1, source_target_pairs={{0,16},{1,17},{2,18},{3,19},{4,20},{5,21},{6,22},{7,23},{8,24},{9,... | collective-permute-start | bytes 983048 | tf_op jit(solution)/shard_map/ppermute | solution.py:70
  596.1 18.8 %collective-permute-start.83 = (bf16[512,768]{1,0:T(8,128)(2,1)S(1)}, bf16[512,768]{1,0:T(8,128)(2,1)S(1)}, u32[]{:S(2)}, u32[]{:S(2)}) collective-permute-start(bf16[512,768]{1,0:T(8,128)(2,1)S(1)} %slice_bitcast_fusion.4), channel_id=1, source_target_pairs={{0,4},{1,5},{2,6},{3,7},{4,0},{5,1},{6,2},{7,3},{8,12},{9,13},{10,... | collective-permute-start | bytes 2359304 | tf_op jit(solution)/shard_map/ppermute | solution.py:70
  597.2 25.5 %collective-permute-start.82 = (bf16[512,768]{1,0:T(8,128)(2,1)S(1)}, bf16[512,768]{1,0:T(8,128)(2,1)S(1)}, u32[]{:S(2)}, u32[]{:S(2)}) collective-permute-start(bf16[512,768]{1,0:T(8,128)(2,1)S(1)} %fusion.21), channel_id=1, source_target_pairs={{0,8},{1,9},{2,10},{3,11},{4,12},{5,13},{6,14},{7,15},{8,0},{9,1},... | collective-permute-start | bytes 2359304 | tf_op jit(solution)/shard_map/ppermute | solution.py:70
  623.9 24.6 %all-to-all-start.5 = ((bf16[8,64,768]{2,1,0:T(8,128)(2,1)}), bf16[8,64,768]{2,1,0:T(8,128)(2,1)S(1)}, u32[]{:S(2)}, u32[]{:S(2)}) async-start(bf16[8,64,768]{2,1,0:T(8,128)(2,1)} %bitcast.105), calls=%async_computation.5 | async-start | bytes 1572864 | tf_op jit(solution)/shard_map/all_to_all | solution.py:482
  627.6 15.2 %collective-permute-start.86 = (bf16[64,2048]{1,0:T(8,128)(2,1)S(1)}, bf16[64,2048]{1,0:T(8,128)(2,1)S(1)}, u32[]{:S(2)}, u32[]{:S(2)}) collective-permute-start(bf16[64,2048]{1,0:T(8,128)(2,1)S(1)} %slice_bitcast_fusion.17), channel_id=1, source_target_pairs={{0,8},{1,9},{2,10},{3,11},{4,12},{5,13},{6,14},{7,15},{8,0},{9,1},... | collective-permute-start | bytes 786440 | tf_op jit(solution)/shard_map/ppermute | solution.py:70
  (150 other events, 1454.9 us)

commit v4 on v3

--- a/solution.py
+++ b/solution.py
@@ -56,7 +56,6 @@
         ]
         devices = range(count)
         self.octets = self.groups(sum(self.team) | 1)
-        self.feed_octets = self.groups(sum(self.feed_team) | 1)
         self.tile_blocks = 2 if self.team[1] < space else 1
         self.devices = devices
 
@@ -352,6 +351,90 @@
         [],
         moving(8 * rows * width),
     )(got, weight, gain)
+
+
+def spread_kernel(places, up, down, gain, out):
+    n = out.shape[2] // 2
+    for i in range(8):
+        at = pl.ds(pl.multiple_of(places[i] * n, n), n)
+        out[i, :, :n] = (up[:, at].astype(f32) * gain[...]).astype(bf16)
+        out[i, :, n:] = down[:, at]
+
+
+def spread(places, up, down, gain):
+    rows, width = up.shape
+    return call(
+        spread_kernel,
+        1,
+        3,
+        (jax.ShapeDtypeStruct((8, rows, width // 4), bf16),),
+        [],
+        moving(8 * rows * width),
+    )(places, up, down, gain)[0]
+
+
+def settle_kernel(places, kept, got, out):
+    rows = kept.shape[1]
+    for i in range(8):
+        at = pl.ds(pl.multiple_of(places[i] * rows, rows), rows)
+        out[at, :] = kept[i] if i < 4 else got[i - 4]
+
+
+def settle(places, kept, got):
+    _, rows, n = kept.shape
+    return call(
+        settle_kernel,
+        1,
+        2,
+        (jax.ShapeDtypeStruct((8 * rows, n), bf16),),
+        [],
+        moving(32 * rows * n),
+    )(places, kept, got)[0]
+
+
+def unsettle_kernel(places, block, kept, sent):
+    rows = kept.shape[1]
+    for i in range(8):
+        value = block[pl.ds(pl.multiple_of(places[i] * rows, rows), rows), :]
+        if i < 4:
+            kept[i] = value
+        else:
+            sent[i - 4] = value
+
+
+def unsettle(places, block):
+    rows, n = block.shape[0] // 8, block.shape[1]
+    half = jax.ShapeDtypeStruct((4, rows, n), bf16)
+    return call(unsettle_kernel, 1, 1, (half, half), [], moving(32 * rows * n))(places, block)
+
+
+def restore_kernel(with_gain, places, got, weight, gain, out, gain_grad):
+    n = got.shape[2]
+    total = None
+    for i in range(8):
+        at = pl.ds(pl.multiple_of(places[i] * n, n), n)
+        value = got[i].astype(f32)
+        if with_gain:
+            part = jnp.sum(value * weight[:, at].astype(f32), axis=1, keepdims=True)
+            total = part if total is None else total + part
+            value = value * gain[...]
+        out[:, at] = value
+    if with_gain:
+        gain_grad[...] = jnp.broadcast_to(total, gain_grad.shape)
+    else:
+        gain_grad[...] = jnp.zeros(gain_grad.shape, f32)
+
+
+def restore(with_gain, places, got, weight, gain):
+    rows, width = weight.shape
+    return call(
+        functools.partial(restore_kernel, with_gain),
+        1,
+        3,
+        (jax.ShapeDtypeStruct((rows, width), f32), jax.ShapeDtypeStruct((rows, 128), f32)),
+        [],
+        moving(8 * rows * width),
+    )(places, got, weight, gain)
 
 
 def attend(plan, info, real, own, other):
@@ -508,7 +591,7 @@
     swap = plan.swap
     attn = Side(plan, me, plan.team, plan.gather, plan.octets, shard, width, rows, rows * 3 // 8)
     feed = Side(
-        plan, me, plan.feed_team, plan.feed_gather, plan.feed_octets, shard, width, rows, rows // 2
+        plan, me, plan.feed_team, plan.feed_gather, None, shard, width, rows, rows // 2
     )
 
     def has(bit):
@@ -517,7 +600,6 @@
     gain_one = gain_attn.astype(f32)[:, None]
     gain_two = gain_mlp.astype(f32)[:, None]
     qkv_scaled = (w_qkv.astype(f32) * gain_one).astype(bf16)
-    up_scaled = (w_up.astype(f32) * gain_two).astype(bf16)
     n_ff = w_up.shape[1] // 8
     qkv_sent = (
         qkv_scaled.reshape(shard, 3, 2, 2, 2, 2, HEAD)
@@ -537,39 +619,53 @@
         for jj in range(2)
         for i in range(3)
     ]
-    ff_columns = [(b, 0, n_ff, b * n_ff) for b in range(8)]
-    up_sent = up_scaled.reshape(shard, 8, n_ff).transpose(1, 0, 2)
-    down_sent = w_down.reshape(shard, 8, n_ff).transpose(1, 0, 2)
+    mine = jnp.where(has(feed.team_hi), 4, 0) + jnp.where(has(feed.team_lo), 2, 0)
+    mine = mine + jnp.where(has(1), 1, 0)
+    codes = [(4 * hi, 2 * lo, c) for hi in range(2) for lo in range(2) for c in range(2)]
+
+    def placed(*axes):
+        ranked = sorted(codes, key=lambda code: [code[i] for i in axes])
+        return jnp.array([sum(code) for code in ranked], jnp.int32) ^ mine
+
+    by_lo_core_hi, by_hi_core_lo, by_core_lo_hi = placed(1, 2, 0), placed(0, 2, 1), placed(2, 1, 0)
+    by_hi_lo_core = placed(0, 1, 2)
+    feed_sent = spread(by_lo_core_hi, w_up, w_down, gain_two)
 
     qkv_sent, tokens = tied(qkv_sent, layer_input[0])
     first_rel = attn.to_rel(tokens, True)
     grad_rel = feed.to_rel(cotangent[0], False)
     qkv_block = attn.octet(qkv_sent).reshape(8 * shard, -1)
-    qkv_block, first_rel, grad_rel, up_sent, down_sent, w_out = tied(
-        qkv_block, first_rel, grad_rel, up_sent, down_sent, w_out
+    feed_lo = swap(feed_sent[4:], feed.team_lo)
+    qkv_block, first_rel, grad_rel, feed_sent, feed_lo, w_out = tied(
+        qkv_block, first_rel, grad_rel, feed_sent, feed_lo, w_out
     )
     first_near = attn.gather_one(first_rel)
     qkv_first = swap(qkv_block, attn.first)
     qkv_second = swap(qkv_block, attn.second)
-    qkv_first, qkv_second, up_sent, first_near, w_out = tied(
-        qkv_first, qkv_second, up_sent, first_near, w_out
+    feed_core = swap(jnp.stack([feed_sent[2:4], feed_lo[2:]]), 1)
+    feed_kept = jnp.stack([jnp.stack([feed_sent[:2], feed_lo[:2]]), feed_core])
+    up_send = feed_kept[:, :, 1, :, :n_ff].reshape(4, shard, n_ff)
+    qkv_first, qkv_second, feed_kept, up_send, first_near, w_out = tied(
+        qkv_first, qkv_second, feed_kept, up_send, first_near, w_out
     )
     qkv_both = swap(qkv_first, attn.second)
     first_far = attn.gather_two(*first_near)
     out_z = swap(w_out, attn.first)
-    up_block = feed.octet(up_sent).reshape(8 * shard, -1)
-    qkv_both, first_far, up_block, down_sent, out_z, w_out, grad_rel = tied(
-        qkv_both, first_far, up_block, down_sent, out_z, w_out, grad_rel
-    )
+    up_got = swap(up_send, feed.team_hi)
+    down_send = feed_kept[:, :, 1, :, n_ff:].reshape(4, shard, n_ff)
+    up_kept = feed_kept[:, :, 0, :, :n_ff].reshape(4, shard, n_ff)
+    qkv_both, first_far, up_got, up_kept, down_send, feed_kept, out_z, w_out, grad_rel = tied(
+        qkv_both, first_far, up_got, up_kept, down_send, feed_kept, out_z, w_out, grad_rel
+    )
+    down_got = swap(down_send, feed.team_hi)
     qkv_mine = attn.joined(qkv_block, qkv_first, qkv_second, qkv_both)
     qkv_other = swap(qkv_mine, 1)
     first_all = team_rows(*first_near, *first_far)
+    up_block = settle(by_hi_core_lo, up_kept, up_got)
     n_block = up_block.shape[0]
     half = n_block // 2
     up_za = swap(up_block[:half], feed.first)
     up_x = swap(up_block, feed.second)
-    grad_near = feed.gather_one(grad_rel)
-    down_block = feed.octet(down_sent).reshape(8 * shard, -1)
 
     team_device = me ^ jnp.array(plan.team_rel, jnp.int32)
     row_index = jnp.arange(rows, dtype=jnp.int32)
@@ -611,20 +707,22 @@
     pick = [(my_head ^ r) ^ core_flip for r in range(4)]
     sent = [lax.dynamic_index_in_dim(stack, pick[r], 0, keepdims=False) for r in range(4)]
     out_pair = jnp.stack([w_out, out_z])
-    sent, up_za, up_x, grad_near, up_block, up_half, down_block, out_z, w_out, out_pair = tied(
-        sent, up_za, up_x, grad_near, up_block, up_block[half:], down_block, out_z, w_out, out_pair
+    sent, up_za, up_x, grad_rel, up_block, up_half, down_got, out_z, w_out, out_pair = tied(
+        sent, up_za, up_x, grad_rel, up_block, up_block[half:], down_got, out_z, w_out, out_pair
     )
     got = [swap(sent[r], plan.head_rel[r]) for r in range(1, 4)]
     up_zb = swap(up_half, feed.first)
     out_x = swap(out_pair, attn.second)
     cut_z = [0, n_block // 2, n_block * 3 // 4, n_block]
-    got, up_za, up_zb, down_block, grad_near, out_x, down_first = tied(
-        got, up_za, up_zb, down_block, grad_near, out_x, down_block[: cut_z[1]]
+    down_kept = feed_kept[:, :, 0, :, n_ff:].reshape(4, shard, n_ff)
+    down_block = settle(by_hi_core_lo, down_kept, down_got)
+    got, up_za, up_zb, down_block, grad_rel, out_x, down_first = tied(
+        got, up_za, up_zb, down_block, grad_rel, out_x, down_block[: cut_z[1]]
     )
     own = jnp.stack([sent[0]] + got).reshape(16, rows, 3 * HEAD)
     down_z = [swap(down_first, feed.first)]
     up_both = [swap(up_za, feed.second), swap(up_zb, feed.second)]
-    grad_far = feed.gather_two(*grad_near)
+    grad_near = feed.gather_one(grad_rel)
     shared = own[:, :, HEAD:]
     other = jnp.stack([swap(shared, rel) for rel in plan.part_rel[1:]])
 
@@ -646,8 +744,8 @@
 
     attended, attended_t, log_total, keys, values = attend(plan, info, frame_real, own, other)
     w_team = jnp.stack([w_out, out_x[0], out_z, out_x[1]])
-    attended, down_z, up_both, grad_far, w_team, down_block, up_x, up_za, up_zb, up_block = tied(
-        attended, down_z, up_both, grad_far, w_team, down_block, up_x, up_za, up_zb, up_block
+    attended, down_z, up_both, grad_near, w_team, down_block, up_x, up_za, up_zb, up_block = tied(
+        attended, down_z, up_both, grad_near, w_team, down_block, up_x, up_za, up_zb, up_block
     )
     w_got = swap(w_team, plan.parts[-1])
     attended = attended.reshape(4, 4 * rows, HEAD)
@@ -662,22 +760,25 @@
             jnp.concatenate([w_team, w_got], axis=1),
         )
     w_team = w_team.reshape(4 * HEAD, width)
-    heads_got, w_team, down_z, grad_far, down_block, up_mine = tied(
-        heads_got, w_team, down_z, grad_far, down_block, up_mine
+    heads_got, w_team, down_z, grad_near, down_block, up_mine = tied(
+        heads_got, w_team, down_z, grad_near, down_block, up_mine
     )
     attended_team = jnp.concatenate([attended[0]] + heads_got, axis=1)
     branch = matmul(attended_team, w_team).astype(bf16)
     branch_near = attn.scatter_one(branch)
     cut_x = n_block * 5 // 8
     down_x = [swap(down_block[:cut_x], feed.second)]
+    grad_far = feed.gather_two(*grad_near)
+    branch_near, down_x, up_mine, down_z, grad_far, down_block = tied(
+        branch_near, down_x, up_mine, down_z, grad_far, down_block
+    )
+    middle = attn.scatter_two(*branch_near)
+    down_x += [swap(down_block[cut_x:], feed.second)]
     up_other = swap(up_mine, 1)
     grad_all = team_rows(*grad_near, *grad_far)
-    branch_near, down_x, up_other, down_z, grad_all, down_block = tied(
-        branch_near, down_x, up_other, down_z, grad_all, down_block
-    )
-    middle = attn.scatter_two(*branch_near)
-    down_x += [swap(down_block[cut_x:], feed.second)]
-    middle, down_x, down_z, down_block = tied(middle, down_x, down_z, down_block)
+    middle, down_x, down_z, down_block, up_other, grad_all = tied(
+        middle, down_x, down_z, down_block, up_other, grad_all
+    )
     middle = inputs + middle
     second_near = feed.gather_one(feed.to_rel(middle, True))
     down_z += [swap(down_block[cut_z[2] :], feed.first)]
@@ -716,29 +817,32 @@
     down_sum = feed.first_sum(down_mine_grad, down_swapped)
     c1, c2, c3 = n_block * 3 // 8, n_block * 3 // 4, n_block * 3 // 8
     down_x3 = [swap(down_sum[3][:c1], feed.second)]
-    second_back, down_x3, down_sum = tied(second_back, down_x3, down_sum)
+    out_parts = (
+        matmul(act_mine, down_mine, ((1,), (1,))) + matmul(act_other, down_other, ((1,), (1,)))
+    ).astype(bf16)
+    second_back, down_x3, down_sum, out_parts, hid_other = tied(
+        second_back, down_x3, down_sum, out_parts, hid_other
+    )
     grad_second = feed.scatter_two(*second_back)
     z1, z2 = n_block * 3 // 16, n_block * 3 // 8
     down_z1 = [swap(added(down_sum[1][:z1], down_x3[0][:z1]), feed.first)]
     down_x3 += [swap(down_sum[3][c1:c2], feed.second)]
-    grad_second, down_z1, down_x3, down_sum, act_mine, act_other = tied(
-        grad_second, down_z1, down_x3, down_sum, act_mine, act_other
+    up_other_grad = matmul(second_all, hid_other, ((0,), (0,))).astype(bf16)
+    down_x32 = jnp.concatenate([down_sum[3][c2:], down_sum[2][:c3]])
+    grad_second, down_z1, down_x3, down_sum, up_other_grad, down_x32, hid_mine = tied(
+        grad_second, down_z1, down_x3, down_sum, up_other_grad, down_x32, hid_mine
     )
     grad_second = feed.from_rel(grad_second)
     grad_middle = grad_out + layer_norm_back(grad_second, normed_two, scale_two)
     middle_near = attn.gather_one(grad_middle.astype(bf16))
-    down_x32 = swap(jnp.concatenate([down_sum[3][c2:], down_sum[2][:c3]]), feed.second)
-    out_parts = (
-        matmul(act_mine, down_mine, ((1,), (1,))) + matmul(act_other, down_other, ((1,), (1,)))
-    ).astype(bf16)
-    middle_near, out_parts, hid_other, hid_mine, down_x32, down_sum, down_x3 = tied(
-        middle_near, out_parts, hid_other, hid_mine, down_x32, down_sum, down_x3
+    down_x32 = swap(down_x32, feed.second)
+    up_swapped = swap(up_other_grad, 1)
+    middle_near, down_x32, up_swapped, hid_mine, down_sum, down_x3, down_x2 = tied(
+        middle_near, down_x32, up_swapped, hid_mine, down_sum, down_x3, down_sum[2][c3:]
     )
     middle_far = attn.gather_two(*middle_near)
     down_x3 = jnp.concatenate([*down_x3, down_x32[: n_block - c2]])
-    down_x2 = [down_x32[n_block - c2 :], swap(down_sum[2][c3:], feed.second)]
-    up_other_grad = matmul(second_all, hid_other, ((0,), (0,))).astype(bf16)
-    up_swapped = swap(up_other_grad, 1)
+    down_x2 = [down_x32[n_block - c2 :], swap(down_x2, feed.second)]
     up_mine_grad = matmul(second_all, hid_mine, ((0,), (0,))).astype(bf16)
     down_z1b = added(down_sum[1][z1:z2], down_x3[z1:z2])
     middle_far, up_swapped, up_mine_grad, down_x2, down_x3, down_sum, down_z1b = tied(
@@ -787,8 +891,9 @@
     got = [swap(triple[r], plan.head_rel[r]) for r in range(1, 4)]
     up_z1a = swap(up_z1a, feed.first)
     down_done = added(down_sum[0], jnp.concatenate(down_x2), jnp.concatenate(down_z1))
-    got, up_z1a, up_z1, down_done, up_sum, out_grad, out_near = tied(
-        got, up_z1a, up_z1, down_done, up_sum, out_grad, out_near
+    down_rows, down_rows_hi = unsettle(by_hi_lo_core, down_done)
+    got, up_z1a, up_z1, down_rows, down_rows_hi, up_sum, out_grad, out_near = tied(
+        got, up_z1a, up_z1, down_rows, down_rows_hi, up_sum, out_grad, out_near
     )
     places = (my_head ^ jnp.arange(4, dtype=jnp.int32)) ^ core_flip
     mixed_grad = turn_back(places, cosine, sine, [triple[0]] + got)
@@ -797,36 +902,49 @@
     out_sum = feed.scatter_two(*out_near)
     kept, sent = out_grad.reshape(2, 2, -1, width)[:, 0], out_grad.reshape(2, 2, -1, width)[:, 1]
     out_grad = added(kept, swap(sent, attn.second))
-    qkv_other_grad, mixed_grad_mine, up_sum, up_z1, down_done, out_sum, out_grad, up_z1b = tied(
-        qkv_other_grad, mixed_grad_mine, up_sum, up_z1, down_done, out_sum, out_grad, up_z1[half:]
+    down_rows = jnp.stack([down_rows, swap(down_rows_hi, feed.team_hi)]).reshape(2, 2, 2, shard, n_ff)
+    qkv_other_grad, mixed_grad_mine, up_sum, down_rows, out_sum, out_grad, up_z1b = tied(
+        qkv_other_grad, mixed_grad_mine, up_sum, down_rows, out_sum, out_grad, up_z1[half:]
     )
     qkv_swapped = swap(qkv_other_grad, 1)
     up_x2 = swap(up_sum[2], feed.second)
     up_z1b = swap(up_z1b, feed.first)
-    down_got = feed.octet(down_done)
+    down_rows_lo = swap(down_rows[:, 1], feed.team_lo)
     qkv_mine_grad = matmul(first_all, mixed_grad_mine, ((0,), (0,))).astype(bf16)
     first_parts = matmul(mixed_grad_mine, qkv_mine, ((1,), (1,))) + matmul(
         mixed_grad_other, qkv_other, ((1,), (1,))
     )
     qkv_sum = attn.first_sum(qkv_mine_grad, qkv_swapped)
-    qkv_sum, first_parts, up_x2, up_sum, up_z1b, down_got, out_grad = tied(
-        qkv_sum, first_parts.astype(bf16), up_x2, up_sum, up_z1b, down_got, out_grad
+    qkv_sum, first_parts, up_x2, up_sum, up_z1b, down_rows, out_grad = tied(
+        qkv_sum,
+        first_parts.astype(bf16),
+        up_x2,
+        up_sum,
+        up_z1b,
+        jnp.stack([down_rows[:, 0], down_rows_lo]),
+        out_grad,
     )
     qkv_x3 = swap(qkv_sum[3], attn.second)
     first_back = attn.scatter_one(first_parts)
     up_done = added(up_sum[0], up_x2, jnp.concatenate([up_z1a, up_z1b]))
-    grad_down = down_got.transpose(1, 0, 2).reshape(shard, 8 * n_ff).astype(f32)
-    up_got = feed.octet(up_done)
-    qkv_x3, first_back, up_got, qkv_sum, grad_down = tied(
-        qkv_x3, first_back, up_got, qkv_sum, grad_down
+    down_rows = jnp.stack([down_rows[:, :, 0], swap(down_rows[:, :, 1], 1)])
+    up_rows, up_rows_hi = unsettle(by_hi_lo_core, up_done)
+    up_rows = jnp.stack([up_rows, swap(up_rows_hi, feed.team_hi)]).reshape(2, 2, 2, shard, n_ff)
+    qkv_x3, first_back, up_rows, qkv_sum, down_rows, up_send = tied(
+        qkv_x3, first_back, up_rows, qkv_sum, down_rows, up_rows[:, 1]
     )
     qkv_z1 = swap(added(qkv_sum[1], qkv_x3), attn.first)
     qkv_x2 = swap(qkv_sum[2], attn.second)
     first_rows = attn.scatter_two(*first_back)
     output = (middle + feed.from_rel(out_sum)).astype(bf16)
-    grad_up, grad_gain_two = deliver(ff_columns, up_got, w_up, gain_two)
-    qkv_z1, qkv_x2, first_rows, out_grad, output, grad_up = tied(
-        qkv_z1, qkv_x2, first_rows, out_grad, output, grad_up
+    grad_down, _ = restore(False, by_core_lo_hi, down_rows.reshape(8, shard, n_ff), w_down, gain_two)
+    up_rows = jnp.stack([up_rows[:, 0], swap(up_send, feed.team_lo)])
+    qkv_z1, qkv_x2, first_rows, out_grad, output, up_rows, grad_down = tied(
+        qkv_z1, qkv_x2, first_rows, out_grad, output, up_rows, grad_down
+    )
+    up_rows = jnp.stack([up_rows[:, :, 0], swap(up_rows[:, :, 1], 1)])
+    grad_up, grad_gain_two = restore(
+        True, by_core_lo_hi, up_rows.reshape(8, shard, n_ff), w_up, gain_two
     )
     qkv_got = attn.octet(added(qkv_sum[0], qkv_x2, qkv_z1))
     grad_first = attn.from_rel(first_rows)

time: 658 us -> 643 us (0.977)
  local copies, waits for them, and re-layouts: 61.7 us -> 39.7 us
  waiting for transfers between devices: 311 us -> 328 us
    ppermute x87 -> x97, waiting for transfers between devices: 291 us -> 326 us  [swap(): return lax.ppermute(value, AXES, [(d, d ^ mask) for d in self.devices])]
    all_to_all x6 -> x2, waiting for transfers between devices: 20.4 us -> 1.78 us  [octet(): return lax.all_to_all(value, AXES, 0, 0, axis_index_groups=self.groups)]
    all_to_all x6 -> x2, starting transfers between devices: 27.4 us -> 10.1 us  [octet(): return lax.all_to_all(value, AXES, 0, 0, axis_index_groups=self.groups)]
    ppermute x87 -> x97, starting transfers between devices: 81.7 us -> 92.5 us  [swap(): return lax.ppermute(value, AXES, [(d, d ^ mask) for d in self.devices])]
    pallas_call x0 -> x7, Pallas kernels: none -> 7.64 us  [the longest x2 4.38 us: restore(): call(functools.partial(restore_kernel, with_gain), 1, 3, (jax.ShapeDtypeS...]
    unnamed x257 -> x243, local copies, waits for them, and re-layouts: 28 us -> 21.9 us
  transfers between devices with their start and end apart: 93 -> 99, of which waited for: 40 -> 47; matrix products, arithmetic and copies ran while one was open for 20% -> 18% of each run, Pallas kernels for 7% -> 7%
where the time goes in v4:
time: 643 us; the launch traced here: 632 us
  waiting for transfers between devices  328 us (51%)
  starting transfers between devices  103 us (16%)
  matrix products  67.8 us (11%)
  other arithmetic  45.6 us (7%)
  Pallas kernels  44 us (7%)
  local copies, waits for them, and re-layouts  39.7 us (6%)
    ppermute x97, waiting for transfers between devices, swap(): return lax.ppermute(value, AXES, [(d, d ^ mask) for d in self.devices])  326 us
    ppermute x97, starting transfers between devices, swap(): return lax.ppermute(value, AXES, [(d, d ^ mask) for d in self.devices])  92.5 us
    dot_general x21, matrix products, matmul(): lax.dot_general(left, right, (dims, ((), ())), preferred_element_type=f32)  67.8 us
    unnamed x243, local copies, waits for them, and re-layouts  21.9 us
    convert_element_type x20, other arithmetic, added(): return sum((v.astype(f32) for v in values)).astype(bf16)  17.6 us
    pallas_call x1, Pallas kernels, attend_back(): call(functools.partial(attend_back_kernel, plan), 2, 6, (shape((blocks, B...  15.4 us
    pallas_call x1, Pallas kernels, attend(): call(functools.partial(attend_kernel, plan), 2, 2, (shape((blocks, BLOCK,...  13.4 us
  transfers between devices with their start and end apart: 99, of which 47 were waited for; matrix products, arithmetic and copies ran while one was open for 18% of the time, Pallas kernels for 7%

profile of v4, /device:TPU:0, one launch (start us, length us, event | category | flops | bytes accessed | tf_op | source)
XLA Modules:
  0.0 631.6 jit_solution(198421650524419916)
XLA Ops:
  5.6 6.3 all-to-all-start
  21.4 25.3 %collective-permute-done = bf16[4,64,2048]{2,1,0:T(8,128)(2,1)} collective-permute-done((bf16[4,64,2048]{2,1,0:T(8,128)(2,1)}, bf16[4,64,2048]{2,1,0:T(8,128)(2,1)}, u32[]{:S(2)}, u32[]{:S(2)}) %collective-permute-start) | collective-permute-done | bytes 1048608 | tf_op jit(solution)/shard_map/ppermute | solution.py:69
  51.6 4.2 collective-permute-start.5
  58.3 16.9 %collective-permute-done.5.b_hi = bf16[80,2048]{1,0:T(8,128)(2,1)S(1)} collective-permute-done((bf16[80,2048]{1,0:T(8,128)(2,1)S(1)}, bf16[80,2048]{1,0:T(8,128)(2,1)S(1)}, u32[]{:S(2)}, u32[]{:S(2)}) %collective-permute-start.5) | collective-permute-done | bytes 327712 | tf_op jit(solution)/shard_map/ppermute | solution.py:69
  76.7 2.8 collective-permute-start.10
  86.1 2.9 collective-permute-done.10
  89.0 12.0 %collective-permute-done.7.a_far = bf16[96,2048]{1,0:T(8,128)(2,1)S(1)} collective-permute-done((bf16[96,2048]{1,0:T(8,128)(2,1)S(1)}, bf16[96,2048]{1,0:T(8,128)(2,1)S(1)}, u32[]{:S(2)}, u32[]{:S(2)}) %collective-permute-start.7) | collective-permute-done | bytes 393248 | tf_op jit(solution)/shard_map/ppermute | solution.py:69
  101.0 4.3 collective-permute-done.9.got
  113.1 4.5 fusion.118
  120.8 3.7 fusion.117
  129.8 7.8 %collective-permute-done.12 = bf16[256,1024]{1,0:T(8,128)(2,1)S(1)} collective-permute-done((bf16[256,1024]{1,0:T(8,128)(2,1)S(1)}, bf16[256,1024]{1,0:T(8,128)(2,1)S(1)}, u32[]{:S(2)}, u32[]{:S(2)}) %collective-permute-start.12) | collective-permute-done | bytes 524320 | tf_op jit(solution)/shard_map/ppermute | solution.py:69
  146.7 15.3 %collective-permute-done.15 = bf16[512,384]{1,0:T(8,128)(2,1)} collective-permute-done((bf16[512,384]{1,0:T(8,128)(2,1)}, bf16[512,384]{1,0:T(8,128)(2,1)}, u32[]{:S(2)}, u32[]{:S(2)}) %collective-permute-start.15) | collective-permute-done | bytes 393248 | tf_op jit(solution)/shard_map/ppermute | solution.py:69
  164.3 6.9 %collective-permute-done.17 = bf16[512,384]{1,0:T(8,128)(2,1)} collective-permute-done((bf16[512,384]{1,0:T(8,128)(2,1)}, bf16[512,384]{1,0:T(8,128)(2,1)}, u32[]{:S(2)}, u32[]{:S(2)}) %collective-permute-start.17) | collective-permute-done | bytes 393248 | tf_op jit(solution)/shard_map/ppermute | solution.py:69
  173.9 2.7 collective-permute-start.21
  181.4 13.4 %shard_map.239 = (bf16[16,128,128]{2,1,0:T(8,128)(2,1)S(1)}, f32[8,128,256]{2,1,0:T(8,128)S(1)}, f32[8,1,256]{2,1,0:T(1,128)S(1)}, bf16[4096,128]{1,0:T(8,128)(2,1)S(1)}, bf16[4096,128]{1,0:T(8,128)(2,1)S(1)}) custom-call(s32[56]{0:T(128)S(1)} %concatenate.187.info, s32[8]{0:T(128)S(1)} %copy-done.32, bf16[16,128,384]{2,1,0:T(8,128)(2,1)S(1)} %bitcast.285, ...), custom_call_target="tpu_custom_call" | custom-call | flops 4294967296 | bytes 8388608 | tf_op jit(solution)/shard_map/pallas_call | solution.py:445
  194.9 5.6 collective-permute-done.21
  207.6 4.3 collective-permute-done.28
  212.4 7.4 %collective-permute-done.30 = bf16[128,1024]{1,0:T(8,128)(2,1)S(1)} collective-permute-done((bf16[128,1024]{1,0:T(8,128)(2,1)S(1)}, bf16[128,1024]{1,0:T(8,128)(2,1)S(1)}, u32[]{:S(2)}, u32[]{:S(2)}) %collective-permute-start.30) | collective-permute-done | bytes 262176 | tf_op jit(solution)/shard_map/ppermute | solution.py:69
  226.6 16.1 %collective-permute-done.31 = bf16[2,48,2048]{2,1,0:T(8,128)(2,1)S(1)} collective-permute-done((bf16[2,48,2048]{2,1,0:T(8,128)(2,1)S(1)}, bf16[2,48,2048]{2,1,0:T(8,128)(2,1)S(1)}, u32[]{:S(2)}, u32[]{:S(2)}) %collective-permute-start.31) | collective-permute-done | bytes 393248 | tf_op jit(solution)/shard_map/ppermute | solution.py:69
  242.7 3.8 collective-permute-done.32
  249.2 5.0 collective-permute-done.36
  254.3 11.0 %collective-permute-done.37 = bf16[80,2048]{1,0:T(8,128)(2,1)S(1)} collective-permute-done((bf16[80,2048]{1,0:T(8,128)(2,1)S(1)}, bf16[80,2048]{1,0:T(8,128)(2,1)S(1)}, u32[]{:S(2)}, u32[]{:S(2)}) %collective-permute-start.37) | collective-permute-done | bytes 327712 | tf_op jit(solution)/shard_map/ppermute | solution.py:69
  267.5 2.8 collective-permute-start.41
  270.9 9.0 %collective-permute-done.43 = bf16[128,1024]{1,0:T(8,128)(2,1)S(1)} collective-permute-done((bf16[128,1024]{1,0:T(8,128)(2,1)S(1)}, bf16[128,1024]{1,0:T(8,128)(2,1)S(1)}, u32[]{:S(2)}, u32[]{:S(2)}) %collective-permute-start.43) | collective-permute-done | bytes 262176 | tf_op jit(solution)/shard_map/ppermute | solution.py:69
  284.4 10.2 %collective-permute-done.45.b_far = bf16[128,2048]{1,0:T(8,128)(2,1)S(1)} collective-permute-done((bf16[128,2048]{1,0:T(8,128)(2,1)S(1)}, bf16[128,2048]{1,0:T(8,128)(2,1)S(1)}, u32[]{:S(2)}, u32[]{:S(2)}) %collective-permute-start.45) | collective-permute-done | bytes 524320 | tf_op jit(solution)/shard_map/ppermute | solution.py:69
  296.5 2.9 collective-permute-done.46
  301.7 4.0 multiply_convert_fusion.1
  305.7 4.4 convolution_convert_fusion.3
  310.1 4.5 multiply_convert_fusion
  316.8 4.4 convolution_convert_fusion.2
  321.2 3.4 fusion.6
  327.1 4.4 fusion.120
  331.5 3.8 fusion.13
  335.3 2.4 add_convert_fusion.5
  339.5 4.4 add_convert_fusion.1
  345.5 5.9 add_convert_fusion.4
  351.5 3.8 collective-permute-done.51
  360.0 2.4 convolution_convert_fusion.1
  362.5 5.6 collective-permute-done.53
  376.7 5.3 collective-permute-done.56.a_lo
  382.0 9.3 %collective-permute-done.57.b_hi = bf16[80,2048]{1,0:T(8,128)(2,1)S(1)} collective-permute-done((bf16[80,2048]{1,0:T(8,128)(2,1)S(1)}, bf16[80,2048]{1,0:T(8,128)(2,1)S(1)}, u32[]{:S(2)}, u32[]{:S(2)}) %collective-permute-start.57) | collective-permute-done | bytes 327712 | tf_op jit(solution)/shard_map/ppermute | solution.py:69
  395.2 2.4 convolution_convert_fusion
  397.6 15.0 %collective-permute-done.60.a_far = bf16[96,2048]{1,0:T(8,128)(2,1)S(1)} collective-permute-done((bf16[96,2048]{1,0:T(8,128)(2,1)S(1)}, bf16[96,2048]{1,0:T(8,128)(2,1)S(1)}, u32[]{:S(2)}, u32[]{:S(2)}) %collective-permute-start.60) | collective-permute-done | bytes 393248 | tf_op jit(solution)/shard_map/ppermute | solution.py:69
  416.9 2.9 collective-permute-start.64
  425.9 2.5 collective-permute-done.64
  428.4 3.4 collective-permute-done.66
  435.0 3.0 collective-permute-start.69
  440.4 15.4 %shard_map.244 = (bf16[16,128,128]{2,1,0:T(8,128)(2,1)S(1)}, bf16[16,128,256]{2,1,0:T(8,128)(2,1)S(1)}, bf16[1,16,128,256]{3,2,1,0:T(8,128)(2,1)}) custom-call(s32[56]{0:T(128)S(1)} %concatenate.187.info, s32[8]{0:T(128)S(1)} %copy-done.32, bf16[16,128,384]{2,1,0:T(8,128)(2,1)S(1)} %bitcast.286, bf16[4096,128]{1,0:T(8,128)(2,1)S(1)} %copy-done.36, ...), custom_call_target="tpu_custom_call" | custom-call | flops 10737418240 | bytes 8388608 | tf_op jit(solution)/shard_map/pallas_call | solution.py:467
  458.4 4.3 collective-permute-done.68
  474.7 14.2 %collective-permute-done.75.refs_3_ = bf16[512,384]{1,0:T(8,128)(2,1)S(1)} collective-permute-done((bf16[512,384]{1,0:T(8,128)(2,1)S(1)}, bf16[512,384]{1,0:T(8,128)(2,1)S(1)}, u32[]{:S(2)}, u32[]{:S(2)}) %collective-permute-start.75) | collective-permute-done | bytes 393248 | tf_op jit(solution)/shard_map/ppermute | solution.py:69
  488.8 11.3 %collective-permute-done.74.refs_2_ = bf16[512,384]{1,0:T(8,128)(2,1)S(1)} collective-permute-done((bf16[512,384]{1,0:T(8,128)(2,1)S(1)}, bf16[512,384]{1,0:T(8,128)(2,1)S(1)}, u32[]{:S(2)}, u32[]{:S(2)}) %collective-permute-start.74) | collective-permute-done | bytes 393248 | tf_op jit(solution)/shard_map/ppermute | solution.py:69
  507.5 3.7 fusion.34
  511.6 7.4 %collective-permute-done.77 = bf16[4,64,1024]{2,1,0:T(8,128)(2,1)S(1)} collective-permute-done((bf16[4,64,1024]{2,1,0:T(8,128)(2,1)S(1)}, bf16[4,64,1024]{2,1,0:T(8,128)(2,1)S(1)}, u32[]{:S(2)}, u32[]{:S(2)}) %collective-permute-start.77) | collective-permute-done | bytes 524320 | tf_op jit(solution)/shard_map/ppermute | solution.py:69
  522.4 3.7 add_convert_fusion.3
  527.1 6.9 %collective-permute-done.84 = bf16[2,2,64,1024]{3,2,0,1:T(8,128)(2,1)S(1)} collective-permute-done((bf16[2,2,64,1024]{3,2,0,1:T(8,128)(2,1)S(1)}, bf16[2,2,64,1024]{3,2,0,1:T(8,128)(2,1)S(1)}, u32[]{:S(2)}, u32[]{:S(2)}) %collective-permute-start.84) | collective-permute-done | bytes 524320 | tf_op jit(solution)/shard_map/ppermute | solution.py:69
  536.0 7.5 %collective-permute-done.83 = bf16[256,1024]{1,0:T(8,128)(2,1)S(1)} collective-permute-done((bf16[256,1024]{1,0:T(8,128)(2,1)S(1)}, bf16[256,1024]{1,0:T(8,128)(2,1)S(1)}, u32[]{:S(2)}, u32[]{:S(2)}) %collective-permute-start.83) | collective-permute-done | bytes 524320 | tf_op jit(solution)/shard_map/ppermute | solution.py:69
  543.5 3.0 collective-permute-done.82
  552.8 15.5 %collective-permute-done.88 = bf16[4,64,1024]{2,1,0:T(8,128)(2,1)S(1)} collective-permute-done((bf16[4,64,1024]{2,1,0:T(8,128)(2,1)S(1)}, bf16[4,64,1024]{2,1,0:T(8,128)(2,1)S(1)}, u32[]{:S(2)}, u32[]{:S(2)}) %collective-permute-start.88) | collective-permute-done | bytes 524320 | tf_op jit(solution)/shard_map/ppermute | solution.py:69
  568.6 3.6 collective-permute-done.86
  576.2 3.2 collective-permute-start.90
  581.5 8.4 %collective-permute-done.93 = bf16[80,2048]{1,0:T(8,128)(2,1)S(1)} collective-permute-done((bf16[80,2048]{1,0:T(8,128)(2,1)S(1)}, bf16[80,2048]{1,0:T(8,128)(2,1)S(1)}, u32[]{:S(2)}, u32[]{:S(2)}) %collective-permute-start.93) | collective-permute-done | bytes 327712 | tf_op jit(solution)/shard_map/ppermute | solution.py:69
  593.5 9.1 %collective-permute-done.90 = bf16[512,768]{1,0:T(8,128)(2,1)S(1)} collective-permute-done((bf16[512,768]{1,0:T(8,128)(2,1)S(1)}, bf16[512,768]{1,0:T(8,128)(2,1)S(1)}, u32[]{:S(2)}, u32[]{:S(2)}) %collective-permute-start.90) | collective-permute-done | bytes 786464 | tf_op jit(solution)/shard_map/ppermute | solution.py:69
  603.7 3.8 all-to-all-start.1
  611.9 10.8 %collective-permute-done.95 = bf16[64,2048]{1,0:T(8,128)(2,1)S(1)} collective-permute-done((bf16[64,2048]{1,0:T(8,128)(2,1)S(1)}, bf16[64,2048]{1,0:T(8,128)(2,1)S(1)}, u32[]{:S(2)}, u32[]{:S(2)}) %collective-permute-start.95) | collective-permute-done | bytes 262176 | tf_op jit(solution)/shard_map/ppermute | solution.py:69
  (616 shorter events, 191.5 us)
Async XLA Ops:
  5.6 41.1 %all-to-all-start = ((bf16[8,64,768]{2,1,0:T(8,128)(2,1)}), bf16[8,64,768]{2,1,0:T(8,128)(2,1)}, u32[]{:S(2)}, u32[]{:S(2)}) async-start(bf16[8,64,768]{2,1,0:T(8,128)(2,1)} %reshape.466), calls=%async_computation | async-start | bytes 1572864 | tf_op jit(solution)/shard_map/all_to_all | solution.py:565
  16.9 29.8 %collective-permute-start = (bf16[4,64,2048]{2,1,0:T(8,128)(2,1)}, bf16[4,64,2048]{2,1,0:T(8,128)(2,1)}, u32[]{:S(2)}, u32[]{:S(2)}) collective-permute-start(bf16[4,64,2048]{2,1,0:T(8,128)(2,1)} %slice.849), channel_id=1, source_target_pairs={{0,2},{1,3},{2,0},{3,1},{4,6},{5,7},{6,4},{7,5},{8,10},{9,11},{10,... | collective-permute-start | bytes 3145736 | tf_op jit(solution)/shard_map/ppermute | solution.py:69
  48.3 26.9 %collective-permute-start.2 = (bf16[512,768]{1,0:T(8,128)(2,1)}, bf16[512,768]{1,0:T(8,128)(2,1)S(1)}, u32[]{:S(2)}, u32[]{:S(2)}) collective-permute-start(bf16[512,768]{1,0:T(8,128)(2,1)} %bitcast.2), channel_id=1, source_target_pairs={{0,4},{1,5},{2,6},{3,7},{4,0},{5,1},{6,2},{7,3},{8,12},{9,13},{10,... | collective-permute-start | bytes 2359304 | tf_op jit(solution)/shard_map/ppermute | solution.py:69
  49.8 26.8 %collective-permute-start.1 = (bf16[512,768]{1,0:T(8,128)(2,1)}, bf16[512,768]{1,0:T(8,128)(2,1)S(1)}, u32[]{:S(2)}, u32[]{:S(2)}) collective-permute-start(bf16[512,768]{1,0:T(8,128)(2,1)} %bitcast.2), channel_id=1, source_target_pairs={{0,8},{1,9},{2,10},{3,11},{4,12},{5,13},{6,14},{7,15},{8,0},{9,1},... | collective-permute-start | bytes 2359304 | tf_op jit(solution)/shard_map/ppermute | solution.py:69
  51.6 23.5 %collective-permute-start.5 = (bf16[80,2048]{1,0:T(8,128)(2,1)S(1)}, bf16[80,2048]{1,0:T(8,128)(2,1)S(1)}, u32[]{:S(2)}, u32[]{:S(2)}) collective-permute-start(bf16[80,2048]{1,0:T(8,128)(2,1)S(1)} %slice.663.b), channel_id=1, source_target_pairs={{0,16},{1,17},{2,18},{3,19},{4,20},{5,21},{6,22},{7,23},{8,24},{9,... | collective-permute-start | bytes 983048 | tf_op jit(solution)/shard_map/ppermute | solution.py:69
  79.5 25.8 %collective-permute-start.6 = (bf16[512,768]{1,0:T(8,128)(2,1)S(1)}, bf16[512,768]{1,0:T(8,128)(2,1)S(1)}, u32[]{:S(2)}, u32[]{:S(2)}) collective-permute-start(bf16[512,768]{1,0:T(8,128)(2,1)S(1)} %collective-permute-done.1), channel_id=1, source_target_pairs={{0,4},{1,5},{2,6},{3,7},{4,0},{5,1},{6,2},{7,3},{8,12},{9,13},{10,... | collective-permute-start | bytes 2359304 | tf_op jit(solution)/shard_map/ppermute | solution.py:69
  80.1 25.2 %collective-permute-start.8 = (bf16[160,2048]{1,0:T(8,128)(2,1)S(1)}, bf16[160,2048]{1,0:T(8,128)(2,1)S(1)}, u32[]{:S(2)}, u32[]{:S(2)}) collective-permute-start(bf16[160,2048]{1,0:T(8,128)(2,1)S(1)} %pad_maximum_fusion.16), channel_id=1, source_target_pairs={{0,2},{1,3},{2,0},{3,1},{4,6},{5,7},{6,4},{7,5},{8,10},{9,11},{10,... | collective-permute-start | bytes 1966088 | tf_op jit(solution)/shard_map/ppermute | solution.py:69
  81.6 19.4 %collective-permute-start.7 = (bf16[96,2048]{1,0:T(8,128)(2,1)S(1)}, bf16[96,2048]{1,0:T(8,128)(2,1)S(1)}, u32[]{:S(2)}, u32[]{:S(2)}) collective-permute-start(bf16[96,2048]{1,0:T(8,128)(2,1)S(1)} %pad_maximum_fusion.34), channel_id=1, source_target_pairs={{0,16},{1,17},{2,18},{3,19},{4,20},{5,21},{6,22},{7,23},{8,24},{9,... | collective-permute-start | bytes 1179656 | tf_op jit(solution)/shard_map/ppermute | solution.py:69
  83.3 22.0 %collective-permute-start.9 = (bf16[4,64,1024]{2,1,0:T(8,128)(2,1)S(1)}, bf16[4,64,1024]{2,1,0:T(8,128)(2,1)S(1)}, u32[]{:S(2)}, u32[]{:S(2)}) collective-permute-start(bf16[4,64,1024]{2,1,0:T(8,128)(2,1)S(1)} %bitcast.338), channel_id=1, source_target_pairs={{0,8},{1,9},{2,10},{3,11},{4,12},{5,13},{6,14},{7,15},{8,0},{9,1},... | collective-permute-start | bytes 1572872 | tf_op jit(solution)/shard_map/ppermute | solution.py:69
  106.7 22.3 %collective-permute-start.14 = (bf16[4,64,1024]{2,1,0:T(8,128)(2,1)}, bf16[4,64,1024]{2,1,0:T(8,128)(2,1)S(1)}, u32[]{:S(2)}, u32[]{:S(2)}) collective-permute-start(bf16[4,64,1024]{2,1,0:T(8,128)(2,1)} %bitcast.339), channel_id=1, source_target_pairs={{0,8},{1,9},{2,10},{3,11},{4,12},{5,13},{6,14},{7,15},{8,0},{9,1},... | collective-permute-start | bytes 1572872 | tf_op jit(solution)/shard_map/ppermute | solution.py:69
  110.2 27.4 %collective-permute-start.13 = (bf16[512,1024]{1,0:T(8,128)(2,1)S(1)}, bf16[512,1024]{1,0:T(8,128)(2,1)S(1)}, u32[]{:S(2)}, u32[]{:S(2)}) collective-permute-start(bf16[512,1024]{1,0:T(8,128)(2,1)S(1)} %shard_map.237), channel_id=1, source_target_pairs={{0,4},{1,5},{2,6},{3,7},{4,0},{5,1},{6,2},{7,3},{8,12},{9,13},{10,... | collective-permute-start | bytes 3145736 | tf_op jit(solution)/shard_map/ppermute | solution.py:69
  111.7 26.0 %collective-permute-start.12 = (bf16[256,1024]{1,0:T(8,128)(2,1)S(1)}, bf16[256,1024]{1,0:T(8,128)(2,1)S(1)}, u32[]{:S(2)}, u32[]{:S(2)}) collective-permute-start(bf16[256,1024]{1,0:T(8,128)(2,1)S(1)} %get-tuple-element.619), channel_id=1, source_target_pairs={{0,16},{1,17},{2,18},{3,19},{4,20},{5,21},{6,22},{7,23},{8,24},{9,... | collective-permute-start | bytes 1572872 | tf_op jit(solution)/shard_map/ppermute | solution.py:69
  138.7 32.5 %collective-permute-start.18 = (bf16[256,1024]{1,0:T(8,128)(2,1)}, bf16[256,1024]{1,0:T(8,128)(2,1)S(1)}, u32[]{:S(2)}, u32[]{:S(2)}) collective-permute-start(bf16[256,1024]{1,0:T(8,128)(2,1)} %get-tuple-element.280), channel_id=1, source_target_pairs={{0,16},{1,17},{2,18},{3,19},{4,20},{5,21},{6,22},{7,23},{8,24},{9,... | collective-permute-start | bytes 1572872 | tf_op jit(solution)/shard_map/ppermute | solution.py:69
  138.7 32.5 %collective-permute-start.19 = (bf16[2,64,2048]{2,1,0:T(8,128)(2,1)}, bf16[2,64,2048]{2,1,0:T(8,128)(2,1)}, u32[]{:S(2)}, u32[]{:S(2)}) collective-permute-start(bf16[2,64,2048]{2,1,0:T(8,128)(2,1)} %pad_maximum_fusion.23), channel_id=1, source_target_pairs={{0,4},{1,5},{2,6},{3,7},{4,0},{5,1},{6,2},{7,3},{8,12},{9,13},{10,... | collective-permute-start | bytes 1572872 | tf_op jit(solution)/shard_map/ppermute | solution.py:69
  140.2 21.8 %collective-permute-start.15 = (bf16[512,384]{1,0:T(8,128)(2,1)}, bf16[512,384]{1,0:T(8,128)(2,1)}, u32[]{:S(2)}, u32[]{:S(2)}) collective-permute-start(bf16[512,384]{1,0:T(8,128)(2,1)} %get-tuple-element.276), channel_id=1, source_target_pairs={{0,4},{1,5},{2,6},{3,7},{4,0},{5,1},{6,2},{7,3},{8,12},{9,13},{10,... | collective-permute-start | bytes 1179656 | tf_op jit(solution)/shard_map/ppermute | solution.py:69
  140.8 23.5 %collective-permute-start.16 = (bf16[512,384]{1,0:T(8,128)(2,1)}, bf16[512,384]{1,0:T(8,128)(2,1)}, u32[]{:S(2)}, u32[]{:S(2)}) collective-permute-start(bf16[512,384]{1,0:T(8,128)(2,1)} %get-tuple-element.277), channel_id=1, source_target_pairs={{0,8},{1,9},{2,10},{3,11},{4,12},{5,13},{6,14},{7,15},{8,0},{9,1},... | collective-permute-start | bytes 1179656 | tf_op jit(solution)/shard_map/ppermute | solution.py:69
  142.4 28.9 %collective-permute-start.17 = (bf16[512,384]{1,0:T(8,128)(2,1)}, bf16[512,384]{1,0:T(8,128)(2,1)}, u32[]{:S(2)}, u32[]{:S(2)}) collective-permute-start(bf16[512,384]{1,0:T(8,128)(2,1)} %get-tuple-element.278), channel_id=1, source_target_pairs={{0,12},{1,13},{2,14},{3,15},{4,8},{5,9},{6,10},{7,11},{8,4},{9,5},... | collective-permute-start | bytes 1179656 | tf_op jit(solution)/shard_map/ppermute | solution.py:69
  173.8 21.0 %collective-permute-start.25 = (bf16[64,2048]{1,0:T(8,128)(2,1)S(1)}, bf16[64,2048]{1,0:T(8,128)(2,1)S(1)}, u32[]{:S(2)}, u32[]{:S(2)}) collective-permute-start(bf16[64,2048]{1,0:T(8,128)(2,1)S(1)} %get-tuple-element.325.b), channel_id=1, source_target_pairs={{0,8},{1,9},{2,10},{3,11},{4,12},{5,13},{6,14},{7,15},{8,0},{9,1},... | collective-permute-start | bytes 786440 | tf_op jit(solution)/shard_map/ppermute | solution.py:69
  173.9 26.6 %collective-permute-start.21 = (bf16[256,1024]{1,0:T(8,128)(2,1)S(1)}, bf16[256,1024]{1,0:T(8,128)(2,1)S(1)}, u32[]{:S(2)}, u32[]{:S(2)}) collective-permute-start(bf16[256,1024]{1,0:T(8,128)(2,1)S(1)} %slice.882), channel_id=1, source_target_pairs={{0,16},{1,17},{2,18},{3,19},{4,20},{5,21},{6,22},{7,23},{8,24},{9,... | collective-permute-start | bytes 1572872 | tf_op jit(solution)/shard_map/ppermute | solution.py:69
  176.6 23.8 %collective-permute-start.22 = (bf16[256,1024]{1,0:T(8,128)(2,1)S(1)}, bf16[256,1024]{1,0:T(8,128)(2,1)S(1)}, u32[]{:S(2)}, u32[]{:S(2)}) collective-permute-start(bf16[256,1024]{1,0:T(8,128)(2,1)S(1)} %copy-done.71), channel_id=1, source_target_pairs={{0,4},{1,5},{2,6},{3,7},{4,0},{5,1},{6,2},{7,3},{8,12},{9,13},{10,... | collective-permute-start | bytes 1572872 | tf_op jit(solution)/shard_map/ppermute | solution.py:69
  177.2 24.5 %collective-permute-start.23 = (bf16[256,1024]{1,0:T(8,128)(2,1)S(1)}, bf16[256,1024]{1,0:T(8,128)(2,1)S(1)}, u32[]{:S(2)}, u32[]{:S(2)}) collective-permute-start(bf16[256,1024]{1,0:T(8,128)(2,1)S(1)} %copy-done.73), channel_id=1, source_target_pairs={{0,4},{1,5},{2,6},{3,7},{4,0},{5,1},{6,2},{7,3},{8,12},{9,13},{10,... | collective-permute-start | bytes 1572872 | tf_op jit(solution)/shard_map/ppermute | solution.py:69
  219.8 22.9 %collective-permute-start.35 = (bf16[128,2048]{1,0:T(8,128)(2,1)S(1)}, bf16[128,2048]{1,0:T(8,128)(2,1)S(1)}, u32[]{:S(2)}, u32[]{:S(2)}) collective-permute-start(bf16[128,2048]{1,0:T(8,128)(2,1)S(1)} %pad_maximum_fusion.26), channel_id=1, source_target_pairs={{0,2},{1,3},{2,0},{3,1},{4,6},{5,7},{6,4},{7,5},{8,10},{9,11},{10,... | collective-permute-start | bytes 1572872 | tf_op jit(solution)/shard_map/ppermute | solution.py:69
  221.3 21.4 %collective-permute-start.34 = (bf16[128,2048]{1,0:T(8,128)(2,1)S(1)}, bf16[128,2048]{1,0:T(8,128)(2,1)S(1)}, u32[]{:S(2)}, u32[]{:S(2)}) collective-permute-start(bf16[128,2048]{1,0:T(8,128)(2,1)S(1)} %pad_maximum_fusion.25), channel_id=1, source_target_pairs={{0,8},{1,9},{2,10},{3,11},{4,12},{5,13},{6,14},{7,15},{8,0},{9,1},... | collective-permute-start | bytes 1572872 | tf_op jit(solution)/shard_map/ppermute | solution.py:69
  221.4 21.3 %collective-permute-start.33 = (bf16[320,1024]{1,0:T(8,128)(2,1)S(1)}, bf16[320,1024]{1,0:T(8,128)(2,1)S(1)}, u32[]{:S(2)}, u32[]{:S(2)}) collective-permute-start(bf16[320,1024]{1,0:T(8,128)(2,1)S(1)} %slice.714), channel_id=1, source_target_pairs={{0,4},{1,5},{2,6},{3,7},{4,0},{5,1},{6,2},{7,3},{8,12},{9,13},{10,... | collective-permute-start | bytes 1966088 | tf_op jit(solution)/shard_map/ppermute | solution.py:69
  223.6 23.0 %collective-permute-start.32 = (bf16[2,80,2048]{2,1,0:T(8,128)(2,1)S(1)}, bf16[2,80,2048]{2,1,0:T(8,128)(2,1)S(1)}, u32[]{:S(2)}, u32[]{:S(2)}) collective-permute-start(bf16[2,80,2048]{2,1,0:T(8,128)(2,1)S(1)} %pad_maximum_fusion.18), channel_id=1, source_target_pairs={{0,2},{1,3},{2,0},{3,1},{4,6},{5,7},{6,4},{7,5},{8,10},{9,11},{10,... | collective-permute-start | bytes 1966088 | tf_op jit(solution)/shard_map/ppermute | solution.py:69
  224.3 18.4 %collective-permute-start.31 = (bf16[2,48,2048]{2,1,0:T(8,128)(2,1)S(1)}, bf16[2,48,2048]{2,1,0:T(8,128)(2,1)S(1)}, u32[]{:S(2)}, u32[]{:S(2)}) collective-permute-start(bf16[2,48,2048]{2,1,0:T(8,128)(2,1)S(1)} %get-tuple-element.552), channel_id=1, source_target_pairs={{0,16},{1,17},{2,18},{3,19},{4,20},{5,21},{6,22},{7,23},{8,24},{9,... | collective-permute-start | bytes 1179656 | tf_op jit(solution)/shard_map/ppermute | solution.py:69
  246.6 18.9 %collective-permute-start.39 = (bf16[2048,1024]{1,0:T(8,128)(2,1)S(1)}, bf16[2048,1024]{1,0:T(8,128)(2,1)S(1)}, u32[]{:S(2)}, u32[]{:S(2)}) collective-permute-start(bf16[2048,1024]{1,0:T(8,128)(2,1)S(1)} %constant_dynamic-update-slice_fusion.4), channel_id=1, source_target_pairs={{0,1},{1,0},{2,3},{3,2},{4,5},{5,4},{6,7},{7,6},{8,9},{9,8},{10,11... | collective-permute-start | bytes 12582920 | tf_op jit(solution)/shard_map/ppermute | solution.py:69
  248.3 16.9 %collective-permute-start.37 = (bf16[80,2048]{1,0:T(8,128)(2,1)S(1)}, bf16[80,2048]{1,0:T(8,128)(2,1)S(1)}, u32[]{:S(2)}, u32[]{:S(2)}) collective-permute-start(bf16[80,2048]{1,0:T(8,128)(2,1)S(1)} %fusion.40), channel_id=1, source_target_pairs={{0,16},{1,17},{2,18},{3,19},{4,20},{5,21},{6,22},{7,23},{8,24},{9,... | collective-permute-start | bytes 983048 | tf_op jit(solution)/shard_map/ppermute | solution.py:69
  248.5 17.0 %collective-permute-start.38 = (bf16[192,1024]{1,0:T(8,128)(2,1)S(1)}, bf16[192,1024]{1,0:T(8,128)(2,1)S(1)}, u32[]{:S(2)}, u32[]{:S(2)}) collective-permute-start(bf16[192,1024]{1,0:T(8,128)(2,1)S(1)} %slice.723), channel_id=1, source_target_pairs={{0,4},{1,5},{2,6},{3,7},{4,0},{5,1},{6,2},{7,3},{8,12},{9,13},{10,... | collective-permute-start | bytes 1179656 | tf_op jit(solution)/shard_map/ppermute | solution.py:69
  265.6 16.2 %collective-permute-start.42 = (bf16[160,1024]{1,0:T(8,128)(2,1)S(1)}, bf16[160,1024]{1,0:T(8,128)(2,1)S(1)}, u32[]{:S(2)}, u32[]{:S(2)}) collective-permute-start(bf16[160,1024]{1,0:T(8,128)(2,1)S(1)} %slice.726), channel_id=1, source_target_pairs={{0,4},{1,5},{2,6},{3,7},{4,0},{5,1},{6,2},{7,3},{8,12},{9,13},{10,... | collective-permute-start | bytes 983048 | tf_op jit(solution)/shard_map/ppermute | solution.py:69
  282.6 16.7 %collective-permute-start.46 = (bf16[352,1024]{1,0:T(8,128)(2,1)S(1)}, bf16[352,1024]{1,0:T(8,128)(2,1)S(1)}, u32[]{:S(2)}, u32[]{:S(2)}) collective-permute-start(bf16[352,1024]{1,0:T(8,128)(2,1)S(1)} %slice.892), channel_id=1, source_target_pairs={{0,4},{1,5},{2,6},{3,7},{4,0},{5,1},{6,2},{7,3},{8,12},{9,13},{10,... | collective-permute-start | bytes 2162696 | tf_op jit(solution)/shard_map/ppermute | solution.py:69
  316.7 21.0 %collective-permute-start.48 = (bf16[2048,1024]{1,0:T(8,128)(2,1)}, bf16[2048,1024]{1,0:T(8,128)(2,1)}, u32[]{:S(2)}, u32[]{:S(2)}) collective-permute-start(bf16[2048,1024]{1,0:T(8,128)(2,1)} %convolution_convert_fusion.3), channel_id=1, source_target_pairs={{0,1},{1,0},{2,3},{3,2},{4,5},{5,4},{6,7},{7,6},{8,9},{9,8},{10,11... | collective-permute-start | bytes 12582920 | tf_op jit(solution)/shard_map/ppermute | solution.py:69
  338.0 17.2 %collective-permute-start.50 = (bf16[2,64,2048]{2,1,0:T(8,128)(2,1)S(1)}, bf16[2,64,2048]{2,1,0:T(8,128)(2,1)S(1)}, u32[]{:S(2)}, u32[]{:S(2)}) collective-permute-start(bf16[2,64,2048]{2,1,0:T(8,128)(2,1)S(1)} %pad_maximum_fusion.30), channel_id=1, source_target_pairs={{0,2},{1,3},{2,0},{3,1},{4,6},{5,7},{6,4},{7,5},{8,10},{9,11},{10,... | collective-permute-start | bytes 1572872 | tf_op jit(solution)/shard_map/ppermute | solution.py:69
  339.5 15.7 %collective-permute-start.49 = (bf16[2,64,2048]{2,1,0:T(8,128)(2,1)S(1)}, bf16[2,64,2048]{2,1,0:T(8,128)(2,1)S(1)}, u32[]{:S(2)}, u32[]{:S(2)}) collective-permute-start(bf16[2,64,2048]{2,1,0:T(8,128)(2,1)S(1)} %get-tuple-element.546), channel_id=1, source_target_pairs={{0,8},{1,9},{2,10},{3,11},{4,12},{5,13},{6,14},{7,15},{8,0},{9,1},... | collective-permute-start | bytes 1572872 | tf_op jit(solution)/shard_map/ppermute | solution.py:69
  368.5 22.8 %collective-permute-start.59 = (bf16[2048,1024]{1,0:T(8,128)(2,1)S(1)}, bf16[2048,1024]{1,0:T(8,128)(2,1)S(1)}, u32[]{:S(2)}, u32[]{:S(2)}) collective-permute-start(bf16[2048,1024]{1,0:T(8,128)(2,1)S(1)} %convolution_convert_fusion.1), channel_id=1, source_target_pairs={{0,1},{1,0},{2,3},{3,2},{4,5},{5,4},{6,7},{7,6},{8,9},{9,8},{10,11... | collective-permute-start | bytes 12582920 | tf_op jit(solution)/shard_map/ppermute | solution.py:69
  369.2 22.1 %collective-permute-start.58 = (bf16[320,1024]{1,0:T(8,128)(2,1)S(1)}, bf16[320,1024]{1,0:T(8,128)(2,1)S(1)}, u32[]{:S(2)}, u32[]{:S(2)}) collective-permute-start(bf16[320,1024]{1,0:T(8,128)(2,1)S(1)} %pad_maximum_fusion.19), channel_id=1, source_target_pairs={{0,4},{1,5},{2,6},{3,7},{4,0},{5,1},{6,2},{7,3},{8,12},{9,13},{10,... | collective-permute-start | bytes 1966088 | tf_op jit(solution)/shard_map/ppermute | solution.py:69
  373.8 17.5 %collective-permute-start.57 = (bf16[80,2048]{1,0:T(8,128)(2,1)S(1)}, bf16[80,2048]{1,0:T(8,128)(2,1)S(1)}, u32[]{:S(2)}, u32[]{:S(2)}) collective-permute-start(bf16[80,2048]{1,0:T(8,128)(2,1)S(1)} %slice.901.b), channel_id=1, source_target_pairs={{0,16},{1,17},{2,18},{3,19},{4,20},{5,21},{6,22},{7,23},{8,24},{9,... | collective-permute-start | bytes 983048 | tf_op jit(solution)/shard_map/ppermute | solution.py:69
  391.4 21.2 %collective-permute-start.61 = (bf16[160,2048]{1,0:T(8,128)(2,1)S(1)}, bf16[160,2048]{1,0:T(8,128)(2,1)S(1)}, u32[]{:S(2)}, u32[]{:S(2)}) collective-permute-start(bf16[160,2048]{1,0:T(8,128)(2,1)S(1)} %pad_maximum_fusion.20), channel_id=1, source_target_pairs={{0,2},{1,3},{2,0},{3,1},{4,6},{5,7},{6,4},{7,5},{8,10},{9,11},{10,... | collective-permute-start | bytes 1966088 | tf_op jit(solution)/shard_map/ppermute | solution.py:69
  392.5 20.1 %collective-permute-start.62 = (bf16[320,1024]{1,0:T(8,128)(2,1)S(1)}, bf16[320,1024]{1,0:T(8,128)(2,1)S(1)}, u32[]{:S(2)}, u32[]{:S(2)}) collective-permute-start(bf16[320,1024]{1,0:T(8,128)(2,1)S(1)} %slice_bitcast_fusion.8), channel_id=1, source_target_pairs={{0,4},{1,5},{2,6},{3,7},{4,0},{5,1},{6,2},{7,3},{8,12},{9,13},{10,... | collective-permute-start | bytes 1966088 | tf_op jit(solution)/shard_map/ppermute | solution.py:69
  393.8 18.8 %collective-permute-start.60 = (bf16[96,2048]{1,0:T(8,128)(2,1)S(1)}, bf16[96,2048]{1,0:T(8,128)(2,1)S(1)}, u32[]{:S(2)}, u32[]{:S(2)}) collective-permute-start(bf16[96,2048]{1,0:T(8,128)(2,1)S(1)} %pad_maximum_fusion.35), channel_id=1, source_target_pairs={{0,16},{1,17},{2,18},{3,19},{4,20},{5,21},{6,22},{7,23},{8,24},{9,... | collective-permute-start | bytes 1179656 | tf_op jit(solution)/shard_map/ppermute | solution.py:69
  434.1 28.7 %collective-permute-start.68 = (bf16[320,1024]{1,0:T(8,128)(2,1)S(1)}, bf16[320,1024]{1,0:T(8,128)(2,1)S(1)}, u32[]{:S(2)}, u32[]{:S(2)}) collective-permute-start(bf16[320,1024]{1,0:T(8,128)(2,1)S(1)} %fusion.22), channel_id=1, source_target_pairs={{0,16},{1,17},{2,18},{3,19},{4,20},{5,21},{6,22},{7,23},{8,24},{9,... | collective-permute-start | bytes 1966088 | tf_op jit(solution)/shard_map/ppermute | solution.py:69
  434.3 24.0 %collective-permute-start.70 = (bf16[2,64,2048]{2,1,0:T(8,128)(2,1)S(1)}, bf16[2,64,2048]{2,1,0:T(8,128)(2,1)S(1)}, u32[]{:S(2)}, u32[]{:S(2)}) collective-permute-start(bf16[2,64,2048]{2,1,0:T(8,128)(2,1)S(1)} %pad_maximum_fusion.33), channel_id=1, source_target_pairs={{0,2},{1,3},{2,0},{3,1},{4,6},{5,7},{6,4},{7,5},{8,10},{9,11},{10,... | collective-permute-start | bytes 1572872 | tf_op jit(solution)/shard_map/ppermute | solution.py:69
  435.0 23.4 %collective-permute-start.69 = (bf16[2,64,2048]{2,1,0:T(8,128)(2,1)S(1)}, bf16[2,64,2048]{2,1,0:T(8,128)(2,1)S(1)}, u32[]{:S(2)}, u32[]{:S(2)}) collective-permute-start(bf16[2,64,2048]{2,1,0:T(8,128)(2,1)S(1)} %get-tuple-element.540), channel_id=1, source_target_pairs={{0,8},{1,9},{2,10},{3,11},{4,12},{5,13},{6,14},{7,15},{8,0},{9,1},... | collective-permute-start | bytes 1572872 | tf_op jit(solution)/shard_map/ppermute | solution.py:69
  437.9 24.8 %collective-permute-start.67 = (bf16[512,1024]{1,0:T(8,128)(2,1)S(1)}, bf16[512,1024]{1,0:T(8,128)(2,1)S(1)}, u32[]{:S(2)}, u32[]{:S(2)}) collective-permute-start(bf16[512,1024]{1,0:T(8,128)(2,1)S(1)} %slice_bitcast_fusion.1), channel_id=1, source_target_pairs={{0,4},{1,5},{2,6},{3,7},{4,0},{5,1},{6,2},{7,3},{8,12},{9,13},{10,... | collective-permute-start | bytes 3145736 | tf_op jit(solution)/shard_map/ppermute | solution.py:69
  439.4 17.4 %collective-permute-start.71 = (bf16[4,64,2048]{2,1,0:T(8,128)(2,1)S(1)}, bf16[4,64,2048]{2,1,0:T(8,128)(2,1)S(1)}, u32[]{:S(2)}, u32[]{:S(2)}) collective-permute-start(bf16[4,64,2048]{2,1,0:T(8,128)(2,1)S(1)} %broadcast_select_fusion), channel_id=1, source_target_pairs={{0,1},{1,0},{2,3},{3,2},{4,5},{5,4},{6,7},{7,6},{8,9},{9,8},{10,11... | collective-permute-start | bytes 3145736 | tf_op jit(solution)/shard_map/ppermute | solution.py:69
  468.0 32.1 %collective-permute-start.76 = (bf16[256,1024]{1,0:T(8,128)(2,1)S(1)}, bf16[256,1024]{1,0:T(8,128)(2,1)S(1)}, u32[]{:S(2)}, u32[]{:S(2)}) collective-permute-start(bf16[256,1024]{1,0:T(8,128)(2,1)S(1)} %slice.912), channel_id=1, source_target_pairs={{0,16},{1,17},{2,18},{3,19},{4,20},{5,21},{6,22},{7,23},{8,24},{9,... | collective-permute-start | bytes 1572872 | tf_op jit(solution)/shard_map/ppermute | solution.py:69
  468.3 20.6 %collective-permute-start.75 = (bf16[512,384]{1,0:T(8,128)(2,1)S(1)}, bf16[512,384]{1,0:T(8,128)(2,1)S(1)}, u32[]{:S(2)}, u32[]{:S(2)}) collective-permute-start(bf16[512,384]{1,0:T(8,128)(2,1)S(1)} %get-tuple-element.564), channel_id=1, source_target_pairs={{0,12},{1,13},{2,14},{3,15},{4,8},{5,9},{6,10},{7,11},{8,4},{9,5},... | collective-permute-start | bytes 1179656 | tf_op jit(solution)/shard_map/ppermute | solution.py:69
  470.3 29.9 %collective-permute-start.74 = (bf16[512,384]{1,0:T(8,128)(2,1)S(1)}, bf16[512,384]{1,0:T(8,128)(2,1)S(1)}, u32[]{:S(2)}, u32[]{:S(2)}) collective-permute-start(bf16[512,384]{1,0:T(8,128)(2,1)S(1)} %get-tuple-element.565), channel_id=1, source_target_pairs={{0,8},{1,9},{2,10},{3,11},{4,12},{5,13},{6,14},{7,15},{8,0},{9,1},... | collective-permute-start | bytes 1179656 | tf_op jit(solution)/shard_map/ppermute | solution.py:69
  471.5 28.7 %collective-permute-start.73 = (bf16[512,384]{1,0:T(8,128)(2,1)S(1)}, bf16[512,384]{1,0:T(8,128)(2,1)S(1)}, u32[]{:S(2)}, u32[]{:S(2)}) collective-permute-start(bf16[512,384]{1,0:T(8,128)(2,1)S(1)} %get-tuple-element.566), channel_id=1, source_target_pairs={{0,4},{1,5},{2,6},{3,7},{4,0},{5,1},{6,2},{7,3},{8,12},{9,13},{10,... | collective-permute-start | bytes 1179656 | tf_op jit(solution)/shard_map/ppermute | solution.py:69
  500.6 18.5 %collective-permute-start.80 = (bf16[2,64,2048]{2,1,0:T(8,128)(2,1)S(1)}, bf16[2,64,2048]{2,1,0:T(8,128)(2,1)S(1)}, u32[]{:S(2)}, u32[]{:S(2)}) collective-permute-start(bf16[2,64,2048]{2,1,0:T(8,128)(2,1)S(1)} %slice_bitcast_fusion.9), channel_id=1, source_target_pairs={{0,4},{1,5},{2,6},{3,7},{4,0},{5,1},{6,2},{7,3},{8,12},{9,13},{10,... | collective-permute-start | bytes 1572872 | tf_op jit(solution)/shard_map/ppermute | solution.py:69
  501.3 17.7 %collective-permute-start.77 = (bf16[4,64,1024]{2,1,0:T(8,128)(2,1)S(1)}, bf16[4,64,1024]{2,1,0:T(8,128)(2,1)S(1)}, u32[]{:S(2)}, u32[]{:S(2)}) collective-permute-start(bf16[4,64,1024]{2,1,0:T(8,128)(2,1)S(1)} %get-tuple-element.445), channel_id=1, source_target_pairs={{0,8},{1,9},{2,10},{3,11},{4,12},{5,13},{6,14},{7,15},{8,0},{9,1},... | collective-permute-start | bytes 1572872 | tf_op jit(solution)/shard_map/ppermute | solution.py:69
  519.2 24.3 %collective-permute-start.83 = (bf16[256,1024]{1,0:T(8,128)(2,1)S(1)}, bf16[256,1024]{1,0:T(8,128)(2,1)S(1)}, u32[]{:S(2)}, u32[]{:S(2)}) collective-permute-start(bf16[256,1024]{1,0:T(8,128)(2,1)S(1)} %slice.800), channel_id=1, source_target_pairs={{0,16},{1,17},{2,18},{3,19},{4,20},{5,21},{6,22},{7,23},{8,24},{9,... | collective-permute-start | bytes 1572872 | tf_op jit(solution)/shard_map/ppermute | solution.py:69
  521.2 25.3 %collective-permute-start.82 = (bf16[512,1024]{1,0:T(8,128)(2,1)S(1)}, bf16[512,1024]{1,0:T(8,128)(2,1)S(1)}, u32[]{:S(2)}, u32[]{:S(2)}) collective-permute-start(bf16[512,1024]{1,0:T(8,128)(2,1)S(1)} %slice_bitcast_fusion), channel_id=1, source_target_pairs={{0,4},{1,5},{2,6},{3,7},{4,0},{5,1},{6,2},{7,3},{8,12},{9,13},{10,... | collective-permute-start | bytes 3145736 | tf_op jit(solution)/shard_map/ppermute | solution.py:69
  547.8 20.5 %collective-permute-start.88 = (bf16[4,64,1024]{2,1,0:T(8,128)(2,1)S(1)}, bf16[4,64,1024]{2,1,0:T(8,128)(2,1)S(1)}, u32[]{:S(2)}, u32[]{:S(2)}) collective-permute-start(bf16[4,64,1024]{2,1,0:T(8,128)(2,1)S(1)} %get-tuple-element.465), channel_id=1, source_target_pairs={{0,8},{1,9},{2,10},{3,11},{4,12},{5,13},{6,14},{7,15},{8,0},{9,1},... | collective-permute-start | bytes 1572872 | tf_op jit(solution)/shard_map/ppermute | solution.py:69
  549.9 22.4 %collective-permute-start.87 = (bf16[2,80,2048]{2,1,0:T(8,128)(2,1)S(1)}, bf16[2,80,2048]{2,1,0:T(8,128)(2,1)S(1)}, u32[]{:S(2)}, u32[]{:S(2)}) collective-permute-start(bf16[2,80,2048]{2,1,0:T(8,128)(2,1)S(1)} %pad_maximum_fusion.22), channel_id=1, source_target_pairs={{0,2},{1,3},{2,0},{3,1},{4,6},{5,7},{6,4},{7,5},{8,10},{9,11},{10,... | collective-permute-start | bytes 1966088 | tf_op jit(solution)/shard_map/ppermute | solution.py:69
  550.3 21.9 %collective-permute-start.85 = (bf16[512,768]{1,0:T(8,128)(2,1)S(1)}, bf16[512,768]{1,0:T(8,128)(2,1)S(1)}, u32[]{:S(2)}, u32[]{:S(2)}) collective-permute-start(bf16[512,768]{1,0:T(8,128)(2,1)S(1)} %slice_bitcast_fusion.5), channel_id=1, source_target_pairs={{0,4},{1,5},{2,6},{3,7},{4,0},{5,1},{6,2},{7,3},{8,12},{9,13},{10,... | collective-permute-start | bytes 2359304 | tf_op jit(solution)/shard_map/ppermute | solution.py:69
  551.1 17.4 %collective-permute-start.89 = (bf16[2,2,64,1024]{3,2,1,0:T(8,128)(2,1)S(1)}, bf16[2,2,64,1024]{3,2,1,0:T(8,128)(2,1)S(1)}, u32[]{:S(2)}, u32[]{:S(2)}) collective-permute-start(bf16[2,2,64,1024]{3,2,1,0:T(8,128)(2,1)S(1)} %get-tuple-element.603), channel_id=1, source_target_pairs={{0,1},{1,0},{2,3},{3,2},{4,5},{5,4},{6,7},{7,6},{8,9},{9,8},{10,11... | collective-permute-start | bytes 1572872 | tf_op jit(solution)/shard_map/ppermute | solution.py:69
  551.3 21.0 %collective-permute-start.86 = (bf16[2,48,2048]{2,1,0:T(8,128)(2,1)S(1)}, bf16[2,48,2048]{2,1,0:T(8,128)(2,1)S(1)}, u32[]{:S(2)}, u32[]{:S(2)}) collective-permute-start(bf16[2,48,2048]{2,1,0:T(8,128)(2,1)S(1)} %get-tuple-element.534), channel_id=1, source_target_pairs={{0,16},{1,17},{2,18},{3,19},{4,20},{5,21},{6,22},{7,23},{8,24},{9,... | collective-permute-start | bytes 1179656 | tf_op jit(solution)/shard_map/ppermute | solution.py:69
  574.3 15.5 %collective-permute-start.93 = (bf16[80,2048]{1,0:T(8,128)(2,1)S(1)}, bf16[80,2048]{1,0:T(8,128)(2,1)S(1)}, u32[]{:S(2)}, u32[]{:S(2)}) collective-permute-start(bf16[80,2048]{1,0:T(8,128)(2,1)S(1)} %fusion.41), channel_id=1, source_target_pairs={{0,16},{1,17},{2,18},{3,19},{4,20},{5,21},{6,22},{7,23},{8,24},{9,... | collective-permute-start | bytes 983048 | tf_op jit(solution)/shard_map/ppermute | solution.py:69
  574.4 16.6 %collective-permute-start.94 = (bf16[2,2,64,1024]{3,2,0,1:T(8,128)(2,1)S(1)}, bf16[2,2,64,1024]{3,2,0,1:T(8,128)(2,1)S(1)}, u32[]{:S(2)}, u32[]{:S(2)}) collective-permute-start(bf16[2,2,64,1024]{3,2,0,1:T(8,128)(2,1)S(1)} %fusion.36), channel_id=1, source_target_pairs={{0,2},{1,3},{2,0},{3,1},{4,6},{5,7},{6,4},{7,5},{8,10},{9,11},{10,... | collective-permute-start | bytes 1572872 | tf_op jit(solution)/shard_map/ppermute | solution.py:69
  574.9 18.6 %collective-permute-start.91 = (bf16[512,768]{1,0:T(8,128)(2,1)S(1)}, bf16[512,768]{1,0:T(8,128)(2,1)S(1)}, u32[]{:S(2)}, u32[]{:S(2)}) collective-permute-start(bf16[512,768]{1,0:T(8,128)(2,1)S(1)} %slice_bitcast_fusion.4), channel_id=1, source_target_pairs={{0,4},{1,5},{2,6},{3,7},{4,0},{5,1},{6,2},{7,3},{8,12},{9,13},{10,... | collective-permute-start | bytes 2359304 | tf_op jit(solution)/shard_map/ppermute | solution.py:69
  576.2 26.4 %collective-permute-start.90 = (bf16[512,768]{1,0:T(8,128)(2,1)S(1)}, bf16[512,768]{1,0:T(8,128)(2,1)S(1)}, u32[]{:S(2)}, u32[]{:S(2)}) collective-permute-start(bf16[512,768]{1,0:T(8,128)(2,1)S(1)} %fusion.21), channel_id=1, source_target_pairs={{0,8},{1,9},{2,10},{3,11},{4,12},{5,13},{6,14},{7,15},{8,0},{9,1},... | collective-permute-start | bytes 2359304 | tf_op jit(solution)/shard_map/ppermute | solution.py:69
  603.7 24.7 %all-to-all-start.1 = ((bf16[8,64,768]{2,1,0:T(8,128)(2,1)}), bf16[8,64,768]{2,1,0:T(8,128)(2,1)S(1)}, u32[]{:S(2)}, u32[]{:S(2)}) async-start(bf16[8,64,768]{2,1,0:T(8,128)(2,1)} %bitcast.129), calls=%async_computation.1 | async-start | bytes 1572864 | tf_op jit(solution)/shard_map/all_to_all | solution.py:565
  608.3 15.2 %collective-permute-start.96 = (bf16[2,2,64,1024]{3,2,1,0:T(8,128)(2,1)S(1)}, bf16[2,2,64,1024]{3,2,1,0:T(8,128)(2,1)S(1)}, u32[]{:S(2)}, u32[]{:S(2)}) collective-permute-start(bf16[2,2,64,1024]{3,2,1,0:T(8,128)(2,1)S(1)} %get-tuple-element.589), channel_id=1, source_target_pairs={{0,1},{1,0},{2,3},{3,2},{4,5},{5,4},{6,7},{7,6},{8,9},{9,8},{10,11... | collective-permute-start | bytes 1572872 | tf_op jit(solution)/shard_map/ppermute | solution.py:69
  (150 other events, 1492.0 us)

commit v5 on v4

--- a/solution.py
+++ b/solution.py
@@ -330,6 +330,24 @@
     )(places, cosine, sine, *heads)[0]
 
 
+def deal_kernel(columns, weight, gain, out):
+    for block, start, end, target in columns:
+        value = weight[:, target : target + end - start].astype(f32) * gain[...]
+        out[block, :, start:end] = value.astype(bf16)
+
+
+def deal(columns, weight, gain):
+    rows, width = weight.shape
+    return call(
+        functools.partial(deal_kernel, columns),
+        0,
+        2,
+        (jax.ShapeDtypeStruct((8, rows, width // 8), bf16),),
+        [],
+        moving(4 * rows * width),
+    )(weight, gain)[0]
+
+
 def deliver_kernel(columns, got, weight, gain, out, gain_grad):
     total = None
     for block, start, end, target in columns:
@@ -599,13 +617,7 @@
 
     gain_one = gain_attn.astype(f32)[:, None]
     gain_two = gain_mlp.astype(f32)[:, None]
-    qkv_scaled = (w_qkv.astype(f32) * gain_one).astype(bf16)
     n_ff = w_up.shape[1] // 8
-    qkv_sent = (
-        qkv_scaled.reshape(shard, 3, 2, 2, 2, 2, HEAD)
-        .transpose(2, 5, 3, 0, 4, 1, 6)
-        .reshape(8, shard, 6 * HEAD)
-    )
     qkv_columns = [
         (
             4 * hi + 2 * lo + c,
@@ -619,6 +631,7 @@
         for jj in range(2)
         for i in range(3)
     ]
+    qkv_sent = deal(qkv_columns, w_qkv, gain_one)
     mine = jnp.where(has(feed.team_hi), 4, 0) + jnp.where(has(feed.team_lo), 2, 0)
     mine = mine + jnp.where(has(1), 1, 0)
     codes = [(4 * hi, 2 * lo, c) for hi in range(2) for lo in range(2) for c in range(2)]
@@ -629,42 +642,44 @@
 
     by_lo_core_hi, by_hi_core_lo, by_core_lo_hi = placed(1, 2, 0), placed(0, 2, 1), placed(2, 1, 0)
     by_hi_lo_core = placed(0, 1, 2)
-    feed_sent = spread(by_lo_core_hi, w_up, w_down, gain_two)
-
-    qkv_sent, tokens = tied(qkv_sent, layer_input[0])
+
+    qkv_sent, tokens, up_in, down_in = tied(qkv_sent, layer_input[0], w_up, w_down)
+    feed_sent = spread(by_lo_core_hi, up_in, down_in, gain_two)
     first_rel = attn.to_rel(tokens, True)
     grad_rel = feed.to_rel(cotangent[0], False)
     qkv_block = attn.octet(qkv_sent).reshape(8 * shard, -1)
-    feed_lo = swap(feed_sent[4:], feed.team_lo)
-    qkv_block, first_rel, grad_rel, feed_sent, feed_lo, w_out = tied(
-        qkv_block, first_rel, grad_rel, feed_sent, feed_lo, w_out
+    out_z = swap(w_out, attn.first)
+    qkv_block, first_rel, grad_rel, feed_sent, feed_send, out_z, w_out = tied(
+        qkv_block, first_rel, grad_rel, feed_sent, feed_sent[4:], out_z, w_out
     )
     first_near = attn.gather_one(first_rel)
     qkv_first = swap(qkv_block, attn.first)
     qkv_second = swap(qkv_block, attn.second)
+    feed_lo = swap(feed_send, feed.team_lo)
+    qkv_first, qkv_second, first_near, feed_sent, feed_lo = tied(
+        qkv_first, qkv_second, first_near, feed_sent, feed_lo
+    )
+    qkv_both = swap(qkv_first, attn.second)
+    first_far = attn.gather_two(*first_near)
     feed_core = swap(jnp.stack([feed_sent[2:4], feed_lo[2:]]), 1)
     feed_kept = jnp.stack([jnp.stack([feed_sent[:2], feed_lo[:2]]), feed_core])
-    up_send = feed_kept[:, :, 1, :, :n_ff].reshape(4, shard, n_ff)
-    qkv_first, qkv_second, feed_kept, up_send, first_near, w_out = tied(
-        qkv_first, qkv_second, feed_kept, up_send, first_near, w_out
-    )
-    qkv_both = swap(qkv_first, attn.second)
-    first_far = attn.gather_two(*first_near)
-    out_z = swap(w_out, attn.first)
+    (up_kept, down_kept), (up_send, down_send) = (
+        [feed_kept[:, :, h, :, part].reshape(4, shard, n_ff) for part in (slice(n_ff), slice(n_ff, None))]
+        for h in range(2)
+    )
     up_got = swap(up_send, feed.team_hi)
-    down_send = feed_kept[:, :, 1, :, n_ff:].reshape(4, shard, n_ff)
-    up_kept = feed_kept[:, :, 0, :, :n_ff].reshape(4, shard, n_ff)
-    qkv_both, first_far, up_got, up_kept, down_send, feed_kept, out_z, w_out, grad_rel = tied(
-        qkv_both, first_far, up_got, up_kept, down_send, feed_kept, out_z, w_out, grad_rel
+    qkv_both, first_far, up_got, up_kept, down_kept, down_send, grad_rel = tied(
+        qkv_both, first_far, up_got, up_kept, down_kept, down_send, grad_rel
     )
     down_got = swap(down_send, feed.team_hi)
+    up_block = settle(by_hi_core_lo, up_kept, up_got)
+    n_block = up_block.shape[0]
+    cut_up = n_block // 2
     qkv_mine = attn.joined(qkv_block, qkv_first, qkv_second, qkv_both)
     qkv_other = swap(qkv_mine, 1)
     first_all = team_rows(*first_near, *first_far)
-    up_block = settle(by_hi_core_lo, up_kept, up_got)
-    n_block = up_block.shape[0]
     half = n_block // 2
-    up_za = swap(up_block[:half], feed.first)
+    up_z = [swap(up_block[:cut_up], feed.first)]
     up_x = swap(up_block, feed.second)
 
     team_device = me ^ jnp.array(plan.team_rel, jnp.int32)
@@ -707,18 +722,18 @@
     pick = [(my_head ^ r) ^ core_flip for r in range(4)]
     sent = [lax.dynamic_index_in_dim(stack, pick[r], 0, keepdims=False) for r in range(4)]
     out_pair = jnp.stack([w_out, out_z])
-    sent, up_za, up_x, grad_rel, up_block, up_half, down_got, out_z, w_out, out_pair = tied(
-        sent, up_za, up_x, grad_rel, up_block, up_block[half:], down_got, out_z, w_out, out_pair
+    sent, up_z, up_x, grad_rel, up_block, up_part, down_got, down_kept, out_pair = tied(
+        sent, up_z, up_x, grad_rel, up_block, up_block[cut_up:], down_got, down_kept, out_pair
     )
     got = [swap(sent[r], plan.head_rel[r]) for r in range(1, 4)]
-    up_zb = swap(up_half, feed.first)
+    up_z += [swap(up_part, feed.first)]
     out_x = swap(out_pair, attn.second)
     cut_z = [0, n_block // 2, n_block * 3 // 4, n_block]
-    down_kept = feed_kept[:, :, 0, :, n_ff:].reshape(4, shard, n_ff)
     down_block = settle(by_hi_core_lo, down_kept, down_got)
-    got, up_za, up_zb, down_block, grad_rel, out_x, down_first = tied(
-        got, up_za, up_zb, down_block, grad_rel, out_x, down_block[: cut_z[1]]
-    )
+    got, up_z, down_block, grad_rel, out_x, down_first = tied(
+        got, up_z, down_block, grad_rel, out_x, down_block[: cut_z[1]]
+    )
+    up_za, up_zb = up_z
     own = jnp.stack([sent[0]] + got).reshape(16, rows, 3 * HEAD)
     down_z = [swap(down_first, feed.first)]
     up_both = [swap(up_za, feed.second), swap(up_zb, feed.second)]
@@ -803,17 +818,17 @@
         down_other_grad, down_other, down_mine, act_mine, act_other
     )
     down_swapped = swap(down_other_grad, 1)
-    down_mine_grad = matmul(grad_all, act_mine, ((0,), (0,))).astype(bf16)
 
     def back(hidden, down):
         return jax.vjp(gelu, hidden)[1](matmul(grad_all, down))[0].astype(bf16)
 
     hid_mine, hid_other = back(hidden_mine, down_mine), back(hidden_other, down_other)
     second_parts = matmul(hid_mine, up_mine, ((1,), (1,))) + matmul(hid_other, up_other, ((1,), (1,)))
-    second_parts, hid_mine, hid_other, down_swapped, down_mine_grad = tied(
-        second_parts.astype(bf16), hid_mine, hid_other, down_swapped, down_mine_grad
+    second_parts, hid_mine, hid_other, down_swapped, act_mine, act_other = tied(
+        second_parts.astype(bf16), hid_mine, hid_other, down_swapped, act_mine, act_other
     )
     second_back = feed.scatter_one(second_parts)
+    down_mine_grad = matmul(grad_all, act_mine, ((0,), (0,))).astype(bf16)
     down_sum = feed.first_sum(down_mine_grad, down_swapped)
     c1, c2, c3 = n_block * 3 // 8, n_block * 3 // 4, n_block * 3 // 8
     down_x3 = [swap(down_sum[3][:c1], feed.second)]
@@ -887,47 +902,78 @@
         dkv = dkv + swap(dkv_other[i], rel).astype(f32)
     triple = jnp.concatenate([dq, dkv.astype(bf16)], axis=2).reshape(4, 4 * rows, 3 * HEAD)
     up_z1 = added(up_sum[1], up_x3)
-    triple, up_sum, up_z1, up_z1a, down_z1 = tied(triple, up_sum, up_z1, up_z1[:half], down_z1)
+    za, zb = n_block * 3 // 8, n_block * 11 // 16
+    out_grad = out_grad.reshape(2, 2, HEAD // len(plan.part_rel), width)
+    triple, up_sum, up_z1, up_z1a, down_z1, out_grad, out_sent = tied(
+        triple, up_sum, up_z1, up_z1[:za], down_z1, out_grad, out_grad[:, 1]
+    )
     got = [swap(triple[r], plan.head_rel[r]) for r in range(1, 4)]
     up_z1a = swap(up_z1a, feed.first)
+    out_grad = added(out_grad[:, 0], swap(out_sent, attn.second))
     down_done = added(down_sum[0], jnp.concatenate(down_x2), jnp.concatenate(down_z1))
     down_rows, down_rows_hi = unsettle(by_hi_lo_core, down_done)
-    got, up_z1a, up_z1, down_rows, down_rows_hi, up_sum, out_grad, out_near = tied(
-        got, up_z1a, up_z1, down_rows, down_rows_hi, up_sum, out_grad, out_near
+    got, up_z1a, up_z1b, up_z1c, down_rows, down_rows_hi, up_sum, out_grad, out_near = tied(
+        got, up_z1a, up_z1[za:zb], up_z1[zb:], down_rows, down_rows_hi, up_sum, out_grad, out_near
     )
     places = (my_head ^ jnp.arange(4, dtype=jnp.int32)) ^ core_flip
     mixed_grad = turn_back(places, cosine, sine, [triple[0]] + got)
     mixed_grad_mine, mixed_grad_other = mixed_grad[0], mixed_grad[1]
     qkv_other_grad = matmul(first_all, mixed_grad_other, ((0,), (0,))).astype(bf16)
     out_sum = feed.scatter_two(*out_near)
-    kept, sent = out_grad.reshape(2, 2, -1, width)[:, 0], out_grad.reshape(2, 2, -1, width)[:, 1]
-    out_grad = added(kept, swap(sent, attn.second))
+    up_x2a = swap(up_sum[2][:half], feed.second)
+    up_z1b = swap(up_z1b, feed.first)
+    (
+        qkv_other_grad,
+        mixed_grad_mine,
+        mixed_grad_other,
+        up_x2a,
+        up_z1b,
+        up_z1c,
+        up_x2b,
+        up_sum,
+        down_rows,
+        down_rows_hi,
+        out_sum,
+    ) = tied(
+        qkv_other_grad,
+        mixed_grad_mine,
+        mixed_grad_other,
+        up_x2a,
+        up_z1b,
+        up_z1c,
+        up_sum[2][half:],
+        up_sum,
+        down_rows,
+        down_rows_hi,
+        out_sum,
+    )
+    qkv_swapped = swap(qkv_other_grad, 1)
+    up_x2b = swap(up_x2b, feed.second)
+    up_z1c = swap(up_z1c, feed.first)
     down_rows = jnp.stack([down_rows, swap(down_rows_hi, feed.team_hi)]).reshape(2, 2, 2, shard, n_ff)
-    qkv_other_grad, mixed_grad_mine, up_sum, down_rows, out_sum, out_grad, up_z1b = tied(
-        qkv_other_grad, mixed_grad_mine, up_sum, down_rows, out_sum, out_grad, up_z1[half:]
-    )
-    qkv_swapped = swap(qkv_other_grad, 1)
-    up_x2 = swap(up_sum[2], feed.second)
-    up_z1b = swap(up_z1b, feed.first)
-    down_rows_lo = swap(down_rows[:, 1], feed.team_lo)
     qkv_mine_grad = matmul(first_all, mixed_grad_mine, ((0,), (0,))).astype(bf16)
     first_parts = matmul(mixed_grad_mine, qkv_mine, ((1,), (1,))) + matmul(
         mixed_grad_other, qkv_other, ((1,), (1,))
     )
     qkv_sum = attn.first_sum(qkv_mine_grad, qkv_swapped)
-    qkv_sum, first_parts, up_x2, up_sum, up_z1b, down_rows, out_grad = tied(
+    qkv_sum, first_parts, up_x2b, up_sum, up_z1c, down_rows, down_send, out_grad = tied(
         qkv_sum,
         first_parts.astype(bf16),
-        up_x2,
+        up_x2b,
         up_sum,
-        up_z1b,
-        jnp.stack([down_rows[:, 0], down_rows_lo]),
+        up_z1c,
+        down_rows,
+        down_rows[:, 1],
         out_grad,
     )
     qkv_x3 = swap(qkv_sum[3], attn.second)
     first_back = attn.scatter_one(first_parts)
-    up_done = added(up_sum[0], up_x2, jnp.concatenate([up_z1a, up_z1b]))
-    down_rows = jnp.stack([down_rows[:, :, 0], swap(down_rows[:, :, 1], 1)])
+    up_done = added(
+        up_sum[0],
+        jnp.concatenate([up_x2a, up_x2b]),
+        jnp.concatenate([up_z1a, up_z1b, up_z1c]),
+    )
+    down_rows = jnp.stack([down_rows[:, 0], swap(down_send, feed.team_lo)])
     up_rows, up_rows_hi = unsettle(by_hi_lo_core, up_done)
     up_rows = jnp.stack([up_rows, swap(up_rows_hi, feed.team_hi)]).reshape(2, 2, 2, shard, n_ff)
     qkv_x3, first_back, up_rows, qkv_sum, down_rows, up_send = tied(
@@ -937,11 +983,12 @@
     qkv_x2 = swap(qkv_sum[2], attn.second)
     first_rows = attn.scatter_two(*first_back)
     output = (middle + feed.from_rel(out_sum)).astype(bf16)
+    up_rows = jnp.stack([up_rows[:, 0], swap(up_send, feed.team_lo)])
+    qkv_z1, qkv_x2, first_rows, out_grad, output, up_rows, down_rows = tied(
+        qkv_z1, qkv_x2, first_rows, out_grad, output, up_rows, down_rows
+    )
+    down_rows = jnp.stack([down_rows[:, :, 0], swap(down_rows[:, :, 1], 1)])
     grad_down, _ = restore(False, by_core_lo_hi, down_rows.reshape(8, shard, n_ff), w_down, gain_two)
-    up_rows = jnp.stack([up_rows[:, 0], swap(up_send, feed.team_lo)])
-    qkv_z1, qkv_x2, first_rows, out_grad, output, up_rows, grad_down = tied(
-        qkv_z1, qkv_x2, first_rows, out_grad, output, up_rows, grad_down
-    )
     up_rows = jnp.stack([up_rows[:, :, 0], swap(up_rows[:, :, 1], 1)])
     grad_up, grad_gain_two = restore(
         True, by_core_lo_hi, up_rows.reshape(8, shard, n_ff), w_up, gain_two

time: 643 us -> 621 us (0.966)
  waiting for transfers between devices: 328 us -> 302 us
  Pallas kernels: 44 us -> 52.5 us
    ppermute x97 -> x99, waiting for transfers between devices: 326 us -> 296 us  [swap(): return lax.ppermute(value, AXES, [(d, d ^ mask) for d in self.devices])]
    unnamed x243 -> x209, local copies, waits for them, and re-layouts: 21.9 us -> 24.9 us
    convert_element_type x20 -> x21, other arithmetic: 17.6 us -> 14.9 us  [added(): return sum((v.astype(f32) for v in values)).astype(bf16)]
    ppermute x97 -> x99, starting transfers between devices: 92.5 us -> 92.2 us  [swap(): return lax.ppermute(value, AXES, [(d, d ^ mask) for d in self.devices])]
  transfers between devices with their start and end apart: 99 -> 101, of which waited for: 47 -> 45; matrix products, arithmetic and copies ran while one was open for 18% -> 18% of each run, Pallas kernels for 7% -> 8%
where the time goes in v5:
time: 621 us; the launch traced here: 611 us
  waiting for transfers between devices  302 us (49%)
  starting transfers between devices  102 us (16%)
  matrix products  72.7 us (12%)
  Pallas kernels  52.5 us (8%)
  other arithmetic  42 us (7%)
  local copies, waits for them, and re-layouts  36.1 us (6%)
    ppermute x99, waiting for transfers between devices, swap(): return lax.ppermute(value, AXES, [(d, d ^ mask) for d in self.devices])  296 us
    ppermute x99, starting transfers between devices, swap(): return lax.ppermute(value, AXES, [(d, d ^ mask) for d in self.devices])  92.2 us
    dot_general x21, matrix products, matmul(): lax.dot_general(left, right, (dims, ((), ())), preferred_element_type=f32)  72.7 us
    unnamed x209, local copies, waits for them, and re-layouts  24.9 us
    pallas_call x1, Pallas kernels, attend_back(): call(functools.partial(attend_back_kernel, plan), 2, 6, (shape((blocks, B...  18.9 us
    pallas_call x1, Pallas kernels, attend(): call(functools.partial(attend_kernel, plan), 2, 2, (shape((blocks, BLOCK,...  17 us
    convert_element_type x21, other arithmetic, added(): return sum((v.astype(f32) for v in values)).astype(bf16)  14.9 us
  transfers between devices with their start and end apart: 101, of which 45 were waited for; matrix products, arithmetic and copies ran while one was open for 18% of the time, Pallas kernels for 8%

profile of v5, /device:TPU:0, one launch (start us, length us, event | category | flops | bytes accessed | tf_op | source)
XLA Modules:
  0.0 610.9 jit_solution(988504578742831232)
XLA Ops:
  3.9 6.3 %all-to-all-start = ((bf16[8,64,768]{2,1,0:T(8,128)(2,1)}), bf16[8,64,768]{2,1,0:T(8,128)(2,1)}, u32[]{:S(2)}, u32[]{:S(2)}) async-start(bf16[8,64,768]{2,1,0:T(8,128)(2,1)} %shard_map.233), calls=%async_computation | async-start | bytes 1572864 | tf_op jit(solution)/shard_map/all_to_all | solution.py:583
  19.5 5.9 collective-permute-done
  25.4 5.9 all-to-all-done
  36.8 23.6 %collective-permute-done.3.a_lo = bf16[48,2048]{1,0:T(8,128)(2,1)S(1)} collective-permute-done((bf16[48,2048]{1,0:T(8,128)(2,1)S(1)}, bf16[48,2048]{1,0:T(8,128)(2,1)S(1)}, u32[]{:S(2)}, u32[]{:S(2)}) %collective-permute-start.3) | collective-permute-done | bytes 196640 | tf_op jit(solution)/shard_map/ppermute | solution.py:69
  65.6 2.5 collective-permute-start.7
  72.1 13.2 %collective-permute-done.7.a_far = bf16[96,2048]{1,0:T(8,128)(2,1)S(1)} collective-permute-done((bf16[96,2048]{1,0:T(8,128)(2,1)S(1)}, bf16[96,2048]{1,0:T(8,128)(2,1)S(1)}, u32[]{:S(2)}, u32[]{:S(2)}) %collective-permute-start.7) | collective-permute-done | bytes 393248 | tf_op jit(solution)/shard_map/ppermute | solution.py:69
  96.9 4.4 fusion.121
  103.7 3.7 fusion.120
  113.6 7.4 %collective-permute-done.12 = bf16[256,1024]{1,0:T(8,128)(2,1)S(1)} collective-permute-done((bf16[256,1024]{1,0:T(8,128)(2,1)S(1)}, bf16[256,1024]{1,0:T(8,128)(2,1)S(1)}, u32[]{:S(2)}, u32[]{:S(2)}) %collective-permute-start.12) | collective-permute-done | bytes 524320 | tf_op jit(solution)/shard_map/ppermute | solution.py:69
  124.2 2.7 collective-permute-start.16
  129.1 16.6 %collective-permute-done.15 = bf16[512,384]{1,0:T(8,128)(2,1)} collective-permute-done((bf16[512,384]{1,0:T(8,128)(2,1)}, bf16[512,384]{1,0:T(8,128)(2,1)}, u32[]{:S(2)}, u32[]{:S(2)}) %collective-permute-start.15) | collective-permute-done | bytes 393248 | tf_op jit(solution)/shard_map/ppermute | solution.py:69
  145.7 2.7 collective-permute-done.16
  148.4 6.3 %collective-permute-done.17 = bf16[512,384]{1,0:T(8,128)(2,1)} collective-permute-done((bf16[512,384]{1,0:T(8,128)(2,1)}, bf16[512,384]{1,0:T(8,128)(2,1)}, u32[]{:S(2)}, u32[]{:S(2)}) %collective-permute-start.17) | collective-permute-done | bytes 393248 | tf_op jit(solution)/shard_map/ppermute | solution.py:69
  165.2 17.0 %shard_map.240 = (bf16[16,128,128]{2,1,0:T(8,128)(2,1)S(1)}, f32[8,128,256]{2,1,0:T(8,128)S(1)}, f32[8,1,256]{2,1,0:T(1,128)S(1)}, bf16[4096,128]{1,0:T(8,128)(2,1)S(1)}, bf16[4096,128]{1,0:T(8,128)(2,1)S(1)}) custom-call(s32[56]{0:T(128)S(1)} %concatenate.190.info, s32[8]{0:T(128)S(1)} %copy-done.36, bf16[16,128,384]{2,1,0:T(8,128)(2,1)S(1)} %bitcast.281, ...), custom_call_target="tpu_custom_call" | custom-call | flops 4294967296 | bytes 8388608 | tf_op jit(solution)/shard_map/pallas_call | solution.py:463
  192.1 4.9 collective-permute-done.27
  196.9 6.0 collective-permute-done.30
  207.9 2.7 collective-permute-start.31
  210.7 15.6 %collective-permute-done.31 = bf16[2,48,2048]{2,1,0:T(8,128)(2,1)S(1)} collective-permute-done((bf16[2,48,2048]{2,1,0:T(8,128)(2,1)S(1)}, bf16[2,48,2048]{2,1,0:T(8,128)(2,1)S(1)}, u32[]{:S(2)}, u32[]{:S(2)}) %collective-permute-start.31) | collective-permute-done | bytes 393248 | tf_op jit(solution)/shard_map/ppermute | solution.py:69
  226.3 3.4 collective-permute-done.32
  233.0 4.3 collective-permute-done.36
  237.4 11.0 %collective-permute-done.37 = bf16[80,2048]{1,0:T(8,128)(2,1)S(1)} collective-permute-done((bf16[80,2048]{1,0:T(8,128)(2,1)S(1)}, bf16[80,2048]{1,0:T(8,128)(2,1)S(1)}, u32[]{:S(2)}, u32[]{:S(2)}) %collective-permute-start.37) | collective-permute-done | bytes 327712 | tf_op jit(solution)/shard_map/ppermute | solution.py:69
  251.6 2.5 collective-permute-start.41
  254.5 8.3 %collective-permute-done.43 = bf16[128,1024]{1,0:T(8,128)(2,1)S(1)} collective-permute-done((bf16[128,1024]{1,0:T(8,128)(2,1)S(1)}, bf16[128,1024]{1,0:T(8,128)(2,1)S(1)}, u32[]{:S(2)}, u32[]{:S(2)}) %collective-permute-start.43) | collective-permute-done | bytes 262176 | tf_op jit(solution)/shard_map/ppermute | solution.py:69
  262.8 2.8 collective-permute-done.41.b_hi
  267.5 10.8 %collective-permute-done.45.b_far = bf16[128,2048]{1,0:T(8,128)(2,1)S(1)} collective-permute-done((bf16[128,2048]{1,0:T(8,128)(2,1)S(1)}, bf16[128,2048]{1,0:T(8,128)(2,1)S(1)}, u32[]{:S(2)}, u32[]{:S(2)}) %collective-permute-start.45) | collective-permute-done | bytes 524320 | tf_op jit(solution)/shard_map/ppermute | solution.py:69
  279.6 3.3 collective-permute-done.46
  285.2 4.0 multiply_convert_fusion.1
  289.2 4.4 convolution_convert_fusion.2
  293.6 4.5 multiply_convert_fusion
  300.2 7.0 %fusion.6 = bf16[512,1024]{1,0:T(8,128)(2,1)S(1)} fusion(f32[512,1024]{1,0:T(8,128)} %get-tuple-element.674, bf16[512,2048]{1,0:T(8,128)(2,1)} %copy-done.12, bf16[2048,1024]{1,0:T(8,128)(2,1)} %copy-done.76), kind=kOutput, calls=%fused_computation.29 | convolution fusion | flops 2157969408 | bytes 9437184 | tf_op jit(solution)/shard_map/dot_general | solution.py:27
  307.2 2.4 fusion.122
  311.0 3.4 fusion.13
  314.5 2.4 add_convert_fusion.5
  319.1 4.9 fusion.124
  325.7 2.4 fusion.123
  328.1 4.3 add_convert_fusion.1
  333.1 5.9 add_convert_fusion.4
  339.1 4.7 collective-permute-done.51
  348.2 2.4 convolution_convert_fusion.1
  350.7 6.0 collective-permute-done.53
  364.2 5.6 collective-permute-done.56.a_lo
  369.8 9.1 %collective-permute-done.57.b_hi = bf16[80,2048]{1,0:T(8,128)(2,1)S(1)} collective-permute-done((bf16[80,2048]{1,0:T(8,128)(2,1)S(1)}, bf16[80,2048]{1,0:T(8,128)(2,1)S(1)}, u32[]{:S(2)}, u32[]{:S(2)}) %collective-permute-start.57) | collective-permute-done | bytes 327712 | tf_op jit(solution)/shard_map/ppermute | solution.py:69
  383.9 2.4 convolution_convert_fusion
  386.3 14.6 %collective-permute-done.60.a_far = bf16[96,2048]{1,0:T(8,128)(2,1)S(1)} collective-permute-done((bf16[96,2048]{1,0:T(8,128)(2,1)S(1)}, bf16[96,2048]{1,0:T(8,128)(2,1)S(1)}, u32[]{:S(2)}, u32[]{:S(2)}) %collective-permute-start.60) | collective-permute-done | bytes 393248 | tf_op jit(solution)/shard_map/ppermute | solution.py:69
  416.1 4.1 collective-permute-done.66
  426.8 18.9 %shard_map.245 = (bf16[16,128,128]{2,1,0:T(8,128)(2,1)S(1)}, bf16[16,128,256]{2,1,0:T(8,128)(2,1)S(1)}, bf16[1,16,128,256]{3,2,1,0:T(8,128)(2,1)S(1)}) custom-call(s32[56]{0:T(128)S(1)} %concatenate.190.info, s32[8]{0:T(128)S(1)} %copy-done.36, bf16[16,128,384]{2,1,0:T(8,128)(2,1)S(1)} %bitcast.282, bf16[4096,128]{1,0:T(8,128)(2,1)S(1)} %copy-done.40, ...), custom_call_target="tpu_custom_call" | custom-call | flops 10737418240 | bytes 8388608 | tf_op jit(solution)/shard_map/pallas_call | solution.py:485
  446.3 4.6 collective-permute-done.68
  460.3 25.9 %collective-permute-done.77 = bf16[2,64,2048]{2,1,0:T(8,128)(2,1)S(1)} collective-permute-done((bf16[2,64,2048]{2,1,0:T(8,128)(2,1)S(1)}, bf16[2,64,2048]{2,1,0:T(8,128)(2,1)S(1)}, u32[]{:S(2)}, u32[]{:S(2)}) %collective-permute-start.77) | collective-permute-done | bytes 524320 | tf_op jit(solution)/shard_map/ppermute | solution.py:69
  491.4 2.4 shard_map.247
  495.7 4.2 collective-permute-done.81
  500.3 5.0 collective-permute-done.79
  510.9 5.8 fusion.125
  516.7 5.0 add_convert_fusion.3
  522.7 3.2 collective-permute-done.85
  529.9 2.6 collective-permute-start.87
  534.8 14.0 %collective-permute-done.89 = bf16[4,64,1024]{2,1,0:T(8,128)(2,1)S(1)} collective-permute-done((bf16[4,64,1024]{2,1,0:T(8,128)(2,1)S(1)}, bf16[4,64,1024]{2,1,0:T(8,128)(2,1)S(1)}, u32[]{:S(2)}, u32[]{:S(2)}) %collective-permute-start.89) | collective-permute-done | bytes 524320 | tf_op jit(solution)/shard_map/ppermute | solution.py:69
  549.1 5.5 collective-permute-done.88
  556.1 2.5 collective-permute-start.94
  562.9 7.3 %collective-permute-done.94 = bf16[80,2048]{1,0:T(8,128)(2,1)S(1)} collective-permute-done((bf16[80,2048]{1,0:T(8,128)(2,1)S(1)}, bf16[80,2048]{1,0:T(8,128)(2,1)S(1)}, u32[]{:S(2)}, u32[]{:S(2)}) %collective-permute-start.94) | collective-permute-done | bytes 327712 | tf_op jit(solution)/shard_map/ppermute | solution.py:69
  571.5 3.0 collective-permute-done.92
  574.4 7.1 %collective-permute-done.91 = bf16[512,768]{1,0:T(8,128)(2,1)S(1)} collective-permute-done((bf16[512,768]{1,0:T(8,128)(2,1)S(1)}, bf16[512,768]{1,0:T(8,128)(2,1)S(1)}, u32[]{:S(2)}, u32[]{:S(2)}) %collective-permute-start.91) | collective-permute-done | bytes 786464 | tf_op jit(solution)/shard_map/ppermute | solution.py:69
  582.7 3.8 all-to-all-start.1
  591.3 10.3 %collective-permute-done.96 = bf16[64,2048]{1,0:T(8,128)(2,1)S(1)} collective-permute-done((bf16[64,2048]{1,0:T(8,128)(2,1)S(1)}, bf16[64,2048]{1,0:T(8,128)(2,1)S(1)}, u32[]{:S(2)}, u32[]{:S(2)}) %collective-permute-start.96) | collective-permute-done | bytes 262176 | tf_op jit(solution)/shard_map/ppermute | solution.py:69
  602.7 2.4 shard_map.250
  (582 shorter events, 185.5 us)
Async XLA Ops:
  3.9 27.4 %all-to-all-start = ((bf16[8,64,768]{2,1,0:T(8,128)(2,1)}), bf16[8,64,768]{2,1,0:T(8,128)(2,1)}, u32[]{:S(2)}, u32[]{:S(2)}) async-start(bf16[8,64,768]{2,1,0:T(8,128)(2,1)} %shard_map.233), calls=%async_computation | async-start | bytes 1572864 | tf_op jit(solution)/shard_map/all_to_all | solution.py:583
  31.3 29.2 %collective-permute-start.5 = (bf16[4,64,2048]{2,1,0:T(8,128)(2,1)}, bf16[4,64,2048]{2,1,0:T(8,128)(2,1)S(1)}, u32[]{:S(2)}, u32[]{:S(2)}) collective-permute-start(bf16[4,64,2048]{2,1,0:T(8,128)(2,1)} %slice.869), channel_id=1, source_target_pairs={{0,2},{1,3},{2,0},{3,1},{4,6},{5,7},{6,4},{7,5},{8,10},{9,11},{10,... | collective-permute-start | bytes 3145736 | tf_op jit(solution)/shard_map/ppermute | solution.py:69
  32.8 27.7 %collective-permute-start.2 = (bf16[512,768]{1,0:T(8,128)(2,1)}, bf16[512,768]{1,0:T(8,128)(2,1)S(1)}, u32[]{:S(2)}, u32[]{:S(2)}) collective-permute-start(bf16[512,768]{1,0:T(8,128)(2,1)} %bitcast.2), channel_id=1, source_target_pairs={{0,4},{1,5},{2,6},{3,7},{4,0},{5,1},{6,2},{7,3},{8,12},{9,13},{10,... | collective-permute-start | bytes 2359304 | tf_op jit(solution)/shard_map/ppermute | solution.py:69
  34.3 26.2 %collective-permute-start.1 = (bf16[512,768]{1,0:T(8,128)(2,1)}, bf16[512,768]{1,0:T(8,128)(2,1)S(1)}, u32[]{:S(2)}, u32[]{:S(2)}) collective-permute-start(bf16[512,768]{1,0:T(8,128)(2,1)} %bitcast.2), channel_id=1, source_target_pairs={{0,8},{1,9},{2,10},{3,11},{4,12},{5,13},{6,14},{7,15},{8,0},{9,1},... | collective-permute-start | bytes 2359304 | tf_op jit(solution)/shard_map/ppermute | solution.py:69
  34.3 26.1 %collective-permute-start.4 = (bf16[80,2048]{1,0:T(8,128)(2,1)S(1)}, bf16[80,2048]{1,0:T(8,128)(2,1)S(1)}, u32[]{:S(2)}, u32[]{:S(2)}) collective-permute-start(bf16[80,2048]{1,0:T(8,128)(2,1)S(1)} %slice.674.b), channel_id=1, source_target_pairs={{0,16},{1,17},{2,18},{3,19},{4,20},{5,21},{6,22},{7,23},{8,24},{9,... | collective-permute-start | bytes 983048 | tf_op jit(solution)/shard_map/ppermute | solution.py:69
  36.4 24.1 %collective-permute-start.3 = (bf16[48,2048]{1,0:T(8,128)(2,1)S(1)}, bf16[48,2048]{1,0:T(8,128)(2,1)S(1)}, u32[]{:S(2)}, u32[]{:S(2)}) collective-permute-start(bf16[48,2048]{1,0:T(8,128)(2,1)S(1)} %slice.673.a), channel_id=1, source_target_pairs={{0,2},{1,3},{2,0},{3,1},{4,6},{5,7},{6,4},{7,5},{8,10},{9,11},{10,... | collective-permute-start | bytes 589832 | tf_op jit(solution)/shard_map/ppermute | solution.py:69
  61.2 24.0 %collective-permute-start.8 = (bf16[160,2048]{1,0:T(8,128)(2,1)S(1)}, bf16[160,2048]{1,0:T(8,128)(2,1)S(1)}, u32[]{:S(2)}, u32[]{:S(2)}) collective-permute-start(bf16[160,2048]{1,0:T(8,128)(2,1)S(1)} %pad_maximum_fusion.15), channel_id=1, source_target_pairs={{0,2},{1,3},{2,0},{3,1},{4,6},{5,7},{6,4},{7,5},{8,10},{9,11},{10,... | collective-permute-start | bytes 1966088 | tf_op jit(solution)/shard_map/ppermute | solution.py:69
  62.8 22.5 %collective-permute-start.6 = (bf16[512,768]{1,0:T(8,128)(2,1)S(1)}, bf16[512,768]{1,0:T(8,128)(2,1)S(1)}, u32[]{:S(2)}, u32[]{:S(2)}) collective-permute-start(bf16[512,768]{1,0:T(8,128)(2,1)S(1)} %collective-permute-done.1), channel_id=1, source_target_pairs={{0,4},{1,5},{2,6},{3,7},{4,0},{5,1},{6,2},{7,3},{8,12},{9,13},{10,... | collective-permute-start | bytes 2359304 | tf_op jit(solution)/shard_map/ppermute | solution.py:69
  65.6 21.9 %collective-permute-start.10 = (bf16[4,64,1024]{2,1,0:T(8,128)(2,1)S(1)}, bf16[4,64,1024]{2,1,0:T(8,128)(2,1)S(1)}, u32[]{:S(2)}, u32[]{:S(2)}) collective-permute-start(bf16[4,64,1024]{2,1,0:T(8,128)(2,1)S(1)} %bitcast.340), channel_id=1, source_target_pairs={{0,8},{1,9},{2,10},{3,11},{4,12},{5,13},{6,14},{7,15},{8,0},{9,1},... | collective-permute-start | bytes 1572872 | tf_op jit(solution)/shard_map/ppermute | solution.py:69
  65.6 19.7 %collective-permute-start.7 = (bf16[96,2048]{1,0:T(8,128)(2,1)S(1)}, bf16[96,2048]{1,0:T(8,128)(2,1)S(1)}, u32[]{:S(2)}, u32[]{:S(2)}) collective-permute-start(bf16[96,2048]{1,0:T(8,128)(2,1)S(1)} %pad_maximum_fusion.34), channel_id=1, source_target_pairs={{0,16},{1,17},{2,18},{3,19},{4,20},{5,21},{6,22},{7,23},{8,24},{9,... | collective-permute-start | bytes 1179656 | tf_op jit(solution)/shard_map/ppermute | solution.py:69
  90.7 22.2 %collective-permute-start.14 = (bf16[4,64,1024]{2,1,0:T(8,128)(2,1)}, bf16[4,64,1024]{2,1,0:T(8,128)(2,1)S(1)}, u32[]{:S(2)}, u32[]{:S(2)}) collective-permute-start(bf16[4,64,1024]{2,1,0:T(8,128)(2,1)} %bitcast.339), channel_id=1, source_target_pairs={{0,8},{1,9},{2,10},{3,11},{4,12},{5,13},{6,14},{7,15},{8,0},{9,1},... | collective-permute-start | bytes 1572872 | tf_op jit(solution)/shard_map/ppermute | solution.py:69
  93.2 27.9 %collective-permute-start.13 = (bf16[512,1024]{1,0:T(8,128)(2,1)S(1)}, bf16[512,1024]{1,0:T(8,128)(2,1)S(1)}, u32[]{:S(2)}, u32[]{:S(2)}) collective-permute-start(bf16[512,1024]{1,0:T(8,128)(2,1)S(1)} %shard_map.238), channel_id=1, source_target_pairs={{0,4},{1,5},{2,6},{3,7},{4,0},{5,1},{6,2},{7,3},{8,12},{9,13},{10,... | collective-permute-start | bytes 3145736 | tf_op jit(solution)/shard_map/ppermute | solution.py:69
  95.1 25.9 %collective-permute-start.12 = (bf16[256,1024]{1,0:T(8,128)(2,1)S(1)}, bf16[256,1024]{1,0:T(8,128)(2,1)S(1)}, u32[]{:S(2)}, u32[]{:S(2)}) collective-permute-start(bf16[256,1024]{1,0:T(8,128)(2,1)S(1)} %get-tuple-element.641), channel_id=1, source_target_pairs={{0,16},{1,17},{2,18},{3,19},{4,20},{5,21},{6,22},{7,23},{8,24},{9,... | collective-permute-start | bytes 1572872 | tf_op jit(solution)/shard_map/ppermute | solution.py:69
  122.2 32.5 %collective-permute-start.18 = (bf16[256,1024]{1,0:T(8,128)(2,1)}, bf16[256,1024]{1,0:T(8,128)(2,1)S(1)}, u32[]{:S(2)}, u32[]{:S(2)}) collective-permute-start(bf16[256,1024]{1,0:T(8,128)(2,1)} %get-tuple-element.289), channel_id=1, source_target_pairs={{0,16},{1,17},{2,18},{3,19},{4,20},{5,21},{6,22},{7,23},{8,24},{9,... | collective-permute-start | bytes 1572872 | tf_op jit(solution)/shard_map/ppermute | solution.py:69
  122.2 32.5 %collective-permute-start.19 = (bf16[2,64,2048]{2,1,0:T(8,128)(2,1)}, bf16[2,64,2048]{2,1,0:T(8,128)(2,1)}, u32[]{:S(2)}, u32[]{:S(2)}) collective-permute-start(bf16[2,64,2048]{2,1,0:T(8,128)(2,1)} %pad_maximum_fusion.23), channel_id=1, source_target_pairs={{0,4},{1,5},{2,6},{3,7},{4,0},{5,1},{6,2},{7,3},{8,12},{9,13},{10,... | collective-permute-start | bytes 1572872 | tf_op jit(solution)/shard_map/ppermute | solution.py:69
  123.2 22.5 %collective-permute-start.15 = (bf16[512,384]{1,0:T(8,128)(2,1)}, bf16[512,384]{1,0:T(8,128)(2,1)}, u32[]{:S(2)}, u32[]{:S(2)}) collective-permute-start(bf16[512,384]{1,0:T(8,128)(2,1)} %get-tuple-element.285), channel_id=1, source_target_pairs={{0,4},{1,5},{2,6},{3,7},{4,0},{5,1},{6,2},{7,3},{8,12},{9,13},{10,... | collective-permute-start | bytes 1179656 | tf_op jit(solution)/shard_map/ppermute | solution.py:69
  124.2 24.2 %collective-permute-start.16 = (bf16[512,384]{1,0:T(8,128)(2,1)}, bf16[512,384]{1,0:T(8,128)(2,1)}, u32[]{:S(2)}, u32[]{:S(2)}) collective-permute-start(bf16[512,384]{1,0:T(8,128)(2,1)} %get-tuple-element.286), channel_id=1, source_target_pairs={{0,8},{1,9},{2,10},{3,11},{4,12},{5,13},{6,14},{7,15},{8,0},{9,1},... | collective-permute-start | bytes 1179656 | tf_op jit(solution)/shard_map/ppermute | solution.py:69
  126.9 27.8 %collective-permute-start.17 = (bf16[512,384]{1,0:T(8,128)(2,1)}, bf16[512,384]{1,0:T(8,128)(2,1)}, u32[]{:S(2)}, u32[]{:S(2)}) collective-permute-start(bf16[512,384]{1,0:T(8,128)(2,1)} %get-tuple-element.287), channel_id=1, source_target_pairs={{0,12},{1,13},{2,14},{3,15},{4,8},{5,9},{6,10},{7,11},{8,4},{9,5},... | collective-permute-start | bytes 1179656 | tf_op jit(solution)/shard_map/ppermute | solution.py:69
  157.3 24.9 %collective-permute-start.25 = (bf16[64,2048]{1,0:T(8,128)(2,1)S(1)}, bf16[64,2048]{1,0:T(8,128)(2,1)S(1)}, u32[]{:S(2)}, u32[]{:S(2)}) collective-permute-start(bf16[64,2048]{1,0:T(8,128)(2,1)S(1)} %get-tuple-element.332.b), channel_id=1, source_target_pairs={{0,8},{1,9},{2,10},{3,11},{4,12},{5,13},{6,14},{7,15},{8,0},{9,1},... | collective-permute-start | bytes 786440 | tf_op jit(solution)/shard_map/ppermute | solution.py:69
  157.4 26.5 %collective-permute-start.21 = (bf16[256,1024]{1,0:T(8,128)(2,1)S(1)}, bf16[256,1024]{1,0:T(8,128)(2,1)S(1)}, u32[]{:S(2)}, u32[]{:S(2)}) collective-permute-start(bf16[256,1024]{1,0:T(8,128)(2,1)S(1)} %slice.906), channel_id=1, source_target_pairs={{0,16},{1,17},{2,18},{3,19},{4,20},{5,21},{6,22},{7,23},{8,24},{9,... | collective-permute-start | bytes 1572872 | tf_op jit(solution)/shard_map/ppermute | solution.py:69
  159.8 24.2 %collective-permute-start.22 = (bf16[256,1024]{1,0:T(8,128)(2,1)S(1)}, bf16[256,1024]{1,0:T(8,128)(2,1)S(1)}, u32[]{:S(2)}, u32[]{:S(2)}) collective-permute-start(bf16[256,1024]{1,0:T(8,128)(2,1)S(1)} %copy-done.58), channel_id=1, source_target_pairs={{0,4},{1,5},{2,6},{3,7},{4,0},{5,1},{6,2},{7,3},{8,12},{9,13},{10,... | collective-permute-start | bytes 1572872 | tf_op jit(solution)/shard_map/ppermute | solution.py:69
  160.8 24.0 %collective-permute-start.23 = (bf16[256,1024]{1,0:T(8,128)(2,1)S(1)}, bf16[256,1024]{1,0:T(8,128)(2,1)S(1)}, u32[]{:S(2)}, u32[]{:S(2)}) collective-permute-start(bf16[256,1024]{1,0:T(8,128)(2,1)S(1)} %copy-done.60), channel_id=1, source_target_pairs={{0,4},{1,5},{2,6},{3,7},{4,0},{5,1},{6,2},{7,3},{8,12},{9,13},{10,... | collective-permute-start | bytes 1572872 | tf_op jit(solution)/shard_map/ppermute | solution.py:69
  164.0 18.3 %collective-permute-start.24 = (bf16[64,2048]{1,0:T(8,128)(2,1)S(1)}, bf16[64,2048]{1,0:T(8,128)(2,1)S(1)}, u32[]{:S(2)}, u32[]{:S(2)}) collective-permute-start(bf16[64,2048]{1,0:T(8,128)(2,1)S(1)} %get-tuple-element.330.a), channel_id=1, source_target_pairs={{0,2},{1,3},{2,0},{3,1},{4,6},{5,7},{6,4},{7,5},{8,10},{9,11},{10,... | collective-permute-start | bytes 786440 | tf_op jit(solution)/shard_map/ppermute | solution.py:69
  202.9 23.4 %collective-permute-start.35 = (bf16[128,2048]{1,0:T(8,128)(2,1)S(1)}, bf16[128,2048]{1,0:T(8,128)(2,1)S(1)}, u32[]{:S(2)}, u32[]{:S(2)}) collective-permute-start(bf16[128,2048]{1,0:T(8,128)(2,1)S(1)} %pad_maximum_fusion.26), channel_id=1, source_target_pairs={{0,2},{1,3},{2,0},{3,1},{4,6},{5,7},{6,4},{7,5},{8,10},{9,11},{10,... | collective-permute-start | bytes 1572872 | tf_op jit(solution)/shard_map/ppermute | solution.py:69
  204.2 22.2 %collective-permute-start.34 = (bf16[128,2048]{1,0:T(8,128)(2,1)S(1)}, bf16[128,2048]{1,0:T(8,128)(2,1)S(1)}, u32[]{:S(2)}, u32[]{:S(2)}) collective-permute-start(bf16[128,2048]{1,0:T(8,128)(2,1)S(1)} %pad_maximum_fusion.25), channel_id=1, source_target_pairs={{0,8},{1,9},{2,10},{3,11},{4,12},{5,13},{6,14},{7,15},{8,0},{9,1},... | collective-permute-start | bytes 1572872 | tf_op jit(solution)/shard_map/ppermute | solution.py:69
  204.3 22.0 %collective-permute-start.33 = (bf16[320,1024]{1,0:T(8,128)(2,1)S(1)}, bf16[320,1024]{1,0:T(8,128)(2,1)S(1)}, u32[]{:S(2)}, u32[]{:S(2)}) collective-permute-start(bf16[320,1024]{1,0:T(8,128)(2,1)S(1)} %slice.730), channel_id=1, source_target_pairs={{0,4},{1,5},{2,6},{3,7},{4,0},{5,1},{6,2},{7,3},{8,12},{9,13},{10,... | collective-permute-start | bytes 1966088 | tf_op jit(solution)/shard_map/ppermute | solution.py:69
  207.4 22.3 %collective-permute-start.32 = (bf16[2,80,2048]{2,1,0:T(8,128)(2,1)S(1)}, bf16[2,80,2048]{2,1,0:T(8,128)(2,1)S(1)}, u32[]{:S(2)}, u32[]{:S(2)}) collective-permute-start(bf16[2,80,2048]{2,1,0:T(8,128)(2,1)S(1)} %pad_maximum_fusion.17), channel_id=1, source_target_pairs={{0,2},{1,3},{2,0},{3,1},{4,6},{5,7},{6,4},{7,5},{8,10},{9,11},{10,... | collective-permute-start | bytes 1966088 | tf_op jit(solution)/shard_map/ppermute | solution.py:69
  207.9 18.4 %collective-permute-start.31 = (bf16[2,48,2048]{2,1,0:T(8,128)(2,1)S(1)}, bf16[2,48,2048]{2,1,0:T(8,128)(2,1)S(1)}, u32[]{:S(2)}, u32[]{:S(2)}) collective-permute-start(bf16[2,48,2048]{2,1,0:T(8,128)(2,1)S(1)} %get-tuple-element.570), channel_id=1, source_target_pairs={{0,16},{1,17},{2,18},{3,19},{4,20},{5,21},{6,22},{7,23},{8,24},{9,... | collective-permute-start | bytes 1179656 | tf_op jit(solution)/shard_map/ppermute | solution.py:69
  229.7 18.9 %collective-permute-start.39 = (bf16[2048,1024]{1,0:T(8,128)(2,1)S(1)}, bf16[2048,1024]{1,0:T(8,128)(2,1)S(1)}, u32[]{:S(2)}, u32[]{:S(2)}) collective-permute-start(bf16[2048,1024]{1,0:T(8,128)(2,1)S(1)} %constant_dynamic-update-slice_fusion.4), channel_id=1, source_target_pairs={{0,1},{1,0},{2,3},{3,2},{4,5},{5,4},{6,7},{7,6},{8,9},{9,8},{10,11... | collective-permute-start | bytes 12582920 | tf_op jit(solution)/shard_map/ppermute | solution.py:69
  231.2 17.2 %collective-permute-start.37 = (bf16[80,2048]{1,0:T(8,128)(2,1)S(1)}, bf16[80,2048]{1,0:T(8,128)(2,1)S(1)}, u32[]{:S(2)}, u32[]{:S(2)}) collective-permute-start(bf16[80,2048]{1,0:T(8,128)(2,1)S(1)} %fusion.43), channel_id=1, source_target_pairs={{0,16},{1,17},{2,18},{3,19},{4,20},{5,21},{6,22},{7,23},{8,24},{9,... | collective-permute-start | bytes 983048 | tf_op jit(solution)/shard_map/ppermute | solution.py:69
  231.3 17.3 %collective-permute-start.38 = (bf16[192,1024]{1,0:T(8,128)(2,1)S(1)}, bf16[192,1024]{1,0:T(8,128)(2,1)S(1)}, u32[]{:S(2)}, u32[]{:S(2)}) collective-permute-start(bf16[192,1024]{1,0:T(8,128)(2,1)S(1)} %slice.739), channel_id=1, source_target_pairs={{0,4},{1,5},{2,6},{3,7},{4,0},{5,1},{6,2},{7,3},{8,12},{9,13},{10,... | collective-permute-start | bytes 1179656 | tf_op jit(solution)/shard_map/ppermute | solution.py:69
  248.7 16.8 %collective-permute-start.42 = (bf16[160,1024]{1,0:T(8,128)(2,1)S(1)}, bf16[160,1024]{1,0:T(8,128)(2,1)S(1)}, u32[]{:S(2)}, u32[]{:S(2)}) collective-permute-start(bf16[160,1024]{1,0:T(8,128)(2,1)S(1)} %slice.742), channel_id=1, source_target_pairs={{0,4},{1,5},{2,6},{3,7},{4,0},{5,1},{6,2},{7,3},{8,12},{9,13},{10,... | collective-permute-start | bytes 983048 | tf_op jit(solution)/shard_map/ppermute | solution.py:69
  300.2 16.7 %collective-permute-start.48 = (bf16[2048,1024]{1,0:T(8,128)(2,1)}, bf16[2048,1024]{1,0:T(8,128)(2,1)}, u32[]{:S(2)}, u32[]{:S(2)}) collective-permute-start(bf16[2048,1024]{1,0:T(8,128)(2,1)} %convolution_convert_fusion.2), channel_id=1, source_target_pairs={{0,1},{1,0},{2,3},{3,2},{4,5},{5,4},{6,7},{7,6},{8,9},{9,8},{10,11... | collective-permute-start | bytes 12582920 | tf_op jit(solution)/shard_map/ppermute | solution.py:69
  324.0 19.8 %collective-permute-start.50 = (bf16[2,64,2048]{2,1,0:T(8,128)(2,1)S(1)}, bf16[2,64,2048]{2,1,0:T(8,128)(2,1)S(1)}, u32[]{:S(2)}, u32[]{:S(2)}) collective-permute-start(bf16[2,64,2048]{2,1,0:T(8,128)(2,1)S(1)} %pad_maximum_fusion.30), channel_id=1, source_target_pairs={{0,2},{1,3},{2,0},{3,1},{4,6},{5,7},{6,4},{7,5},{8,10},{9,11},{10,... | collective-permute-start | bytes 1572872 | tf_op jit(solution)/shard_map/ppermute | solution.py:69
  325.7 18.1 %collective-permute-start.49 = (bf16[2,64,2048]{2,1,0:T(8,128)(2,1)S(1)}, bf16[2,64,2048]{2,1,0:T(8,128)(2,1)S(1)}, u32[]{:S(2)}, u32[]{:S(2)}) collective-permute-start(bf16[2,64,2048]{2,1,0:T(8,128)(2,1)S(1)} %get-tuple-element.564), channel_id=1, source_target_pairs={{0,8},{1,9},{2,10},{3,11},{4,12},{5,13},{6,14},{7,15},{8,0},{9,1},... | collective-permute-start | bytes 1572872 | tf_op jit(solution)/shard_map/ppermute | solution.py:69
  357.1 21.9 %collective-permute-start.59 = (bf16[2048,1024]{1,0:T(8,128)(2,1)S(1)}, bf16[2048,1024]{1,0:T(8,128)(2,1)S(1)}, u32[]{:S(2)}, u32[]{:S(2)}) collective-permute-start(bf16[2048,1024]{1,0:T(8,128)(2,1)S(1)} %convolution_convert_fusion.1), channel_id=1, source_target_pairs={{0,1},{1,0},{2,3},{3,2},{4,5},{5,4},{6,7},{7,6},{8,9},{9,8},{10,11... | collective-permute-start | bytes 12582920 | tf_op jit(solution)/shard_map/ppermute | solution.py:69
  357.7 21.2 %collective-permute-start.58 = (bf16[320,1024]{1,0:T(8,128)(2,1)S(1)}, bf16[320,1024]{1,0:T(8,128)(2,1)S(1)}, u32[]{:S(2)}, u32[]{:S(2)}) collective-permute-start(bf16[320,1024]{1,0:T(8,128)(2,1)S(1)} %pad_maximum_fusion.18), channel_id=1, source_target_pairs={{0,4},{1,5},{2,6},{3,7},{4,0},{5,1},{6,2},{7,3},{8,12},{9,13},{10,... | collective-permute-start | bytes 1966088 | tf_op jit(solution)/shard_map/ppermute | solution.py:69
  361.2 17.7 %collective-permute-start.57 = (bf16[80,2048]{1,0:T(8,128)(2,1)S(1)}, bf16[80,2048]{1,0:T(8,128)(2,1)S(1)}, u32[]{:S(2)}, u32[]{:S(2)}) collective-permute-start(bf16[80,2048]{1,0:T(8,128)(2,1)S(1)} %slice.925.b), channel_id=1, source_target_pairs={{0,16},{1,17},{2,18},{3,19},{4,20},{5,21},{6,22},{7,23},{8,24},{9,... | collective-permute-start | bytes 983048 | tf_op jit(solution)/shard_map/ppermute | solution.py:69
  379.0 22.0 %collective-permute-start.61 = (bf16[160,2048]{1,0:T(8,128)(2,1)S(1)}, bf16[160,2048]{1,0:T(8,128)(2,1)S(1)}, u32[]{:S(2)}, u32[]{:S(2)}) collective-permute-start(bf16[160,2048]{1,0:T(8,128)(2,1)S(1)} %pad_maximum_fusion.19), channel_id=1, source_target_pairs={{0,2},{1,3},{2,0},{3,1},{4,6},{5,7},{6,4},{7,5},{8,10},{9,11},{10,... | collective-permute-start | bytes 1966088 | tf_op jit(solution)/shard_map/ppermute | solution.py:69
  380.2 20.8 %collective-permute-start.62 = (bf16[320,1024]{1,0:T(8,128)(2,1)S(1)}, bf16[320,1024]{1,0:T(8,128)(2,1)S(1)}, u32[]{:S(2)}, u32[]{:S(2)}) collective-permute-start(bf16[320,1024]{1,0:T(8,128)(2,1)S(1)} %slice_bitcast_fusion.5), channel_id=1, source_target_pairs={{0,4},{1,5},{2,6},{3,7},{4,0},{5,1},{6,2},{7,3},{8,12},{9,13},{10,... | collective-permute-start | bytes 1966088 | tf_op jit(solution)/shard_map/ppermute | solution.py:69
  382.5 18.5 %collective-permute-start.60 = (bf16[96,2048]{1,0:T(8,128)(2,1)S(1)}, bf16[96,2048]{1,0:T(8,128)(2,1)S(1)}, u32[]{:S(2)}, u32[]{:S(2)}) collective-permute-start(bf16[96,2048]{1,0:T(8,128)(2,1)S(1)} %pad_maximum_fusion.35), channel_id=1, source_target_pairs={{0,16},{1,17},{2,18},{3,19},{4,20},{5,21},{6,22},{7,23},{8,24},{9,... | collective-permute-start | bytes 1179656 | tf_op jit(solution)/shard_map/ppermute | solution.py:69
  421.5 29.4 %collective-permute-start.68 = (bf16[320,1024]{1,0:T(8,128)(2,1)S(1)}, bf16[320,1024]{1,0:T(8,128)(2,1)S(1)}, u32[]{:S(2)}, u32[]{:S(2)}) collective-permute-start(bf16[320,1024]{1,0:T(8,128)(2,1)S(1)} %fusion.22), channel_id=1, source_target_pairs={{0,16},{1,17},{2,18},{3,19},{4,20},{5,21},{6,22},{7,23},{8,24},{9,... | collective-permute-start | bytes 1966088 | tf_op jit(solution)/shard_map/ppermute | solution.py:69
  421.9 24.4 %collective-permute-start.70 = (bf16[2,64,2048]{2,1,0:T(8,128)(2,1)S(1)}, bf16[2,64,2048]{2,1,0:T(8,128)(2,1)S(1)}, u32[]{:S(2)}, u32[]{:S(2)}) collective-permute-start(bf16[2,64,2048]{2,1,0:T(8,128)(2,1)S(1)} %pad_maximum_fusion.33), channel_id=1, source_target_pairs={{0,2},{1,3},{2,0},{3,1},{4,6},{5,7},{6,4},{7,5},{8,10},{9,11},{10,... | collective-permute-start | bytes 1572872 | tf_op jit(solution)/shard_map/ppermute | solution.py:69
  423.1 23.3 %collective-permute-start.69 = (bf16[2,64,2048]{2,1,0:T(8,128)(2,1)S(1)}, bf16[2,64,2048]{2,1,0:T(8,128)(2,1)S(1)}, u32[]{:S(2)}, u32[]{:S(2)}) collective-permute-start(bf16[2,64,2048]{2,1,0:T(8,128)(2,1)S(1)} %get-tuple-element.558), channel_id=1, source_target_pairs={{0,8},{1,9},{2,10},{3,11},{4,12},{5,13},{6,14},{7,15},{8,0},{9,1},... | collective-permute-start | bytes 1572872 | tf_op jit(solution)/shard_map/ppermute | solution.py:69
  425.2 25.8 %collective-permute-start.67 = (bf16[512,1024]{1,0:T(8,128)(2,1)S(1)}, bf16[512,1024]{1,0:T(8,128)(2,1)S(1)}, u32[]{:S(2)}, u32[]{:S(2)}) collective-permute-start(bf16[512,1024]{1,0:T(8,128)(2,1)S(1)} %slice_bitcast_fusion), channel_id=1, source_target_pairs={{0,4},{1,5},{2,6},{3,7},{4,0},{5,1},{6,2},{7,3},{8,12},{9,13},{10,... | collective-permute-start | bytes 3145736 | tf_op jit(solution)/shard_map/ppermute | solution.py:69
  425.8 20.0 %collective-permute-start.71 = (bf16[4,64,2048]{2,1,0:T(8,128)(2,1)S(1)}, bf16[4,64,2048]{2,1,0:T(8,128)(2,1)S(1)}, u32[]{:S(2)}, u32[]{:S(2)}) collective-permute-start(bf16[4,64,2048]{2,1,0:T(8,128)(2,1)S(1)} %broadcast_select_fusion), channel_id=1, source_target_pairs={{0,1},{1,0},{2,3},{3,2},{4,5},{5,4},{6,7},{7,6},{8,9},{9,8},{10,11... | collective-permute-start | bytes 3145736 | tf_op jit(solution)/shard_map/ppermute | solution.py:69
  454.4 32.7 %collective-permute-start.75 = (bf16[512,384]{1,0:T(8,128)(2,1)S(1)}, bf16[512,384]{1,0:T(8,128)(2,1)S(1)}, u32[]{:S(2)}, u32[]{:S(2)}) collective-permute-start(bf16[512,384]{1,0:T(8,128)(2,1)S(1)} %get-tuple-element.586), channel_id=1, source_target_pairs={{0,12},{1,13},{2,14},{3,15},{4,8},{5,9},{6,10},{7,11},{8,4},{9,5},... | collective-permute-start | bytes 1179656 | tf_op jit(solution)/shard_map/ppermute | solution.py:69
  454.5 32.6 %collective-permute-start.74 = (bf16[512,384]{1,0:T(8,128)(2,1)S(1)}, bf16[512,384]{1,0:T(8,128)(2,1)S(1)}, u32[]{:S(2)}, u32[]{:S(2)}) collective-permute-start(bf16[512,384]{1,0:T(8,128)(2,1)S(1)} %get-tuple-element.587), channel_id=1, source_target_pairs={{0,8},{1,9},{2,10},{3,11},{4,12},{5,13},{6,14},{7,15},{8,0},{9,1},... | collective-permute-start | bytes 1179656 | tf_op jit(solution)/shard_map/ppermute | solution.py:69
  456.6 30.6 %collective-permute-start.73 = (bf16[512,384]{1,0:T(8,128)(2,1)S(1)}, bf16[512,384]{1,0:T(8,128)(2,1)S(1)}, u32[]{:S(2)}, u32[]{:S(2)}) collective-permute-start(bf16[512,384]{1,0:T(8,128)(2,1)S(1)} %get-tuple-element.588), channel_id=1, source_target_pairs={{0,4},{1,5},{2,6},{3,7},{4,0},{5,1},{6,2},{7,3},{8,12},{9,13},{10,... | collective-permute-start | bytes 1179656 | tf_op jit(solution)/shard_map/ppermute | solution.py:69
  458.0 29.2 %collective-permute-start.76 = (bf16[192,1024]{1,0:T(8,128)(2,1)S(1)}, bf16[192,1024]{1,0:T(8,128)(2,1)S(1)}, u32[]{:S(2)}, u32[]{:S(2)}) collective-permute-start(bf16[192,1024]{1,0:T(8,128)(2,1)S(1)} %slice.936), channel_id=1, source_target_pairs={{0,16},{1,17},{2,18},{3,19},{4,20},{5,21},{6,22},{7,23},{8,24},{9,... | collective-permute-start | bytes 1179656 | tf_op jit(solution)/shard_map/ppermute | solution.py:69
  458.3 27.9 %collective-permute-start.77 = (bf16[2,64,2048]{2,1,0:T(8,128)(2,1)S(1)}, bf16[2,64,2048]{2,1,0:T(8,128)(2,1)S(1)}, u32[]{:S(2)}, u32[]{:S(2)}) collective-permute-start(bf16[2,64,2048]{2,1,0:T(8,128)(2,1)S(1)} %slice_bitcast_fusion.6), channel_id=1, source_target_pairs={{0,4},{1,5},{2,6},{3,7},{4,0},{5,1},{6,2},{7,3},{8,12},{9,13},{10,... | collective-permute-start | bytes 1572872 | tf_op jit(solution)/shard_map/ppermute | solution.py:69
  487.9 17.3 %collective-permute-start.79 = (bf16[160,1024]{1,0:T(8,128)(2,1)S(1)}, bf16[160,1024]{1,0:T(8,128)(2,1)S(1)}, u32[]{:S(2)}, u32[]{:S(2)}) collective-permute-start(bf16[160,1024]{1,0:T(8,128)(2,1)S(1)} %get-tuple-element.454), channel_id=1, source_target_pairs={{0,16},{1,17},{2,18},{3,19},{4,20},{5,21},{6,22},{7,23},{8,24},{9,... | collective-permute-start | bytes 983048 | tf_op jit(solution)/shard_map/ppermute | solution.py:69
  505.2 21.9 %collective-permute-start.84 = (bf16[160,1024]{1,0:T(8,128)(2,1)S(1)}, bf16[160,1024]{1,0:T(8,128)(2,1)S(1)}, u32[]{:S(2)}, u32[]{:S(2)}) collective-permute-start(bf16[160,1024]{1,0:T(8,128)(2,1)S(1)} %get-tuple-element.467), channel_id=1, source_target_pairs={{0,16},{1,17},{2,18},{3,19},{4,20},{5,21},{6,22},{7,23},{8,24},{9,... | collective-permute-start | bytes 983048 | tf_op jit(solution)/shard_map/ppermute | solution.py:69
  505.2 21.9 %collective-permute-start.83 = (bf16[256,1024]{1,0:T(8,128)(2,1)S(1)}, bf16[256,1024]{1,0:T(8,128)(2,1)S(1)}, u32[]{:S(2)}, u32[]{:S(2)}) collective-permute-start(bf16[256,1024]{1,0:T(8,128)(2,1)S(1)} %get-tuple-element.465), channel_id=1, source_target_pairs={{0,4},{1,5},{2,6},{3,7},{4,0},{5,1},{6,2},{7,3},{8,12},{9,13},{10,... | collective-permute-start | bytes 1572872 | tf_op jit(solution)/shard_map/ppermute | solution.py:69
  506.2 19.8 %collective-permute-start.85 = (bf16[4,64,1024]{2,1,0:T(8,128)(2,1)S(1)}, bf16[4,64,1024]{2,1,0:T(8,128)(2,1)S(1)}, u32[]{:S(2)}, u32[]{:S(2)}) collective-permute-start(bf16[4,64,1024]{2,1,0:T(8,128)(2,1)S(1)} %get-tuple-element.469), channel_id=1, source_target_pairs={{0,8},{1,9},{2,10},{3,11},{4,12},{5,13},{6,14},{7,15},{8,0},{9,1},... | collective-permute-start | bytes 1572872 | tf_op jit(solution)/shard_map/ppermute | solution.py:69
  508.8 17.4 %collective-permute-start.82 = (bf16[2048,768]{1,0:T(8,128)(2,1)S(1)}, bf16[2048,768]{1,0:T(8,128)(2,1)S(1)}, u32[]{:S(2)}, u32[]{:S(2)}) collective-permute-start(bf16[2048,768]{1,0:T(8,128)(2,1)S(1)} %convolution_convert_fusion.4), channel_id=1, source_target_pairs={{0,1},{1,0},{2,3},{3,2},{4,5},{5,4},{6,7},{7,6},{8,9},{9,8},{10,11... | collective-permute-start | bytes 9437192 | tf_op jit(solution)/shard_map/ppermute | solution.py:69
  528.7 20.1 %collective-permute-start.89 = (bf16[4,64,1024]{2,1,0:T(8,128)(2,1)S(1)}, bf16[4,64,1024]{2,1,0:T(8,128)(2,1)S(1)}, u32[]{:S(2)}, u32[]{:S(2)}) collective-permute-start(bf16[4,64,1024]{2,1,0:T(8,128)(2,1)S(1)} %get-tuple-element.480), channel_id=1, source_target_pairs={{0,8},{1,9},{2,10},{3,11},{4,12},{5,13},{6,14},{7,15},{8,0},{9,1},... | collective-permute-start | bytes 1572872 | tf_op jit(solution)/shard_map/ppermute | solution.py:69
  528.8 20.2 %collective-permute-start.90 = (bf16[2,2,64,1024]{3,2,0,1:T(8,128)(2,1)S(1)}, bf16[2,2,64,1024]{3,2,0,1:T(8,128)(2,1)S(1)}, u32[]{:S(2)}, u32[]{:S(2)}) collective-permute-start(bf16[2,2,64,1024]{3,2,0,1:T(8,128)(2,1)S(1)} %fusion.37), channel_id=1, source_target_pairs={{0,2},{1,3},{2,0},{3,1},{4,6},{5,7},{6,4},{7,5},{8,10},{9,11},{10,... | collective-permute-start | bytes 1572872 | tf_op jit(solution)/shard_map/ppermute | solution.py:69
  529.9 19.2 %collective-permute-start.87 = (bf16[2,48,2048]{2,1,0:T(8,128)(2,1)S(1)}, bf16[2,48,2048]{2,1,0:T(8,128)(2,1)S(1)}, u32[]{:S(2)}, u32[]{:S(2)}) collective-permute-start(bf16[2,48,2048]{2,1,0:T(8,128)(2,1)S(1)} %get-tuple-element.552), channel_id=1, source_target_pairs={{0,16},{1,17},{2,18},{3,19},{4,20},{5,21},{6,22},{7,23},{8,24},{9,... | collective-permute-start | bytes 1179656 | tf_op jit(solution)/shard_map/ppermute | solution.py:69
  532.6 22.1 %collective-permute-start.88 = (bf16[2,80,2048]{2,1,0:T(8,128)(2,1)S(1)}, bf16[2,80,2048]{2,1,0:T(8,128)(2,1)S(1)}, u32[]{:S(2)}, u32[]{:S(2)}) collective-permute-start(bf16[2,80,2048]{2,1,0:T(8,128)(2,1)S(1)} %pad_maximum_fusion.21), channel_id=1, source_target_pairs={{0,2},{1,3},{2,0},{3,1},{4,6},{5,7},{6,4},{7,5},{8,10},{9,11},{10,... | collective-permute-start | bytes 1966088 | tf_op jit(solution)/shard_map/ppermute | solution.py:69
  533.6 21.0 %collective-permute-start.86 = (bf16[512,768]{1,0:T(8,128)(2,1)S(1)}, bf16[512,768]{1,0:T(8,128)(2,1)S(1)}, u32[]{:S(2)}, u32[]{:S(2)}) collective-permute-start(bf16[512,768]{1,0:T(8,128)(2,1)S(1)} %slice_bitcast_fusion.4), channel_id=1, source_target_pairs={{0,4},{1,5},{2,6},{3,7},{4,0},{5,1},{6,2},{7,3},{8,12},{9,13},{10,... | collective-permute-start | bytes 2359304 | tf_op jit(solution)/shard_map/ppermute | solution.py:69
  560.7 20.8 %collective-permute-start.91 = (bf16[512,768]{1,0:T(8,128)(2,1)S(1)}, bf16[512,768]{1,0:T(8,128)(2,1)S(1)}, u32[]{:S(2)}, u32[]{:S(2)}) collective-permute-start(bf16[512,768]{1,0:T(8,128)(2,1)S(1)} %fusion.21), channel_id=1, source_target_pairs={{0,8},{1,9},{2,10},{3,11},{4,12},{5,13},{6,14},{7,15},{8,0},{9,1},... | collective-permute-start | bytes 2359304 | tf_op jit(solution)/shard_map/ppermute | solution.py:69
  582.7 25.1 %all-to-all-start.1 = ((bf16[8,64,768]{2,1,0:T(8,128)(2,1)}), bf16[8,64,768]{2,1,0:T(8,128)(2,1)S(1)}, u32[]{:S(2)}, u32[]{:S(2)}) async-start(bf16[8,64,768]{2,1,0:T(8,128)(2,1)} %bitcast.315), calls=%async_computation.1 | async-start | bytes 1572864 | tf_op jit(solution)/shard_map/all_to_all | solution.py:583
  587.9 17.2 %collective-permute-start.98 = (bf16[2,2,64,1024]{3,2,1,0:T(8,128)(2,1)S(1)}, bf16[2,2,64,1024]{3,2,1,0:T(8,128)(2,1)S(1)}, u32[]{:S(2)}, u32[]{:S(2)}) collective-permute-start(bf16[2,2,64,1024]{3,2,1,0:T(8,128)(2,1)S(1)} %get-tuple-element.611), channel_id=1, source_target_pairs={{0,1},{1,0},{2,3},{3,2},{4,5},{5,4},{6,7},{7,6},{8,9},{9,8},{10,11... | collective-permute-start | bytes 1572872 | tf_op jit(solution)/shard_map/ppermute | solution.py:69
  (135 other events, 1202.4 us)

commit v6 on v5

--- a/solution.py
+++ b/solution.py
@@ -649,8 +649,9 @@
     grad_rel = feed.to_rel(cotangent[0], False)
     qkv_block = attn.octet(qkv_sent).reshape(8 * shard, -1)
     out_z = swap(w_out, attn.first)
-    qkv_block, first_rel, grad_rel, feed_sent, feed_send, out_z, w_out = tied(
-        qkv_block, first_rel, grad_rel, feed_sent, feed_sent[4:], out_z, w_out
+    grad_near = feed.gather_one(grad_rel)
+    qkv_block, first_rel, grad_near, feed_sent, feed_send, out_z, w_out = tied(
+        qkv_block, first_rel, grad_near, feed_sent, feed_sent[4:], out_z, w_out
     )
     first_near = attn.gather_one(first_rel)
     qkv_first = swap(qkv_block, attn.first)
@@ -668,8 +669,8 @@
         for h in range(2)
     )
     up_got = swap(up_send, feed.team_hi)
-    qkv_both, first_far, up_got, up_kept, down_kept, down_send, grad_rel = tied(
-        qkv_both, first_far, up_got, up_kept, down_kept, down_send, grad_rel
+    qkv_both, first_far, up_got, up_kept, down_kept, down_send, grad_near = tied(
+        qkv_both, first_far, up_got, up_kept, down_kept, down_send, grad_near
     )
     down_got = swap(down_send, feed.team_hi)
     up_block = settle(by_hi_core_lo, up_kept, up_got)
@@ -722,22 +723,22 @@
     pick = [(my_head ^ r) ^ core_flip for r in range(4)]
     sent = [lax.dynamic_index_in_dim(stack, pick[r], 0, keepdims=False) for r in range(4)]
     out_pair = jnp.stack([w_out, out_z])
-    sent, up_z, up_x, grad_rel, up_block, up_part, down_got, down_kept, out_pair = tied(
-        sent, up_z, up_x, grad_rel, up_block, up_block[cut_up:], down_got, down_kept, out_pair
+    sent, up_z, up_x, grad_near, up_block, up_part, down_got, down_kept, out_pair = tied(
+        sent, up_z, up_x, grad_near, up_block, up_block[cut_up:], down_got, down_kept, out_pair
     )
     got = [swap(sent[r], plan.head_rel[r]) for r in range(1, 4)]
     up_z += [swap(up_part, feed.first)]
     out_x = swap(out_pair, attn.second)
-    cut_z = [0, n_block // 2, n_block * 3 // 4, n_block]
+    cut_z = [0, n_block // 2, n_block * 3 // 4, n_block * 15 // 16, n_block]
     down_block = settle(by_hi_core_lo, down_kept, down_got)
-    got, up_z, down_block, grad_rel, out_x, down_first = tied(
-        got, up_z, down_block, grad_rel, out_x, down_block[: cut_z[1]]
+    got, up_z, down_block, grad_near, out_x, down_first = tied(
+        got, up_z, down_block, grad_near, out_x, down_block[: cut_z[1]]
     )
     up_za, up_zb = up_z
     own = jnp.stack([sent[0]] + got).reshape(16, rows, 3 * HEAD)
     down_z = [swap(down_first, feed.first)]
     up_both = [swap(up_za, feed.second), swap(up_zb, feed.second)]
-    grad_near = feed.gather_one(grad_rel)
+    grad_far = feed.gather_two(*grad_near)
     shared = own[:, :, HEAD:]
     other = jnp.stack([swap(shared, rel) for rel in plan.part_rel[1:]])
 
@@ -759,14 +760,13 @@
 
     attended, attended_t, log_total, keys, values = attend(plan, info, frame_real, own, other)
     w_team = jnp.stack([w_out, out_x[0], out_z, out_x[1]])
-    attended, down_z, up_both, grad_near, w_team, down_block, up_x, up_za, up_zb, up_block = tied(
-        attended, down_z, up_both, grad_near, w_team, down_block, up_x, up_za, up_zb, up_block
+    attended, down_z, up_both, grad_far, w_team, down_block, up_x, up_za, up_zb, up_block = tied(
+        attended, down_z, up_both, grad_far, w_team, down_block, up_x, up_za, up_zb, up_block
     )
     w_got = swap(w_team, plan.parts[-1])
     attended = attended.reshape(4, 4 * rows, HEAD)
     heads_got = [swap(attended[r], plan.head_rel[r]) for r in range(1, 4)]
     down_z += [swap(down_block[cut_z[1] : cut_z[2]], feed.first)]
-    up_mine = feed.joined(up_block, up_za, up_zb, up_x, *up_both)
     for bit in reversed(plan.parts):
         w_got = w_got if bit == plan.parts[-1] else swap(w_team, bit)
         w_team = jnp.where(
@@ -775,34 +775,55 @@
             jnp.concatenate([w_team, w_got], axis=1),
         )
     w_team = w_team.reshape(4 * HEAD, width)
-    heads_got, w_team, down_z, grad_near, down_block, up_mine = tied(
-        heads_got, w_team, down_z, grad_near, down_block, up_mine
+    cut_x = n_block * 5 // 8
+    heads_got, w_team, down_z, grad_far, down_block, down_part, up_both, up_block = tied(
+        heads_got, w_team, down_z, grad_far, down_block, down_block[:cut_x], up_both, up_block
     )
     attended_team = jnp.concatenate([attended[0]] + heads_got, axis=1)
     branch = matmul(attended_team, w_team).astype(bf16)
     branch_near = attn.scatter_one(branch)
-    cut_x = n_block * 5 // 8
-    down_x = [swap(down_block[:cut_x], feed.second)]
-    grad_far = feed.gather_two(*grad_near)
-    branch_near, down_x, up_mine, down_z, grad_far, down_block = tied(
-        branch_near, down_x, up_mine, down_z, grad_far, down_block
+    down_x = [swap(down_part, feed.second)]
+    up_mine = feed.joined(up_block, up_za, up_zb, up_x, *up_both)
+    cuts = [0, n_block * 5 // 16, n_block * 9 // 16, n_block * 15 // 16, n_block]
+    branch_near, down_x, up_mine, down_z, grad_far, down_block, down_part, both_part = tied(
+        branch_near,
+        down_x,
+        up_mine,
+        down_z,
+        grad_far,
+        down_block,
+        down_block[cut_x:],
+        down_z[0][: cuts[1]],
     )
     middle = attn.scatter_two(*branch_near)
-    down_x += [swap(down_block[cut_x:], feed.second)]
+    down_x += [swap(down_part, feed.second)]
+    down_both = [swap(both_part, feed.second)]
     up_other = swap(up_mine, 1)
     grad_all = team_rows(*grad_near, *grad_far)
-    middle, down_x, down_z, down_block, up_other, grad_all = tied(
-        middle, down_x, down_z, down_block, up_other, grad_all
+    both_part = jnp.concatenate(down_z)[cuts[1] : cuts[2]]
+    middle, down_x, down_z, down_block, up_other, grad_all, down_both, both_part, down_part = tied(
+        middle,
+        down_x,
+        down_z,
+        down_block,
+        up_other,
+        grad_all,
+        down_both,
+        both_part,
+        down_block[cut_z[2] : cut_z[3]],
     )
     middle = inputs + middle
     second_near = feed.gather_one(feed.to_rel(middle, True))
-    down_z += [swap(down_block[cut_z[2] :], feed.first)]
-    cut_both = n_block * 5 // 16
-    down_both = [swap(down_z[0][:cut_both], feed.second)]
-    second_near, down_both, down_z = tied(second_near, down_both, down_z)
+    down_z += [swap(down_part, feed.first)]
+    down_both += [swap(both_part, feed.second)]
+    second_near, down_both, down_z, down_part = tied(
+        second_near, down_both, down_z, down_block[cut_z[3] :]
+    )
     second_far = feed.gather_two(*second_near)
+    both_part = jnp.concatenate(down_z)[cuts[2] : cuts[3]]
+    down_z += [swap(down_part, feed.first)]
+    down_both += [swap(both_part, feed.second), swap(down_z[-1], feed.second)]
     down_z = jnp.concatenate(down_z)
-    down_both += [swap(down_z[cut_both:], feed.second)]
     second_far, down_both, down_z = tied(second_far, down_both, down_z)
     down_mine = feed.joined(down_block, down_z, *down_x, *down_both)
     down_other = swap(down_mine, 1)
@@ -830,16 +851,11 @@
     second_back = feed.scatter_one(second_parts)
     down_mine_grad = matmul(grad_all, act_mine, ((0,), (0,))).astype(bf16)
     down_sum = feed.first_sum(down_mine_grad, down_swapped)
-    c1, c2, c3 = n_block * 3 // 8, n_block * 3 // 4, n_block * 3 // 8
+    c1, c2, c3 = n_block // 4, n_block * 5 // 8, n_block // 4
     down_x3 = [swap(down_sum[3][:c1], feed.second)]
-    out_parts = (
-        matmul(act_mine, down_mine, ((1,), (1,))) + matmul(act_other, down_other, ((1,), (1,)))
-    ).astype(bf16)
-    second_back, down_x3, down_sum, out_parts, hid_other = tied(
-        second_back, down_x3, down_sum, out_parts, hid_other
-    )
+    second_back, down_x3, down_sum, hid_other = tied(second_back, down_x3, down_sum, hid_other)
     grad_second = feed.scatter_two(*second_back)
-    z1, z2 = n_block * 3 // 16, n_block * 3 // 8
+    z1, z2 = n_block // 4, n_block * 3 // 8
     down_z1 = [swap(added(down_sum[1][:z1], down_x3[0][:z1]), feed.first)]
     down_x3 += [swap(down_sum[3][c1:c2], feed.second)]
     up_other_grad = matmul(second_all, hid_other, ((0,), (0,))).astype(bf16)
@@ -852,16 +868,41 @@
     middle_near = attn.gather_one(grad_middle.astype(bf16))
     down_x32 = swap(down_x32, feed.second)
     up_swapped = swap(up_other_grad, 1)
-    middle_near, down_x32, up_swapped, hid_mine, down_sum, down_x3, down_x2 = tied(
-        middle_near, down_x32, up_swapped, hid_mine, down_sum, down_x3, down_sum[2][c3:]
+    (
+        middle_near,
+        down_x32,
+        up_swapped,
+        hid_mine,
+        down_sum,
+        down_x3,
+        down_x2,
+        act_mine,
+        act_other,
+        down_mine,
+        down_other,
+    ) = tied(
+        middle_near,
+        down_x32,
+        up_swapped,
+        hid_mine,
+        down_sum,
+        down_x3,
+        down_sum[2][c3:],
+        act_mine,
+        act_other,
+        down_mine,
+        down_other,
     )
     middle_far = attn.gather_two(*middle_near)
     down_x3 = jnp.concatenate([*down_x3, down_x32[: n_block - c2]])
     down_x2 = [down_x32[n_block - c2 :], swap(down_x2, feed.second)]
     up_mine_grad = matmul(second_all, hid_mine, ((0,), (0,))).astype(bf16)
     down_z1b = added(down_sum[1][z1:z2], down_x3[z1:z2])
-    middle_far, up_swapped, up_mine_grad, down_x2, down_x3, down_sum, down_z1b = tied(
-        middle_far, up_swapped, up_mine_grad, down_x2, down_x3, down_sum, down_z1b
+    out_parts = (
+        matmul(act_mine, down_mine, ((1,), (1,))) + matmul(act_other, down_other, ((1,), (1,)))
+    ).astype(bf16)
+    middle_far, up_swapped, up_mine_grad, down_x2, down_x3, down_sum, down_z1b, out_parts = tied(
+        middle_far, up_swapped, up_mine_grad, down_x2, down_x3, down_sum, down_z1b, out_parts
     )
     middle_all = team_rows(*middle_near, *middle_far)
     grad_heads = matmul(middle_all, w_team, ((1,), (1,))).astype(bf16)
@@ -902,14 +943,13 @@
         dkv = dkv + swap(dkv_other[i], rel).astype(f32)
     triple = jnp.concatenate([dq, dkv.astype(bf16)], axis=2).reshape(4, 4 * rows, 3 * HEAD)
     up_z1 = added(up_sum[1], up_x3)
-    za, zb = n_block * 3 // 8, n_block * 11 // 16
+    za, zb = n_block // 2, n_block * 11 // 16
     out_grad = out_grad.reshape(2, 2, HEAD // len(plan.part_rel), width)
     triple, up_sum, up_z1, up_z1a, down_z1, out_grad, out_sent = tied(
         triple, up_sum, up_z1, up_z1[:za], down_z1, out_grad, out_grad[:, 1]
     )
     got = [swap(triple[r], plan.head_rel[r]) for r in range(1, 4)]
     up_z1a = swap(up_z1a, feed.first)
-    out_grad = added(out_grad[:, 0], swap(out_sent, attn.second))
     down_done = added(down_sum[0], jnp.concatenate(down_x2), jnp.concatenate(down_z1))
     down_rows, down_rows_hi = unsettle(by_hi_lo_core, down_done)
     got, up_z1a, up_z1b, up_z1c, down_rows, down_rows_hi, up_sum, out_grad, out_near = tied(
@@ -984,8 +1024,8 @@
     first_rows = attn.scatter_two(*first_back)
     output = (middle + feed.from_rel(out_sum)).astype(bf16)
     up_rows = jnp.stack([up_rows[:, 0], swap(up_send, feed.team_lo)])
-    qkv_z1, qkv_x2, first_rows, out_grad, output, up_rows, down_rows = tied(
-        qkv_z1, qkv_x2, first_rows, out_grad, output, up_rows, down_rows
+    qkv_z1, qkv_x2, first_rows, out_grad, out_sent, output, up_rows, down_rows = tied(
+        qkv_z1, qkv_x2, first_rows, out_grad, out_sent, output, up_rows, down_rows
     )
     down_rows = jnp.stack([down_rows[:, :, 0], swap(down_rows[:, :, 1], 1)])
     grad_down, _ = restore(False, by_core_lo_hi, down_rows.reshape(8, shard, n_ff), w_down, gain_two)
@@ -996,6 +1036,7 @@
     qkv_got = attn.octet(added(qkv_sum[0], qkv_x2, qkv_z1))
     grad_first = attn.from_rel(first_rows)
     grad_inputs = grad_middle + layer_norm_back(grad_first, *layer_norm(inputs))
+    out_grad = added(out_grad[:, 0], swap(out_sent, attn.second))
     out_grad = out_grad[0].astype(f32) + swap(out_grad[1], attn.first).astype(f32)
     grad_qkv, grad_gain_one = deliver(qkv_columns, qkv_got, w_qkv, gain_one)
     return (

time: 621 us -> 603 us (0.971)
  waiting for transfers between devices: 302 us -> 278 us
  starting transfers between devices: 102 us -> 117 us
  matrix products: 72.7 us -> 58.8 us
  other arithmetic: 42 us -> 49.1 us
    ppermute x99 -> x102, waiting for transfers between devices: 296 us -> 278 us  [swap(): return lax.ppermute(value, AXES, [(d, d ^ mask) for d in self.devices])]
    ppermute x99 -> x102, starting transfers between devices: 92.2 us -> 107 us  [swap(): return lax.ppermute(value, AXES, [(d, d ^ mask) for d in self.devices])]
    dot_general x21, matrix products: 72.7 us -> 58.8 us  [matmul(): lax.dot_general(left, right, (dims, ((), ())), preferred_element_type=f32)]
    unnamed x209 -> x205, local copies, waits for them, and re-layouts: 24.9 us -> 14.4 us
  transfers between devices with their start and end apart: 101 -> 104, of which waited for: 45 -> 46; matrix products, arithmetic and copies ran while one was open for 18% -> 19% of each run, Pallas kernels for 8% -> 8%
where the time goes in v6:
time: 603 us; the launch traced here: 593 us
  waiting for transfers between devices  278 us (46%)
  starting transfers between devices  117 us (19%)
  matrix products  58.8 us (10%)
  Pallas kernels  52.5 us (9%)
  other arithmetic  49.1 us (8%)
  local copies, waits for them, and re-layouts  33.8 us (6%)
    ppermute x102, waiting for transfers between devices, swap(): return lax.ppermute(value, AXES, [(d, d ^ mask) for d in self.devices])  278 us
    ppermute x102, starting transfers between devices, swap(): return lax.ppermute(value, AXES, [(d, d ^ mask) for d in self.devices])  107 us
    dot_general x21, matrix products, matmul(): lax.dot_general(left, right, (dims, ((), ())), preferred_element_type=f32)  58.8 us
    convert_element_type x21, other arithmetic, added(): return sum((v.astype(f32) for v in values)).astype(bf16)  19 us
    pallas_call x1, Pallas kernels, attend_back(): call(functools.partial(attend_back_kernel, plan), 2, 6, (shape((blocks, B...  18 us
    pallas_call x1, Pallas kernels, attend(): call(functools.partial(attend_kernel, plan), 2, 2, (shape((blocks, BLOCK,...  16.9 us
    unnamed x205, local copies, waits for them, and re-layouts  14.4 us
  transfers between devices with their start and end apart: 104, of which 46 were waited for; matrix products, arithmetic and copies ran while one was open for 19% of the time, Pallas kernels for 8%

profile of v6, /device:TPU:0, one launch (start us, length us, event | category | flops | bytes accessed | tf_op | source)
XLA Modules:
  0.0 592.5 jit_solution(12332192253722955173)
XLA Ops:
  3.9 6.4 %all-to-all-start = ((bf16[8,64,768]{2,1,0:T(8,128)(2,1)}), bf16[8,64,768]{2,1,0:T(8,128)(2,1)}, u32[]{:S(2)}, u32[]{:S(2)}) async-start(bf16[8,64,768]{2,1,0:T(8,128)(2,1)} %shard_map.233), calls=%async_computation | async-start | bytes 1572864 | tf_op jit(solution)/shard_map/all_to_all | solution.py:583
  20.1 5.7 collective-permute-done.2
  25.8 7.6 %collective-permute-done.1.b_hi = bf16[64,2048]{1,0:T(8,128)(2,1)} collective-permute-done((bf16[64,2048]{1,0:T(8,128)(2,1)S(1)}, bf16[64,2048]{1,0:T(8,128)(2,1)}, u32[]{:S(2)}, u32[]{:S(2)}) %collective-permute-start.1) | collective-permute-done | bytes 262176 | tf_op jit(solution)/shard_map/ppermute | solution.py:69
  37.9 3.6 collective-permute-start.6
  43.0 19.6 %collective-permute-done.5.a_lo = bf16[48,2048]{1,0:T(8,128)(2,1)S(1)} collective-permute-done((bf16[48,2048]{1,0:T(8,128)(2,1)S(1)}, bf16[48,2048]{1,0:T(8,128)(2,1)S(1)}, u32[]{:S(2)}, u32[]{:S(2)}) %collective-permute-start.5) | collective-permute-done | bytes 196640 | tf_op jit(solution)/shard_map/ppermute | solution.py:69
  68.9 2.6 collective-permute-start.9
  75.4 13.3 %collective-permute-done.9.a_far = bf16[96,2048]{1,0:T(8,128)(2,1)S(1)} collective-permute-done((bf16[96,2048]{1,0:T(8,128)(2,1)S(1)}, bf16[96,2048]{1,0:T(8,128)(2,1)S(1)}, u32[]{:S(2)}, u32[]{:S(2)}) %collective-permute-start.9) | collective-permute-done | bytes 393248 | tf_op jit(solution)/shard_map/ppermute | solution.py:69
  92.7 3.3 collective-permute-start.16
  98.2 4.4 fusion.120
  105.0 3.7 fusion.119
  112.2 5.4 collective-permute-done.16.got
  117.6 6.4 %collective-permute-done.14 = bf16[256,1024]{1,0:T(8,128)(2,1)S(1)} collective-permute-done((bf16[256,1024]{1,0:T(8,128)(2,1)S(1)}, bf16[256,1024]{1,0:T(8,128)(2,1)S(1)}, u32[]{:S(2)}, u32[]{:S(2)}) %collective-permute-start.14) | collective-permute-done | bytes 524320 | tf_op jit(solution)/shard_map/ppermute | solution.py:69
  129.9 17.3 %collective-permute-done.17 = bf16[512,384]{1,0:T(8,128)(2,1)S(1)} collective-permute-done((bf16[512,384]{1,0:T(8,128)(2,1)S(1)}, bf16[512,384]{1,0:T(8,128)(2,1)S(1)}, u32[]{:S(2)}, u32[]{:S(2)}) %collective-permute-start.17) | collective-permute-done | bytes 393248 | tf_op jit(solution)/shard_map/ppermute | solution.py:69
  149.3 6.4 %collective-permute-done.19 = bf16[512,384]{1,0:T(8,128)(2,1)S(1)} collective-permute-done((bf16[512,384]{1,0:T(8,128)(2,1)S(1)}, bf16[512,384]{1,0:T(8,128)(2,1)S(1)}, u32[]{:S(2)}, u32[]{:S(2)}) %collective-permute-start.19) | collective-permute-done | bytes 393248 | tf_op jit(solution)/shard_map/ppermute | solution.py:69
  166.9 16.9 %shard_map.240 = (bf16[16,128,128]{2,1,0:T(8,128)(2,1)S(1)}, f32[8,128,256]{2,1,0:T(8,128)S(1)}, f32[8,1,256]{2,1,0:T(1,128)S(1)}, bf16[4096,128]{1,0:T(8,128)(2,1)S(1)}, bf16[4096,128]{1,0:T(8,128)(2,1)S(1)}) custom-call(s32[56]{0:T(128)S(1)} %concatenate.196.info, s32[8]{0:T(128)S(1)} %copy-done.29, bf16[16,128,384]{2,1,0:T(8,128)(2,1)S(1)} %bitcast.283, ...), custom_call_target="tpu_custom_call" | custom-call | flops 4294967296 | bytes 8388608 | tf_op jit(solution)/shard_map/pallas_call | solution.py:463
  183.9 2.7 collective-permute-done.26.a_far
  196.0 6.2 %collective-permute-done.29 = bf16[512,128]{1,0:T(8,128)(2,1)S(1)} collective-permute-done((bf16[512,128]{1,0:T(8,128)(2,1)S(1)}, bf16[512,128]{1,0:T(8,128)(2,1)S(1)}, u32[]{:S(2)}, u32[]{:S(2)}) %collective-permute-start.29) | collective-permute-done | bytes 131104 | tf_op jit(solution)/shard_map/ppermute | solution.py:69
  202.2 4.5 collective-permute-done.32
  211.5 16.8 %collective-permute-done.33 = bf16[2,48,2048]{2,1,0:T(8,128)(2,1)S(1)} collective-permute-done((bf16[2,48,2048]{2,1,0:T(8,128)(2,1)S(1)}, bf16[2,48,2048]{2,1,0:T(8,128)(2,1)S(1)}, u32[]{:S(2)}, u32[]{:S(2)}) %collective-permute-start.33) | collective-permute-done | bytes 393248 | tf_op jit(solution)/shard_map/ppermute | solution.py:69
  232.9 3.1 collective-permute-done.36
  236.0 10.5 %collective-permute-done.37 = bf16[80,2048]{1,0:T(8,128)(2,1)S(1)} collective-permute-done((bf16[80,2048]{1,0:T(8,128)(2,1)S(1)}, bf16[80,2048]{1,0:T(8,128)(2,1)S(1)}, u32[]{:S(2)}, u32[]{:S(2)}) %collective-permute-start.37) | collective-permute-done | bytes 327712 | tf_op jit(solution)/shard_map/ppermute | solution.py:69
  250.0 2.5 collective-permute-start.42
  253.8 9.7 %collective-permute-done.44 = bf16[96,1024]{1,0:T(8,128)(2,1)S(1)} collective-permute-done((bf16[96,1024]{1,0:T(8,128)(2,1)S(1)}, bf16[96,1024]{1,0:T(8,128)(2,1)S(1)}, u32[]{:S(2)}, u32[]{:S(2)}) %collective-permute-start.44) | collective-permute-done | bytes 196640 | tf_op jit(solution)/shard_map/ppermute | solution.py:69
  268.7 6.5 %collective-permute-done.48 = bf16[32,1024]{1,0:T(8,128)(2,1)S(1)} collective-permute-done((bf16[32,1024]{1,0:T(8,128)(2,1)S(1)}, bf16[32,1024]{1,0:T(8,128)(2,1)S(1)}, u32[]{:S(2)}, u32[]{:S(2)}) %collective-permute-start.48) | collective-permute-done | bytes 65568 | tf_op jit(solution)/shard_map/ppermute | solution.py:69
  276.7 2.7 collective-permute-done.49
  280.0 4.0 multiply_convert_fusion.1
  283.9 2.4 convolution_convert_fusion.2
  286.4 3.0 multiply_convert_fusion
  290.0 3.4 fusion.6
  293.4 4.5 fusion.121
  297.9 3.4 fusion.13
  301.3 2.4 add_convert_fusion.5
  307.5 3.2 collective-permute-start.52
  310.7 2.8 fusion.122
  313.5 4.3 add_convert_fusion.1
  321.6 6.3 %collective-permute-done.54 = bf16[128,1024]{1,0:T(8,128)(2,1)S(1)} collective-permute-done((bf16[128,1024]{1,0:T(8,128)(2,1)}, bf16[128,1024]{1,0:T(8,128)(2,1)S(1)}, u32[]{:S(2)}, u32[]{:S(2)}) %collective-permute-start.54) | collective-permute-done | bytes 262176 | tf_op jit(solution)/shard_map/ppermute | solution.py:69
  337.2 2.4 convolution_convert_fusion.1
  340.6 4.0 collective-permute-done.56
  354.2 4.4 collective-permute-done.59.a_lo
  358.6 9.9 %collective-permute-done.60.b_hi = bf16[80,2048]{1,0:T(8,128)(2,1)S(1)} collective-permute-done((bf16[80,2048]{1,0:T(8,128)(2,1)S(1)}, bf16[80,2048]{1,0:T(8,128)(2,1)S(1)}, u32[]{:S(2)}, u32[]{:S(2)}) %collective-permute-start.60) | collective-permute-done | bytes 327712 | tf_op jit(solution)/shard_map/ppermute | solution.py:69
  374.5 2.6 add_convert_fusion.4
  378.3 2.4 convolution_convert_fusion
  380.7 7.6 %collective-permute-done.63.a_far = bf16[96,2048]{1,0:T(8,128)(2,1)S(1)} collective-permute-done((bf16[96,2048]{1,0:T(8,128)(2,1)S(1)}, bf16[96,2048]{1,0:T(8,128)(2,1)S(1)}, u32[]{:S(2)}, u32[]{:S(2)}) %collective-permute-start.63) | collective-permute-done | bytes 393248 | tf_op jit(solution)/shard_map/ppermute | solution.py:69
  392.8 2.5 collective-permute-start.68
  409.6 18.0 %shard_map.245 = (bf16[16,128,128]{2,1,0:T(8,128)(2,1)S(1)}, bf16[16,128,256]{2,1,0:T(8,128)(2,1)S(1)}, bf16[1,16,128,256]{3,2,1,0:T(8,128)(2,1)S(1)}) custom-call(s32[56]{0:T(128)S(1)} %concatenate.196.info, s32[8]{0:T(128)S(1)} %copy-done.29, bf16[16,128,384]{2,1,0:T(8,128)(2,1)S(1)} %bitcast.284, bf16[4096,128]{1,0:T(8,128)(2,1)S(1)} %copy-done.33, ...), custom_call_target="tpu_custom_call" | custom-call | flops 10737418240 | bytes 8388608 | tf_op jit(solution)/shard_map/pallas_call | solution.py:485
  429.4 3.5 collective-permute-done.71
  436.5 3.3 collective-permute-start.78
  443.7 13.4 %collective-permute-done.78.refs_3_ = bf16[512,384]{1,0:T(8,128)(2,1)S(1)} collective-permute-done((bf16[512,384]{1,0:T(8,128)(2,1)S(1)}, bf16[512,384]{1,0:T(8,128)(2,1)S(1)}, u32[]{:S(2)}, u32[]{:S(2)}) %collective-permute-start.78) | collective-permute-done | bytes 393248 | tf_op jit(solution)/shard_map/ppermute | solution.py:69
  457.1 11.3 %collective-permute-done.77.refs_2_ = bf16[512,384]{1,0:T(8,128)(2,1)S(1)} collective-permute-done((bf16[512,384]{1,0:T(8,128)(2,1)S(1)}, bf16[512,384]{1,0:T(8,128)(2,1)S(1)}, u32[]{:S(2)}, u32[]{:S(2)}) %collective-permute-start.77) | collective-permute-done | bytes 393248 | tf_op jit(solution)/shard_map/ppermute | solution.py:69
  478.1 2.5 collective-permute-done.83
  480.9 3.7 collective-permute-done.80
  490.4 3.7 fusion.124
  494.1 3.7 add_convert_fusion.3
  498.8 5.6 collective-permute-done.87
  508.2 2.8 collective-permute-start.89
  512.9 13.1 %collective-permute-done.91 = bf16[4,64,1024]{2,1,0:T(8,128)(2,1)S(1)} collective-permute-done((bf16[4,64,1024]{2,1,0:T(8,128)(2,1)S(1)}, bf16[4,64,1024]{2,1,0:T(8,128)(2,1)S(1)}, u32[]{:S(2)}, u32[]{:S(2)}) %collective-permute-start.91) | collective-permute-done | bytes 524320 | tf_op jit(solution)/shard_map/ppermute | solution.py:69
  526.2 7.0 %collective-permute-done.90 = bf16[2,80,2048]{2,1,0:T(8,128)(2,1)S(1)} collective-permute-done((bf16[2,80,2048]{2,1,0:T(8,128)(2,1)S(1)}, bf16[2,80,2048]{2,1,0:T(8,128)(2,1)S(1)}, u32[]{:S(2)}, u32[]{:S(2)}) %collective-permute-start.90) | collective-permute-done | bytes 655392 | tf_op jit(solution)/shard_map/ppermute | solution.py:69
  534.3 2.8 collective-permute-start.96
  541.5 3.8 collective-permute-done.96
  550.6 6.4 %collective-permute-done.93 = bf16[512,768]{1,0:T(8,128)(2,1)S(1)} collective-permute-done((bf16[512,768]{1,0:T(8,128)(2,1)S(1)}, bf16[512,768]{1,0:T(8,128)(2,1)S(1)}, u32[]{:S(2)}, u32[]{:S(2)}) %collective-permute-start.93) | collective-permute-done | bytes 786464 | tf_op jit(solution)/shard_map/ppermute | solution.py:69
  558.2 3.8 all-to-all-start.1
  568.7 7.6 %collective-permute-done.98 = bf16[2,64,2048]{2,1,0:T(8,128)(2,1)S(1)} collective-permute-done((bf16[2,64,2048]{2,1,0:T(8,128)(2,1)S(1)}, bf16[2,64,2048]{2,1,0:T(8,128)(2,1)S(1)}, u32[]{:S(2)}, u32[]{:S(2)}) %collective-permute-start.98) | collective-permute-done | bytes 524320 | tf_op jit(solution)/shard_map/ppermute | solution.py:69
  577.6 2.4 shard_map.250
  582.7 5.8 collective-permute-done.99
  (587 shorter events, 201.7 us)
Async XLA Ops:
  3.9 29.5 %all-to-all-start = ((bf16[8,64,768]{2,1,0:T(8,128)(2,1)}), bf16[8,64,768]{2,1,0:T(8,128)(2,1)}, u32[]{:S(2)}, u32[]{:S(2)}) async-start(bf16[8,64,768]{2,1,0:T(8,128)(2,1)} %shard_map.233), calls=%async_computation | async-start | bytes 1572864 | tf_op jit(solution)/shard_map/all_to_all | solution.py:583
  10.3 15.5 %collective-permute-start.2 = (bf16[64,2048]{1,0:T(8,128)(2,1)}, bf16[64,2048]{1,0:T(8,128)(2,1)}, u32[]{:S(2)}, u32[]{:S(2)}) collective-permute-start(bf16[64,2048]{1,0:T(8,128)(2,1)} %param.22), channel_id=1, source_target_pairs={{0,8},{1,9},{2,10},{3,11},{4,12},{5,13},{6,14},{7,15},{8,0},{9,1},... | collective-permute-start | bytes 786440 | tf_op jit(solution)/shard_map/ppermute | solution.py:69
  13.3 20.1 %collective-permute-start.1 = (bf16[64,2048]{1,0:T(8,128)(2,1)S(1)}, bf16[64,2048]{1,0:T(8,128)(2,1)}, u32[]{:S(2)}, u32[]{:S(2)}) collective-permute-start(bf16[64,2048]{1,0:T(8,128)(2,1)S(1)} %get-tuple-element.339.b), channel_id=1, source_target_pairs={{0,8},{1,9},{2,10},{3,11},{4,12},{5,13},{6,14},{7,15},{8,0},{9,1},... | collective-permute-start | bytes 786440 | tf_op jit(solution)/shard_map/ppermute | solution.py:69
  13.7 19.6 %collective-permute-start = (bf16[64,2048]{1,0:T(8,128)(2,1)}, bf16[64,2048]{1,0:T(8,128)(2,1)}, u32[]{:S(2)}, u32[]{:S(2)}) collective-permute-start(bf16[64,2048]{1,0:T(8,128)(2,1)} %get-tuple-element.337.a), channel_id=1, source_target_pairs={{0,2},{1,3},{2,0},{3,1},{4,6},{5,7},{6,4},{7,5},{8,10},{9,11},{10,... | collective-permute-start | bytes 786440 | tf_op jit(solution)/shard_map/ppermute | solution.py:69
  33.4 29.2 %collective-permute-start.7 = (bf16[4,64,2048]{2,1,0:T(8,128)(2,1)}, bf16[4,64,2048]{2,1,0:T(8,128)(2,1)S(1)}, u32[]{:S(2)}, u32[]{:S(2)}) collective-permute-start(bf16[4,64,2048]{2,1,0:T(8,128)(2,1)} %slice.875), channel_id=1, source_target_pairs={{0,2},{1,3},{2,0},{3,1},{4,6},{5,7},{6,4},{7,5},{8,10},{9,11},{10,... | collective-permute-start | bytes 3145736 | tf_op jit(solution)/shard_map/ppermute | solution.py:69
  35.1 27.6 %collective-permute-start.4 = (bf16[512,768]{1,0:T(8,128)(2,1)}, bf16[512,768]{1,0:T(8,128)(2,1)S(1)}, u32[]{:S(2)}, u32[]{:S(2)}) collective-permute-start(bf16[512,768]{1,0:T(8,128)(2,1)} %bitcast.2), channel_id=1, source_target_pairs={{0,4},{1,5},{2,6},{3,7},{4,0},{5,1},{6,2},{7,3},{8,12},{9,13},{10,... | collective-permute-start | bytes 2359304 | tf_op jit(solution)/shard_map/ppermute | solution.py:69
  36.5 26.1 %collective-permute-start.3 = (bf16[512,768]{1,0:T(8,128)(2,1)}, bf16[512,768]{1,0:T(8,128)(2,1)S(1)}, u32[]{:S(2)}, u32[]{:S(2)}) collective-permute-start(bf16[512,768]{1,0:T(8,128)(2,1)} %bitcast.2), channel_id=1, source_target_pairs={{0,8},{1,9},{2,10},{3,11},{4,12},{5,13},{6,14},{7,15},{8,0},{9,1},... | collective-permute-start | bytes 2359304 | tf_op jit(solution)/shard_map/ppermute | solution.py:69
  37.9 24.7 %collective-permute-start.6 = (bf16[80,2048]{1,0:T(8,128)(2,1)S(1)}, bf16[80,2048]{1,0:T(8,128)(2,1)S(1)}, u32[]{:S(2)}, u32[]{:S(2)}) collective-permute-start(bf16[80,2048]{1,0:T(8,128)(2,1)S(1)} %slice.679.b), channel_id=1, source_target_pairs={{0,16},{1,17},{2,18},{3,19},{4,20},{5,21},{6,22},{7,23},{8,24},{9,... | collective-permute-start | bytes 983048 | tf_op jit(solution)/shard_map/ppermute | solution.py:69
  42.4 20.2 %collective-permute-start.5 = (bf16[48,2048]{1,0:T(8,128)(2,1)S(1)}, bf16[48,2048]{1,0:T(8,128)(2,1)S(1)}, u32[]{:S(2)}, u32[]{:S(2)}) collective-permute-start(bf16[48,2048]{1,0:T(8,128)(2,1)S(1)} %slice.678.a), channel_id=1, source_target_pairs={{0,2},{1,3},{2,0},{3,1},{4,6},{5,7},{6,4},{7,5},{8,10},{9,11},{10,... | collective-permute-start | bytes 589832 | tf_op jit(solution)/shard_map/ppermute | solution.py:69
  63.4 26.0 %collective-permute-start.10 = (bf16[160,2048]{1,0:T(8,128)(2,1)S(1)}, bf16[160,2048]{1,0:T(8,128)(2,1)S(1)}, u32[]{:S(2)}, u32[]{:S(2)}) collective-permute-start(bf16[160,2048]{1,0:T(8,128)(2,1)S(1)} %pad_maximum_fusion.16), channel_id=1, source_target_pairs={{0,2},{1,3},{2,0},{3,1},{4,6},{5,7},{6,4},{7,5},{8,10},{9,11},{10,... | collective-permute-start | bytes 1966088 | tf_op jit(solution)/shard_map/ppermute | solution.py:69
  64.9 25.5 %collective-permute-start.8 = (bf16[512,768]{1,0:T(8,128)(2,1)S(1)}, bf16[512,768]{1,0:T(8,128)(2,1)S(1)}, u32[]{:S(2)}, u32[]{:S(2)}) collective-permute-start(bf16[512,768]{1,0:T(8,128)(2,1)S(1)} %collective-permute-done.3), channel_id=1, source_target_pairs={{0,4},{1,5},{2,6},{3,7},{4,0},{5,1},{6,2},{7,3},{8,12},{9,13},{10,... | collective-permute-start | bytes 2359304 | tf_op jit(solution)/shard_map/ppermute | solution.py:69
  67.7 22.7 %collective-permute-start.12 = (bf16[4,64,1024]{2,1,0:T(8,128)(2,1)S(1)}, bf16[4,64,1024]{2,1,0:T(8,128)(2,1)S(1)}, u32[]{:S(2)}, u32[]{:S(2)}) collective-permute-start(bf16[4,64,1024]{2,1,0:T(8,128)(2,1)S(1)} %bitcast.330), channel_id=1, source_target_pairs={{0,8},{1,9},{2,10},{3,11},{4,12},{5,13},{6,14},{7,15},{8,0},{9,1},... | collective-permute-start | bytes 1572872 | tf_op jit(solution)/shard_map/ppermute | solution.py:69
  68.9 19.9 %collective-permute-start.9 = (bf16[96,2048]{1,0:T(8,128)(2,1)S(1)}, bf16[96,2048]{1,0:T(8,128)(2,1)S(1)}, u32[]{:S(2)}, u32[]{:S(2)}) collective-permute-start(bf16[96,2048]{1,0:T(8,128)(2,1)S(1)} %pad_maximum_fusion.36), channel_id=1, source_target_pairs={{0,16},{1,17},{2,18},{3,19},{4,20},{5,21},{6,22},{7,23},{8,24},{9,... | collective-permute-start | bytes 1179656 | tf_op jit(solution)/shard_map/ppermute | solution.py:69
  92.7 24.9 %collective-permute-start.16 = (bf16[4,64,1024]{2,1,0:T(8,128)(2,1)}, bf16[4,64,1024]{2,1,0:T(8,128)(2,1)S(1)}, u32[]{:S(2)}, u32[]{:S(2)}) collective-permute-start(bf16[4,64,1024]{2,1,0:T(8,128)(2,1)} %bitcast.14), channel_id=1, source_target_pairs={{0,8},{1,9},{2,10},{3,11},{4,12},{5,13},{6,14},{7,15},{8,0},{9,1},... | collective-permute-start | bytes 1572872 | tf_op jit(solution)/shard_map/ppermute | solution.py:69
  96.6 27.3 %collective-permute-start.15 = (bf16[512,1024]{1,0:T(8,128)(2,1)S(1)}, bf16[512,1024]{1,0:T(8,128)(2,1)S(1)}, u32[]{:S(2)}, u32[]{:S(2)}) collective-permute-start(bf16[512,1024]{1,0:T(8,128)(2,1)S(1)} %shard_map.238), channel_id=1, source_target_pairs={{0,4},{1,5},{2,6},{3,7},{4,0},{5,1},{6,2},{7,3},{8,12},{9,13},{10,... | collective-permute-start | bytes 3145736 | tf_op jit(solution)/shard_map/ppermute | solution.py:69
  97.9 26.0 %collective-permute-start.14 = (bf16[256,1024]{1,0:T(8,128)(2,1)S(1)}, bf16[256,1024]{1,0:T(8,128)(2,1)S(1)}, u32[]{:S(2)}, u32[]{:S(2)}) collective-permute-start(bf16[256,1024]{1,0:T(8,128)(2,1)S(1)} %get-tuple-element.689), channel_id=1, source_target_pairs={{0,16},{1,17},{2,18},{3,19},{4,20},{5,21},{6,22},{7,23},{8,24},{9,... | collective-permute-start | bytes 1572872 | tf_op jit(solution)/shard_map/ppermute | solution.py:69
  123.9 31.7 %collective-permute-start.20 = (bf16[256,1024]{1,0:T(8,128)(2,1)S(1)}, bf16[256,1024]{1,0:T(8,128)(2,1)S(1)}, u32[]{:S(2)}, u32[]{:S(2)}) collective-permute-start(bf16[256,1024]{1,0:T(8,128)(2,1)S(1)} %get-tuple-element.320), channel_id=1, source_target_pairs={{0,16},{1,17},{2,18},{3,19},{4,20},{5,21},{6,22},{7,23},{8,24},{9,... | collective-permute-start | bytes 1572872 | tf_op jit(solution)/shard_map/ppermute | solution.py:69
  124.0 31.7 %collective-permute-start.21 = (bf16[2,64,2048]{2,1,0:T(8,128)(2,1)S(1)}, bf16[2,64,2048]{2,1,0:T(8,128)(2,1)S(1)}, u32[]{:S(2)}, u32[]{:S(2)}) collective-permute-start(bf16[2,64,2048]{2,1,0:T(8,128)(2,1)S(1)} %pad_maximum_fusion.24), channel_id=1, source_target_pairs={{0,4},{1,5},{2,6},{3,7},{4,0},{5,1},{6,2},{7,3},{8,12},{9,13},{10,... | collective-permute-start | bytes 1572872 | tf_op jit(solution)/shard_map/ppermute | solution.py:69
  124.9 22.3 %collective-permute-start.17 = (bf16[512,384]{1,0:T(8,128)(2,1)S(1)}, bf16[512,384]{1,0:T(8,128)(2,1)S(1)}, u32[]{:S(2)}, u32[]{:S(2)}) collective-permute-start(bf16[512,384]{1,0:T(8,128)(2,1)S(1)} %get-tuple-element.316), channel_id=1, source_target_pairs={{0,4},{1,5},{2,6},{3,7},{4,0},{5,1},{6,2},{7,3},{8,12},{9,13},{10,... | collective-permute-start | bytes 1179656 | tf_op jit(solution)/shard_map/ppermute | solution.py:69
  126.1 23.2 %collective-permute-start.18 = (bf16[512,384]{1,0:T(8,128)(2,1)S(1)}, bf16[512,384]{1,0:T(8,128)(2,1)S(1)}, u32[]{:S(2)}, u32[]{:S(2)}) collective-permute-start(bf16[512,384]{1,0:T(8,128)(2,1)S(1)} %get-tuple-element.317), channel_id=1, source_target_pairs={{0,8},{1,9},{2,10},{3,11},{4,12},{5,13},{6,14},{7,15},{8,0},{9,1},... | collective-permute-start | bytes 1179656 | tf_op jit(solution)/shard_map/ppermute | solution.py:69
  127.6 28.1 %collective-permute-start.19 = (bf16[512,384]{1,0:T(8,128)(2,1)S(1)}, bf16[512,384]{1,0:T(8,128)(2,1)S(1)}, u32[]{:S(2)}, u32[]{:S(2)}) collective-permute-start(bf16[512,384]{1,0:T(8,128)(2,1)S(1)} %get-tuple-element.318), channel_id=1, source_target_pairs={{0,12},{1,13},{2,14},{3,15},{4,8},{5,9},{6,10},{7,11},{8,4},{9,5},... | collective-permute-start | bytes 1179656 | tf_op jit(solution)/shard_map/ppermute | solution.py:69
  159.5 24.4 %collective-permute-start.27 = (bf16[128,2048]{1,0:T(8,128)(2,1)S(1)}, bf16[128,2048]{1,0:T(8,128)(2,1)S(1)}, u32[]{:S(2)}, u32[]{:S(2)}) collective-permute-start(bf16[128,2048]{1,0:T(8,128)(2,1)S(1)} %pad_maximum_fusion.26), channel_id=1, source_target_pairs={{0,2},{1,3},{2,0},{3,1},{4,6},{5,7},{6,4},{7,5},{8,10},{9,11},{10,... | collective-permute-start | bytes 1572872 | tf_op jit(solution)/shard_map/ppermute | solution.py:69
  161.7 24.9 %collective-permute-start.26 = (bf16[128,2048]{1,0:T(8,128)(2,1)S(1)}, bf16[128,2048]{1,0:T(8,128)(2,1)S(1)}, u32[]{:S(2)}, u32[]{:S(2)}) collective-permute-start(bf16[128,2048]{1,0:T(8,128)(2,1)S(1)} %pad_maximum_fusion.25), channel_id=1, source_target_pairs={{0,8},{1,9},{2,10},{3,11},{4,12},{5,13},{6,14},{7,15},{8,0},{9,1},... | collective-permute-start | bytes 1572872 | tf_op jit(solution)/shard_map/ppermute | solution.py:69
  161.8 26.5 %collective-permute-start.23 = (bf16[256,1024]{1,0:T(8,128)(2,1)}, bf16[256,1024]{1,0:T(8,128)(2,1)S(1)}, u32[]{:S(2)}, u32[]{:S(2)}) collective-permute-start(bf16[256,1024]{1,0:T(8,128)(2,1)} %slice.912), channel_id=1, source_target_pairs={{0,16},{1,17},{2,18},{3,19},{4,20},{5,21},{6,22},{7,23},{8,24},{9,... | collective-permute-start | bytes 1572872 | tf_op jit(solution)/shard_map/ppermute | solution.py:69
  163.6 24.7 %collective-permute-start.24 = (bf16[256,1024]{1,0:T(8,128)(2,1)S(1)}, bf16[256,1024]{1,0:T(8,128)(2,1)S(1)}, u32[]{:S(2)}, u32[]{:S(2)}) collective-permute-start(bf16[256,1024]{1,0:T(8,128)(2,1)S(1)} %copy-done.52), channel_id=1, source_target_pairs={{0,4},{1,5},{2,6},{3,7},{4,0},{5,1},{6,2},{7,3},{8,12},{9,13},{10,... | collective-permute-start | bytes 1572872 | tf_op jit(solution)/shard_map/ppermute | solution.py:69
  165.4 23.2 %collective-permute-start.25 = (bf16[256,1024]{1,0:T(8,128)(2,1)S(1)}, bf16[256,1024]{1,0:T(8,128)(2,1)S(1)}, u32[]{:S(2)}, u32[]{:S(2)}) collective-permute-start(bf16[256,1024]{1,0:T(8,128)(2,1)S(1)} %copy-done.54), channel_id=1, source_target_pairs={{0,4},{1,5},{2,6},{3,7},{4,0},{5,1},{6,2},{7,3},{8,12},{9,13},{10,... | collective-permute-start | bytes 1572872 | tf_op jit(solution)/shard_map/ppermute | solution.py:69
  208.2 20.1 %collective-permute-start.35 = (bf16[320,1024]{1,0:T(8,128)(2,1)S(1)}, bf16[320,1024]{1,0:T(8,128)(2,1)S(1)}, u32[]{:S(2)}, u32[]{:S(2)}) collective-permute-start(bf16[320,1024]{1,0:T(8,128)(2,1)S(1)} %slice.727), channel_id=1, source_target_pairs={{0,4},{1,5},{2,6},{3,7},{4,0},{5,1},{6,2},{7,3},{8,12},{9,13},{10,... | collective-permute-start | bytes 1966088 | tf_op jit(solution)/shard_map/ppermute | solution.py:69
  209.8 18.6 %collective-permute-start.33 = (bf16[2,48,2048]{2,1,0:T(8,128)(2,1)S(1)}, bf16[2,48,2048]{2,1,0:T(8,128)(2,1)S(1)}, u32[]{:S(2)}, u32[]{:S(2)}) collective-permute-start(bf16[2,48,2048]{2,1,0:T(8,128)(2,1)S(1)} %get-tuple-element.620), channel_id=1, source_target_pairs={{0,16},{1,17},{2,18},{3,19},{4,20},{5,21},{6,22},{7,23},{8,24},{9,... | collective-permute-start | bytes 1179656 | tf_op jit(solution)/shard_map/ppermute | solution.py:69
  209.8 18.5 %collective-permute-start.34 = (bf16[2,80,2048]{2,1,0:T(8,128)(2,1)S(1)}, bf16[2,80,2048]{2,1,0:T(8,128)(2,1)S(1)}, u32[]{:S(2)}, u32[]{:S(2)}) collective-permute-start(bf16[2,80,2048]{2,1,0:T(8,128)(2,1)S(1)} %pad_maximum_fusion.18), channel_id=1, source_target_pairs={{0,2},{1,3},{2,0},{3,1},{4,6},{5,7},{6,4},{7,5},{8,10},{9,11},{10,... | collective-permute-start | bytes 1966088 | tf_op jit(solution)/shard_map/ppermute | solution.py:69
  228.3 19.5 %collective-permute-start.39 = (bf16[2048,1024]{1,0:T(8,128)(2,1)S(1)}, bf16[2048,1024]{1,0:T(8,128)(2,1)S(1)}, u32[]{:S(2)}, u32[]{:S(2)}) collective-permute-start(bf16[2048,1024]{1,0:T(8,128)(2,1)S(1)} %constant_dynamic-update-slice_fusion.4), channel_id=1, source_target_pairs={{0,1},{1,0},{2,3},{3,2},{4,5},{5,4},{6,7},{7,6},{8,9},{9,8},{10,11... | collective-permute-start | bytes 12582920 | tf_op jit(solution)/shard_map/ppermute | solution.py:69
  229.4 17.1 %collective-permute-start.37 = (bf16[80,2048]{1,0:T(8,128)(2,1)S(1)}, bf16[80,2048]{1,0:T(8,128)(2,1)S(1)}, u32[]{:S(2)}, u32[]{:S(2)}) collective-permute-start(bf16[80,2048]{1,0:T(8,128)(2,1)S(1)} %fusion.42), channel_id=1, source_target_pairs={{0,16},{1,17},{2,18},{3,19},{4,20},{5,21},{6,22},{7,23},{8,24},{9,... | collective-permute-start | bytes 983048 | tf_op jit(solution)/shard_map/ppermute | solution.py:69
  229.5 17.2 %collective-permute-start.40 = (bf16[160,1024]{1,0:T(8,128)(2,1)S(1)}, bf16[160,1024]{1,0:T(8,128)(2,1)S(1)}, u32[]{:S(2)}, u32[]{:S(2)}) collective-permute-start(bf16[160,1024]{1,0:T(8,128)(2,1)S(1)} %slice.735), channel_id=1, source_target_pairs={{0,4},{1,5},{2,6},{3,7},{4,0},{5,1},{6,2},{7,3},{8,12},{9,13},{10,... | collective-permute-start | bytes 983048 | tf_op jit(solution)/shard_map/ppermute | solution.py:69
  230.4 17.4 %collective-permute-start.38 = (bf16[192,1024]{1,0:T(8,128)(2,1)S(1)}, bf16[192,1024]{1,0:T(8,128)(2,1)S(1)}, u32[]{:S(2)}, u32[]{:S(2)}) collective-permute-start(bf16[192,1024]{1,0:T(8,128)(2,1)S(1)} %slice.734), channel_id=1, source_target_pairs={{0,4},{1,5},{2,6},{3,7},{4,0},{5,1},{6,2},{7,3},{8,12},{9,13},{10,... | collective-permute-start | bytes 1179656 | tf_op jit(solution)/shard_map/ppermute | solution.py:69
  247.8 15.7 %collective-permute-start.43 = (bf16[128,1024]{1,0:T(8,128)(2,1)S(1)}, bf16[128,1024]{1,0:T(8,128)(2,1)S(1)}, u32[]{:S(2)}, u32[]{:S(2)}) collective-permute-start(bf16[128,1024]{1,0:T(8,128)(2,1)S(1)} %pad_maximum_fusion.38), channel_id=1, source_target_pairs={{0,4},{1,5},{2,6},{3,7},{4,0},{5,1},{6,2},{7,3},{8,12},{9,13},{10,... | collective-permute-start | bytes 786440 | tf_op jit(solution)/shard_map/ppermute | solution.py:69
  263.5 15.9 %collective-permute-start.46 = (bf16[128,2048]{1,0:T(8,128)(2,1)S(1)}, bf16[128,2048]{1,0:T(8,128)(2,1)S(1)}, u32[]{:S(2)}, u32[]{:S(2)}) collective-permute-start(bf16[128,2048]{1,0:T(8,128)(2,1)S(1)} %pad_maximum_fusion.29), channel_id=1, source_target_pairs={{0,2},{1,3},{2,0},{3,1},{4,6},{5,7},{6,4},{7,5},{8,10},{9,11},{10,... | collective-permute-start | bytes 1572872 | tf_op jit(solution)/shard_map/ppermute | solution.py:69
  306.5 21.4 %collective-permute-start.53 = (bf16[2,64,2048]{2,1,0:T(8,128)(2,1)}, bf16[2,64,2048]{2,1,0:T(8,128)(2,1)}, u32[]{:S(2)}, u32[]{:S(2)}) collective-permute-start(bf16[2,64,2048]{2,1,0:T(8,128)(2,1)} %pad_maximum_fusion.31), channel_id=1, source_target_pairs={{0,2},{1,3},{2,0},{3,1},{4,6},{5,7},{6,4},{7,5},{8,10},{9,11},{10,... | collective-permute-start | bytes 1572872 | tf_op jit(solution)/shard_map/ppermute | solution.py:69
  307.5 20.5 %collective-permute-start.52 = (bf16[2,64,2048]{2,1,0:T(8,128)(2,1)}, bf16[2,64,2048]{2,1,0:T(8,128)(2,1)}, u32[]{:S(2)}, u32[]{:S(2)}) collective-permute-start(bf16[2,64,2048]{2,1,0:T(8,128)(2,1)} %get-tuple-element.614), channel_id=1, source_target_pairs={{0,8},{1,9},{2,10},{3,11},{4,12},{5,13},{6,14},{7,15},{8,0},{9,1},... | collective-permute-start | bytes 1572872 | tf_op jit(solution)/shard_map/ppermute | solution.py:69
  330.2 16.6 %collective-permute-start.57 = (bf16[128,1024]{1,0:T(8,128)(2,1)S(1)}, bf16[128,1024]{1,0:T(8,128)(2,1)S(1)}, u32[]{:S(2)}, u32[]{:S(2)}) collective-permute-start(bf16[128,1024]{1,0:T(8,128)(2,1)S(1)} %fusion.41), channel_id=1, source_target_pairs={{0,16},{1,17},{2,18},{3,19},{4,20},{5,21},{6,22},{7,23},{8,24},{9,... | collective-permute-start | bytes 786440 | tf_op jit(solution)/shard_map/ppermute | solution.py:69
  346.9 21.7 %collective-permute-start.62 = (bf16[2048,1024]{1,0:T(8,128)(2,1)S(1)}, bf16[2048,1024]{1,0:T(8,128)(2,1)S(1)}, u32[]{:S(2)}, u32[]{:S(2)}) collective-permute-start(bf16[2048,1024]{1,0:T(8,128)(2,1)S(1)} %convolution_convert_fusion.1), channel_id=1, source_target_pairs={{0,1},{1,0},{2,3},{3,2},{4,5},{5,4},{6,7},{7,6},{8,9},{9,8},{10,11... | collective-permute-start | bytes 12582920 | tf_op jit(solution)/shard_map/ppermute | solution.py:69
  347.3 21.3 %collective-permute-start.61 = (bf16[320,1024]{1,0:T(8,128)(2,1)S(1)}, bf16[320,1024]{1,0:T(8,128)(2,1)S(1)}, u32[]{:S(2)}, u32[]{:S(2)}) collective-permute-start(bf16[320,1024]{1,0:T(8,128)(2,1)S(1)} %pad_maximum_fusion.19), channel_id=1, source_target_pairs={{0,4},{1,5},{2,6},{3,7},{4,0},{5,1},{6,2},{7,3},{8,12},{9,13},{10,... | collective-permute-start | bytes 1966088 | tf_op jit(solution)/shard_map/ppermute | solution.py:69
  351.4 17.1 %collective-permute-start.60 = (bf16[80,2048]{1,0:T(8,128)(2,1)S(1)}, bf16[80,2048]{1,0:T(8,128)(2,1)S(1)}, u32[]{:S(2)}, u32[]{:S(2)}) collective-permute-start(bf16[80,2048]{1,0:T(8,128)(2,1)S(1)} %slice.930.b), channel_id=1, source_target_pairs={{0,16},{1,17},{2,18},{3,19},{4,20},{5,21},{6,22},{7,23},{8,24},{9,... | collective-permute-start | bytes 983048 | tf_op jit(solution)/shard_map/ppermute | solution.py:69
  368.6 19.7 %collective-permute-start.63 = (bf16[96,2048]{1,0:T(8,128)(2,1)S(1)}, bf16[96,2048]{1,0:T(8,128)(2,1)S(1)}, u32[]{:S(2)}, u32[]{:S(2)}) collective-permute-start(bf16[96,2048]{1,0:T(8,128)(2,1)S(1)} %pad_maximum_fusion.37), channel_id=1, source_target_pairs={{0,16},{1,17},{2,18},{3,19},{4,20},{5,21},{6,22},{7,23},{8,24},{9,... | collective-permute-start | bytes 1179656 | tf_op jit(solution)/shard_map/ppermute | solution.py:69
  368.8 19.5 %collective-permute-start.64 = (bf16[160,2048]{1,0:T(8,128)(2,1)S(1)}, bf16[160,2048]{1,0:T(8,128)(2,1)S(1)}, u32[]{:S(2)}, u32[]{:S(2)}) collective-permute-start(bf16[160,2048]{1,0:T(8,128)(2,1)S(1)} %pad_maximum_fusion.20), channel_id=1, source_target_pairs={{0,2},{1,3},{2,0},{3,1},{4,6},{5,7},{6,4},{7,5},{8,10},{9,11},{10,... | collective-permute-start | bytes 1966088 | tf_op jit(solution)/shard_map/ppermute | solution.py:69
  369.9 19.2 %collective-permute-start.65 = (bf16[384,1024]{1,0:T(8,128)(2,1)S(1)}, bf16[384,1024]{1,0:T(8,128)(2,1)S(1)}, u32[]{:S(2)}, u32[]{:S(2)}) collective-permute-start(bf16[384,1024]{1,0:T(8,128)(2,1)S(1)} %slice_bitcast_fusion.5), channel_id=1, source_target_pairs={{0,4},{1,5},{2,6},{3,7},{4,0},{5,1},{6,2},{7,3},{8,12},{9,13},{10,... | collective-permute-start | bytes 2359304 | tf_op jit(solution)/shard_map/ppermute | solution.py:69
  405.7 27.3 %collective-permute-start.71 = (bf16[320,1024]{1,0:T(8,128)(2,1)S(1)}, bf16[320,1024]{1,0:T(8,128)(2,1)S(1)}, u32[]{:S(2)}, u32[]{:S(2)}) collective-permute-start(bf16[320,1024]{1,0:T(8,128)(2,1)S(1)} %fusion.22), channel_id=1, source_target_pairs={{0,16},{1,17},{2,18},{3,19},{4,20},{5,21},{6,22},{7,23},{8,24},{9,... | collective-permute-start | bytes 1966088 | tf_op jit(solution)/shard_map/ppermute | solution.py:69
  406.9 21.2 %collective-permute-start.73 = (bf16[2,64,2048]{2,1,0:T(8,128)(2,1)S(1)}, bf16[2,64,2048]{2,1,0:T(8,128)(2,1)S(1)}, u32[]{:S(2)}, u32[]{:S(2)}) collective-permute-start(bf16[2,64,2048]{2,1,0:T(8,128)(2,1)S(1)} %pad_maximum_fusion.34), channel_id=1, source_target_pairs={{0,2},{1,3},{2,0},{3,1},{4,6},{5,7},{6,4},{7,5},{8,10},{9,11},{10,... | collective-permute-start | bytes 1572872 | tf_op jit(solution)/shard_map/ppermute | solution.py:69
  408.0 21.4 %collective-permute-start.72 = (bf16[2,64,2048]{2,1,0:T(8,128)(2,1)S(1)}, bf16[2,64,2048]{2,1,0:T(8,128)(2,1)S(1)}, u32[]{:S(2)}, u32[]{:S(2)}) collective-permute-start(bf16[2,64,2048]{2,1,0:T(8,128)(2,1)S(1)} %get-tuple-element.608), channel_id=1, source_target_pairs={{0,8},{1,9},{2,10},{3,11},{4,12},{5,13},{6,14},{7,15},{8,0},{9,1},... | collective-permute-start | bytes 1572872 | tf_op jit(solution)/shard_map/ppermute | solution.py:69
  408.2 24.8 %collective-permute-start.70 = (bf16[512,1024]{1,0:T(8,128)(2,1)S(1)}, bf16[512,1024]{1,0:T(8,128)(2,1)S(1)}, u32[]{:S(2)}, u32[]{:S(2)}) collective-permute-start(bf16[512,1024]{1,0:T(8,128)(2,1)S(1)} %slice_bitcast_fusion), channel_id=1, source_target_pairs={{0,4},{1,5},{2,6},{3,7},{4,0},{5,1},{6,2},{7,3},{8,12},{9,13},{10,... | collective-permute-start | bytes 3145736 | tf_op jit(solution)/shard_map/ppermute | solution.py:69
  409.4 18.1 %collective-permute-start.74 = (bf16[4,64,2048]{2,1,0:T(8,128)(2,1)S(1)}, bf16[4,64,2048]{2,1,0:T(8,128)(2,1)S(1)}, u32[]{:S(2)}, u32[]{:S(2)}) collective-permute-start(bf16[4,64,2048]{2,1,0:T(8,128)(2,1)S(1)} %broadcast_select_fusion), channel_id=1, source_target_pairs={{0,1},{1,0},{2,3},{3,2},{4,5},{5,4},{6,7},{7,6},{8,9},{9,8},{10,11... | collective-permute-start | bytes 3145736 | tf_op jit(solution)/shard_map/ppermute | solution.py:69
  436.3 32.1 %collective-permute-start.79 = (bf16[256,1024]{1,0:T(8,128)(2,1)S(1)}, bf16[256,1024]{1,0:T(8,128)(2,1)S(1)}, u32[]{:S(2)}, u32[]{:S(2)}) collective-permute-start(bf16[256,1024]{1,0:T(8,128)(2,1)S(1)} %slice.941), channel_id=1, source_target_pairs={{0,16},{1,17},{2,18},{3,19},{4,20},{5,21},{6,22},{7,23},{8,24},{9,... | collective-permute-start | bytes 1572872 | tf_op jit(solution)/shard_map/ppermute | solution.py:69
  436.5 20.6 %collective-permute-start.78 = (bf16[512,384]{1,0:T(8,128)(2,1)S(1)}, bf16[512,384]{1,0:T(8,128)(2,1)S(1)}, u32[]{:S(2)}, u32[]{:S(2)}) collective-permute-start(bf16[512,384]{1,0:T(8,128)(2,1)S(1)} %get-tuple-element.636), channel_id=1, source_target_pairs={{0,12},{1,13},{2,14},{3,15},{4,8},{5,9},{6,10},{7,11},{8,4},{9,5},... | collective-permute-start | bytes 1179656 | tf_op jit(solution)/shard_map/ppermute | solution.py:69
  439.8 28.6 %collective-permute-start.77 = (bf16[512,384]{1,0:T(8,128)(2,1)S(1)}, bf16[512,384]{1,0:T(8,128)(2,1)S(1)}, u32[]{:S(2)}, u32[]{:S(2)}) collective-permute-start(bf16[512,384]{1,0:T(8,128)(2,1)S(1)} %get-tuple-element.637), channel_id=1, source_target_pairs={{0,8},{1,9},{2,10},{3,11},{4,12},{5,13},{6,14},{7,15},{8,0},{9,1},... | collective-permute-start | bytes 1179656 | tf_op jit(solution)/shard_map/ppermute | solution.py:69
  439.8 28.6 %collective-permute-start.76 = (bf16[512,384]{1,0:T(8,128)(2,1)S(1)}, bf16[512,384]{1,0:T(8,128)(2,1)S(1)}, u32[]{:S(2)}, u32[]{:S(2)}) collective-permute-start(bf16[512,384]{1,0:T(8,128)(2,1)S(1)} %get-tuple-element.638), channel_id=1, source_target_pairs={{0,4},{1,5},{2,6},{3,7},{4,0},{5,1},{6,2},{7,3},{8,12},{9,13},{10,... | collective-permute-start | bytes 1179656 | tf_op jit(solution)/shard_map/ppermute | solution.py:69
  484.6 21.0 %collective-permute-start.86 = (bf16[160,1024]{1,0:T(8,128)(2,1)S(1)}, bf16[160,1024]{1,0:T(8,128)(2,1)S(1)}, u32[]{:S(2)}, u32[]{:S(2)}) collective-permute-start(bf16[160,1024]{1,0:T(8,128)(2,1)S(1)} %slice.809), channel_id=1, source_target_pairs={{0,16},{1,17},{2,18},{3,19},{4,20},{5,21},{6,22},{7,23},{8,24},{9,... | collective-permute-start | bytes 983048 | tf_op jit(solution)/shard_map/ppermute | solution.py:69
  485.9 19.7 %collective-permute-start.85 = (bf16[256,1024]{1,0:T(8,128)(2,1)S(1)}, bf16[256,1024]{1,0:T(8,128)(2,1)S(1)}, u32[]{:S(2)}, u32[]{:S(2)}) collective-permute-start(bf16[256,1024]{1,0:T(8,128)(2,1)S(1)} %get-tuple-element.513), channel_id=1, source_target_pairs={{0,4},{1,5},{2,6},{3,7},{4,0},{5,1},{6,2},{7,3},{8,12},{9,13},{10,... | collective-permute-start | bytes 1572872 | tf_op jit(solution)/shard_map/ppermute | solution.py:69
  486.5 17.9 %collective-permute-start.87 = (bf16[4,64,1024]{2,1,0:T(8,128)(2,1)S(1)}, bf16[4,64,1024]{2,1,0:T(8,128)(2,1)S(1)}, u32[]{:S(2)}, u32[]{:S(2)}) collective-permute-start(bf16[4,64,1024]{2,1,0:T(8,128)(2,1)S(1)} %get-tuple-element.517), channel_id=1, source_target_pairs={{0,8},{1,9},{2,10},{3,11},{4,12},{5,13},{6,14},{7,15},{8,0},{9,1},... | collective-permute-start | bytes 1572872 | tf_op jit(solution)/shard_map/ppermute | solution.py:69
  488.2 16.4 %collective-permute-start.84 = (bf16[2048,768]{1,0:T(8,128)(2,1)S(1)}, bf16[2048,768]{1,0:T(8,128)(2,1)S(1)}, u32[]{:S(2)}, u32[]{:S(2)}) collective-permute-start(bf16[2048,768]{1,0:T(8,128)(2,1)S(1)} %convolution_convert_fusion.4), channel_id=1, source_target_pairs={{0,1},{1,0},{2,3},{3,2},{4,5},{5,4},{6,7},{7,6},{8,9},{9,8},{10,11... | collective-permute-start | bytes 9437192 | tf_op jit(solution)/shard_map/ppermute | solution.py:69
  507.1 18.8 %collective-permute-start.91 = (bf16[4,64,1024]{2,1,0:T(8,128)(2,1)S(1)}, bf16[4,64,1024]{2,1,0:T(8,128)(2,1)S(1)}, u32[]{:S(2)}, u32[]{:S(2)}) collective-permute-start(bf16[4,64,1024]{2,1,0:T(8,128)(2,1)S(1)} %get-tuple-element.528), channel_id=1, source_target_pairs={{0,8},{1,9},{2,10},{3,11},{4,12},{5,13},{6,14},{7,15},{8,0},{9,1},... | collective-permute-start | bytes 1572872 | tf_op jit(solution)/shard_map/ppermute | solution.py:69
  507.4 18.6 %collective-permute-start.92 = (bf16[2,2,64,1024]{3,2,0,1:T(8,128)(2,1)S(1)}, bf16[2,2,64,1024]{3,2,0,1:T(8,128)(2,1)S(1)}, u32[]{:S(2)}, u32[]{:S(2)}) collective-permute-start(bf16[2,2,64,1024]{3,2,0,1:T(8,128)(2,1)S(1)} %fusion.37), channel_id=1, source_target_pairs={{0,2},{1,3},{2,0},{3,1},{4,6},{5,7},{6,4},{7,5},{8,10},{9,11},{10,... | collective-permute-start | bytes 1572872 | tf_op jit(solution)/shard_map/ppermute | solution.py:69
  508.2 18.0 %collective-permute-start.89 = (bf16[2,48,2048]{2,1,0:T(8,128)(2,1)S(1)}, bf16[2,48,2048]{2,1,0:T(8,128)(2,1)S(1)}, u32[]{:S(2)}, u32[]{:S(2)}) collective-permute-start(bf16[2,48,2048]{2,1,0:T(8,128)(2,1)S(1)} %get-tuple-element.602), channel_id=1, source_target_pairs={{0,16},{1,17},{2,18},{3,19},{4,20},{5,21},{6,22},{7,23},{8,24},{9,... | collective-permute-start | bytes 1179656 | tf_op jit(solution)/shard_map/ppermute | solution.py:69
  511.0 22.2 %collective-permute-start.90 = (bf16[2,80,2048]{2,1,0:T(8,128)(2,1)S(1)}, bf16[2,80,2048]{2,1,0:T(8,128)(2,1)S(1)}, u32[]{:S(2)}, u32[]{:S(2)}) collective-permute-start(bf16[2,80,2048]{2,1,0:T(8,128)(2,1)S(1)} %pad_maximum_fusion.22), channel_id=1, source_target_pairs={{0,2},{1,3},{2,0},{3,1},{4,6},{5,7},{6,4},{7,5},{8,10},{9,11},{10,... | collective-permute-start | bytes 1966088 | tf_op jit(solution)/shard_map/ppermute | solution.py:69
  512.5 20.7 %collective-permute-start.88 = (bf16[512,768]{1,0:T(8,128)(2,1)S(1)}, bf16[512,768]{1,0:T(8,128)(2,1)S(1)}, u32[]{:S(2)}, u32[]{:S(2)}) collective-permute-start(bf16[512,768]{1,0:T(8,128)(2,1)S(1)} %slice_bitcast_fusion.4), channel_id=1, source_target_pairs={{0,4},{1,5},{2,6},{3,7},{4,0},{5,1},{6,2},{7,3},{8,12},{9,13},{10,... | collective-permute-start | bytes 2359304 | tf_op jit(solution)/shard_map/ppermute | solution.py:69
  538.8 18.2 %collective-permute-start.93 = (bf16[512,768]{1,0:T(8,128)(2,1)S(1)}, bf16[512,768]{1,0:T(8,128)(2,1)S(1)}, u32[]{:S(2)}, u32[]{:S(2)}) collective-permute-start(bf16[512,768]{1,0:T(8,128)(2,1)S(1)} %fusion.21), channel_id=1, source_target_pairs={{0,8},{1,9},{2,10},{3,11},{4,12},{5,13},{6,14},{7,15},{8,0},{9,1},... | collective-permute-start | bytes 2359304 | tf_op jit(solution)/shard_map/ppermute | solution.py:69
  558.2 31.2 %all-to-all-start.1 = ((bf16[8,64,768]{2,1,0:T(8,128)(2,1)}), bf16[8,64,768]{2,1,0:T(8,128)(2,1)S(1)}, u32[]{:S(2)}, u32[]{:S(2)}) async-start(bf16[8,64,768]{2,1,0:T(8,128)(2,1)} %bitcast.122), calls=%async_computation.1 | async-start | bytes 1572864 | tf_op jit(solution)/shard_map/all_to_all | solution.py:583
  (136 other events, 1171.2 us)

commit v7 on v6

--- a/solution.py
+++ b/solution.py
@@ -839,17 +839,23 @@
         down_other_grad, down_other, down_mine, act_mine, act_other
     )
     down_swapped = swap(down_other_grad, 1)
+    down_mine_grad = matmul(grad_all, act_mine, ((0,), (0,))).astype(bf16)
 
     def back(hidden, down):
         return jax.vjp(gelu, hidden)[1](matmul(grad_all, down))[0].astype(bf16)
 
     hid_mine, hid_other = back(hidden_mine, down_mine), back(hidden_other, down_other)
     second_parts = matmul(hid_mine, up_mine, ((1,), (1,))) + matmul(hid_other, up_other, ((1,), (1,)))
-    second_parts, hid_mine, hid_other, down_swapped, act_mine, act_other = tied(
-        second_parts.astype(bf16), hid_mine, hid_other, down_swapped, act_mine, act_other
+    second_parts, hid_mine, hid_other, down_swapped, down_mine_grad, act_mine, act_other = tied(
+        second_parts.astype(bf16),
+        hid_mine,
+        hid_other,
+        down_swapped,
+        down_mine_grad,
+        act_mine,
+        act_other,
     )
     second_back = feed.scatter_one(second_parts)
-    down_mine_grad = matmul(grad_all, act_mine, ((0,), (0,))).astype(bf16)
     down_sum = feed.first_sum(down_mine_grad, down_swapped)
     c1, c2, c3 = n_block // 4, n_block * 5 // 8, n_block // 4
     down_x3 = [swap(down_sum[3][:c1], feed.second)]
@@ -943,7 +949,7 @@
         dkv = dkv + swap(dkv_other[i], rel).astype(f32)
     triple = jnp.concatenate([dq, dkv.astype(bf16)], axis=2).reshape(4, 4 * rows, 3 * HEAD)
     up_z1 = added(up_sum[1], up_x3)
-    za, zb = n_block // 2, n_block * 11 // 16
+    za, zb = n_block * 3 // 8, n_block * 5 // 8
     out_grad = out_grad.reshape(2, 2, HEAD // len(plan.part_rel), width)
     triple, up_sum, up_z1, up_z1a, down_z1, out_grad, out_sent = tied(
         triple, up_sum, up_z1, up_z1[:za], down_z1, out_grad, out_grad[:, 1]

time: 603 us -> 599 us (level)
    unnamed x205 -> x201, local copies, waits for them, and re-layouts: 14.4 us -> 14.4 us
  transfers between devices with their start and end apart: 104 -> 104, of which waited for: 46 -> 46; matrix products, arithmetic and copies ran while one was open for 19% -> 19% of each run, Pallas kernels for 8% -> 9%
where the time goes in v7:
time: 599 us; the launch traced here: 588 us
  waiting for transfers between devices  273 us (46%)
  starting transfers between devices  115 us (19%)
  matrix products  57.5 us (10%)
  Pallas kernels  56 us (9%)
  other arithmetic  49 us (8%)
  local copies, waits for them, and re-layouts  33.9 us (6%)
    ppermute x102, waiting for transfers between devices, swap(): return lax.ppermute(value, AXES, [(d, d ^ mask) for d in self.devices])  273 us
    ppermute x102, starting transfers between devices, swap(): return lax.ppermute(value, AXES, [(d, d ^ mask) for d in self.devices])  105 us
    dot_general x21, matrix products, matmul(): lax.dot_general(left, right, (dims, ((), ())), preferred_element_type=f32)  57.5 us
    pallas_call x1, Pallas kernels, attend_back(): call(functools.partial(attend_back_kernel, plan), 2, 6, (shape((blocks, B...  20 us
    convert_element_type x21, other arithmetic, added(): return sum((v.astype(f32) for v in values)).astype(bf16)  18.9 us
    pallas_call x1, Pallas kernels, attend(): call(functools.partial(attend_kernel, plan), 2, 2, (shape((blocks, BLOCK,...  18.4 us
    unnamed x201, local copies, waits for them, and re-layouts  14.4 us
  transfers between devices with their start and end apart: 104, of which 46 were waited for; matrix products, arithmetic and copies ran while one was open for 19% of the time, Pallas kernels for 9%

profile of v7, /device:TPU:0, one launch (start us, length us, event | category | flops | bytes accessed | tf_op | source)
XLA Modules:
  0.0 588.5 jit_solution(14750734814819908094)
XLA Ops:
  3.9 6.4 %all-to-all-start = ((bf16[8,64,768]{2,1,0:T(8,128)(2,1)}), bf16[8,64,768]{2,1,0:T(8,128)(2,1)}, u32[]{:S(2)}, u32[]{:S(2)}) async-start(bf16[8,64,768]{2,1,0:T(8,128)(2,1)} %shard_map.233), calls=%async_computation | async-start | bytes 1572864 | tf_op jit(solution)/shard_map/all_to_all | solution.py:583
  20.2 5.7 collective-permute-done.2
  25.8 7.6 %collective-permute-done.1.b_hi = bf16[64,2048]{1,0:T(8,128)(2,1)} collective-permute-done((bf16[64,2048]{1,0:T(8,128)(2,1)S(1)}, bf16[64,2048]{1,0:T(8,128)(2,1)}, u32[]{:S(2)}, u32[]{:S(2)}) %collective-permute-start.1) | collective-permute-done | bytes 262176 | tf_op jit(solution)/shard_map/ppermute | solution.py:69
  37.9 3.6 collective-permute-start.6
  43.0 19.6 %collective-permute-done.5.a_lo = bf16[48,2048]{1,0:T(8,128)(2,1)S(1)} collective-permute-done((bf16[48,2048]{1,0:T(8,128)(2,1)S(1)}, bf16[48,2048]{1,0:T(8,128)(2,1)S(1)}, u32[]{:S(2)}, u32[]{:S(2)}) %collective-permute-start.5) | collective-permute-done | bytes 196640 | tf_op jit(solution)/shard_map/ppermute | solution.py:69
  68.9 2.6 collective-permute-start.9
  75.5 13.3 %collective-permute-done.9.a_far = bf16[96,2048]{1,0:T(8,128)(2,1)S(1)} collective-permute-done((bf16[96,2048]{1,0:T(8,128)(2,1)S(1)}, bf16[96,2048]{1,0:T(8,128)(2,1)S(1)}, u32[]{:S(2)}, u32[]{:S(2)}) %collective-permute-start.9) | collective-permute-done | bytes 393248 | tf_op jit(solution)/shard_map/ppermute | solution.py:69
  92.7 3.3 collective-permute-start.16
  98.2 4.4 fusion.120
  105.1 3.7 fusion.119
  112.2 5.4 collective-permute-done.16.got
  117.6 6.4 %collective-permute-done.14 = bf16[256,1024]{1,0:T(8,128)(2,1)S(1)} collective-permute-done((bf16[256,1024]{1,0:T(8,128)(2,1)S(1)}, bf16[256,1024]{1,0:T(8,128)(2,1)S(1)}, u32[]{:S(2)}, u32[]{:S(2)}) %collective-permute-start.14) | collective-permute-done | bytes 524320 | tf_op jit(solution)/shard_map/ppermute | solution.py:69
  130.0 17.3 %collective-permute-done.17 = bf16[512,384]{1,0:T(8,128)(2,1)S(1)} collective-permute-done((bf16[512,384]{1,0:T(8,128)(2,1)S(1)}, bf16[512,384]{1,0:T(8,128)(2,1)S(1)}, u32[]{:S(2)}, u32[]{:S(2)}) %collective-permute-start.17) | collective-permute-done | bytes 393248 | tf_op jit(solution)/shard_map/ppermute | solution.py:69
  149.3 6.4 %collective-permute-done.19 = bf16[512,384]{1,0:T(8,128)(2,1)S(1)} collective-permute-done((bf16[512,384]{1,0:T(8,128)(2,1)S(1)}, bf16[512,384]{1,0:T(8,128)(2,1)S(1)}, u32[]{:S(2)}, u32[]{:S(2)}) %collective-permute-start.19) | collective-permute-done | bytes 393248 | tf_op jit(solution)/shard_map/ppermute | solution.py:69
  167.0 18.4 %shard_map.240 = (bf16[16,128,128]{2,1,0:T(8,128)(2,1)S(1)}, f32[8,128,256]{2,1,0:T(8,128)S(1)}, f32[8,1,256]{2,1,0:T(1,128)S(1)}, bf16[4096,128]{1,0:T(8,128)(2,1)S(1)}, bf16[4096,128]{1,0:T(8,128)(2,1)S(1)}) custom-call(s32[56]{0:T(128)S(1)} %concatenate.196.info, s32[8]{0:T(128)S(1)} %copy-done.29, bf16[16,128,384]{2,1,0:T(8,128)(2,1)S(1)} %bitcast.283, ...), custom_call_target="tpu_custom_call" | custom-call | flops 4294967296 | bytes 8388608 | tf_op jit(solution)/shard_map/pallas_call | solution.py:463
  196.0 6.2 %collective-permute-done.29 = bf16[512,128]{1,0:T(8,128)(2,1)S(1)} collective-permute-done((bf16[512,128]{1,0:T(8,128)(2,1)S(1)}, bf16[512,128]{1,0:T(8,128)(2,1)S(1)}, u32[]{:S(2)}, u32[]{:S(2)}) %collective-permute-start.29) | collective-permute-done | bytes 131104 | tf_op jit(solution)/shard_map/ppermute | solution.py:69
  202.2 4.5 collective-permute-done.32
  211.5 16.8 %collective-permute-done.33 = bf16[2,48,2048]{2,1,0:T(8,128)(2,1)S(1)} collective-permute-done((bf16[2,48,2048]{2,1,0:T(8,128)(2,1)S(1)}, bf16[2,48,2048]{2,1,0:T(8,128)(2,1)S(1)}, u32[]{:S(2)}, u32[]{:S(2)}) %collective-permute-start.33) | collective-permute-done | bytes 393248 | tf_op jit(solution)/shard_map/ppermute | solution.py:69
  232.9 3.1 collective-permute-done.36
  236.1 10.5 %collective-permute-done.37 = bf16[80,2048]{1,0:T(8,128)(2,1)S(1)} collective-permute-done((bf16[80,2048]{1,0:T(8,128)(2,1)S(1)}, bf16[80,2048]{1,0:T(8,128)(2,1)S(1)}, u32[]{:S(2)}, u32[]{:S(2)}) %collective-permute-start.37) | collective-permute-done | bytes 327712 | tf_op jit(solution)/shard_map/ppermute | solution.py:69
  250.0 2.5 collective-permute-start.42
  253.8 9.7 %collective-permute-done.44 = bf16[96,1024]{1,0:T(8,128)(2,1)S(1)} collective-permute-done((bf16[96,1024]{1,0:T(8,128)(2,1)S(1)}, bf16[96,1024]{1,0:T(8,128)(2,1)S(1)}, u32[]{:S(2)}, u32[]{:S(2)}) %collective-permute-start.44) | collective-permute-done | bytes 196640 | tf_op jit(solution)/shard_map/ppermute | solution.py:69
  268.8 6.5 %collective-permute-done.48 = bf16[32,1024]{1,0:T(8,128)(2,1)S(1)} collective-permute-done((bf16[32,1024]{1,0:T(8,128)(2,1)S(1)}, bf16[32,1024]{1,0:T(8,128)(2,1)S(1)}, u32[]{:S(2)}, u32[]{:S(2)}) %collective-permute-start.48) | collective-permute-done | bytes 65568 | tf_op jit(solution)/shard_map/ppermute | solution.py:69
  276.8 2.7 collective-permute-done.49
  280.0 2.7 multiply_convert_fusion.1
  282.8 4.4 convolution_convert_fusion.3
  287.2 3.0 multiply_convert_fusion
  290.8 2.4 convolution_convert_fusion.2
  293.2 3.4 fusion.6
  296.7 2.4 fusion.121
  299.1 3.4 fusion.13
  302.5 2.8 add_convert_fusion.5
  309.1 3.2 collective-permute-start.52
  312.3 4.3 add_convert_fusion.1
  320.3 5.8 collective-permute-done.54
  335.4 2.4 convolution_convert_fusion.1
  338.9 3.5 collective-permute-done.56
  351.9 4.5 collective-permute-done.59.a_lo
  356.3 9.9 %collective-permute-done.60.b_hi = bf16[80,2048]{1,0:T(8,128)(2,1)S(1)} collective-permute-done((bf16[80,2048]{1,0:T(8,128)(2,1)S(1)}, bf16[80,2048]{1,0:T(8,128)(2,1)S(1)}, u32[]{:S(2)}, u32[]{:S(2)}) %collective-permute-start.60) | collective-permute-done | bytes 327712 | tf_op jit(solution)/shard_map/ppermute | solution.py:69
  369.7 2.4 fusion.122
  372.1 2.6 add_convert_fusion.4
  376.0 2.4 convolution_convert_fusion
  378.4 7.6 %collective-permute-done.63.a_far = bf16[96,2048]{1,0:T(8,128)(2,1)S(1)} collective-permute-done((bf16[96,2048]{1,0:T(8,128)(2,1)S(1)}, bf16[96,2048]{1,0:T(8,128)(2,1)S(1)}, u32[]{:S(2)}, u32[]{:S(2)}) %collective-permute-start.63) | collective-permute-done | bytes 393248 | tf_op jit(solution)/shard_map/ppermute | solution.py:69
  390.4 2.5 collective-permute-start.68
  407.2 20.0 %shard_map.245 = (bf16[16,128,128]{2,1,0:T(8,128)(2,1)S(1)}, bf16[16,128,256]{2,1,0:T(8,128)(2,1)S(1)}, bf16[1,16,128,256]{3,2,1,0:T(8,128)(2,1)S(1)}) custom-call(s32[56]{0:T(128)S(1)} %concatenate.196.info, s32[8]{0:T(128)S(1)} %copy-done.29, bf16[16,128,384]{2,1,0:T(8,128)(2,1)S(1)} %bitcast.284, bf16[4096,128]{1,0:T(8,128)(2,1)S(1)} %copy-done.33, ...), custom_call_target="tpu_custom_call" | custom-call | flops 10737418240 | bytes 8388608 | tf_op jit(solution)/shard_map/pallas_call | solution.py:485
  427.8 2.8 collective-permute-done.71
  434.2 3.0 collective-permute-start.77
  441.2 14.2 %collective-permute-done.78.refs_3_ = bf16[512,384]{1,0:T(8,128)(2,1)S(1)} collective-permute-done((bf16[512,384]{1,0:T(8,128)(2,1)S(1)}, bf16[512,384]{1,0:T(8,128)(2,1)S(1)}, u32[]{:S(2)}, u32[]{:S(2)}) %collective-permute-start.78) | collective-permute-done | bytes 393248 | tf_op jit(solution)/shard_map/ppermute | solution.py:69
  455.5 7.7 %collective-permute-done.77.refs_2_ = bf16[512,384]{1,0:T(8,128)(2,1)S(1)} collective-permute-done((bf16[512,384]{1,0:T(8,128)(2,1)S(1)}, bf16[512,384]{1,0:T(8,128)(2,1)S(1)}, u32[]{:S(2)}, u32[]{:S(2)}) %collective-permute-start.77) | collective-permute-done | bytes 393248 | tf_op jit(solution)/shard_map/ppermute | solution.py:69
  467.8 2.3 shard_map.247
  474.5 4.3 collective-permute-done.81
  485.1 3.7 fusion.123
  488.9 3.7 add_convert_fusion.3
  493.6 6.8 %collective-permute-done.87 = bf16[4,64,1024]{2,1,0:T(8,128)(2,1)S(1)} collective-permute-done((bf16[4,64,1024]{2,1,0:T(8,128)(2,1)S(1)}, bf16[4,64,1024]{2,1,0:T(8,128)(2,1)S(1)}, u32[]{:S(2)}, u32[]{:S(2)}) %collective-permute-start.87) | collective-permute-done | bytes 524320 | tf_op jit(solution)/shard_map/ppermute | solution.py:69
  504.6 2.3 collective-permute-start.89
  509.5 11.6 %collective-permute-done.91 = bf16[4,64,1024]{2,1,0:T(8,128)(2,1)S(1)} collective-permute-done((bf16[4,64,1024]{2,1,0:T(8,128)(2,1)S(1)}, bf16[4,64,1024]{2,1,0:T(8,128)(2,1)S(1)}, u32[]{:S(2)}, u32[]{:S(2)}) %collective-permute-start.91) | collective-permute-done | bytes 524320 | tf_op jit(solution)/shard_map/ppermute | solution.py:69
  521.3 8.0 %collective-permute-done.90 = bf16[2,80,2048]{2,1,0:T(8,128)(2,1)S(1)} collective-permute-done((bf16[2,80,2048]{2,1,0:T(8,128)(2,1)S(1)}, bf16[2,80,2048]{2,1,0:T(8,128)(2,1)S(1)}, u32[]{:S(2)}, u32[]{:S(2)}) %collective-permute-start.90) | collective-permute-done | bytes 655392 | tf_op jit(solution)/shard_map/ppermute | solution.py:69
  537.6 3.5 collective-permute-done.96
  544.6 2.4 collective-permute-done.94
  546.9 6.8 %collective-permute-done.93 = bf16[512,768]{1,0:T(8,128)(2,1)S(1)} collective-permute-done((bf16[512,768]{1,0:T(8,128)(2,1)S(1)}, bf16[512,768]{1,0:T(8,128)(2,1)S(1)}, u32[]{:S(2)}, u32[]{:S(2)}) %collective-permute-start.93) | collective-permute-done | bytes 786464 | tf_op jit(solution)/shard_map/ppermute | solution.py:69
  555.0 3.8 all-to-all-start.1
  564.3 8.8 %collective-permute-done.98 = bf16[2,64,2048]{2,1,0:T(8,128)(2,1)S(1)} collective-permute-done((bf16[2,64,2048]{2,1,0:T(8,128)(2,1)S(1)}, bf16[2,64,2048]{2,1,0:T(8,128)(2,1)S(1)}, u32[]{:S(2)}, u32[]{:S(2)}) %collective-permute-start.98) | collective-permute-done | bytes 524320 | tf_op jit(solution)/shard_map/ppermute | solution.py:69
  573.5 2.4 shard_map.250
  578.7 5.8 collective-permute-done.99
  (583 shorter events, 198.8 us)
Async XLA Ops:
  3.9 29.5 %all-to-all-start = ((bf16[8,64,768]{2,1,0:T(8,128)(2,1)}), bf16[8,64,768]{2,1,0:T(8,128)(2,1)}, u32[]{:S(2)}, u32[]{:S(2)}) async-start(bf16[8,64,768]{2,1,0:T(8,128)(2,1)} %shard_map.233), calls=%async_computation | async-start | bytes 1572864 | tf_op jit(solution)/shard_map/all_to_all | solution.py:583
  10.3 15.5 %collective-permute-start.2 = (bf16[64,2048]{1,0:T(8,128)(2,1)}, bf16[64,2048]{1,0:T(8,128)(2,1)}, u32[]{:S(2)}, u32[]{:S(2)}) collective-permute-start(bf16[64,2048]{1,0:T(8,128)(2,1)} %param.22), channel_id=1, source_target_pairs={{0,8},{1,9},{2,10},{3,11},{4,12},{5,13},{6,14},{7,15},{8,0},{9,1},... | collective-permute-start | bytes 786440 | tf_op jit(solution)/shard_map/ppermute | solution.py:69
  13.3 20.1 %collective-permute-start.1 = (bf16[64,2048]{1,0:T(8,128)(2,1)S(1)}, bf16[64,2048]{1,0:T(8,128)(2,1)}, u32[]{:S(2)}, u32[]{:S(2)}) collective-permute-start(bf16[64,2048]{1,0:T(8,128)(2,1)S(1)} %get-tuple-element.340.b), channel_id=1, source_target_pairs={{0,8},{1,9},{2,10},{3,11},{4,12},{5,13},{6,14},{7,15},{8,0},{9,1},... | collective-permute-start | bytes 786440 | tf_op jit(solution)/shard_map/ppermute | solution.py:69
  13.8 19.6 %collective-permute-start = (bf16[64,2048]{1,0:T(8,128)(2,1)}, bf16[64,2048]{1,0:T(8,128)(2,1)}, u32[]{:S(2)}, u32[]{:S(2)}) collective-permute-start(bf16[64,2048]{1,0:T(8,128)(2,1)} %get-tuple-element.338.a), channel_id=1, source_target_pairs={{0,2},{1,3},{2,0},{3,1},{4,6},{5,7},{6,4},{7,5},{8,10},{9,11},{10,... | collective-permute-start | bytes 786440 | tf_op jit(solution)/shard_map/ppermute | solution.py:69
  33.4 29.2 %collective-permute-start.7 = (bf16[4,64,2048]{2,1,0:T(8,128)(2,1)}, bf16[4,64,2048]{2,1,0:T(8,128)(2,1)S(1)}, u32[]{:S(2)}, u32[]{:S(2)}) collective-permute-start(bf16[4,64,2048]{2,1,0:T(8,128)(2,1)} %slice.875), channel_id=1, source_target_pairs={{0,2},{1,3},{2,0},{3,1},{4,6},{5,7},{6,4},{7,5},{8,10},{9,11},{10,... | collective-permute-start | bytes 3145736 | tf_op jit(solution)/shard_map/ppermute | solution.py:69
  35.1 27.6 %collective-permute-start.4 = (bf16[512,768]{1,0:T(8,128)(2,1)}, bf16[512,768]{1,0:T(8,128)(2,1)S(1)}, u32[]{:S(2)}, u32[]{:S(2)}) collective-permute-start(bf16[512,768]{1,0:T(8,128)(2,1)} %bitcast.2), channel_id=1, source_target_pairs={{0,4},{1,5},{2,6},{3,7},{4,0},{5,1},{6,2},{7,3},{8,12},{9,13},{10,... | collective-permute-start | bytes 2359304 | tf_op jit(solution)/shard_map/ppermute | solution.py:69
  36.5 26.1 %collective-permute-start.3 = (bf16[512,768]{1,0:T(8,128)(2,1)}, bf16[512,768]{1,0:T(8,128)(2,1)S(1)}, u32[]{:S(2)}, u32[]{:S(2)}) collective-permute-start(bf16[512,768]{1,0:T(8,128)(2,1)} %bitcast.2), channel_id=1, source_target_pairs={{0,8},{1,9},{2,10},{3,11},{4,12},{5,13},{6,14},{7,15},{8,0},{9,1},... | collective-permute-start | bytes 2359304 | tf_op jit(solution)/shard_map/ppermute | solution.py:69
  37.9 24.7 %collective-permute-start.6 = (bf16[80,2048]{1,0:T(8,128)(2,1)S(1)}, bf16[80,2048]{1,0:T(8,128)(2,1)S(1)}, u32[]{:S(2)}, u32[]{:S(2)}) collective-permute-start(bf16[80,2048]{1,0:T(8,128)(2,1)S(1)} %slice.679.b), channel_id=1, source_target_pairs={{0,16},{1,17},{2,18},{3,19},{4,20},{5,21},{6,22},{7,23},{8,24},{9,... | collective-permute-start | bytes 983048 | tf_op jit(solution)/shard_map/ppermute | solution.py:69
  42.4 20.2 %collective-permute-start.5 = (bf16[48,2048]{1,0:T(8,128)(2,1)S(1)}, bf16[48,2048]{1,0:T(8,128)(2,1)S(1)}, u32[]{:S(2)}, u32[]{:S(2)}) collective-permute-start(bf16[48,2048]{1,0:T(8,128)(2,1)S(1)} %slice.678.a), channel_id=1, source_target_pairs={{0,2},{1,3},{2,0},{3,1},{4,6},{5,7},{6,4},{7,5},{8,10},{9,11},{10,... | collective-permute-start | bytes 589832 | tf_op jit(solution)/shard_map/ppermute | solution.py:69
  63.4 26.0 %collective-permute-start.10 = (bf16[160,2048]{1,0:T(8,128)(2,1)S(1)}, bf16[160,2048]{1,0:T(8,128)(2,1)S(1)}, u32[]{:S(2)}, u32[]{:S(2)}) collective-permute-start(bf16[160,2048]{1,0:T(8,128)(2,1)S(1)} %pad_maximum_fusion.16), channel_id=1, source_target_pairs={{0,2},{1,3},{2,0},{3,1},{4,6},{5,7},{6,4},{7,5},{8,10},{9,11},{10,... | collective-permute-start | bytes 1966088 | tf_op jit(solution)/shard_map/ppermute | solution.py:69
  64.9 25.5 %collective-permute-start.8 = (bf16[512,768]{1,0:T(8,128)(2,1)S(1)}, bf16[512,768]{1,0:T(8,128)(2,1)S(1)}, u32[]{:S(2)}, u32[]{:S(2)}) collective-permute-start(bf16[512,768]{1,0:T(8,128)(2,1)S(1)} %collective-permute-done.3), channel_id=1, source_target_pairs={{0,4},{1,5},{2,6},{3,7},{4,0},{5,1},{6,2},{7,3},{8,12},{9,13},{10,... | collective-permute-start | bytes 2359304 | tf_op jit(solution)/shard_map/ppermute | solution.py:69
  67.7 22.7 %collective-permute-start.12 = (bf16[4,64,1024]{2,1,0:T(8,128)(2,1)S(1)}, bf16[4,64,1024]{2,1,0:T(8,128)(2,1)S(1)}, u32[]{:S(2)}, u32[]{:S(2)}) collective-permute-start(bf16[4,64,1024]{2,1,0:T(8,128)(2,1)S(1)} %bitcast.330), channel_id=1, source_target_pairs={{0,8},{1,9},{2,10},{3,11},{4,12},{5,13},{6,14},{7,15},{8,0},{9,1},... | collective-permute-start | bytes 1572872 | tf_op jit(solution)/shard_map/ppermute | solution.py:69
  68.9 19.9 %collective-permute-start.9 = (bf16[96,2048]{1,0:T(8,128)(2,1)S(1)}, bf16[96,2048]{1,0:T(8,128)(2,1)S(1)}, u32[]{:S(2)}, u32[]{:S(2)}) collective-permute-start(bf16[96,2048]{1,0:T(8,128)(2,1)S(1)} %pad_maximum_fusion.36), channel_id=1, source_target_pairs={{0,16},{1,17},{2,18},{3,19},{4,20},{5,21},{6,22},{7,23},{8,24},{9,... | collective-permute-start | bytes 1179656 | tf_op jit(solution)/shard_map/ppermute | solution.py:69
  92.7 24.9 %collective-permute-start.16 = (bf16[4,64,1024]{2,1,0:T(8,128)(2,1)}, bf16[4,64,1024]{2,1,0:T(8,128)(2,1)S(1)}, u32[]{:S(2)}, u32[]{:S(2)}) collective-permute-start(bf16[4,64,1024]{2,1,0:T(8,128)(2,1)} %bitcast.14), channel_id=1, source_target_pairs={{0,8},{1,9},{2,10},{3,11},{4,12},{5,13},{6,14},{7,15},{8,0},{9,1},... | collective-permute-start | bytes 1572872 | tf_op jit(solution)/shard_map/ppermute | solution.py:69
  96.7 27.3 %collective-permute-start.15 = (bf16[512,1024]{1,0:T(8,128)(2,1)S(1)}, bf16[512,1024]{1,0:T(8,128)(2,1)S(1)}, u32[]{:S(2)}, u32[]{:S(2)}) collective-permute-start(bf16[512,1024]{1,0:T(8,128)(2,1)S(1)} %shard_map.238), channel_id=1, source_target_pairs={{0,4},{1,5},{2,6},{3,7},{4,0},{5,1},{6,2},{7,3},{8,12},{9,13},{10,... | collective-permute-start | bytes 3145736 | tf_op jit(solution)/shard_map/ppermute | solution.py:69
  98.0 26.0 %collective-permute-start.14 = (bf16[256,1024]{1,0:T(8,128)(2,1)S(1)}, bf16[256,1024]{1,0:T(8,128)(2,1)S(1)}, u32[]{:S(2)}, u32[]{:S(2)}) collective-permute-start(bf16[256,1024]{1,0:T(8,128)(2,1)S(1)} %get-tuple-element.691), channel_id=1, source_target_pairs={{0,16},{1,17},{2,18},{3,19},{4,20},{5,21},{6,22},{7,23},{8,24},{9,... | collective-permute-start | bytes 1572872 | tf_op jit(solution)/shard_map/ppermute | solution.py:69
  124.0 31.7 %collective-permute-start.20 = (bf16[256,1024]{1,0:T(8,128)(2,1)S(1)}, bf16[256,1024]{1,0:T(8,128)(2,1)S(1)}, u32[]{:S(2)}, u32[]{:S(2)}) collective-permute-start(bf16[256,1024]{1,0:T(8,128)(2,1)S(1)} %get-tuple-element.321), channel_id=1, source_target_pairs={{0,16},{1,17},{2,18},{3,19},{4,20},{5,21},{6,22},{7,23},{8,24},{9,... | collective-permute-start | bytes 1572872 | tf_op jit(solution)/shard_map/ppermute | solution.py:69
  124.0 31.7 %collective-permute-start.21 = (bf16[2,64,2048]{2,1,0:T(8,128)(2,1)S(1)}, bf16[2,64,2048]{2,1,0:T(8,128)(2,1)S(1)}, u32[]{:S(2)}, u32[]{:S(2)}) collective-permute-start(bf16[2,64,2048]{2,1,0:T(8,128)(2,1)S(1)} %pad_maximum_fusion.24), channel_id=1, source_target_pairs={{0,4},{1,5},{2,6},{3,7},{4,0},{5,1},{6,2},{7,3},{8,12},{9,13},{10,... | collective-permute-start | bytes 1572872 | tf_op jit(solution)/shard_map/ppermute | solution.py:69
  125.0 22.3 %collective-permute-start.17 = (bf16[512,384]{1,0:T(8,128)(2,1)S(1)}, bf16[512,384]{1,0:T(8,128)(2,1)S(1)}, u32[]{:S(2)}, u32[]{:S(2)}) collective-permute-start(bf16[512,384]{1,0:T(8,128)(2,1)S(1)} %get-tuple-element.317), channel_id=1, source_target_pairs={{0,4},{1,5},{2,6},{3,7},{4,0},{5,1},{6,2},{7,3},{8,12},{9,13},{10,... | collective-permute-start | bytes 1179656 | tf_op jit(solution)/shard_map/ppermute | solution.py:69
  126.1 23.2 %collective-permute-start.18 = (bf16[512,384]{1,0:T(8,128)(2,1)S(1)}, bf16[512,384]{1,0:T(8,128)(2,1)S(1)}, u32[]{:S(2)}, u32[]{:S(2)}) collective-permute-start(bf16[512,384]{1,0:T(8,128)(2,1)S(1)} %get-tuple-element.318), channel_id=1, source_target_pairs={{0,8},{1,9},{2,10},{3,11},{4,12},{5,13},{6,14},{7,15},{8,0},{9,1},... | collective-permute-start | bytes 1179656 | tf_op jit(solution)/shard_map/ppermute | solution.py:69
  127.6 28.1 %collective-permute-start.19 = (bf16[512,384]{1,0:T(8,128)(2,1)S(1)}, bf16[512,384]{1,0:T(8,128)(2,1)S(1)}, u32[]{:S(2)}, u32[]{:S(2)}) collective-permute-start(bf16[512,384]{1,0:T(8,128)(2,1)S(1)} %get-tuple-element.319), channel_id=1, source_target_pairs={{0,12},{1,13},{2,14},{3,15},{4,8},{5,9},{6,10},{7,11},{8,4},{9,5},... | collective-permute-start | bytes 1179656 | tf_op jit(solution)/shard_map/ppermute | solution.py:69
  159.5 25.9 %collective-permute-start.27 = (bf16[128,2048]{1,0:T(8,128)(2,1)S(1)}, bf16[128,2048]{1,0:T(8,128)(2,1)S(1)}, u32[]{:S(2)}, u32[]{:S(2)}) collective-permute-start(bf16[128,2048]{1,0:T(8,128)(2,1)S(1)} %pad_maximum_fusion.26), channel_id=1, source_target_pairs={{0,2},{1,3},{2,0},{3,1},{4,6},{5,7},{6,4},{7,5},{8,10},{9,11},{10,... | collective-permute-start | bytes 1572872 | tf_op jit(solution)/shard_map/ppermute | solution.py:69
  161.7 24.9 %collective-permute-start.26 = (bf16[128,2048]{1,0:T(8,128)(2,1)S(1)}, bf16[128,2048]{1,0:T(8,128)(2,1)S(1)}, u32[]{:S(2)}, u32[]{:S(2)}) collective-permute-start(bf16[128,2048]{1,0:T(8,128)(2,1)S(1)} %pad_maximum_fusion.25), channel_id=1, source_target_pairs={{0,8},{1,9},{2,10},{3,11},{4,12},{5,13},{6,14},{7,15},{8,0},{9,1},... | collective-permute-start | bytes 1572872 | tf_op jit(solution)/shard_map/ppermute | solution.py:69
  161.8 26.5 %collective-permute-start.23 = (bf16[256,1024]{1,0:T(8,128)(2,1)}, bf16[256,1024]{1,0:T(8,128)(2,1)S(1)}, u32[]{:S(2)}, u32[]{:S(2)}) collective-permute-start(bf16[256,1024]{1,0:T(8,128)(2,1)} %slice.912), channel_id=1, source_target_pairs={{0,16},{1,17},{2,18},{3,19},{4,20},{5,21},{6,22},{7,23},{8,24},{9,... | collective-permute-start | bytes 1572872 | tf_op jit(solution)/shard_map/ppermute | solution.py:69
  163.6 24.7 %collective-permute-start.24 = (bf16[256,1024]{1,0:T(8,128)(2,1)S(1)}, bf16[256,1024]{1,0:T(8,128)(2,1)S(1)}, u32[]{:S(2)}, u32[]{:S(2)}) collective-permute-start(bf16[256,1024]{1,0:T(8,128)(2,1)S(1)} %copy-done.52), channel_id=1, source_target_pairs={{0,4},{1,5},{2,6},{3,7},{4,0},{5,1},{6,2},{7,3},{8,12},{9,13},{10,... | collective-permute-start | bytes 1572872 | tf_op jit(solution)/shard_map/ppermute | solution.py:69
  165.4 23.2 %collective-permute-start.25 = (bf16[256,1024]{1,0:T(8,128)(2,1)S(1)}, bf16[256,1024]{1,0:T(8,128)(2,1)S(1)}, u32[]{:S(2)}, u32[]{:S(2)}) collective-permute-start(bf16[256,1024]{1,0:T(8,128)(2,1)S(1)} %copy-done.54), channel_id=1, source_target_pairs={{0,4},{1,5},{2,6},{3,7},{4,0},{5,1},{6,2},{7,3},{8,12},{9,13},{10,... | collective-permute-start | bytes 1572872 | tf_op jit(solution)/shard_map/ppermute | solution.py:69
  208.3 20.1 %collective-permute-start.35 = (bf16[320,1024]{1,0:T(8,128)(2,1)S(1)}, bf16[320,1024]{1,0:T(8,128)(2,1)S(1)}, u32[]{:S(2)}, u32[]{:S(2)}) collective-permute-start(bf16[320,1024]{1,0:T(8,128)(2,1)S(1)} %slice.727), channel_id=1, source_target_pairs={{0,4},{1,5},{2,6},{3,7},{4,0},{5,1},{6,2},{7,3},{8,12},{9,13},{10,... | collective-permute-start | bytes 1966088 | tf_op jit(solution)/shard_map/ppermute | solution.py:69
  209.8 18.6 %collective-permute-start.33 = (bf16[2,48,2048]{2,1,0:T(8,128)(2,1)S(1)}, bf16[2,48,2048]{2,1,0:T(8,128)(2,1)S(1)}, u32[]{:S(2)}, u32[]{:S(2)}) collective-permute-start(bf16[2,48,2048]{2,1,0:T(8,128)(2,1)S(1)} %get-tuple-element.622), channel_id=1, source_target_pairs={{0,16},{1,17},{2,18},{3,19},{4,20},{5,21},{6,22},{7,23},{8,24},{9,... | collective-permute-start | bytes 1179656 | tf_op jit(solution)/shard_map/ppermute | solution.py:69
  209.9 18.5 %collective-permute-start.34 = (bf16[2,80,2048]{2,1,0:T(8,128)(2,1)S(1)}, bf16[2,80,2048]{2,1,0:T(8,128)(2,1)S(1)}, u32[]{:S(2)}, u32[]{:S(2)}) collective-permute-start(bf16[2,80,2048]{2,1,0:T(8,128)(2,1)S(1)} %pad_maximum_fusion.18), channel_id=1, source_target_pairs={{0,2},{1,3},{2,0},{3,1},{4,6},{5,7},{6,4},{7,5},{8,10},{9,11},{10,... | collective-permute-start | bytes 1966088 | tf_op jit(solution)/shard_map/ppermute | solution.py:69
  228.4 19.5 %collective-permute-start.39 = (bf16[2048,1024]{1,0:T(8,128)(2,1)S(1)}, bf16[2048,1024]{1,0:T(8,128)(2,1)S(1)}, u32[]{:S(2)}, u32[]{:S(2)}) collective-permute-start(bf16[2048,1024]{1,0:T(8,128)(2,1)S(1)} %constant_dynamic-update-slice_fusion.4), channel_id=1, source_target_pairs={{0,1},{1,0},{2,3},{3,2},{4,5},{5,4},{6,7},{7,6},{8,9},{9,8},{10,11... | collective-permute-start | bytes 12582920 | tf_op jit(solution)/shard_map/ppermute | solution.py:69
  229.5 17.1 %collective-permute-start.37 = (bf16[80,2048]{1,0:T(8,128)(2,1)S(1)}, bf16[80,2048]{1,0:T(8,128)(2,1)S(1)}, u32[]{:S(2)}, u32[]{:S(2)}) collective-permute-start(bf16[80,2048]{1,0:T(8,128)(2,1)S(1)} %fusion.42), channel_id=1, source_target_pairs={{0,16},{1,17},{2,18},{3,19},{4,20},{5,21},{6,22},{7,23},{8,24},{9,... | collective-permute-start | bytes 983048 | tf_op jit(solution)/shard_map/ppermute | solution.py:69
  229.6 17.2 %collective-permute-start.40 = (bf16[160,1024]{1,0:T(8,128)(2,1)S(1)}, bf16[160,1024]{1,0:T(8,128)(2,1)S(1)}, u32[]{:S(2)}, u32[]{:S(2)}) collective-permute-start(bf16[160,1024]{1,0:T(8,128)(2,1)S(1)} %slice.735), channel_id=1, source_target_pairs={{0,4},{1,5},{2,6},{3,7},{4,0},{5,1},{6,2},{7,3},{8,12},{9,13},{10,... | collective-permute-start | bytes 983048 | tf_op jit(solution)/shard_map/ppermute | solution.py:69
  230.4 17.4 %collective-permute-start.38 = (bf16[192,1024]{1,0:T(8,128)(2,1)S(1)}, bf16[192,1024]{1,0:T(8,128)(2,1)S(1)}, u32[]{:S(2)}, u32[]{:S(2)}) collective-permute-start(bf16[192,1024]{1,0:T(8,128)(2,1)S(1)} %slice.734), channel_id=1, source_target_pairs={{0,4},{1,5},{2,6},{3,7},{4,0},{5,1},{6,2},{7,3},{8,12},{9,13},{10,... | collective-permute-start | bytes 1179656 | tf_op jit(solution)/shard_map/ppermute | solution.py:69
  247.9 15.7 %collective-permute-start.43 = (bf16[128,1024]{1,0:T(8,128)(2,1)S(1)}, bf16[128,1024]{1,0:T(8,128)(2,1)S(1)}, u32[]{:S(2)}, u32[]{:S(2)}) collective-permute-start(bf16[128,1024]{1,0:T(8,128)(2,1)S(1)} %pad_maximum_fusion.38), channel_id=1, source_target_pairs={{0,4},{1,5},{2,6},{3,7},{4,0},{5,1},{6,2},{7,3},{8,12},{9,13},{10,... | collective-permute-start | bytes 786440 | tf_op jit(solution)/shard_map/ppermute | solution.py:69
  263.6 15.9 %collective-permute-start.46 = (bf16[128,2048]{1,0:T(8,128)(2,1)S(1)}, bf16[128,2048]{1,0:T(8,128)(2,1)S(1)}, u32[]{:S(2)}, u32[]{:S(2)}) collective-permute-start(bf16[128,2048]{1,0:T(8,128)(2,1)S(1)} %pad_maximum_fusion.29), channel_id=1, source_target_pairs={{0,2},{1,3},{2,0},{3,1},{4,6},{5,7},{6,4},{7,5},{8,10},{9,11},{10,... | collective-permute-start | bytes 1572872 | tf_op jit(solution)/shard_map/ppermute | solution.py:69
  308.2 18.0 %collective-permute-start.53 = (bf16[2,64,2048]{2,1,0:T(8,128)(2,1)}, bf16[2,64,2048]{2,1,0:T(8,128)(2,1)}, u32[]{:S(2)}, u32[]{:S(2)}) collective-permute-start(bf16[2,64,2048]{2,1,0:T(8,128)(2,1)} %pad_maximum_fusion.31), channel_id=1, source_target_pairs={{0,2},{1,3},{2,0},{3,1},{4,6},{5,7},{6,4},{7,5},{8,10},{9,11},{10,... | collective-permute-start | bytes 1572872 | tf_op jit(solution)/shard_map/ppermute | solution.py:69
  309.1 17.0 %collective-permute-start.52 = (bf16[2,64,2048]{2,1,0:T(8,128)(2,1)}, bf16[2,64,2048]{2,1,0:T(8,128)(2,1)}, u32[]{:S(2)}, u32[]{:S(2)}) collective-permute-start(bf16[2,64,2048]{2,1,0:T(8,128)(2,1)} %get-tuple-element.616), channel_id=1, source_target_pairs={{0,8},{1,9},{2,10},{3,11},{4,12},{5,13},{6,14},{7,15},{8,0},{9,1},... | collective-permute-start | bytes 1572872 | tf_op jit(solution)/shard_map/ppermute | solution.py:69
  328.4 16.1 %collective-permute-start.57 = (bf16[128,1024]{1,0:T(8,128)(2,1)S(1)}, bf16[128,1024]{1,0:T(8,128)(2,1)S(1)}, u32[]{:S(2)}, u32[]{:S(2)}) collective-permute-start(bf16[128,1024]{1,0:T(8,128)(2,1)S(1)} %fusion.41), channel_id=1, source_target_pairs={{0,16},{1,17},{2,18},{3,19},{4,20},{5,21},{6,22},{7,23},{8,24},{9,... | collective-permute-start | bytes 786440 | tf_op jit(solution)/shard_map/ppermute | solution.py:69
  344.5 21.7 %collective-permute-start.62 = (bf16[2048,1024]{1,0:T(8,128)(2,1)S(1)}, bf16[2048,1024]{1,0:T(8,128)(2,1)S(1)}, u32[]{:S(2)}, u32[]{:S(2)}) collective-permute-start(bf16[2048,1024]{1,0:T(8,128)(2,1)S(1)} %convolution_convert_fusion.1), channel_id=1, source_target_pairs={{0,1},{1,0},{2,3},{3,2},{4,5},{5,4},{6,7},{7,6},{8,9},{9,8},{10,11... | collective-permute-start | bytes 12582920 | tf_op jit(solution)/shard_map/ppermute | solution.py:69
  344.9 21.3 %collective-permute-start.61 = (bf16[320,1024]{1,0:T(8,128)(2,1)S(1)}, bf16[320,1024]{1,0:T(8,128)(2,1)S(1)}, u32[]{:S(2)}, u32[]{:S(2)}) collective-permute-start(bf16[320,1024]{1,0:T(8,128)(2,1)S(1)} %pad_maximum_fusion.19), channel_id=1, source_target_pairs={{0,4},{1,5},{2,6},{3,7},{4,0},{5,1},{6,2},{7,3},{8,12},{9,13},{10,... | collective-permute-start | bytes 1966088 | tf_op jit(solution)/shard_map/ppermute | solution.py:69
  349.1 17.1 %collective-permute-start.60 = (bf16[80,2048]{1,0:T(8,128)(2,1)S(1)}, bf16[80,2048]{1,0:T(8,128)(2,1)S(1)}, u32[]{:S(2)}, u32[]{:S(2)}) collective-permute-start(bf16[80,2048]{1,0:T(8,128)(2,1)S(1)} %slice.930.b), channel_id=1, source_target_pairs={{0,16},{1,17},{2,18},{3,19},{4,20},{5,21},{6,22},{7,23},{8,24},{9,... | collective-permute-start | bytes 983048 | tf_op jit(solution)/shard_map/ppermute | solution.py:69
  366.3 19.7 %collective-permute-start.63 = (bf16[96,2048]{1,0:T(8,128)(2,1)S(1)}, bf16[96,2048]{1,0:T(8,128)(2,1)S(1)}, u32[]{:S(2)}, u32[]{:S(2)}) collective-permute-start(bf16[96,2048]{1,0:T(8,128)(2,1)S(1)} %pad_maximum_fusion.37), channel_id=1, source_target_pairs={{0,16},{1,17},{2,18},{3,19},{4,20},{5,21},{6,22},{7,23},{8,24},{9,... | collective-permute-start | bytes 1179656 | tf_op jit(solution)/shard_map/ppermute | solution.py:69
  366.4 19.6 %collective-permute-start.64 = (bf16[160,2048]{1,0:T(8,128)(2,1)S(1)}, bf16[160,2048]{1,0:T(8,128)(2,1)S(1)}, u32[]{:S(2)}, u32[]{:S(2)}) collective-permute-start(bf16[160,2048]{1,0:T(8,128)(2,1)S(1)} %pad_maximum_fusion.20), channel_id=1, source_target_pairs={{0,2},{1,3},{2,0},{3,1},{4,6},{5,7},{6,4},{7,5},{8,10},{9,11},{10,... | collective-permute-start | bytes 1966088 | tf_op jit(solution)/shard_map/ppermute | solution.py:69
  367.5 19.2 %collective-permute-start.65 = (bf16[384,1024]{1,0:T(8,128)(2,1)S(1)}, bf16[384,1024]{1,0:T(8,128)(2,1)S(1)}, u32[]{:S(2)}, u32[]{:S(2)}) collective-permute-start(bf16[384,1024]{1,0:T(8,128)(2,1)S(1)} %slice_bitcast_fusion.5), channel_id=1, source_target_pairs={{0,4},{1,5},{2,6},{3,7},{4,0},{5,1},{6,2},{7,3},{8,12},{9,13},{10,... | collective-permute-start | bytes 2359304 | tf_op jit(solution)/shard_map/ppermute | solution.py:69
  403.3 27.3 %collective-permute-start.71 = (bf16[320,1024]{1,0:T(8,128)(2,1)S(1)}, bf16[320,1024]{1,0:T(8,128)(2,1)S(1)}, u32[]{:S(2)}, u32[]{:S(2)}) collective-permute-start(bf16[320,1024]{1,0:T(8,128)(2,1)S(1)} %fusion.22), channel_id=1, source_target_pairs={{0,16},{1,17},{2,18},{3,19},{4,20},{5,21},{6,22},{7,23},{8,24},{9,... | collective-permute-start | bytes 1966088 | tf_op jit(solution)/shard_map/ppermute | solution.py:69
  404.6 23.2 %collective-permute-start.73 = (bf16[2,64,2048]{2,1,0:T(8,128)(2,1)S(1)}, bf16[2,64,2048]{2,1,0:T(8,128)(2,1)S(1)}, u32[]{:S(2)}, u32[]{:S(2)}) collective-permute-start(bf16[2,64,2048]{2,1,0:T(8,128)(2,1)S(1)} %pad_maximum_fusion.34), channel_id=1, source_target_pairs={{0,2},{1,3},{2,0},{3,1},{4,6},{5,7},{6,4},{7,5},{8,10},{9,11},{10,... | collective-permute-start | bytes 1572872 | tf_op jit(solution)/shard_map/ppermute | solution.py:69
  405.6 22.2 %collective-permute-start.72 = (bf16[2,64,2048]{2,1,0:T(8,128)(2,1)S(1)}, bf16[2,64,2048]{2,1,0:T(8,128)(2,1)S(1)}, u32[]{:S(2)}, u32[]{:S(2)}) collective-permute-start(bf16[2,64,2048]{2,1,0:T(8,128)(2,1)S(1)} %get-tuple-element.610), channel_id=1, source_target_pairs={{0,8},{1,9},{2,10},{3,11},{4,12},{5,13},{6,14},{7,15},{8,0},{9,1},... | collective-permute-start | bytes 1572872 | tf_op jit(solution)/shard_map/ppermute | solution.py:69
  405.8 24.8 %collective-permute-start.70 = (bf16[512,1024]{1,0:T(8,128)(2,1)S(1)}, bf16[512,1024]{1,0:T(8,128)(2,1)S(1)}, u32[]{:S(2)}, u32[]{:S(2)}) collective-permute-start(bf16[512,1024]{1,0:T(8,128)(2,1)S(1)} %slice_bitcast_fusion), channel_id=1, source_target_pairs={{0,4},{1,5},{2,6},{3,7},{4,0},{5,1},{6,2},{7,3},{8,12},{9,13},{10,... | collective-permute-start | bytes 3145736 | tf_op jit(solution)/shard_map/ppermute | solution.py:69
  407.1 20.1 %collective-permute-start.74 = (bf16[4,64,2048]{2,1,0:T(8,128)(2,1)S(1)}, bf16[4,64,2048]{2,1,0:T(8,128)(2,1)S(1)}, u32[]{:S(2)}, u32[]{:S(2)}) collective-permute-start(bf16[4,64,2048]{2,1,0:T(8,128)(2,1)S(1)} %broadcast_select_fusion), channel_id=1, source_target_pairs={{0,1},{1,0},{2,3},{3,2},{4,5},{5,4},{6,7},{7,6},{8,9},{9,8},{10,11... | collective-permute-start | bytes 3145736 | tf_op jit(solution)/shard_map/ppermute | solution.py:69
  434.1 21.4 %collective-permute-start.78 = (bf16[512,384]{1,0:T(8,128)(2,1)S(1)}, bf16[512,384]{1,0:T(8,128)(2,1)S(1)}, u32[]{:S(2)}, u32[]{:S(2)}) collective-permute-start(bf16[512,384]{1,0:T(8,128)(2,1)S(1)} %get-tuple-element.638), channel_id=1, source_target_pairs={{0,12},{1,13},{2,14},{3,15},{4,8},{5,9},{6,10},{7,11},{8,4},{9,5},... | collective-permute-start | bytes 1179656 | tf_op jit(solution)/shard_map/ppermute | solution.py:69
  434.2 29.0 %collective-permute-start.77 = (bf16[512,384]{1,0:T(8,128)(2,1)S(1)}, bf16[512,384]{1,0:T(8,128)(2,1)S(1)}, u32[]{:S(2)}, u32[]{:S(2)}) collective-permute-start(bf16[512,384]{1,0:T(8,128)(2,1)S(1)} %get-tuple-element.639), channel_id=1, source_target_pairs={{0,8},{1,9},{2,10},{3,11},{4,12},{5,13},{6,14},{7,15},{8,0},{9,1},... | collective-permute-start | bytes 1179656 | tf_op jit(solution)/shard_map/ppermute | solution.py:69
  437.1 26.0 %collective-permute-start.76 = (bf16[512,384]{1,0:T(8,128)(2,1)S(1)}, bf16[512,384]{1,0:T(8,128)(2,1)S(1)}, u32[]{:S(2)}, u32[]{:S(2)}) collective-permute-start(bf16[512,384]{1,0:T(8,128)(2,1)S(1)} %get-tuple-element.640), channel_id=1, source_target_pairs={{0,4},{1,5},{2,6},{3,7},{4,0},{5,1},{6,2},{7,3},{8,12},{9,13},{10,... | collective-permute-start | bytes 1179656 | tf_op jit(solution)/shard_map/ppermute | solution.py:69
  437.6 25.5 %collective-permute-start.79 = (bf16[192,1024]{1,0:T(8,128)(2,1)S(1)}, bf16[192,1024]{1,0:T(8,128)(2,1)S(1)}, u32[]{:S(2)}, u32[]{:S(2)}) collective-permute-start(bf16[192,1024]{1,0:T(8,128)(2,1)S(1)} %slice.941), channel_id=1, source_target_pairs={{0,16},{1,17},{2,18},{3,19},{4,20},{5,21},{6,22},{7,23},{8,24},{9,... | collective-permute-start | bytes 1179656 | tf_op jit(solution)/shard_map/ppermute | solution.py:69
  479.1 22.5 %collective-permute-start.86 = (bf16[192,1024]{1,0:T(8,128)(2,1)S(1)}, bf16[192,1024]{1,0:T(8,128)(2,1)S(1)}, u32[]{:S(2)}, u32[]{:S(2)}) collective-permute-start(bf16[192,1024]{1,0:T(8,128)(2,1)S(1)} %slice.809), channel_id=1, source_target_pairs={{0,16},{1,17},{2,18},{3,19},{4,20},{5,21},{6,22},{7,23},{8,24},{9,... | collective-permute-start | bytes 1179656 | tf_op jit(solution)/shard_map/ppermute | solution.py:69
  480.6 20.9 %collective-permute-start.85 = (bf16[256,1024]{1,0:T(8,128)(2,1)S(1)}, bf16[256,1024]{1,0:T(8,128)(2,1)S(1)}, u32[]{:S(2)}, u32[]{:S(2)}) collective-permute-start(bf16[256,1024]{1,0:T(8,128)(2,1)S(1)} %get-tuple-element.515), channel_id=1, source_target_pairs={{0,4},{1,5},{2,6},{3,7},{4,0},{5,1},{6,2},{7,3},{8,12},{9,13},{10,... | collective-permute-start | bytes 1572872 | tf_op jit(solution)/shard_map/ppermute | solution.py:69
  481.2 19.3 %collective-permute-start.87 = (bf16[4,64,1024]{2,1,0:T(8,128)(2,1)S(1)}, bf16[4,64,1024]{2,1,0:T(8,128)(2,1)S(1)}, u32[]{:S(2)}, u32[]{:S(2)}) collective-permute-start(bf16[4,64,1024]{2,1,0:T(8,128)(2,1)S(1)} %get-tuple-element.519), channel_id=1, source_target_pairs={{0,8},{1,9},{2,10},{3,11},{4,12},{5,13},{6,14},{7,15},{8,0},{9,1},... | collective-permute-start | bytes 1572872 | tf_op jit(solution)/shard_map/ppermute | solution.py:69
  483.0 17.6 %collective-permute-start.84 = (bf16[2048,768]{1,0:T(8,128)(2,1)S(1)}, bf16[2048,768]{1,0:T(8,128)(2,1)S(1)}, u32[]{:S(2)}, u32[]{:S(2)}) collective-permute-start(bf16[2048,768]{1,0:T(8,128)(2,1)S(1)} %convolution_convert_fusion.5), channel_id=1, source_target_pairs={{0,1},{1,0},{2,3},{3,2},{4,5},{5,4},{6,7},{7,6},{8,9},{9,8},{10,11... | collective-permute-start | bytes 9437192 | tf_op jit(solution)/shard_map/ppermute | solution.py:69
  503.1 17.9 %collective-permute-start.91 = (bf16[4,64,1024]{2,1,0:T(8,128)(2,1)S(1)}, bf16[4,64,1024]{2,1,0:T(8,128)(2,1)S(1)}, u32[]{:S(2)}, u32[]{:S(2)}) collective-permute-start(bf16[4,64,1024]{2,1,0:T(8,128)(2,1)S(1)} %get-tuple-element.530), channel_id=1, source_target_pairs={{0,8},{1,9},{2,10},{3,11},{4,12},{5,13},{6,14},{7,15},{8,0},{9,1},... | collective-permute-start | bytes 1572872 | tf_op jit(solution)/shard_map/ppermute | solution.py:69
  503.5 17.7 %collective-permute-start.92 = (bf16[2,2,64,1024]{3,2,0,1:T(8,128)(2,1)S(1)}, bf16[2,2,64,1024]{3,2,0,1:T(8,128)(2,1)S(1)}, u32[]{:S(2)}, u32[]{:S(2)}) collective-permute-start(bf16[2,2,64,1024]{3,2,0,1:T(8,128)(2,1)S(1)} %fusion.37), channel_id=1, source_target_pairs={{0,2},{1,3},{2,0},{3,1},{4,6},{5,7},{6,4},{7,5},{8,10},{9,11},{10,... | collective-permute-start | bytes 1572872 | tf_op jit(solution)/shard_map/ppermute | solution.py:69
  504.6 16.7 %collective-permute-start.89 = (bf16[2,48,2048]{2,1,0:T(8,128)(2,1)S(1)}, bf16[2,48,2048]{2,1,0:T(8,128)(2,1)S(1)}, u32[]{:S(2)}, u32[]{:S(2)}) collective-permute-start(bf16[2,48,2048]{2,1,0:T(8,128)(2,1)S(1)} %get-tuple-element.604), channel_id=1, source_target_pairs={{0,16},{1,17},{2,18},{3,19},{4,20},{5,21},{6,22},{7,23},{8,24},{9,... | collective-permute-start | bytes 1179656 | tf_op jit(solution)/shard_map/ppermute | solution.py:69
  507.0 22.3 %collective-permute-start.90 = (bf16[2,80,2048]{2,1,0:T(8,128)(2,1)S(1)}, bf16[2,80,2048]{2,1,0:T(8,128)(2,1)S(1)}, u32[]{:S(2)}, u32[]{:S(2)}) collective-permute-start(bf16[2,80,2048]{2,1,0:T(8,128)(2,1)S(1)} %pad_maximum_fusion.22), channel_id=1, source_target_pairs={{0,2},{1,3},{2,0},{3,1},{4,6},{5,7},{6,4},{7,5},{8,10},{9,11},{10,... | collective-permute-start | bytes 1966088 | tf_op jit(solution)/shard_map/ppermute | solution.py:69
  508.9 20.4 %collective-permute-start.88 = (bf16[512,768]{1,0:T(8,128)(2,1)S(1)}, bf16[512,768]{1,0:T(8,128)(2,1)S(1)}, u32[]{:S(2)}, u32[]{:S(2)}) collective-permute-start(bf16[512,768]{1,0:T(8,128)(2,1)S(1)} %slice_bitcast_fusion.4), channel_id=1, source_target_pairs={{0,4},{1,5},{2,6},{3,7},{4,0},{5,1},{6,2},{7,3},{8,12},{9,13},{10,... | collective-permute-start | bytes 2359304 | tf_op jit(solution)/shard_map/ppermute | solution.py:69
  535.4 18.4 %collective-permute-start.93 = (bf16[512,768]{1,0:T(8,128)(2,1)S(1)}, bf16[512,768]{1,0:T(8,128)(2,1)S(1)}, u32[]{:S(2)}, u32[]{:S(2)}) collective-permute-start(bf16[512,768]{1,0:T(8,128)(2,1)S(1)} %fusion.21), channel_id=1, source_target_pairs={{0,8},{1,9},{2,10},{3,11},{4,12},{5,13},{6,14},{7,15},{8,0},{9,1},... | collective-permute-start | bytes 2359304 | tf_op jit(solution)/shard_map/ppermute | solution.py:69
  555.0 30.4 %all-to-all-start.1 = ((bf16[8,64,768]{2,1,0:T(8,128)(2,1)}), bf16[8,64,768]{2,1,0:T(8,128)(2,1)S(1)}, u32[]{:S(2)}, u32[]{:S(2)}) async-start(bf16[8,64,768]{2,1,0:T(8,128)(2,1)} %bitcast.122), calls=%async_computation.1 | async-start | bytes 1572864 | tf_op jit(solution)/shard_map/all_to_all | solution.py:583
  (134 other events, 1132.4 us)
